TPU v7x, 32 devices: a whole 2x2x4 slice. The times are simulated.
32 devices in a mesh: rep: 4 (over x, core), tm: 8 (over z, y).
Axes of the slice: x: 2, y: 2, z: 4, core: 2. Of those that a mesh axis runs over, the one named last changes fastest.
Arguments:
- frames: bfloat16 [4, 32768, 512], P('rep', 'tm'), may hold values from -20 to 20
- first_weight: bfloat16 [2, 512, 512], replicated, may hold values from -0.1875 to 0.1875
- first_bias: float32 [512], replicated, may hold values from -4 to 4
- second_weight: bfloat16 [2, 512, 256], replicated, may hold values from -0.1875 to 0.1875
Outputs:
- propagated: float32 [4, 32768, 256], P('rep', 'tm')
- residual: float32 [4, 32768, 256], P('rep', 'tm')
All inputs are finite; a program needn't handle non-finite values.
Results may differ from a plain program's by a relative error of at most 0.008.
Values may be sent and summed in bfloat16 or wider, within the bound.
No kernel may reach another device: no remote copies, remote signals or barrier semaphores. Data moves between devices by JAX's collectives and lax.ppermute only.
A program may use at most 64 MiB of HBM per device.

v0:
```python
import jax
import jax.numpy as jnp
from jax import lax
from jax.sharding import PartitionSpec as P

FEAT = 256
D1 = 32
D2 = 256
LAG = 1024


ridge_level = 0.001


def passed_along(value, axis, steps):
    count = lax.axis_size(axis)
    first, last = (max(0, -steps), min(count, count - steps))
    return lax.ppermute(value, axis, [(source, source + steps) for source in range(first, last)])


def layer_pair(current, previous, weights):
    return jnp.dot(current, weights[0], preferred_element_type=jnp.float32) + jnp.dot(
        previous, weights[1], preferred_element_type=jnp.float32
    )


def outer_scaled(vector, factor):
    return factor * (vector[:, None] * vector[None, :])


def on_device(frames, first_weight, first_bias, second_weight):
    frame_block = frames[0]
    row_count = frame_block.shape[0]
    tm_index = lax.axis_index("tm")
    tm_count = lax.axis_size("tm")
    before = passed_along(frame_block[row_count - D1 :], "tm", 1)
    earlier_frames = jnp.concatenate([before, frame_block[: row_count - D1]], 0)
    hidden = jax.nn.silu(layer_pair(frame_block, earlier_frames, first_weight) + first_bias).astype(
        jnp.bfloat16
    )
    earlier = passed_along(hidden[row_count - D2 :], "tm", 1)
    earlier_hidden = jnp.concatenate([earlier, hidden[: row_count - D2]], 0)
    feature = layer_pair(hidden, earlier_hidden, second_weight).astype(jnp.bfloat16)
    ahead_rows = passed_along(feature[:LAG], "tm", -1)
    valid_rows = jnp.where(tm_index == tm_count - 1, row_count - LAG, row_count)
    keep_mask = (jnp.arange(row_count) < valid_rows)[:, None]
    lagged = jnp.concatenate([feature[LAG:], ahead_rows], 0)
    paired = jnp.where(
        keep_mask, jnp.concatenate([feature, lagged], 1), jnp.zeros((), jnp.bfloat16)
    )
    gram_full = lax.dot_general(
        paired, paired, (((0,), (0,)), ((), ())), preferred_element_type=jnp.float32
    )
    second = gram_full[:FEAT, :FEAT] + gram_full[FEAT:, FEAT:]
    cross_sum = gram_full[:FEAT, FEAT:] + gram_full[FEAT:, :FEAT]
    column_sums = jnp.sum(paired, axis=0, dtype=jnp.float32)
    feature_sum = column_sums[:FEAT] + column_sums[FEAT:]
    pair_count = valid_rows.astype(jnp.float32)
    total_count, sum_all, second_all, cross_all = lax.psum(
        (pair_count, feature_sum, second, cross_sum), ("rep", "tm")
    )
    mean_vec = sum_all / (2.0 * total_count)
    centre = outer_scaled(mean_vec, 2.0 * total_count)
    inst_moment = second_all - centre
    lag_moment = cross_all - centre
    identity = jnp.eye(FEAT, dtype=jnp.float32)
    factor = jnp.linalg.cholesky(inst_moment / (2.0 * total_count) + ridge_level * identity)
    inverse = lax.linalg.triangular_solve(factor, identity, left_side=True, lower=True)
    half_step = jnp.dot(inverse, lag_moment / (2.0 * total_count), precision=lax.Precision.HIGHEST)
    koopman = jnp.dot(half_step, inverse.T, precision=lax.Precision.HIGHEST)
    stacked = jnp.concatenate([feature, ahead_rows], 0).astype(jnp.float32) - mean_vec
    whitened = jnp.dot(stacked, inverse.T, precision=lax.Precision.HIGHEST)
    propagated = jnp.dot(whitened[:row_count], koopman.T, precision=lax.Precision.HIGHEST)
    residual = jnp.where(keep_mask, whitened[LAG:] - propagated, jnp.zeros((), jnp.float32))
    return (propagated[None], residual[None])


def solution(mesh):
    placed = (P("rep", "tm", None), P(), P(), P())
    return jax.shard_map(
        on_device,
        mesh=mesh,
        in_specs=placed,
        out_specs=(P("rep", "tm", None), P("rep", "tm", None)),
        check_vma=False,
    )
```

profile of v0, /device:TPU:0, one launch (start us, length us, event | category | flops | bytes accessed | tf_op | source)
XLA Modules:
  0.0 273.4 jit_solution(13074566178308913507)
XLA Ops:
  7.2 0.9 slice_bitcast_fusion.5
  8.1 5.0 %collective-permute-start = (bf16[32,512]{1,0:T(8,128)(2,1)S(1)}, bf16[32,512]{1,0:T(8,128)(2,1)S(1)}, u32[]{:S(2)}, u32[]{:S(2)}) collective-permute-start(bf16[32,512]{1,0:T(8,128)(2,1)S(1)} %slice_bitcast_fusion.5), channel_id=1, source_target_pairs={{0,1},{1,2},{2,3},{3,4},{4,5},{5,6},{6,7},{8,9},{9,10},{10,11},{11... | collective-permute-start | bytes 98312 | tf_op jit(solution)/shard_map/ppermute | solution.py:18
  13.1 2.4 slice_bitcast_fusion
  15.6 2.3 fusion.14
  18.0 4.1 %multiply_convert_fusion = bf16[4096,512]{1,0:T(8,128)(2,1)S(1)} fusion(f32[4096,512]{1,0:T(8,128)S(1)} %fusion.14, bf16[4064,512]{1,0:T(8,128)(2,1)S(1)} %slice_bitcast_fusion, bf16[32,512]{1,0:T(8,128)(2,1)S(1)} %collective-permute-done, f32[512]{0:T(512)S(1)} %copy-done.5, bf16[2,512,512]{2,1,0:T(8,128)(2,1)S(1)} %copy-done.2), kind=kOutput, calls=%fused_computation.3 | convolution fusion | flops 2170552320 | bytes 17303552 | tf_op jit(solution)/shard_map/dot_general | solution.py:22
  22.4 3.4 %collective-permute-start.1 = (bf16[256,512]{1,0:T(8,128)(2,1)S(1)}, bf16[256,512]{1,0:T(8,128)(2,1)S(1)}, u32[]{:S(2)}, u32[]{:S(2)}) collective-permute-start(bf16[256,512]{1,0:T(8,128)(2,1)S(1)} %slice.134), channel_id=1, source_target_pairs={{0,1},{1,2},{2,3},{3,4},{4,5},{5,6},{6,7},{8,9},{9,10},{10,11},{11... | collective-permute-start | bytes 786440 | tf_op jit(solution)/shard_map/ppermute | solution.py:18
  25.8 1.2 fusion.26
  27.1 4.0 %collective-permute-done.1 = bf16[256,512]{1,0:T(8,128)(2,1)S(1)} collective-permute-done((bf16[256,512]{1,0:T(8,128)(2,1)S(1)}, bf16[256,512]{1,0:T(8,128)(2,1)S(1)}, u32[]{:S(2)}, u32[]{:S(2)}) %collective-permute-start.1) | collective-permute-done | bytes 262176 | tf_op jit(solution)/shard_map/ppermute | solution.py:18
  31.1 1.3 fusion.3
  32.4 1.3 collective-permute-start.2
  33.9 13.6 %collective-permute-done.2 = bf16[1024,256]{1,0:T(8,128)(2,1)S(1)} collective-permute-done((bf16[1024,256]{1,0:T(8,128)(2,1)S(1)}, bf16[1024,256]{1,0:T(8,128)(2,1)S(1)}, u32[]{:S(2)}, u32[]{:S(2)}) %collective-permute-start.2) | collective-permute-done | bytes 524320 | tf_op jit(solution)/shard_map/ppermute | solution.py:18
  47.5 7.3 %convert_reduce_fusion = (f32[512]{0:T(512)S(1)}, bf16[4096,512]{1,0:T(8,128)(2,1)S(1)}) fusion(bf16[1024,256]{1,0:T(8,128)(2,1)S(1)} %collective-permute-done.2, bf16[3072,256]{1,0:T(8,128)(2,1)S(1)} %slice.137, bf16[4096,256]{1,0:T(8,128)(2,1)S(1)} %fusion.3, pred[4096]{0:T(1024)(128)(4,1)S(1)} %iota_compare_fusion.4), kind=kLoop, calls=%fused_computation.2 | loop fusion | flops 18873856 | bytes 8394752 | tf_op jit(solution)/shard_map/reduce_sum | solution.py:56
  54.8 2.4 fusion.51
  57.2 0.9 slice_add_fusion.1
  58.1 42.1 %all-reduce.1 = (f32[256]{0:T(256)S(1)}, f32[]{:T(128)}) all-reduce(f32[256]{0:T(256)S(1)} %slice_add_fusion.2, f32[]{:T(128)S(6)} %convert_element_type.20), channel_id=1, replica_groups=mesh['rep'=4,'tm'=8] {'rep','tm'}, use_global_device_ids=true, to_apply=%region_1.2 | all-reduce | flops 257 | bytes 2056 | tf_op jit(solution)/shard_map/psum | solution.py:59
  100.9 87.0 %all-reduce.5.cloned.1.call-done = (f32[256,256]{0,1:T(8,128)}, f32[256,256]{0,1:T(8,128)}) async-done(((f32[256,256]{0,1:T(8,128)}, f32[256,256]{0,1:T(8,128)}), (f32[256,256]{0,1:T(8,128)}, f32[256,256]{0,1:T(8,128)})) %all-reduce.5.cloned.1.call-update) | async-done | bytes 524304 | tf_op jit(solution)/shard_map/psum | solution.py:59
  187.8 1.1 select_add_fusion
  189.0 1.1 fusion.24
  190.1 11.7 %cholesky.49 = f32[128,128]{1,0:T(8,128)S(1)} custom-call(f32[128,128]{1,0:T(8,128)S(1)} %cholesky.115), custom_call_target="Cholesky" | custom-call | tf_op jit(solution)/shard_map/jit(cholesky)/cholesky | solution.py:67
  201.9 9.8 %custom-call.14 = f32[1,128,128]{1,2,0:T(8,128)S(1)} custom-call(f32[1,128,128]{2,1,0:T(8,128)S(1)} %get-tuple-element.33), custom_call_target="InvertDiagBlocksLowerTriangular" | custom-call | tf_op jit(solution)/shard_map/jit(cholesky)/cholesky | solution.py:67
  212.2 11.7 %cholesky.103 = f32[128,128]{1,0:T(8,128)S(1)} custom-call(f32[128,128]{1,0:T(8,128)S(1)} %convolution_subtract_fusion.1), custom_call_target="Cholesky" | custom-call | tf_op jit(solution)/shard_map/jit(cholesky)/cholesky | solution.py:67
  224.2 0.6 compare_reduce_fusion
  226.4 5.4 %while.1 = (s32[]{:T(128)}, f32[256,256]{0,1:T(8,128)S(1)}, s32[2,2]{1,0:T(2,128)S(1)}, f32[2,128,128]{2,1,0:T(8,128)}, s32[]{:T(128)}) while((s32[]{:T(128)}, f32[256,256]{0,1:T(8,128)S(1)}, s32[2,2]{1,0:T(2,128)S(1)}, f32[2,128,128]{2,1,0:T(8,128)}, s32[]{:T(128)}) %tuple.28), condition=%wide.while_cond, body=%wide.while_body.sunk | while | flops 2 | bytes 393829 | solution.py:68
  226.4 0.6 fusion.62
  226.9 1.4 dynamic-slice.7
  228.4 0.6 bitcast_dynamic-update-slice_fusion.2
  229.7 1.4 dynamic-slice.7
  231.2 0.6 bitcast_dynamic-update-slice_fusion.2
  231.8 20.5 %custom-call.15 = f32[2,128,128]{1,2,0:T(8,128)S(1)} custom-call(f32[2,128,128]{2,1,0:T(8,128)} %get-tuple-element.9), custom_call_target="InvertDiagBlocksLowerTriangular" | custom-call | tf_op jit(solution)/shard_map/triangular_solve | solution.py:68
  254.2 4.6 %fusion = f32[5120,256]{1,0:T(8,128)S(1)} fusion(bf16[1024,256]{1,0:T(8,128)(2,1)S(1)} %collective-permute-done.2, bf16[4096,256]{1,0:T(8,128)(2,1)S(1)} %fusion.3, f32[256]{0:T(256)S(1)} %broadcast_divide_fusion, f32[128,256]{1,0:T(8,128)S(1)} %fusion.40, f32[128,256]{1,0:T(8,128)S(1)} %fusion.37), kind=kOutput, calls=%fused_computation.5 | convolution fusion | flops 4033150976 | bytes 8127488 | tf_op jit(solution)/shard_map/dot_general | solution.py:72
  258.8 3.7 %fusion.6 = f32[4096,256]{1,0:T(8,128)S(1)} fusion(f32[256,256]{1,0:T(8,128)S(1)} %fusion.33, f32[5120,256]{1,0:T(8,128)S(1)} %fusion), kind=kOutput, calls=%fused_computation.12 | convolution fusion | flops 3221225472 | bytes 8650752 | tf_op jit(solution)/shard_map/dot_general | solution.py:73
  262.5 4.0 %fusion.5 = f32[1,4096,256]{2,1,0:T(8,128)} fusion(f32[4096,256]{1,0:T(8,128)S(1)} %fusion.6, f32[5120,256]{1,0:T(8,128)S(1)} %fusion, pred[4096]{0:T(1024)(128)(4,1)S(1)} %iota_compare_fusion.4), kind=kLoop, calls=%fused_computation.11 | loop fusion | flops 2097152 | bytes 12587008 | tf_op jit(solution)/shard_map/broadcast_in_dim | solution.py:75
  (49 shorter events, 4.3 us)
Async XLA Ops:
  7.2 8.4 %copy-start.2 = (bf16[2,512,512]{2,1,0:T(8,128)(2,1)S(1)}, bf16[2,512,512]{2,1,0:T(8,128)(2,1)}, u32[]{:S(2)}) copy-start(bf16[2,512,512]{2,1,0:T(8,128)(2,1)} %param.5) | copy-start | bytes 3145732
  7.2 180.7 %all-reduce.5.cloned.1.call-start = ((), (), s32[]{:S(2)}) async-start(), calls=%async_computation | async-start | bytes 1048576 | tf_op jit(solution)/shard_map/psum | solution.py:59
  7.2 8.4 %copy-start = (bf16[1,4096,512]{2,1,0:T(8,128)(2,1)S(1)}, bf16[1,4096,512]{2,1,0:T(8,128)(2,1)}, u32[]{:S(2)}) copy-start(bf16[1,4096,512]{2,1,0:T(8,128)(2,1)} %param.4) | copy-start | bytes 12582916
  8.1 9.8 %collective-permute-start = (bf16[32,512]{1,0:T(8,128)(2,1)S(1)}, bf16[32,512]{1,0:T(8,128)(2,1)S(1)}, u32[]{:S(2)}, u32[]{:S(2)}) collective-permute-start(bf16[32,512]{1,0:T(8,128)(2,1)S(1)} %slice_bitcast_fusion.5), channel_id=1, source_target_pairs={{0,1},{1,2},{2,3},{3,4},{4,5},{5,6},{6,7},{8,9},{9,10},{10,11},{11... | collective-permute-start | bytes 98312 | tf_op jit(solution)/shard_map/ppermute | solution.py:18
  15.6 2.4 copy-start.5
  22.1 3.7 %copy-start.3 = (bf16[2,512,256]{2,1,0:T(8,128)(2,1)S(1)}, bf16[2,512,256]{2,1,0:T(8,128)(2,1)}, u32[]{:S(2)}) copy-start(bf16[2,512,256]{2,1,0:T(8,128)(2,1)} %param.7) | copy-start | bytes 1572868
  22.4 8.7 %collective-permute-start.1 = (bf16[256,512]{1,0:T(8,128)(2,1)S(1)}, bf16[256,512]{1,0:T(8,128)(2,1)S(1)}, u32[]{:S(2)}, u32[]{:S(2)}) collective-permute-start(bf16[256,512]{1,0:T(8,128)(2,1)S(1)} %slice.134), channel_id=1, source_target_pairs={{0,1},{1,2},{2,3},{3,4},{4,5},{5,6},{6,7},{8,9},{9,10},{10,11},{11... | collective-permute-start | bytes 786440 | tf_op jit(solution)/shard_map/ppermute | solution.py:18
  32.4 15.1 %collective-permute-start.2 = (bf16[1024,256]{1,0:T(8,128)(2,1)S(1)}, bf16[1024,256]{1,0:T(8,128)(2,1)S(1)}, u32[]{:S(2)}, u32[]{:S(2)}) collective-permute-start(bf16[1024,256]{1,0:T(8,128)(2,1)S(1)} %slice.136), channel_id=1, source_target_pairs={{1,0},{2,1},{3,2},{4,3},{5,4},{6,5},{7,6},{9,8},{10,9},{11,10},{12... | collective-permute-start | bytes 1572872 | tf_op jit(solution)/shard_map/ppermute | solution.py:18
  190.1 63.2 %copy-start.4 = (f32[256,256]{0,1:T(8,128)S(1)}, f32[256,256]{0,1:T(8,128)}, u32[]{:S(2)}) copy-start(f32[256,256]{0,1:T(8,128)} %get-tuple-element.24) | copy-start | bytes 786436
  262.5 4.0 %copy-start.1 = (f32[4096,256]{1,0:T(8,128)}, f32[4096,256]{1,0:T(8,128)S(1)}, u32[]{:S(2)}) copy-start(f32[4096,256]{1,0:T(8,128)S(1)} %fusion.6) | copy-start | bytes 12582916
Sparse Core Ops, SparseCore 0:
  58.2 129.5 all-reduce.4
where the time goes:
time: 274 us; the launch traced here: 273 us
  waiting for transfers between devices  105 us (38%)
  other arithmetic  68.9 us (25%)
  blocking collectives  42.1 us (15%)
  matrix products  21.9 us (8%)
  between operations  16.4 us (6%)
  starting transfers between devices  9.75 us (4%)
  local copies, waits for them, and re-layouts  9.74 us (4%)
    psum x1, waiting for transfers between devices, on_device(): lax.psum((pair_count, feature_sum, second, cross_sum), ('rep', 'tm'))  87 us
    psum x1, blocking collectives, on_device(): lax.psum((pair_count, feature_sum, second, cross_sum), ('rep', 'tm'))  42.1 us
    another operation x6, other arithmetic, on_device(): jnp.linalg.cholesky(inst_moment / (2.0 * total_count) + ridge_level * ide...  34 us
    another operation x3, other arithmetic, on_device(): lax.linalg.triangular_solve(factor, identity, left_side=True, lower=True)  20.5 us
    ppermute x3, waiting for transfers between devices, passed_along(): lax.ppermute(value, axis, [(source, source + steps) for source in range(f...  17.6 us
    ppermute x3, starting transfers between devices, passed_along(): lax.ppermute(value, axis, [(source, source + steps) for source in range(f...  9.72 us
    reduce_sum x1, other arithmetic, on_device(): column_sums = jnp.sum(paired, axis=0, dtype=jnp.float32)  7.32 us
  transfers between devices with their start and end apart: 4, of which 3 were waited for; matrix products, arithmetic and copies ran while one was open for 2% of the time, Pallas kernels for 0%

commit v1 on v0

v1 whole, which is shorter than its diff:
```python
from functools import partial

import jax
import jax.numpy as jnp
from jax import lax
from jax.experimental import pallas as pl
from jax.experimental.pallas import tpu as pltpu
from jax.sharding import PartitionSpec as P

D1 = 32
D2 = 256
LAG = 1024
RIDGE = 0.001
CHUNK = 512
PANEL = 16
VMEM_LIMIT = 56 * 1024 * 1024

F32 = jnp.float32
BF16 = jnp.bfloat16
HIGHEST = lax.Precision.HIGHEST


def passed_along(value, axis, steps):
    count = lax.axis_size(axis)
    first, last = (max(0, -steps), min(count, count - steps))
    return lax.ppermute(value, axis, [(source, source + steps) for source in range(first, last)])


def across(a, b, precision=None):
    return lax.dot_general(a, b, (((1,), (1,)), ((), ())), precision=precision, preferred_element_type=F32)


def gram(a, b):
    return lax.dot_general(a, b, (((0,), (0,)), ((), ())), preferred_element_type=F32)


def silu(x):
    half = 0.5 * x
    return half + half * jnp.tanh(half)


def feature_kernel(live_ref, x_ref, halo_ref, w1_ref, b1_ref, w2_ref, out_ref, last_x, last_h):
    bias = b1_ref[...]

    def hidden_of(current, previous):
        both = jnp.concatenate([current, previous], 1)
        return silu(jnp.dot(both, w1_ref[...], preferred_element_type=F32) + bias).astype(BF16)

    @pl.when(pl.program_id(0) == 0)
    def _():
        rows = halo_ref.shape[0]
        live = live_ref[0] > 0
        previous_x = halo_ref[rows - D1 :, :]
        before = hidden_of(halo_ref[rows - D2 :, :], halo_ref[rows - D2 - D1 : rows - D1, :])
        last_x[...] = jnp.where(live, previous_x, jnp.zeros_like(previous_x))
        last_h[...] = jnp.where(live, before, jnp.zeros_like(before))

    rows = x_ref.shape[0]
    x = x_ref[...]
    hidden = hidden_of(x, jnp.concatenate([last_x[...], x[: rows - D1]], 0))
    earlier = jnp.concatenate([last_h[...], hidden[: rows - D2]], 0)
    both = jnp.concatenate([hidden, earlier], 1)
    out_ref[...] = jnp.dot(both, w2_ref[...], preferred_element_type=F32).astype(BF16)
    last_x[...] = x[rows - D1 :]
    last_h[...] = hidden[rows - D2 :]


def features(live, frames, first_block, block_count, halo, halo_block, w1, b1, w2):
    channels, hid, feat = frames.shape[1], w1.shape[1], w2.shape[1]
    whole = lambda i: (0, 0)
    return pl.pallas_call(
        feature_kernel,
        grid=(block_count,),
        in_specs=[
            pl.BlockSpec(memory_space=pltpu.SMEM),
            pl.BlockSpec((CHUNK, channels), lambda i: (i + first_block, 0)),
            pl.BlockSpec((halo_block, channels), whole),
            pl.BlockSpec(w1.shape, whole),
            pl.BlockSpec(b1.shape, whole),
            pl.BlockSpec(w2.shape, whole),
        ],
        out_specs=pl.BlockSpec((CHUNK, feat), lambda i: (i, 0)),
        out_shape=jax.ShapeDtypeStruct((block_count * CHUNK, feat), BF16),
        scratch_shapes=[pltpu.VMEM((D1, channels), BF16), pltpu.VMEM((D2, hid), BF16)],
        compiler_params=pltpu.CompilerParams(vmem_limit_bytes=VMEM_LIMIT),
    )(live, frames, halo, w1, b1, w2)


def column_sum(rows):
    ones = jnp.ones((8, rows.shape[0]), BF16)
    return jnp.dot(ones, rows, preferred_element_type=F32)[0:1]


def moment_kernel(edge_ref, head_ref, body_ref, ahead_ref, out_ref, inst, lag, total):
    feat = head_ref.shape[1]
    lag_chunks = LAG // CHUNK
    chunks = 1 + body_ref.shape[0] // CHUNK

    def chunk(index):
        if index == 0:
            return head_ref[...]
        if index < chunks:
            return body_ref[(index - 1) * CHUNK : index * CHUNK, :]
        return ahead_ref[(index - chunks) * CHUNK : (index - chunks + 1) * CHUNK, :]

    weights = [2.0 - edge_ref[0].astype(F32), 2.0, 2.0 - edge_ref[1].astype(F32)]
    inst[...] = jnp.zeros_like(inst)
    lag[...] = jnp.zeros_like(lag)
    total[...] = jnp.zeros_like(total)
    for index in range(chunks):
        weight = weights[(index >= lag_chunks) + (index >= chunks - lag_chunks)]
        now = chunk(index)
        inst[...] += weight * gram(now, now)
        lag[...] += gram(now, chunk(index + lag_chunks))
        total[...] += weight * column_sum(now)

    both = lag[...] + lag[...].T
    row = lax.broadcasted_iota(jnp.int32, (feat, feat), 0)
    column = lax.broadcasted_iota(jnp.int32, (feat, feat), 1)
    out_ref[:, :feat] = jnp.where(column >= row, inst[...], both)
    out_ref[:, feat:] = jnp.zeros((feat, out_ref.shape[1] - feat), F32)
    diagonal = jnp.sum(jnp.where(column == row, both, 0.0), 0, keepdims=True)
    for half in range(feat // 128):
        part = slice(half * 128, half * 128 + 128)
        out_ref[half : half + 1, feat:] = total[:, part]
        out_ref[half + 2 : half + 3, feat:] = diagonal[:, part]


def moments(edge, head, body, ahead):
    feat = body.shape[1]
    vmem = pl.BlockSpec(memory_space=pltpu.VMEM)
    return pl.pallas_call(
        moment_kernel,
        in_specs=[pl.BlockSpec(memory_space=pltpu.SMEM), vmem, vmem, vmem],
        out_specs=vmem,
        out_shape=jax.ShapeDtypeStruct((feat, feat + 128), F32),
        scratch_shapes=[pltpu.VMEM((feat, feat), F32), pltpu.VMEM((feat, feat), F32), pltpu.VMEM((1, feat), F32)],
        compiler_params=pltpu.CompilerParams(vmem_limit_bytes=VMEM_LIMIT),
    )(edge, head, body, ahead)


def three_parts(x):
    high = x.astype(BF16)
    rest = x - high.astype(F32)
    middle = rest.astype(BF16)
    low = (rest - middle.astype(F32)).astype(BF16)
    return high, middle, low


def inverse_factor(work):
    size = work.shape[0]
    lane = lax.broadcasted_iota(jnp.int32, (PANEL, size), 1)
    sub = lax.broadcasted_iota(jnp.int32, (PANEL, size), 0)
    sub_narrow = lax.broadcasted_iota(jnp.int32, (PANEL, 128), 0)
    for start in range(0, size, PANEL):
        stop = start + PANEL
        panel = work[start:stop, :]
        columns = [
            jnp.broadcast_to(panel[:, start + k : start + k + 1], (PANEL, 128)) for k in range(PANEL)
        ]
        panel = jnp.where(
            (lane >= start) & (lane < stop), jnp.where(lane - start == sub, 1.0, 0.0), panel
        )
        pivots = jnp.ones((PANEL, 128), F32)
        for j in range(PANEL):
            pivot = columns[j][j : j + 1, :]
            factor = columns[j] * (1.0 / pivot)
            pivots = jnp.where(sub_narrow == j, pivot, pivots)
            for k in range(j + 1, PANEL):
                columns[k] = columns[k] - factor * columns[k][j : j + 1, :]
            if j + 1 < PANEL:
                below = jnp.where(sub_narrow > j, factor, 0.0)
                wide = jnp.concatenate([below] * (size // 128), 1)
                panel = panel - wide * panel[j : j + 1, :]
        scale = lax.rsqrt(pivots)
        panel = panel * jnp.concatenate([scale] * (size // 128), 1)
        work[start:stop, :] = panel
        if stop < size:
            high, middle, low = three_parts(panel)
            left = jnp.concatenate([high, high, middle, high, low, middle], 0)
            right = jnp.concatenate([high, middle, high, low, high, middle], 0)
            first = stop // 128 * 128
            update = gram(left[:, first:], right)
            kept = lax.broadcasted_iota(jnp.int32, (size - stop, size), 1)
            kept = (kept < start) | (kept >= stop)
            work[stop:, :] = jnp.where(kept, work[stop:, :], 0.0) - update[stop - first :]
    row = lax.broadcasted_iota(jnp.int32, (size, size), 0)
    column = lax.broadcasted_iota(jnp.int32, (size, size), 1)
    return jnp.where(column <= row, work[...], 0.0)


def koopman_kernel(scale_ref, packed_ref, split_ref, shift_ref, work):
    feat = packed_ref.shape[0]
    scale = scale_ref[0]
    packed = packed_ref[:, :feat]
    extra = packed_ref[0:8, feat:]
    halves = feat // 128
    mean = jnp.concatenate([extra[h : h + 1] for h in range(halves)], 1) * scale
    diagonal = jnp.concatenate([extra[2 + h : 3 + h] for h in range(halves)], 1)
    row = lax.broadcasted_iota(jnp.int32, (feat, feat), 0)
    column = lax.broadcasted_iota(jnp.int32, (feat, feat), 1)
    turned = packed.T
    centre = jnp.broadcast_to(mean, (feat, feat))
    centre = centre * centre.T
    inst = jnp.where(column >= row, packed, turned)
    lag = jnp.where(column < row, packed, turned)
    lag = jnp.where(column == row, jnp.broadcast_to(diagonal, (feat, feat)), lag)
    work[...] = inst * scale - centre + jnp.where(column == row, RIDGE, 0.0)
    lag = lag * scale - centre
    inverse = inverse_factor(work)
    half_step = jnp.dot(inverse, lag, precision=HIGHEST, preferred_element_type=F32)
    koopman = across(half_step, inverse, HIGHEST)
    moved = jnp.dot(koopman, inverse, precision=HIGHEST, preferred_element_type=F32)
    for index, matrix in enumerate((inverse, moved)):
        high = matrix.astype(BF16)
        split_ref[2 * index] = high
        split_ref[2 * index + 1] = (matrix - high.astype(F32)).astype(BF16)
        rows = jnp.broadcast_to(mean, (8, feat))
        shift_ref[index] = across(rows, matrix, HIGHEST)


def koopman_parts(scale, packed):
    feat = packed.shape[0]
    vmem = pl.BlockSpec(memory_space=pltpu.VMEM)
    return pl.pallas_call(
        koopman_kernel,
        in_specs=[pl.BlockSpec(memory_space=pltpu.SMEM), vmem],
        out_specs=(vmem, vmem),
        out_shape=(
            jax.ShapeDtypeStruct((4, feat, feat), BF16),
            jax.ShapeDtypeStruct((2, 8, feat), F32),
        ),
        scratch_shapes=[pltpu.VMEM((feat, feat), F32)],
        compiler_params=pltpu.CompilerParams(vmem_limit_bytes=VMEM_LIMIT),
    )(scale, packed)


def project_kernel(
    edge_ref, head_ref, body_ref, later_ref, ahead_ref, split_ref, shift_ref, moved_ref, residual_ref
):
    step = pl.program_id(0)
    steps = pl.num_programs(0)
    lag_steps = LAG // CHUNK

    def product(block, index):
        return across(block, split_ref[2 * index]) + across(block, split_ref[2 * index + 1]) - shift_ref[index][0:1]

    current = jnp.where(step == 0, head_ref[...], body_ref[...])
    inside = step < steps - lag_steps
    later = jnp.where(inside, later_ref[...], ahead_ref[...])
    moved = product(current, 1)
    moved_ref[...] = moved
    live = inside | (edge_ref[1] == 0)
    residual_ref[...] = jnp.where(live, product(later, 0) - moved, 0.0)


def project(edge, head, body, ahead, split, shift):
    feat = body.shape[1]
    body_blocks = body.shape[0] // CHUNK
    steps = body_blocks + 1
    lag_steps = LAG // CHUNK
    block = (CHUNK, feat)
    out = jax.ShapeDtypeStruct((steps * CHUNK, feat), F32)
    return pl.pallas_call(
        project_kernel,
        grid=(steps,),
        in_specs=[
            pl.BlockSpec(memory_space=pltpu.SMEM),
            pl.BlockSpec(block, lambda i: (0, 0)),
            pl.BlockSpec(block, lambda i: (jnp.maximum(i - 1, 0), 0)),
            pl.BlockSpec(block, lambda i: (jnp.minimum(i - 1 + lag_steps, body_blocks - 1), 0)),
            pl.BlockSpec(block, lambda i: (jnp.maximum(i - (steps - lag_steps), 0), 0)),
            pl.BlockSpec(split.shape, lambda i: (0, 0, 0)),
            pl.BlockSpec(shift.shape, lambda i: (0, 0, 0)),
        ],
        out_specs=(pl.BlockSpec(block, lambda i: (i, 0)), pl.BlockSpec(block, lambda i: (i, 0))),
        out_shape=(out, out),
        compiler_params=pltpu.CompilerParams(vmem_limit_bytes=VMEM_LIMIT),
    )(edge, head, body, body, ahead, split, shift)


def summed(packed, axes, count):
    feat, width = packed.shape
    parts = packed.reshape(count, feat // count, width)
    parts = lax.all_to_all(parts, axes, 0, 0, tiled=True)
    mine = jnp.sum(parts, 0)
    return lax.all_gather(mine, axes, axis=0, tiled=True)


def on_device(device_count, frames, first_weight, first_bias, second_weight):
    frame_block = frames[0]
    row_count, channels = frame_block.shape
    hid, feat = second_weight.shape[1:]
    tm_index = lax.axis_index("tm")
    tm_count = lax.axis_size("tm")
    w1 = first_weight.reshape(2 * channels, hid)
    w2 = second_weight.reshape(2 * hid, feat)
    b1 = first_bias.reshape(1, hid)

    halo = passed_along(frame_block[row_count - D1 - D2 :], "tm", 1)
    yes = jnp.ones((1,), jnp.int32)
    body = features(yes, frame_block, 1, row_count // CHUNK - 1, frame_block, CHUNK, w1, b1, w2)
    live = (tm_index > 0).astype(jnp.int32).reshape(1)
    head = features(live, frame_block, 0, 1, halo, D1 + D2, w1, b1, w2)

    ahead = passed_along(jnp.concatenate([head, body[: LAG - CHUNK]], 0), "tm", -1)
    edge = jnp.stack([tm_index == 0, tm_index == tm_count - 1]).astype(jnp.int32)
    packed = moments(edge, head, body, ahead)
    packed = summed(packed, ("rep", "tm"), device_count)
    pair_count = lax.axis_size("rep") * (row_count * tm_count - LAG)
    scale = jnp.full((1,), 1.0 / (2.0 * pair_count), F32)
    split, shift = koopman_parts(scale, packed)
    propagated, residual = project(edge, head, body, ahead, split, shift)
    return (propagated[None], residual[None])


def solution(mesh):
    placed = (P("rep", "tm", None), P(), P(), P())
    return jax.shard_map(
        partial(on_device, mesh.size),
        mesh=mesh,
        in_specs=placed,
        out_specs=(P("rep", "tm", None), P("rep", "tm", None)),
        check_vma=False,
    )
```

time: 274 us -> 156 us (0.57)
  waiting for transfers between devices: 105 us -> 13.3 us
  other arithmetic: 68.9 us -> 1.69 us
  blocking collectives: 42.1 us -> 90.7 us
  Pallas kernels: 0 us -> 40.7 us
  matrix products: 21.9 us -> 0 us
  between operations: 16.4 us -> 0.68 us
  local copies, waits for them, and re-layouts: 9.74 us -> 2.51 us
  starting transfers between devices: 9.75 us -> 6.18 us
    psum x1 -> x0, waiting for transfers between devices: 87 us -> none  [on_device(): lax.psum((pair_count, feature_sum, second, cross_sum), ('rep', 'tm'))]
    all_gather x0 -> x1, blocking collectives: none -> 71.5 us  [summed(): return lax.all_gather(mine, axes, axis=0, tiled=True)]
    another operation x9 -> x0, other arithmetic: 54.5 us -> none  [the longest x6 34 us: on_device(): jnp.linalg.cholesky(inst_moment / (2.0 * total_count) + ridge_level * ide...]
    psum x1 -> x0, blocking collectives: 42.1 us -> none  [on_device(): lax.psum((pair_count, feature_sum, second, cross_sum), ('rep', 'tm'))]
    pallas_call x0 -> x5, Pallas kernels: none -> 40.7 us  [the longest x2 16.8 us: features(): pl.pallas_call(feature_kernel, grid=(block_count,), in_specs=[pl.BlockSpe...]
    dot_general x9 -> x0, matrix products: 20.4 us -> none  [the longest x2 5.32 us: layer_pair(): jnp.dot(previous, weights[1], preferred_element_type=jnp.float32)]
    all_to_all x0 -> x1, blocking collectives: none -> 19.3 us  [summed(): parts = lax.all_to_all(parts, axes, 0, 0, tiled=True)]
    reduce_sum x1, other arithmetic: 7.32 us -> 0.04 us  [summed(): mine = jnp.sum(parts, 0)]
  transfers between devices with their start and end apart: 4 -> 2, of which waited for: 3 -> 1; matrix products, arithmetic and copies ran while one was open for 2% -> 0% of each run, Pallas kernels for 0% -> 8%
where the time goes in v1:
time: 156 us
  blocking collectives  90.7 us (58%)
  Pallas kernels  40.7 us (26%)
  waiting for transfers between devices  13.3 us (9%)
  starting transfers between devices  6.18 us (4%)
  local copies, waits for them, and re-layouts  2.51 us (2%)
  other arithmetic  1.69 us (1%)
    all_gather x1, blocking collectives, summed(): return lax.all_gather(mine, axes, axis=0, tiled=True)  71.5 us
    all_to_all x1, blocking collectives, summed(): parts = lax.all_to_all(parts, axes, 0, 0, tiled=True)  19.3 us
    pallas_call x2, Pallas kernels, features(): pl.pallas_call(feature_kernel, grid=(block_count,), in_specs=[pl.BlockSpe...  16.8 us
    ppermute x2, waiting for transfers between devices, passed_along(): lax.ppermute(value, axis, [(source, source + steps) for source in range(f...  13.3 us
    pallas_call x1, Pallas kernels, koopman_parts(): pl.pallas_call(koopman_kernel, in_specs=[pl.BlockSpec(memory_space=pltpu....  10.6 us
    pallas_call x1, Pallas kernels, project(): pl.pallas_call(project_kernel, grid=(steps,), in_specs=[pl.BlockSpec(memo...  9.22 us
    ppermute x2, starting transfers between devices, passed_along(): lax.ppermute(value, axis, [(source, source + steps) for source in range(f...  6.18 us
    pallas_call x1, Pallas kernels, moments(): pl.pallas_call(moment_kernel, in_specs=[pl.BlockSpec(memory_space=pltpu.S...  4.07 us
  transfers between devices with their start and end apart: 2, of which 1 were waited for; matrix products, arithmetic and copies ran while one was open for 0% of the time, Pallas kernels for 8%

profile of v1, /device:TPU:0, one launch (start us, length us, event | category | flops | bytes accessed | tf_op | source)
XLA Modules:
  0.0 155.9 jit_solution(181787267076720970)
XLA Ops:
  0.6 1.0 slice_bitcast_fusion
  1.6 4.9 %collective-permute-start = (bf16[288,512]{1,0:T(8,128)(2,1)S(1)}, bf16[288,512]{1,0:T(8,128)(2,1)S(1)}, u32[]{:S(2)}, u32[]{:S(2)}) collective-permute-start(bf16[288,512]{1,0:T(8,128)(2,1)S(1)} %slice_bitcast_fusion), channel_id=1, source_target_pairs={{0,1},{1,2},{2,3},{3,4},{4,5},{5,6},{6,7},{8,9},{9,10},{10,11},{11... | collective-permute-start | bytes 884744 | tf_op jit(solution)/shard_map/ppermute | solution.py:26
  6.5 12.8 %shard_map.60.body_ref.later_ref = bf16[3584,256]{1,0:T(8,128)(2,1)} custom-call(s32[1]{0:T(128)} %constant.3.clone.1.live_ref, bf16[4096,512]{1,0:T(8,128)(2,1)} %bitcast.12, bf16[4096,512]{1,0:T(8,128)(2,1)} %bitcast.13, bf16[1024,512]{1,0:T(8,128)(2,1)} %bitcast.15, f32[1,512]{1,0:T(1,128)} %bitcast.20, bf16[1024,256]{1,0:T(8,128)(2,1)} %bitcast.17), custom_call_target="tpu_custom_call" | custom-call | tf_op jit(solution)/shard_map/pallas_call | solution.py:71
  19.3 0.0 slice-start
  19.3 0.0 collective-permute-done.halo_ref
  19.3 0.0 copy-start.1
  19.3 0.7 copy-done.1
  20.1 4.0 %shard_map.59.head_ref = bf16[512,256]{1,0:T(8,128)(2,1)} custom-call(s32[1]{0:T(128)} %bitcast.2.live_ref, bf16[4096,512]{1,0:T(8,128)(2,1)} %bitcast.14, bf16[288,512]{1,0:T(8,128)(2,1)} %copy-done.1, bf16[1024,512]{1,0:T(8,128)(2,1)} %bitcast.16, f32[1,512]{1,0:T(1,128)} %bitcast.21, bf16[1024,256]{1,0:T(8,128)(2,1)} %bitcast.18), custom_call_target="tpu_custom_call" | custom-call | tf_op jit(solution)/shard_map/pallas_call | solution.py:71
  24.0 0.0 slice-done
  24.0 1.0 pad_maximum_fusion
  25.0 1.3 collective-permute-start.1
  26.3 0.7 add_convert_fusion.edge_ref
  27.0 13.3 %collective-permute-done.1.ahead_ref = bf16[1024,256]{1,0:T(8,128)(2,1)S(1)} collective-permute-done((bf16[1024,256]{1,0:T(8,128)(2,1)S(1)}, bf16[1024,256]{1,0:T(8,128)(2,1)S(1)}, u32[]{:S(2)}, u32[]{:S(2)}) %collective-permute-start.1) | collective-permute-done | bytes 524320 | tf_op jit(solution)/shard_map/ppermute | solution.py:26
  40.3 0.0 copy-start
  40.3 0.8 copy-done
  41.1 4.1 %shard_map.61 = f32[256,384]{1,0:T(8,128)} custom-call(s32[2]{0:T(128)} %add_convert_fusion.edge_ref, bf16[512,256]{1,0:T(8,128)(2,1)} %shard_map.59.head_ref, bf16[3584,256]{1,0:T(8,128)(2,1)} %shard_map.60.body_ref.later_ref, bf16[1024,256]{1,0:T(8,128)(2,1)} %copy-done), custom_call_target="tpu_custom_call" | custom-call | tf_op jit(solution)/shard_map/pallas_call | solution.py:132
  45.2 19.3 %all_to_all.5 = f32[32,8,384]{2,1,0:T(8,128)S(1)} all-to-all(f32[32,8,384]{2,1,0:T(8,128)} %bitcast.19), channel_id=1, replica_groups=mesh['rep'=4,'tm'=8] {'rep','tm'}, dimensions={0} | all-to-all | bytes 786432 | tf_op jit(solution)/shard_map/all_to_all | solution.py:285
  64.5 71.5 %all_gather.3.packed_ref = f32[256,384]{1,0:T(8,128)} all-gather(f32[8,384]{1,0:T(8,128)S(1)} %reduce_sum.9), channel_id=1, replica_groups=mesh['rep'=4,'tm'=8] {'rep','tm'}, dimensions={0}, use_global_device_ids=true | all-gather | bytes 405504 | tf_op jit(solution)/shard_map/all_gather | solution.py:287
  136.0 10.6 %shard_map.62 = (bf16[4,256,256]{2,1,0:T(8,128)(2,1)}, f32[2,8,256]{2,1,0:T(8,128)}) custom-call(f32[1]{0:T(128)} %constant.4.clone.1.scale_ref, f32[256,384]{1,0:T(8,128)} %all_gather.3.packed_ref), custom_call_target="tpu_custom_call" | custom-call | tf_op jit(solution)/shard_map/pallas_call | solution.py:225
  146.6 9.2 %shard_map.63 = (f32[4096,256]{1,0:T(8,128)}, f32[4096,256]{1,0:T(8,128)}) custom-call(s32[2]{0:T(128)} %add_convert_fusion.edge_ref, bf16[512,256]{1,0:T(8,128)(2,1)} %shard_map.59.head_ref, bf16[3584,256]{1,0:T(8,128)(2,1)} %shard_map.60.body_ref.later_ref, bf16[3584,256]{1,0:T(8,128)(2,1)} %shard_map.60.body_ref.later_ref, bf16[1024,256]{1,0:T(8,128)(2,1)} %copy-done, ...), custom_call_target="tpu_custom_call" | custom-call | tf_op jit(solution)/shard_map/pallas_call | solution.py:264
  (1 shorter events, 0.0 us)
Async XLA Ops:
  1.6 17.7 %collective-permute-start = (bf16[288,512]{1,0:T(8,128)(2,1)S(1)}, bf16[288,512]{1,0:T(8,128)(2,1)S(1)}, u32[]{:S(2)}, u32[]{:S(2)}) collective-permute-start(bf16[288,512]{1,0:T(8,128)(2,1)S(1)} %slice_bitcast_fusion), channel_id=1, source_target_pairs={{0,1},{1,2},{2,3},{3,4},{4,5},{5,6},{6,7},{8,9},{9,10},{10,11},{11... | collective-permute-start | bytes 884744 | tf_op jit(solution)/shard_map/ppermute | solution.py:26
  19.3 4.7 %slice-start = ((bf16[3584,256]{1,0:T(8,128)(2,1)}), bf16[512,256]{1,0:T(8,128)(2,1)S(1)}, s32[]{:S(2)}) async-start(bf16[3584,256]{1,0:T(8,128)(2,1)} %shard_map.60.body_ref.later_ref), calls=%async_computation.1 | async-start | bytes 524288 | tf_op jit(solution)/shard_map/slice | solution.py:306
  19.3 0.7 copy-start.1
  25.0 15.3 %collective-permute-start.1 = (bf16[1024,256]{1,0:T(8,128)(2,1)S(1)}, bf16[1024,256]{1,0:T(8,128)(2,1)S(1)}, u32[]{:S(2)}, u32[]{:S(2)}) collective-permute-start(bf16[1024,256]{1,0:T(8,128)(2,1)S(1)} %pad_maximum_fusion), channel_id=1, source_target_pairs={{1,0},{2,1},{3,2},{4,3},{5,4},{6,5},{7,6},{9,8},{10,9},{11,10},{12... | collective-permute-start | bytes 1572872 | tf_op jit(solution)/shard_map/ppermute | solution.py:26
  40.3 0.8 copy-start

commit v2 on v1

v2 whole, which is shorter than its diff:
```python
import jax
import jax.numpy as jnp
from jax import lax
from jax.experimental import pallas as pl
from jax.experimental.pallas import tpu as pltpu
from jax.sharding import PartitionSpec as P

D1 = 32
D2 = 256
LAG = 1024
RIDGE = 0.001
CHUNK = 512
BLOCK = 256
PANEL = 16
VMEM_LIMIT = 56 * 1024 * 1024

F32 = jnp.float32
BF16 = jnp.bfloat16
HIGHEST = lax.Precision.HIGHEST


def passed_along(value, axis, steps):
    count = lax.axis_size(axis)
    first, last = (max(0, -steps), min(count, count - steps))
    return lax.ppermute(value, axis, [(source, source + steps) for source in range(first, last)])


def across(a, b, precision=None):
    return lax.dot_general(a, b, (((1,), (1,)), ((), ())), precision=precision, preferred_element_type=F32)


def gram(a, b):
    return lax.dot_general(a, b, (((0,), (0,)), ((), ())), preferred_element_type=F32)


def silu(x):
    half = 0.5 * x
    return half + half * jnp.tanh(half)


def feature_steps(xs, hs, out_ref, out_start, count, w1_ref, b1_ref, w2_ref, begin, finish):
    channels = xs.shape[1]
    hid = hs.shape[1]
    bias = b1_ref[...]

    def hidden(step):
        at = pl.ds(step * BLOCK, BLOCK)
        after = pl.ds(step * BLOCK + D1, BLOCK)
        z = jnp.dot(xs[after, :], w1_ref[:channels, :], preferred_element_type=F32)
        z += jnp.dot(xs[at, :], w1_ref[channels:, :], preferred_element_type=F32)
        return silu(z + bias).astype(BF16)

    def feature(step):
        now = hs[pl.ds(step * BLOCK + D2, BLOCK), :]
        then = hs[pl.ds(step * BLOCK, BLOCK), :]
        value = jnp.dot(now, w2_ref[:hid, :], preferred_element_type=F32)
        value += jnp.dot(then, w2_ref[hid:, :], preferred_element_type=F32)
        value = value.astype(BF16)
        out_ref[pl.ds(out_start + step * BLOCK, BLOCK), :] = value
        return value

    for step in range(count + 1):
        begin(step)
        fresh = hidden(step)
        if step >= 2:
            finish(step - 2, feature(step - 2))
        hs[step * BLOCK : (step + 1) * BLOCK, :] = fresh
        if step == 0:
            yield
    finish(count - 1, feature(count - 1))


def run_steps(steps, after_first=None):
    for _ in steps:
        if after_first is not None:
            after_first()


def nothing(*_):
    return None


def early_kernel(frames_ref, w1_ref, b1_ref, w2_ref, out_ref, xs, hs, sem):
    copy = pltpu.make_async_copy(frames_ref.at[pl.ds(LAG // 2 - D1 - D2, xs.shape[0])], xs, sem)
    copy.start()
    copy.wait()
    run_steps(
        feature_steps(
            xs, hs, out_ref, 0, out_ref.shape[0] // BLOCK, w1_ref, b1_ref, w2_ref, nothing, nothing
        )
    )


def head_kernel(live_ref, frames_ref, halo_ref, w1_ref, b1_ref, w2_ref, out_ref, xs, hs, sem):
    halo_rows = halo_ref.shape[0]
    copy = pltpu.make_async_copy(
        frames_ref.at[pl.ds(0, out_ref.shape[0])], xs.at[pl.ds(halo_rows, out_ref.shape[0])], sem
    )
    copy.start()
    xs[:halo_rows, :] = halo_ref[...]
    copy.wait()

    def clear():
        before = hs[:D2, :]
        hs[:D2, :] = jnp.where(live_ref[0] > 0, before, jnp.zeros_like(before))

    run_steps(
        feature_steps(
            xs, hs, out_ref, 0, out_ref.shape[0] // BLOCK, w1_ref, b1_ref, w2_ref, nothing, nothing
        ),
        clear,
    )


def feature_scratch(rows, channels, hid):
    return [
        pltpu.VMEM((rows + D1 + D2, channels), BF16),
        pltpu.VMEM((rows + D2, hid), BF16),
    ]


def first_rows(kernel, operands, specs, w1, b1, w2):
    vmem = pl.BlockSpec(memory_space=pltpu.VMEM)
    rows = LAG // 2
    return pl.pallas_call(
        kernel,
        in_specs=specs + [vmem, vmem, vmem],
        out_specs=vmem,
        out_shape=jax.ShapeDtypeStruct((rows, w2.shape[1]), BF16),
        scratch_shapes=feature_scratch(rows, w1.shape[0] // 2, w1.shape[1]) + [pltpu.SemaphoreType.DMA],
        compiler_params=pltpu.CompilerParams(vmem_limit_bytes=VMEM_LIMIT),
    )(*operands, w1, b1, w2)


def column_sum(rows):
    ones = jnp.ones((8, rows.shape[0]), BF16)
    return jnp.dot(ones, rows, preferred_element_type=F32)


def body_kernel(
    edge_ref, frames_ref, head_ref, early_ref, w1_ref, b1_ref, w2_ref, out_ref, inst, lag, total, xs, hs, sems
):
    rows, feat = out_ref.shape
    first = LAG - D1 - D2
    count = (rows - LAG) // BLOCK
    pieces = [0] + [BLOCK * (2 * k + 1) + D1 for k in range(count // 2 + 1)]
    pieces = [p for p in pieces if p < rows - first] + [rows - first]
    copies = []
    for index, (lo, hi) in enumerate(zip(pieces[:-1], pieces[1:])):
        copy = pltpu.make_async_copy(
            frames_ref.at[pl.ds(first + lo, hi - lo)], xs.at[pl.ds(lo, hi - lo)], sems.at[index]
        )
        copy.start()
        copies.append((lo, copy))
    half = LAG // 2
    out_ref[:half, :] = head_ref[...]
    out_ref[half:LAG, :] = early_ref[...]
    weights = [2.0 - edge_ref[0].astype(F32), 2.0, 2.0 - edge_ref[1].astype(F32)]
    start = out_ref[:LAG, :]
    inst[...] = weights[0] * gram(start, start)
    total[...] = weights[0] * column_sum(start)
    lag[...] = jnp.zeros_like(lag)

    def begin(step):
        while copies and copies[0][0] < (step + 1) * BLOCK + D1:
            copies.pop(0)[1].wait()

    def finish(step, value):
        at = LAG + step * BLOCK
        weight = weights[2] if at >= rows - LAG else weights[1]
        both = gram(value, jnp.concatenate([value, out_ref[at - LAG : at - LAG + BLOCK, :]], 1))
        inst[...] += weight * both[:, :feat]
        lag[...] += both[:, feat:]
        total[...] += weight * column_sum(value)

    run_steps(feature_steps(xs, hs, out_ref, LAG, count, w1_ref, b1_ref, w2_ref, begin, finish))


def body(edge, frames, head, early, w1, b1, w2):
    rows, channels = frames.shape
    hid, feat = w1.shape[1], w2.shape[1]
    vmem = pl.BlockSpec(memory_space=pltpu.VMEM)
    square = jax.ShapeDtypeStruct((feat, feat), F32)
    return pl.pallas_call(
        body_kernel,
        in_specs=[pl.BlockSpec(memory_space=pltpu.SMEM), pl.BlockSpec(memory_space=pl.ANY)] + [vmem] * 5,
        out_specs=(vmem,) * 4,
        out_shape=(
            jax.ShapeDtypeStruct((rows, feat), BF16),
            square,
            square,
            jax.ShapeDtypeStruct((8, feat), F32),
        ),
        scratch_shapes=feature_scratch(rows - LAG, channels, hid)
        + [pltpu.SemaphoreType.DMA((rows // BLOCK,))],
        compiler_params=pltpu.CompilerParams(vmem_limit_bytes=VMEM_LIMIT),
    )(edge, frames, head, early, w1, b1, w2)


def pack_kernel(feature_ref, ahead_head_ref, ahead_early_ref, inst, lag, total, out_ref):
    feat = inst.shape[0]
    half = LAG // 2
    edge = feature_ref.shape[0] - LAG
    cross = lag[...] + gram(ahead_head_ref[...], feature_ref[edge : edge + half, :])
    cross += gram(ahead_early_ref[...], feature_ref[edge + half :, :])
    both = cross + cross.T
    row = lax.broadcasted_iota(jnp.int32, (feat, feat), 0)
    column = lax.broadcasted_iota(jnp.int32, (feat, feat), 1)
    out_ref[:feat, :] = jnp.where(column >= row, inst[...], both)
    out_ref[feat:, :] = jnp.zeros((out_ref.shape[0] - feat, feat), F32)
    out_ref[feat : feat + 1, :] = total[0:1, :]
    out_ref[feat + 1 : feat + 2, :] = jnp.sum(jnp.where(column == row, both, 0.0), 0, keepdims=True)


def pack(feature, ahead_head, ahead_early, inst, lag, total, packed_rows):
    vmem = pl.BlockSpec(memory_space=pltpu.VMEM)
    return pl.pallas_call(
        pack_kernel,
        in_specs=[vmem] * 6,
        out_specs=vmem,
        out_shape=jax.ShapeDtypeStruct((packed_rows, inst.shape[0]), F32),
        compiler_params=pltpu.CompilerParams(vmem_limit_bytes=VMEM_LIMIT),
    )(feature, ahead_head, ahead_early, inst, lag, total)


def three_parts(x):
    high = x.astype(BF16)
    rest = x - high.astype(F32)
    middle = rest.astype(BF16)
    low = (rest - middle.astype(F32)).astype(BF16)
    return high, middle, low


def inverse_factor(work):
    size = work.shape[0]
    lane = lax.broadcasted_iota(jnp.int32, (PANEL, size), 1)
    sub = lax.broadcasted_iota(jnp.int32, (PANEL, size), 0)
    sub_narrow = lax.broadcasted_iota(jnp.int32, (PANEL, 128), 0)
    for start in range(0, size, PANEL):
        stop = start + PANEL
        panel = work[start:stop, :]
        columns = [
            jnp.broadcast_to(panel[:, start + k : start + k + 1], (PANEL, 128)) for k in range(PANEL)
        ]
        panel = jnp.where(
            (lane >= start) & (lane < stop), jnp.where(lane - start == sub, 1.0, 0.0), panel
        )
        pivots = jnp.ones((PANEL, 128), F32)
        for j in range(PANEL):
            pivot = columns[j][j : j + 1, :]
            factor = columns[j] * (1.0 / pivot)
            pivots = jnp.where(sub_narrow == j, pivot, pivots)
            for k in range(j + 1, PANEL):
                columns[k] = columns[k] - factor * columns[k][j : j + 1, :]
            if j + 1 < PANEL:
                below = jnp.where(sub_narrow > j, factor, 0.0)
                wide = jnp.concatenate([below] * (size // 128), 1)
                panel = panel - wide * panel[j : j + 1, :]
        scale = lax.rsqrt(pivots)
        panel = panel * jnp.concatenate([scale] * (size // 128), 1)
        work[start:stop, :] = panel
        if stop < size:
            high, middle, low = three_parts(panel)
            left = jnp.concatenate([high, high, middle, high, low, middle], 0)
            right = jnp.concatenate([high, middle, high, low, high, middle], 0)
            first = stop // 128 * 128
            update = gram(left[:, first:], right)
            kept = lax.broadcasted_iota(jnp.int32, (size - stop, size), 1)
            kept = (kept < start) | (kept >= stop)
            work[stop:, :] = jnp.where(kept, work[stop:, :], 0.0) - update[stop - first :]
    row = lax.broadcasted_iota(jnp.int32, (size, size), 0)
    column = lax.broadcasted_iota(jnp.int32, (size, size), 1)
    return jnp.where(column <= row, work[...], 0.0)


def koopman_kernel(scale_ref, packed_ref, split_ref, shift_ref, work):
    feat = packed_ref.shape[1]
    scale = scale_ref[0]
    packed = packed_ref[:feat, :]
    mean = packed_ref[feat : feat + 1, :] * scale
    diagonal = packed_ref[feat + 1 : feat + 2, :]
    row = lax.broadcasted_iota(jnp.int32, (feat, feat), 0)
    column = lax.broadcasted_iota(jnp.int32, (feat, feat), 1)
    turned = packed.T
    centre = jnp.broadcast_to(mean, (feat, feat))
    centre = centre * centre.T
    inst = jnp.where(column >= row, packed, turned)
    lag = jnp.where(column < row, packed, turned)
    lag = jnp.where(column == row, jnp.broadcast_to(diagonal, (feat, feat)), lag)
    work[...] = inst * scale - centre + jnp.where(column == row, RIDGE, 0.0)
    lag = lag * scale - centre
    inverse = inverse_factor(work)
    half_step = jnp.dot(inverse, lag, precision=HIGHEST, preferred_element_type=F32)
    koopman = across(half_step, inverse, HIGHEST)
    moved = jnp.dot(koopman, inverse, precision=HIGHEST, preferred_element_type=F32)
    for index, matrix in enumerate((inverse, moved)):
        turned = matrix.T
        high = turned.astype(BF16)
        split_ref[2 * index] = high
        split_ref[2 * index + 1] = (turned - high.astype(F32)).astype(BF16)
        rows = jnp.broadcast_to(mean, (8, feat))
        shift_ref[index] = jnp.dot(rows, turned, precision=HIGHEST, preferred_element_type=F32)


def koopman_parts(scale, packed):
    feat = packed.shape[1]
    vmem = pl.BlockSpec(memory_space=pltpu.VMEM)
    return pl.pallas_call(
        koopman_kernel,
        in_specs=[pl.BlockSpec(memory_space=pltpu.SMEM), vmem],
        out_specs=(vmem, vmem),
        out_shape=(
            jax.ShapeDtypeStruct((4, feat, feat), BF16),
            jax.ShapeDtypeStruct((2, 8, feat), F32),
        ),
        scratch_shapes=[pltpu.VMEM((feat, feat), F32)],
        compiler_params=pltpu.CompilerParams(vmem_limit_bytes=VMEM_LIMIT),
    )(scale, packed)


def project_kernel(
    edge_ref, feature_ref, ahead_head_ref, ahead_early_ref, split_ref, shift_ref, moved_ref, residual_ref
):
    step = pl.program_id(0)
    inside = feature_ref.shape[0] // CHUNK - 2

    def product(block, index):
        value = jnp.dot(block, split_ref[2 * index], preferred_element_type=F32)
        value += jnp.dot(block, split_ref[2 * index + 1], preferred_element_type=F32)
        return value - shift_ref[index][0:1]

    def moved():
        value = product(feature_ref[pl.ds(pl.multiple_of(step * CHUNK, CHUNK), CHUNK), :], 1)
        moved_ref[...] = value
        return value

    @pl.when(step < inside)
    def _():
        later = feature_ref[pl.ds(pl.multiple_of(step * CHUNK + LAG, CHUNK), CHUNK), :]
        residual_ref[...] = product(later, 0) - moved()

    for index, ahead_ref in enumerate((ahead_head_ref, ahead_early_ref)):

        @pl.when(step == inside + index)
        def _():
            value = product(ahead_ref[...], 0) - moved()
            residual_ref[...] = jnp.where(edge_ref[1] > 0, 0.0, value)


def project(edge, feature, ahead_head, ahead_early, split, shift):
    rows, feat = feature.shape
    vmem = pl.BlockSpec(memory_space=pltpu.VMEM)
    out = jax.ShapeDtypeStruct((rows, feat), F32)
    block = pl.BlockSpec((CHUNK, feat), lambda i: (i, 0))
    return pl.pallas_call(
        project_kernel,
        grid=(rows // CHUNK,),
        in_specs=[pl.BlockSpec(memory_space=pltpu.SMEM)] + [vmem] * 5,
        out_specs=(block, block),
        out_shape=(out, out),
        compiler_params=pltpu.CompilerParams(vmem_limit_bytes=VMEM_LIMIT),
    )(edge, feature, ahead_head, ahead_early, split, shift)


def from_all(value, axis):
    copies = jnp.broadcast_to(value[None], (lax.axis_size(axis), *value.shape))
    return lax.all_to_all(copies, axis, 0, 0, tiled=True)


def summed(packed):
    rows, feat = packed.shape
    parts = packed.reshape(lax.axis_size("rep"), -1, feat)
    mine = jnp.sum(lax.all_to_all(parts, "rep", 0, 0, tiled=True), 0)
    mine = jnp.sum(from_all(mine, "tm"), 0)
    return from_all(mine, "rep").reshape(rows, feat)


def on_device(frames, first_weight, first_bias, second_weight):
    frame_block = frames[0]
    row_count, channels = frame_block.shape
    hid, feat = second_weight.shape[1:]
    tm_index = lax.axis_index("tm")
    tm_count = lax.axis_size("tm")
    rep_count = lax.axis_size("rep")
    weights = (
        first_weight.reshape(2 * channels, hid),
        first_bias.reshape(1, hid),
        second_weight.reshape(2 * hid, feat),
    )
    smem, anywhere, vmem = (pl.BlockSpec(memory_space=m) for m in (pltpu.SMEM, pl.ANY, pltpu.VMEM))

    halo = passed_along(frame_block[row_count - D1 - D2 :], "tm", 1)
    early = first_rows(early_kernel, (frame_block,), [anywhere], *weights)
    ahead_early = passed_along(early, "tm", -1)
    live = (tm_index > 0).astype(jnp.int32).reshape(1)
    head = first_rows(head_kernel, (live, frame_block, halo), [smem, anywhere, vmem], *weights)
    ahead_head = passed_along(head, "tm", -1)
    edge = jnp.stack([tm_index == 0, tm_index == tm_count - 1]).astype(jnp.int32)
    feature, inst, lag, total = body(edge, frame_block, head, early, *weights)
    unit = 8 * rep_count
    packed_rows = -(-(feat + 2) // unit) * unit
    packed = summed(pack(feature, ahead_head, ahead_early, inst, lag, total, packed_rows))
    pair_count = rep_count * (row_count * tm_count - LAG)
    scale = jnp.full((1,), 1.0 / (2.0 * pair_count), F32)
    split, shift = koopman_parts(scale, packed)
    propagated, residual = project(edge, feature, ahead_head, ahead_early, split, shift)
    return (propagated[None], residual[None])


def solution(mesh):
    placed = (P("rep", "tm", None), P(), P(), P())
    return jax.shard_map(
        on_device,
        mesh=mesh,
        in_specs=placed,
        out_specs=(P("rep", "tm", None), P("rep", "tm", None)),
        check_vma=False,
    )
```

time: 156 us -> 102 us (0.65)
  blocking collectives: 90.7 us -> 44.5 us
  waiting for transfers between devices: 13.3 us -> 0.31 us
  Pallas kernels: 40.7 us -> 45.2 us
    all_gather x1 -> x0, blocking collectives: 71.5 us -> none  [summed(): return lax.all_gather(mine, axes, axis=0, tiled=True)]
    all_to_all x1 -> x3, blocking collectives: 19.3 us -> 44.5 us  [the longest x2 34.7 us: from_all(): return lax.all_to_all(copies, axis, 0, 0, tiled=True)]
    ppermute x2 -> x3, waiting for transfers between devices: 13.3 us -> 0.31 us  [passed_along(): lax.ppermute(value, axis, [(source, source + steps) for source in range(f...]
    pallas_call x4 -> x5, Pallas kernels: 30.1 us -> 34.6 us  [the longest x1 14.5 us: body(): pl.pallas_call(body_kernel, in_specs=[pl.BlockSpec(memory_space=pltpu.SME...]
    ppermute x2 -> x3, starting transfers between devices: 6.18 us -> 7.47 us  [passed_along(): lax.ppermute(value, axis, [(source, source + steps) for source in range(f...]
  transfers between devices with their start and end apart: 2 -> 3, of which waited for: 1 -> 1; matrix products, arithmetic and copies ran while one was open for 0% -> 1% of each run, Pallas kernels for 8% -> 23%
where the time goes in v2:
time: 102 us; the launch traced here: 101 us
  Pallas kernels  45.2 us (44%)
  blocking collectives  44.5 us (44%)
  starting transfers between devices  7.47 us (7%)
  local copies, waits for them, and re-layouts  2.54 us (2%)
    all_to_all x2, blocking collectives, from_all(): return lax.all_to_all(copies, axis, 0, 0, tiled=True)  34.7 us
    pallas_call x1, Pallas kernels, body(): pl.pallas_call(body_kernel, in_specs=[pl.BlockSpec(memory_space=pltpu.SME...  14.5 us
    pallas_call x1, Pallas kernels, koopman_parts(): pl.pallas_call(koopman_kernel, in_specs=[pl.BlockSpec(memory_space=pltpu....  10.6 us
    all_to_all x1, blocking collectives, summed(): mine = jnp.sum(lax.all_to_all(parts, 'rep', 0, 0, tiled=True), 0)  9.81 us
    pallas_call x2, Pallas kernels, first_rows(): pl.pallas_call(kernel, in_specs=specs + [vmem, vmem, vmem], out_specs=vme...  9.2 us
    pallas_call x1, Pallas kernels, project(): pl.pallas_call(project_kernel, grid=(rows // CHUNK,), in_specs=[pl.BlockS...  8.01 us
    ppermute x3, starting transfers between devices, passed_along(): lax.ppermute(value, axis, [(source, source + steps) for source in range(f...  7.47 us
    pallas_call x1, Pallas kernels, pack(): pl.pallas_call(pack_kernel, in_specs=[vmem] * 6, out_specs=vmem, out_shap...  2.95 us
  transfers between devices with their start and end apart: 3, of which 1 were waited for; matrix products, arithmetic and copies ran while one was open for 1% of the time, Pallas kernels for 23%

profile of v2, /device:TPU:0, one launch (start us, length us, event | category | flops | bytes accessed | tf_op | source)
XLA Modules:
  0.0 101.4 jit_solution(7935766723240910400)
XLA Ops:
  0.6 1.0 slice_bitcast_fusion
  1.6 4.9 %collective-permute-start = (bf16[288,512]{1,0:T(8,128)(2,1)S(1)}, bf16[288,512]{1,0:T(8,128)(2,1)S(1)}, u32[]{:S(2)}, u32[]{:S(2)}) collective-permute-start(bf16[288,512]{1,0:T(8,128)(2,1)S(1)} %slice_bitcast_fusion), channel_id=1, source_target_pairs={{0,1},{1,2},{2,3},{3,4},{4,5},{5,6},{6,7},{8,9},{9,10},{10,11},{11... | collective-permute-start | bytes 884744 | tf_op jit(solution)/shard_map/ppermute | solution.py:25
  6.5 4.6 %shard_map.60.early_ref = bf16[512,256]{1,0:T(8,128)(2,1)} custom-call(bf16[4096,512]{1,0:T(8,128)(2,1)} %bitcast.13, bf16[1024,512]{1,0:T(8,128)(2,1)} %bitcast.16, f32[1,512]{1,0:T(1,128)} %bitcast.24, bf16[1024,256]{1,0:T(8,128)(2,1)} %bitcast.19), custom_call_target="tpu_custom_call" | custom-call | tf_op jit(solution)/shard_map/pallas_call | solution.py:125
  11.1 1.3 %collective-permute-start.2 = (bf16[512,256]{1,0:T(8,128)(2,1)}, bf16[512,256]{1,0:T(8,128)(2,1)S(1)}, u32[]{:S(2)}, u32[]{:S(2)}) collective-permute-start(bf16[512,256]{1,0:T(8,128)(2,1)} %shard_map.60.early_ref), channel_id=1, source_target_pairs={{1,0},{2,1},{3,2},{4,3},{5,4},{6,5},{7,6},{9,8},{10,9},{11,10},{12... | collective-permute-start | bytes 786440 | tf_op jit(solution)/shard_map/ppermute | solution.py:25
  12.4 0.3 collective-permute-done.halo_ref
  12.7 0.0 copy-start.2
  12.7 0.7 copy-done.2
  13.5 4.6 %shard_map.59.head_ref = bf16[512,256]{1,0:T(8,128)(2,1)} custom-call(s32[1]{0:T(128)} %bitcast.3.live_ref, bf16[4096,512]{1,0:T(8,128)(2,1)} %bitcast.14, bf16[288,512]{1,0:T(8,128)(2,1)} %copy-done.2, bf16[1024,512]{1,0:T(8,128)(2,1)} %bitcast.17, f32[1,512]{1,0:T(1,128)} %bitcast.25, bf16[1024,256]{1,0:T(8,128)(2,1)} %bitcast.20), custom_call_target="tpu_custom_call" | custom-call | tf_op jit(solution)/shard_map/pallas_call | solution.py:125
  18.1 1.3 %collective-permute-start.1 = (bf16[512,256]{1,0:T(8,128)(2,1)}, bf16[512,256]{1,0:T(8,128)(2,1)S(1)}, u32[]{:S(2)}, u32[]{:S(2)}) collective-permute-start(bf16[512,256]{1,0:T(8,128)(2,1)} %shard_map.59.head_ref), channel_id=1, source_target_pairs={{1,0},{2,1},{3,2},{4,3},{5,4},{6,5},{7,6},{9,8},{10,9},{11,10},{12... | collective-permute-start | bytes 786440 | tf_op jit(solution)/shard_map/ppermute | solution.py:25
  19.4 0.6 add_convert_fusion.edge_ref
  20.0 14.5 %shard_map.61 = (bf16[4096,256]{1,0:T(8,128)(2,1)}, f32[256,256]{1,0:T(8,128)}, f32[256,256]{1,0:T(8,128)}, f32[8,256]{1,0:T(8,128)}) custom-call(s32[2]{0:T(128)} %add_convert_fusion.edge_ref, bf16[4096,512]{1,0:T(8,128)(2,1)} %bitcast.15, bf16[512,256]{1,0:T(8,128)(2,1)} %shard_map.59.head_ref, bf16[512,256]{1,0:T(8,128)(2,1)} %shard_map.60.early_ref, ...), custom_call_target="tpu_custom_call" | custom-call | tf_op jit(solution)/shard_map/pallas_call | solution.py:184
  34.4 0.0 collective-permute-done.2.ahead_early_ref
  34.4 0.0 copy-start
  34.4 0.0 collective-permute-done.1.ahead_head_ref
  34.5 0.0 copy-start.1
  34.5 0.7 copy-done
  35.1 0.1 copy-done.1
  35.2 3.0 %shard_map.62 = f32[288,256]{1,0:T(8,128)} custom-call(bf16[4096,256]{1,0:T(8,128)(2,1)} %get-tuple-element.10.feature_ref, bf16[512,256]{1,0:T(8,128)(2,1)} %copy-done.1, bf16[512,256]{1,0:T(8,128)(2,1)} %copy-done, f32[256,256]{1,0:T(8,128)} %get-tuple-element.11.inst, f32[256,256]{1,0:T(8,128)} %get-tuple-element.12.lag, f32[8,256]{1,0:T(8,128)} %get-tuple-element.13.total), custom_call_target="tpu_custom_call" | custom-call | tf_op jit(solution)/shard_map/pallas_call | solution.py:217
  38.2 9.8 %all_to_all.15 = f32[4,72,256]{2,1,0:T(8,128)S(1)} all-to-all(f32[4,72,256]{2,1,0:T(8,128)} %bitcast.23), channel_id=1, replica_groups=mesh['rep'=4,'tm'=8] {'rep'}, dimensions={0} | all-to-all | bytes 589824 | tf_op jit(solution)/shard_map/all_to_all | solution.py:373
  48.1 25.3 %all_to_all.16 = f32[8,72,256]{2,1,0:T(8,128)S(1)} all-to-all(f32[8,72,256]{2,1,0:T(8,128)S(1)} %broadcast_in_dim.8), channel_id=1, replica_groups=mesh['rep'=4,'tm'=8] {'tm'}, dimensions={0} | all-to-all | bytes 1179648 | tf_op jit(solution)/shard_map/all_to_all | solution.py:367
  73.4 9.5 %all_to_all.17 = f32[4,72,256]{2,1,0:T(8,128)} all-to-all(f32[4,72,256]{2,1,0:T(8,128)S(1)} %broadcast_in_dim.9), channel_id=1, replica_groups=mesh['rep'=4,'tm'=8] {'rep'}, dimensions={0} | all-to-all | bytes 589824 | tf_op jit(solution)/shard_map/all_to_all | solution.py:367
  82.9 10.6 %shard_map.63 = (bf16[4,256,256]{2,1,0:T(8,128)(2,1)}, f32[2,8,256]{2,1,0:T(8,128)}) custom-call(f32[1]{0:T(128)} %constant.3.clone.1.scale_ref, f32[288,256]{1,0:T(8,128)} %bitcast.22), custom_call_target="tpu_custom_call" | custom-call | tf_op jit(solution)/shard_map/pallas_call | solution.py:308
  93.4 8.0 %shard_map.64 = (f32[4096,256]{1,0:T(8,128)}, f32[4096,256]{1,0:T(8,128)}) custom-call(s32[2]{0:T(128)} %add_convert_fusion.edge_ref, bf16[4096,256]{1,0:T(8,128)(2,1)} %get-tuple-element.10.feature_ref, bf16[512,256]{1,0:T(8,128)(2,1)} %copy-done.1, bf16[512,256]{1,0:T(8,128)(2,1)} %copy-done, bf16[4,256,256]{2,1,0:T(8,128)(2,1)} %get-tuple-element.14.split_ref, ...), custom_call_target="tpu_custom_call" | custom-call | tf_op jit(solution)/shard_map/pallas_call | solution.py:355
  (4 shorter events, 0.1 us)
Async XLA Ops:
  1.6 11.1 %collective-permute-start = (bf16[288,512]{1,0:T(8,128)(2,1)S(1)}, bf16[288,512]{1,0:T(8,128)(2,1)S(1)}, u32[]{:S(2)}, u32[]{:S(2)}) collective-permute-start(bf16[288,512]{1,0:T(8,128)(2,1)S(1)} %slice_bitcast_fusion), channel_id=1, source_target_pairs={{0,1},{1,2},{2,3},{3,4},{4,5},{5,6},{6,7},{8,9},{9,10},{10,11},{11... | collective-permute-start | bytes 884744 | tf_op jit(solution)/shard_map/ppermute | solution.py:25
  11.1 23.3 %collective-permute-start.2 = (bf16[512,256]{1,0:T(8,128)(2,1)}, bf16[512,256]{1,0:T(8,128)(2,1)S(1)}, u32[]{:S(2)}, u32[]{:S(2)}) collective-permute-start(bf16[512,256]{1,0:T(8,128)(2,1)} %shard_map.60.early_ref), channel_id=1, source_target_pairs={{1,0},{2,1},{3,2},{4,3},{5,4},{6,5},{7,6},{9,8},{10,9},{11,10},{12... | collective-permute-start | bytes 786440 | tf_op jit(solution)/shard_map/ppermute | solution.py:25
  12.7 0.7 copy-start.2
  18.1 16.4 %collective-permute-start.1 = (bf16[512,256]{1,0:T(8,128)(2,1)}, bf16[512,256]{1,0:T(8,128)(2,1)S(1)}, u32[]{:S(2)}, u32[]{:S(2)}) collective-permute-start(bf16[512,256]{1,0:T(8,128)(2,1)} %shard_map.59.head_ref), channel_id=1, source_target_pairs={{1,0},{2,1},{3,2},{4,3},{5,4},{6,5},{7,6},{9,8},{10,9},{11,10},{12... | collective-permute-start | bytes 786440 | tf_op jit(solution)/shard_map/ppermute | solution.py:25
  34.4 0.7 copy-start
  34.5 0.8 copy-start.1

commit v3 on v2

v3 whole, which is shorter than its diff:
```python
import jax
import jax.numpy as jnp
from jax import lax
from jax.experimental import pallas as pl
from jax.experimental.pallas import tpu as pltpu
from jax.sharding import Mesh, PartitionSpec as P

D1 = 32
D2 = 256
LAG = 1024
RIDGE = 0.001
CHUNK = 512
PANEL = 16
MIB = 1024 * 1024

F32 = jnp.float32
BF16 = jnp.bfloat16
HIGHEST = lax.Precision.HIGHEST


def passed_along(value, axis, steps):
    count = lax.axis_size(axis)
    first, last = (max(0, -steps), min(count, count - steps))
    return lax.ppermute(value, axis, [(source, source + steps) for source in range(first, last)])


def across(a, b, precision=None):
    return lax.dot_general(a, b, (((1,), (1,)), ((), ())), precision=precision, preferred_element_type=F32)


def gram(a, b):
    return lax.dot_general(a, b, (((0,), (0,)), ((), ())), preferred_element_type=F32)


def silu(x):
    half = 0.5 * x
    return half + half * jnp.tanh(half)


def hidden_rows(xs, hs, at, rows, w1_ref, b1_ref):
    channels = xs.shape[1]
    z = jnp.dot(xs[pl.ds(at + D1, rows), :], w1_ref[:channels, :], preferred_element_type=F32)
    z += jnp.dot(xs[pl.ds(at, rows), :], w1_ref[channels:, :], preferred_element_type=F32)
    return silu(z + b1_ref[...]).astype(BF16)


def feature_rows(hs, at, rows, w2_ref):
    hid = hs.shape[1]
    value = jnp.dot(hs[pl.ds(at + D2, rows), :], w2_ref[:hid, :], preferred_element_type=F32)
    value += jnp.dot(hs[pl.ds(at, rows), :], w2_ref[hid:, :], preferred_element_type=F32)
    return value.astype(BF16)


def early_kernel(frames_ref, w1_ref, b1_ref, w2_ref, out_ref, xs, hs, sem):
    copy = pltpu.make_async_copy(frames_ref.at[pl.ds(LAG // 2 - D1 - D2, xs.shape[0])], xs, sem)
    copy.start()
    copy.wait()
    for at in range(0, hs.shape[0], D2):
        hs[at : at + D2, :] = hidden_rows(xs, hs, at, D2, w1_ref, b1_ref)
    out_ref[...] = feature_rows(hs, 0, out_ref.shape[0], w2_ref)


def head_kernel(frames_ref, halo_ref, w1_ref, b1_ref, w2_ref, out_ref, xs, hs, sem):
    halo_rows = halo_ref.shape[0]
    copy = pltpu.make_async_copy(
        frames_ref.at[pl.ds(0, out_ref.shape[0])], xs.at[pl.ds(halo_rows, out_ref.shape[0])], sem
    )
    copy.start()
    xs[:halo_rows, :] = halo_ref[...]
    before = hidden_rows(xs, hs, 0, D2, w1_ref, b1_ref)
    hs[:D2, :] = jnp.where(lax.axis_index("tm") > 0, before, jnp.zeros_like(before))
    copy.wait()
    for at in range(D2, hs.shape[0], D2):
        hs[at : at + D2, :] = hidden_rows(xs, hs, at, D2, w1_ref, b1_ref)
    out_ref[...] = feature_rows(hs, 0, out_ref.shape[0], w2_ref)


def feature_scratch(rows, channels, hid):
    return [
        pltpu.VMEM((rows + D1 + D2, channels), BF16),
        pltpu.VMEM((rows + D2, hid), BF16),
    ]


def first_rows(kernel, operands, specs, w1, b1, w2):
    vmem = pl.BlockSpec(memory_space=pltpu.VMEM)
    rows = LAG // 2
    return pl.pallas_call(
        kernel,
        in_specs=specs + [vmem, vmem, vmem],
        out_specs=vmem,
        out_shape=jax.ShapeDtypeStruct((rows, w2.shape[1]), BF16),
        scratch_shapes=feature_scratch(rows, w1.shape[0] // 2, w1.shape[1]) + [pltpu.SemaphoreType.DMA],
        compiler_params=pltpu.CompilerParams(vmem_limit_bytes=8 * MIB),
    )(*operands, w1, b1, w2)


def column_sum(rows):
    ones = jnp.ones((8, rows.shape[0]), BF16)
    return jnp.dot(ones, rows, preferred_element_type=F32)


def body_kernel(frames_ref, head_ref, early_ref, w1_ref, b1_ref, w2_ref, out_ref, inst, lag, total, xs, hs, sems):
    rows, feat = out_ref.shape
    first = LAG - D1 - D2
    steps = (rows - LAG) // CHUNK

    def arriving(step):
        start = step * CHUNK + D1 + D2
        return pltpu.make_async_copy(
            frames_ref.at[pl.ds(first + start, CHUNK)], xs.at[pl.ds(start, CHUNK)], sems.at[step]
        )

    opening = pltpu.make_async_copy(
        frames_ref.at[pl.ds(first, D1 + D2)], xs.at[pl.ds(0, D1 + D2)], sems.at[steps]
    )
    opening.start()
    for step in range(steps):
        arriving(step).start()
    half = LAG // 2
    out_ref[:half, :] = head_ref[...]
    out_ref[half:LAG, :] = early_ref[...]
    tm_index, tm_last = lax.axis_index("tm"), lax.axis_size("tm") - 1
    first_weight = jnp.where(tm_index == 0, 1.0, 2.0)
    last_weight = jnp.where(tm_index == tm_last, 1.0, 2.0)
    start = out_ref[:LAG, :]
    inst[...] = first_weight * gram(start, start)
    total[...] = first_weight * column_sum(start)
    lag[...] = jnp.zeros_like(lag)
    opening.wait()
    hs[:D2, :] = hidden_rows(xs, hs, 0, D2, w1_ref, b1_ref)
    arriving(0).wait()
    hs[D2 : D2 + CHUNK, :] = hidden_rows(xs, hs, D2, CHUNK, w1_ref, b1_ref)

    def finish(step):
        value = feature_rows(hs, step * CHUNK, CHUNK, w2_ref)
        out_ref[pl.ds(LAG + step * CHUNK, CHUNK), :] = value
        weight = jnp.where(step >= steps - LAG // CHUNK, last_weight, 2.0)
        both = gram(value, jnp.concatenate([value, out_ref[pl.ds(step * CHUNK, CHUNK), :]], 1))
        inst[...] += weight * both[:, :feat]
        lag[...] += both[:, feat:]
        total[...] += weight * column_sum(value)

    def loop(step, carry):
        arriving(step + 1).wait()
        at = pl.multiple_of((step + 1) * CHUNK + D2, D2)
        fresh = hidden_rows(xs, hs, at, CHUNK, w1_ref, b1_ref)
        finish(step)
        hs[pl.ds(at, CHUNK), :] = fresh
        return carry

    lax.fori_loop(0, steps - 1, loop, 0)
    finish(steps - 1)


def body(frames, head, early, w1, b1, w2):
    rows, channels = frames.shape
    hid, feat = w1.shape[1], w2.shape[1]
    vmem = pl.BlockSpec(memory_space=pltpu.VMEM)
    square = jax.ShapeDtypeStruct((feat, feat), F32)
    return pl.pallas_call(
        body_kernel,
        in_specs=[pl.BlockSpec(memory_space=pl.ANY)] + [vmem] * 5,
        out_specs=(vmem,) * 4,
        out_shape=(
            jax.ShapeDtypeStruct((rows, feat), BF16),
            square,
            square,
            jax.ShapeDtypeStruct((8, feat), F32),
        ),
        scratch_shapes=feature_scratch(rows - LAG, channels, hid)
        + [pltpu.SemaphoreType.DMA((rows // CHUNK,))],
        compiler_params=pltpu.CompilerParams(vmem_limit_bytes=24 * MIB),
    )(frames, head, early, w1, b1, w2)


def pack_kernel(feature_ref, ahead_head_ref, ahead_early_ref, inst, lag, total, kept_ref, sent_ref, packed):
    feat = inst.shape[0]
    half = LAG // 2
    edge = feature_ref.shape[0] - LAG
    cross = lag[...] + gram(ahead_head_ref[...], feature_ref[edge : edge + half, :])
    cross += gram(ahead_early_ref[...], feature_ref[edge + half :, :])
    both = cross + cross.T
    row = lax.broadcasted_iota(jnp.int32, (feat, feat), 0)
    column = lax.broadcasted_iota(jnp.int32, (feat, feat), 1)
    packed[:, :feat] = jnp.where(column >= row, inst[...], both)
    packed[:, feat:] = jnp.zeros((feat, packed.shape[1] - feat), F32)
    diagonal = jnp.sum(jnp.where(column == row, both, 0.0), 0, keepdims=True)
    for index in range(feat // 128):
        part = slice(index * 128, index * 128 + 128)
        packed[index : index + 1, feat:] = total[0:1, part]
        packed[index + 2 : index + 3, feat:] = diagonal[:, part]
    share = kept_ref.shape[0]
    core = lax.axis_index("core")
    kept_ref[...] = packed[pl.ds(pl.multiple_of(core * share, share), share), :]
    sent_ref[...] = packed[pl.ds(pl.multiple_of((1 - core) * share, share), share), :]


def pack(feature, ahead_head, ahead_early, inst, lag, total):
    vmem = pl.BlockSpec(memory_space=pltpu.VMEM)
    feat = inst.shape[0]
    share = jax.ShapeDtypeStruct((feat // 2, feat + 128), F32)
    return pl.pallas_call(
        pack_kernel,
        in_specs=[vmem] * 6,
        out_specs=(vmem, vmem),
        out_shape=(share, share),
        scratch_shapes=[pltpu.VMEM((feat, feat + 128), F32)],
        compiler_params=pltpu.CompilerParams(vmem_limit_bytes=8 * MIB),
    )(feature, ahead_head, ahead_early, inst, lag, total)


def three_parts(x):
    high = x.astype(BF16)
    rest = x - high.astype(F32)
    middle = rest.astype(BF16)
    low = (rest - middle.astype(F32)).astype(BF16)
    return high, middle, low


def inverse_factor(work):
    size = work.shape[0]
    lane = lax.broadcasted_iota(jnp.int32, (PANEL, size), 1)
    sub = lax.broadcasted_iota(jnp.int32, (PANEL, size), 0)
    sub_narrow = lax.broadcasted_iota(jnp.int32, (PANEL, 128), 0)
    for start in range(0, size, PANEL):
        stop = start + PANEL
        panel = work[start:stop, :]
        columns = [
            jnp.broadcast_to(panel[:, start + k : start + k + 1], (PANEL, 128)) for k in range(PANEL)
        ]
        panel = jnp.where(
            (lane >= start) & (lane < stop), jnp.where(lane - start == sub, 1.0, 0.0), panel
        )
        pivots = jnp.ones((PANEL, 128), F32)
        for j in range(PANEL):
            pivot = columns[j][j : j + 1, :]
            factor = columns[j] * (1.0 / pivot)
            pivots = jnp.where(sub_narrow == j, pivot, pivots)
            for k in range(j + 1, PANEL):
                columns[k] = columns[k] - factor * columns[k][j : j + 1, :]
            if j + 1 < PANEL:
                below = jnp.where(sub_narrow > j, factor, 0.0)
                wide = jnp.concatenate([below] * (size // 128), 1)
                panel = panel - wide * panel[j : j + 1, :]
        scale = lax.rsqrt(pivots)
        panel = panel * jnp.concatenate([scale] * (size // 128), 1)
        work[start:stop, :] = panel
        if stop < size:
            high, middle, low = three_parts(panel)
            left = jnp.concatenate([high, high, middle, high, low, middle], 0)
            right = jnp.concatenate([high, middle, high, low, high, middle], 0)
            first = stop // 128 * 128
            update = gram(left[:, first:], right)
            kept = lax.broadcasted_iota(jnp.int32, (size - stop, size), 1)
            kept = (kept < start) | (kept >= stop)
            work[stop:, :] = jnp.where(kept, work[stop:, :], 0.0) - update[stop - first :]
    row = lax.broadcasted_iota(jnp.int32, (size, size), 0)
    column = lax.broadcasted_iota(jnp.int32, (size, size), 1)
    return jnp.where(column <= row, work[...], 0.0)


def koopman_kernel(scale_ref, mine_ref, other_ref, split_ref, shift_ref, work, packed_ref):
    share = mine_ref.shape[0]
    feat = 2 * share
    scale = scale_ref[0]
    core = lax.axis_index("core")
    packed_ref[pl.ds(pl.multiple_of(core * share, share), share), :] = mine_ref[...]
    packed_ref[pl.ds(pl.multiple_of((1 - core) * share, share), share), :] = other_ref[...]
    packed = packed_ref[:, :feat]
    halves = feat // 128
    mean = jnp.concatenate([packed_ref[h : h + 1, feat:] for h in range(halves)], 1) * scale
    diagonal = jnp.concatenate([packed_ref[2 + h : 3 + h, feat:] for h in range(halves)], 1)
    row = lax.broadcasted_iota(jnp.int32, (feat, feat), 0)
    column = lax.broadcasted_iota(jnp.int32, (feat, feat), 1)
    turned = packed.T
    centre = jnp.broadcast_to(mean, (feat, feat))
    centre = centre * centre.T
    inst = jnp.where(column >= row, packed, turned)
    lag = jnp.where(column < row, packed, turned)
    lag = jnp.where(column == row, jnp.broadcast_to(diagonal, (feat, feat)), lag)
    work[...] = inst * scale - centre + jnp.where(column == row, RIDGE, 0.0)
    lag = lag * scale - centre
    inverse = inverse_factor(work)
    half_step = jnp.dot(inverse, lag, precision=HIGHEST, preferred_element_type=F32)
    koopman = across(half_step, inverse, HIGHEST)
    moved = jnp.dot(koopman, inverse, precision=HIGHEST, preferred_element_type=F32)
    for index, matrix in enumerate((inverse, moved)):
        turned = matrix.T
        high = turned.astype(BF16)
        split_ref[2 * index] = high
        split_ref[2 * index + 1] = (turned - high.astype(F32)).astype(BF16)
        rows = jnp.broadcast_to(mean, (8, feat))
        shift_ref[index] = jnp.dot(rows, turned, precision=HIGHEST, preferred_element_type=F32)


def koopman_parts(scale, mine, other):
    feat = 2 * mine.shape[0]
    vmem = pl.BlockSpec(memory_space=pltpu.VMEM)
    return pl.pallas_call(
        koopman_kernel,
        in_specs=[pl.BlockSpec(memory_space=pltpu.SMEM), vmem, vmem],
        out_specs=(vmem, vmem),
        out_shape=(
            jax.ShapeDtypeStruct((4, feat, feat), BF16),
            jax.ShapeDtypeStruct((2, 8, feat), F32),
        ),
        scratch_shapes=[pltpu.VMEM((feat, feat), F32), pltpu.VMEM((feat, mine.shape[1]), F32)],
        compiler_params=pltpu.CompilerParams(vmem_limit_bytes=12 * MIB),
    )(scale, mine, other)


def project_kernel(
    feature_ref, ahead_head_ref, ahead_early_ref, split_ref, shift_ref, moved_ref, residual_ref
):
    step = pl.program_id(0)
    inside = feature_ref.shape[0] // CHUNK - 2

    def product(block, index):
        value = jnp.dot(block, split_ref[2 * index], preferred_element_type=F32)
        value += jnp.dot(block, split_ref[2 * index + 1], preferred_element_type=F32)
        return value - shift_ref[index][0:1]

    def moved():
        value = product(feature_ref[pl.ds(pl.multiple_of(step * CHUNK, CHUNK), CHUNK), :], 1)
        moved_ref[...] = value
        return value

    @pl.when(step < inside)
    def _():
        later = feature_ref[pl.ds(pl.multiple_of(step * CHUNK + LAG, CHUNK), CHUNK), :]
        residual_ref[...] = product(later, 0) - moved()

    for index, ahead_ref in enumerate((ahead_head_ref, ahead_early_ref)):

        @pl.when(step == inside + index)
        def _():
            value = product(ahead_ref[...], 0) - moved()
            at_end = lax.axis_index("tm") == lax.axis_size("tm") - 1
            residual_ref[...] = jnp.where(at_end, 0.0, value)


def project(feature, ahead_head, ahead_early, split, shift):
    rows, feat = feature.shape
    vmem = pl.BlockSpec(memory_space=pltpu.VMEM)
    out = jax.ShapeDtypeStruct((rows, feat), F32)
    block = pl.BlockSpec((CHUNK, feat), lambda i: (i, 0))
    return pl.pallas_call(
        project_kernel,
        grid=(rows // CHUNK,),
        in_specs=[vmem] * 5,
        out_specs=(block, block),
        out_shape=(out, out),
        compiler_params=pltpu.CompilerParams(vmem_limit_bytes=16 * MIB),
    )(feature, ahead_head, ahead_early, split, shift)


def summed(kept, sent):
    swap = [(0, 1), (1, 0)]
    chips = ("x", "tm")
    count = lax.axis_size("x") * lax.axis_size("tm")
    share, width = kept.shape
    parts = (kept + lax.ppermute(sent, "core", swap)).reshape(count, share // count, width)
    mine = jnp.sum(lax.all_to_all(parts, chips, 0, 0, tiled=True), 0)
    copies = jnp.broadcast_to(mine[None], parts.shape)
    mine = lax.all_to_all(copies, chips, 0, 0, tiled=True).reshape(share, width)
    return mine, lax.ppermute(mine, "core", swap)


def on_device(frames, first_weight, first_bias, second_weight):
    frame_block = frames[0]
    row_count, channels = frame_block.shape
    hid, feat = second_weight.shape[1:]
    weights = (
        first_weight.reshape(2 * channels, hid),
        first_bias.reshape(1, hid),
        second_weight.reshape(2 * hid, feat),
    )
    anywhere, vmem = (pl.BlockSpec(memory_space=m) for m in (pl.ANY, pltpu.VMEM))

    halo = passed_along(frame_block[row_count - D1 - D2 :], "tm", 1)
    early = first_rows(early_kernel, (frame_block,), [anywhere], *weights)
    ahead_early = passed_along(early, "tm", -1)
    head = first_rows(head_kernel, (frame_block, halo), [anywhere, vmem], *weights)
    ahead_head = passed_along(head, "tm", -1)
    feature, inst, lag, total = body(frame_block, head, early, *weights)
    mine, other = summed(*pack(feature, ahead_head, ahead_early, inst, lag, total))
    replicas = lax.axis_size("x") * lax.axis_size("core")
    pair_count = replicas * (row_count * lax.axis_size("tm") - LAG)
    scale = jnp.full((1,), 1.0 / (2.0 * pair_count), F32)
    split, shift = koopman_parts(scale, mine, other)
    propagated, residual = project(feature, ahead_head, ahead_early, split, shift)
    return (propagated[None], residual[None])


def solution(mesh):
    replicas, blocks = mesh.devices.shape
    chips = Mesh(mesh.devices.reshape(replicas // 2, 2, blocks), ("x", "core", "tm"))
    split = P(("x", "core"), "tm", None)
    return jax.shard_map(
        on_device,
        mesh=chips,
        in_specs=(split, P(), P(), P()),
        out_specs=(split, split),
        check_vma=False,
    )
```

time: 102 us -> 78.4 us (0.77)
  Pallas kernels: 45.2 us -> 30.5 us
  blocking collectives: 44.5 us -> 29.9 us
  local copies, waits for them, and re-layouts: 2.54 us -> 6.21 us
  waiting for transfers between devices: 0.31 us -> 2.88 us
    all_to_all x3 -> x2, blocking collectives: 44.5 us -> 29.9 us  [the longest x1 18.5 us: summed(): mine = jnp.sum(lax.all_to_all(parts, chips, 0, 0, tiled=True), 0)]
    pallas_call x3, Pallas kernels: 25.4 us -> 18.3 us  [the longest x1 11.7 us: body(): pl.pallas_call(body_kernel, in_specs=[pl.BlockSpec(memory_space=pl.ANY)]...]
    pallas_call x2, Pallas kernels: 9.2 us -> 3.11 us  [first_rows(): pl.pallas_call(kernel, in_specs=specs + [vmem, vmem, vmem], out_specs=vme...]
    unnamed x6 -> x16, local copies, waits for them, and re-layouts: 1.5 us -> 5.15 us
    ppermute x0 -> x2, waiting for transfers between devices: none -> 2.87 us  [the longest x1 1.44 us: summed(): return (mine, lax.ppermute(mine, 'core', swap))]
    pallas_call x1, Pallas kernels: 10.6 us -> 9.03 us  [koopman_parts(): pl.pallas_call(koopman_kernel, in_specs=[pl.BlockSpec(memory_space=pltpu....]
  transfers between devices with their start and end apart: 3 -> 5, of which waited for: 1 -> 2; matrix products, arithmetic and copies ran while one was open for 1% -> 0% of each run, Pallas kernels for 23% -> 19%
where the time goes in v3:
time: 78.4 us; the launch traced here: 78.1 us
  Pallas kernels  30.5 us (39%)
  blocking collectives  29.9 us (38%)
  starting transfers between devices  7.81 us (10%)
  local copies, waits for them, and re-layouts  6.21 us (8%)
  waiting for transfers between devices  2.88 us (4%)
  between operations  0.8 us (1%)
    all_to_all x1, blocking collectives, summed(): mine = jnp.sum(lax.all_to_all(parts, chips, 0, 0, tiled=True), 0)  18.5 us
    pallas_call x1, Pallas kernels, body(): pl.pallas_call(body_kernel, in_specs=[pl.BlockSpec(memory_space=pl.ANY)]...  11.7 us
    all_to_all x1, blocking collectives, summed(): mine = lax.all_to_all(copies, chips, 0, 0, tiled=True).reshape(share, width)  11.4 us
    pallas_call x1, Pallas kernels, koopman_parts(): pl.pallas_call(koopman_kernel, in_specs=[pl.BlockSpec(memory_space=pltpu....  9.03 us
    ppermute x3, starting transfers between devices, passed_along(): lax.ppermute(value, axis, [(source, source + steps) for source in range(f...  7.74 us
    pallas_call x1, Pallas kernels, project(): pl.pallas_call(project_kernel, grid=(rows // CHUNK,), in_specs=[vmem] * 5...  6.1 us
    unnamed x16, local copies, waits for them, and re-layouts  5.15 us
    pallas_call x2, Pallas kernels, first_rows(): pl.pallas_call(kernel, in_specs=specs + [vmem, vmem, vmem], out_specs=vme...  3.11 us
  transfers between devices with their start and end apart: 5, of which 2 were waited for; matrix products, arithmetic and copies ran while one was open for 0% of the time, Pallas kernels for 19%

profile of v3, /device:TPU:0, one launch (start us, length us, event | category | flops | bytes accessed | tf_op | source)
XLA Modules:
  0.0 78.1 jit_solution(743618554162189285)
XLA Ops:
  0.6 0.0 copy-start.5
  0.6 1.0 %slice_bitcast_fusion = bf16[288,512]{1,0:T(8,128)(2,1)S(1)} fusion(bf16[1,4096,512]{2,1,0:T(8,128)(2,1)} %param.4), kind=kLoop, calls=%fused_computation | loop fusion | bytes 589824 | tf_op jit(solution)/shard_map/slice | solution.py:381
  1.7 4.9 %collective-permute-start = (bf16[288,512]{1,0:T(8,128)(2,1)S(1)}, bf16[288,512]{1,0:T(8,128)(2,1)S(1)}, u32[]{:S(2)}, u32[]{:S(2)}) collective-permute-start(bf16[288,512]{1,0:T(8,128)(2,1)S(1)} %slice_bitcast_fusion), channel_id=1, source_target_pairs={{0,1},{1,2},{2,3},{3,4},{4,5},{5,6},{6,7},{8,9},{9,10},{10,11},{11... | collective-permute-start | bytes 884744 | tf_op jit(solution)/shard_map/ppermute | solution.py:24
  6.6 0.0 copy-start
  6.6 2.2 %copy-done = bf16[1,4096,512]{2,1,0:T(8,128)(2,1)S(1)} copy-done((bf16[1,4096,512]{2,1,0:T(8,128)(2,1)S(1)}, bf16[1,4096,512]{2,1,0:T(8,128)(2,1)}, u32[]{:S(2)}) %copy-start) | copy-done | bytes 4194328
  8.8 0.0 copy-start.2
  8.8 1.2 %copy-done.2 = bf16[2,512,512]{2,1,0:T(8,128)(2,1)S(1)} copy-done((bf16[2,512,512]{2,1,0:T(8,128)(2,1)S(1)}, bf16[2,512,512]{2,1,0:T(8,128)(2,1)}, u32[]{:S(2)}) %copy-start.2) | copy-done | bytes 1048600
  10.0 1.0 %copy-done.4 = bf16[2,512,256]{2,1,0:T(8,128)(2,1)S(1)} copy-done((bf16[2,512,256]{2,1,0:T(8,128)(2,1)S(1)}, bf16[2,512,256]{2,1,0:T(8,128)(2,1)}, u32[]{:S(2)}) %copy-start.4) | copy-done | bytes 524312
  11.0 0.7 copy-done.6
  11.7 1.5 %shard_map.60.early_ref = bf16[512,256]{1,0:T(8,128)(2,1)S(1)} custom-call(bf16[4096,512]{1,0:T(8,128)(2,1)S(1)} %bitcast.11, bf16[1024,512]{1,0:T(8,128)(2,1)S(1)} %bitcast.14, f32[1,512]{1,0:T(1,128)S(1)} %bitcast.22, bf16[1024,256]{1,0:T(8,128)(2,1)S(1)} %bitcast.17), custom_call_target="tpu_custom_call" | custom-call | tf_op jit(solution)/shard_map/pallas_call | solution.py:88
  13.2 0.0 copy-start.1
  13.2 0.0 copy-start.7
  13.2 1.6 %collective-permute-start.2 = (bf16[512,256]{1,0:T(8,128)(2,1)S(1)}, bf16[512,256]{1,0:T(8,128)(2,1)S(1)}, u32[]{:S(2)}, u32[]{:S(2)}) collective-permute-start(bf16[512,256]{1,0:T(8,128)(2,1)S(1)} %shard_map.60.early_ref), channel_id=1, source_target_pairs={{1,0},{2,1},{3,2},{4,3},{5,4},{6,5},{7,6},{9,8},{10,9},{11,10},{12... | collective-permute-start | bytes 786440 | tf_op jit(solution)/shard_map/ppermute | solution.py:24
  14.8 0.0 collective-permute-done.halo_ref
  14.8 0.0 copy-done.5
  14.8 0.0 copy-done.3
  14.8 1.6 %shard_map.59.head_ref = bf16[512,256]{1,0:T(8,128)(2,1)S(1)} custom-call(bf16[4096,512]{1,0:T(8,128)(2,1)S(1)} %bitcast.12, bf16[288,512]{1,0:T(8,128)(2,1)S(1)} %collective-permute-done.halo_ref, bf16[1024,512]{1,0:T(8,128)(2,1)S(1)} %bitcast.15, f32[1,512]{1,0:T(1,128)S(1)} %bitcast.23, bf16[1024,256]{1,0:T(8,128)(2,1)S(1)} %bitcast.18), custom_call_target="tpu_custom_call" | custom-call | tf_op jit(solution)/shard_map/pallas_call | solution.py:88
  16.5 1.3 %collective-permute-start.1 = (bf16[512,256]{1,0:T(8,128)(2,1)S(1)}, bf16[512,256]{1,0:T(8,128)(2,1)S(1)}, u32[]{:S(2)}, u32[]{:S(2)}) collective-permute-start(bf16[512,256]{1,0:T(8,128)(2,1)S(1)} %shard_map.59.head_ref), channel_id=1, source_target_pairs={{1,0},{2,1},{3,2},{4,3},{5,4},{6,5},{7,6},{9,8},{10,9},{11,10},{12... | collective-permute-start | bytes 786440 | tf_op jit(solution)/shard_map/ppermute | solution.py:24
  17.8 0.0 copy-done.1
  17.8 0.0 copy-done.7
  17.8 11.7 %shard_map.61 = (bf16[4096,256]{1,0:T(8,128)(2,1)S(1)}, f32[256,256]{1,0:T(8,128)S(1)}, f32[256,256]{1,0:T(8,128)S(1)}, f32[8,256]{1,0:T(8,128)S(1)}) custom-call(bf16[4096,512]{1,0:T(8,128)(2,1)S(1)} %bitcast.13, bf16[512,256]{1,0:T(8,128)(2,1)S(1)} %shard_map.59.head_ref, bf16[512,256]{1,0:T(8,128)(2,1)S(1)} %shard_map.60.early_ref, ...), custom_call_target="tpu_custom_call" | custom-call | tf_op jit(solution)/shard_map/pallas_call | solution.py:161
  29.5 0.0 collective-permute-done.2.ahead_early_ref
  29.5 0.0 collective-permute-done.1.ahead_head_ref
  29.5 0.5 shard_map.62
  30.0 0.1 collective-permute-start.3
  30.1 1.4 %collective-permute-done.3 = f32[128,384]{1,0:T(8,128)S(1)} collective-permute-done((f32[128,384]{1,0:T(8,128)S(1)}, f32[128,384]{1,0:T(8,128)S(1)}, u32[]{:S(2)}, u32[]{:S(2)}) %collective-permute-start.3) | collective-permute-done | bytes 196640 | tf_op jit(solution)/shard_map/ppermute | solution.py:363
  31.6 18.5 %all_to_all.10 = f32[16,8,384]{2,1,0:T(8,128)S(1)} all-to-all(f32[16,8,384]{2,1,0:T(8,128)S(1)} %add_bitcast_fusion), channel_id=1, replica_groups=mesh['x'=2,'core'=2,'tm'=8] {'x','tm'}, dimensions={0} | all-to-all | bytes 393216 | tf_op jit(solution)/shard_map/all_to_all | solution.py:364
  50.1 11.4 %all_to_all.11 = f32[16,8,384]{2,1,0:T(8,128)S(1)} all-to-all(f32[16,8,384]{2,1,0:T(8,128)S(1)} %broadcast_in_dim.12), channel_id=1, replica_groups=mesh['x'=2,'core'=2,'tm'=8] {'x','tm'}, dimensions={0} | all-to-all | bytes 393216 | tf_op jit(solution)/shard_map/all_to_all | solution.py:366
  61.5 0.0 collective-permute-start.4
  61.5 1.4 %collective-permute-done.4.other_ref = f32[128,384]{1,0:T(8,128)S(1)} collective-permute-done((f32[128,384]{1,0:T(8,128)S(1)}, f32[128,384]{1,0:T(8,128)S(1)}, u32[]{:S(2)}, u32[]{:S(2)}) %collective-permute-start.4) | collective-permute-done | bytes 196640 | tf_op jit(solution)/shard_map/ppermute | solution.py:367
  62.9 9.0 %shard_map.63 = (bf16[4,256,256]{2,1,0:T(8,128)(2,1)S(1)}, f32[2,8,256]{2,1,0:T(8,128)S(1)}) custom-call(f32[1]{0:T(128)} %constant.0.clone.1.scale_ref, f32[128,384]{1,0:T(8,128)S(1)} %bitcast.21, f32[128,384]{1,0:T(8,128)S(1)} %collective-permute-done.4.other_ref), custom_call_target="tpu_custom_call" | custom-call | tf_op jit(solution)/shard_map/pallas_call | solution.py:300
  71.9 6.1 %shard_map.64 = (f32[4096,256]{1,0:T(8,128)}, f32[4096,256]{1,0:T(8,128)}) custom-call(bf16[4096,256]{1,0:T(8,128)(2,1)S(1)} %get-tuple-element.12.feature_ref, bf16[512,256]{1,0:T(8,128)(2,1)S(1)} %collective-permute-done.1.ahead_head_ref, bf16[512,256]{1,0:T(8,128)(2,1)S(1)} %collective-permute-done.2.ahead_early_ref, ...), custom_call_target="tpu_custom_call" | custom-call | tf_op jit(solution)/shard_map/pallas_call | solution.py:348
  (6 shorter events, 0.1 us)
Async XLA Ops:
  0.6 14.2 %copy-start.5 = (bf16[2,512,256]{2,1,0:T(8,128)(2,1)S(1)}, bf16[2,512,256]{2,1,0:T(8,128)(2,1)}, u32[]{:S(2)}) copy-start(bf16[2,512,256]{2,1,0:T(8,128)(2,1)} %param.7) | copy-start | bytes 1572868
  1.7 13.1 %collective-permute-start = (bf16[288,512]{1,0:T(8,128)(2,1)S(1)}, bf16[288,512]{1,0:T(8,128)(2,1)S(1)}, u32[]{:S(2)}, u32[]{:S(2)}) collective-permute-start(bf16[288,512]{1,0:T(8,128)(2,1)S(1)} %slice_bitcast_fusion), channel_id=1, source_target_pairs={{0,1},{1,2},{2,3},{3,4},{4,5},{5,6},{6,7},{8,9},{9,10},{10,11},{11... | collective-permute-start | bytes 884744 | tf_op jit(solution)/shard_map/ppermute | solution.py:24
  6.6 2.2 %copy-start = (bf16[1,4096,512]{2,1,0:T(8,128)(2,1)S(1)}, bf16[1,4096,512]{2,1,0:T(8,128)(2,1)}, u32[]{:S(2)}) copy-start(bf16[1,4096,512]{2,1,0:T(8,128)(2,1)} %param.4) | copy-start | bytes 12582916
  8.8 1.2 %copy-start.2 = (bf16[2,512,512]{2,1,0:T(8,128)(2,1)S(1)}, bf16[2,512,512]{2,1,0:T(8,128)(2,1)}, u32[]{:S(2)}) copy-start(bf16[2,512,512]{2,1,0:T(8,128)(2,1)} %param.5) | copy-start | bytes 3145732
  10.0 1.0 %copy-start.4 = (bf16[2,512,256]{2,1,0:T(8,128)(2,1)S(1)}, bf16[2,512,256]{2,1,0:T(8,128)(2,1)}, u32[]{:S(2)}) copy-start(bf16[2,512,256]{2,1,0:T(8,128)(2,1)} %param.7) | copy-start | bytes 1572868
  11.0 0.7 copy-start.6
  11.7 3.1 %copy-start.3 = (bf16[2,512,512]{2,1,0:T(8,128)(2,1)S(1)}, bf16[2,512,512]{2,1,0:T(8,128)(2,1)}, u32[]{:S(2)}) copy-start(bf16[2,512,512]{2,1,0:T(8,128)(2,1)} %param.5) | copy-start | bytes 3145732
  13.2 4.6 %copy-start.1 = (bf16[1,4096,512]{2,1,0:T(8,128)(2,1)S(1)}, bf16[1,4096,512]{2,1,0:T(8,128)(2,1)}, u32[]{:S(2)}) copy-start(bf16[1,4096,512]{2,1,0:T(8,128)(2,1)} %param.4) | copy-start | bytes 12582916
  13.2 4.6 %copy-start.7 = (f32[512]{0:T(512)S(1)}, f32[512]{0:T(512)}, u32[]{:S(2)}) copy-start(f32[512]{0:T(512)} %param.6) | copy-start | bytes 6148
  13.2 16.3 %collective-permute-start.2 = (bf16[512,256]{1,0:T(8,128)(2,1)S(1)}, bf16[512,256]{1,0:T(8,128)(2,1)S(1)}, u32[]{:S(2)}, u32[]{:S(2)}) collective-permute-start(bf16[512,256]{1,0:T(8,128)(2,1)S(1)} %shard_map.60.early_ref), channel_id=1, source_target_pairs={{1,0},{2,1},{3,2},{4,3},{5,4},{6,5},{7,6},{9,8},{10,9},{11,10},{12... | collective-permute-start | bytes 786440 | tf_op jit(solution)/shard_map/ppermute | solution.py:24
  16.5 13.1 %collective-permute-start.1 = (bf16[512,256]{1,0:T(8,128)(2,1)S(1)}, bf16[512,256]{1,0:T(8,128)(2,1)S(1)}, u32[]{:S(2)}, u32[]{:S(2)}) collective-permute-start(bf16[512,256]{1,0:T(8,128)(2,1)S(1)} %shard_map.59.head_ref), channel_id=1, source_target_pairs={{1,0},{2,1},{3,2},{4,3},{5,4},{6,5},{7,6},{9,8},{10,9},{11,10},{12... | collective-permute-start | bytes 786440 | tf_op jit(solution)/shard_map/ppermute | solution.py:24
  30.0 1.5 %collective-permute-start.3 = (f32[128,384]{1,0:T(8,128)S(1)}, f32[128,384]{1,0:T(8,128)S(1)}, u32[]{:S(2)}, u32[]{:S(2)}) collective-permute-start(f32[128,384]{1,0:T(8,128)S(1)} %get-tuple-element.17), channel_id=1, source_target_pairs={{0,8},{8,0},{1,9},{9,1},{2,10},{10,2},{3,11},{11,3},{4,12},{12,4},... | collective-permute-start | bytes 589832 | tf_op jit(solution)/shard_map/ppermute | solution.py:363
  61.5 1.4 %collective-permute-start.4 = (f32[128,384]{1,0:T(8,128)S(1)}, f32[128,384]{1,0:T(8,128)S(1)}, u32[]{:S(2)}, u32[]{:S(2)}) collective-permute-start(f32[128,384]{1,0:T(8,128)S(1)} %bitcast.20), channel_id=1, source_target_pairs={{0,8},{8,0},{1,9},{9,1},{2,10},{10,2},{3,11},{11,3},{4,12},{12,4},... | collective-permute-start | bytes 589832 | tf_op jit(solution)/shard_map/ppermute | solution.py:367

commit v4 on v3

v4 whole, which is shorter than its diff:
```python
import jax
import jax.numpy as jnp
from jax import lax
from jax.experimental import pallas as pl
from jax.experimental.pallas import tpu as pltpu
from jax.sharding import Mesh, PartitionSpec as P

D1 = 32
D2 = 256
LAG = 1024
RIDGE = 0.001
CHUNK = 512
PANEL = 16
MIB = 1024 * 1024

F32 = jnp.float32
BF16 = jnp.bfloat16
HIGHEST = lax.Precision.HIGHEST


def passed_along(value, axis, steps):
    count = lax.axis_size(axis)
    first, last = (max(0, -steps), min(count, count - steps))
    return lax.ppermute(value, axis, [(source, source + steps) for source in range(first, last)])


def across(a, b, precision=None):
    return lax.dot_general(a, b, (((1,), (1,)), ((), ())), precision=precision, preferred_element_type=F32)


def gram(a, b):
    return lax.dot_general(a, b, (((0,), (0,)), ((), ())), preferred_element_type=F32)


def silu(x):
    half = 0.5 * x
    return half + half * jnp.tanh(half)


def hidden_rows(xs, at, rows, w1_ref, b1_ref):
    channels = xs.shape[1]
    z = jnp.dot(xs[pl.ds(at + D1, rows), :], w1_ref[:channels, :], preferred_element_type=F32)
    z += jnp.dot(xs[pl.ds(at, rows), :], w1_ref[channels:, :], preferred_element_type=F32)
    return silu(z + b1_ref[...]).astype(BF16)


def feature_rows(hs, at, rows, w2_ref):
    hid = hs.shape[1]
    value = jnp.dot(hs[pl.ds(at + D2, rows), :], w2_ref[:hid, :], preferred_element_type=F32)
    value += jnp.dot(hs[pl.ds(at, rows), :], w2_ref[hid:, :], preferred_element_type=F32)
    return value.astype(BF16)


def early_kernel(frames_ref, w1_in, b1_in, w2_in, out_ref, near_ref, w1_ref, b1_ref, w2_ref, hs, sems):
    half = LAG // 2
    first = half - D1 - D2
    rows = [(first, LAG - first), (0, first)]
    copies = [
        (frames_ref.at[pl.ds(at, count)], near_ref.at[pl.ds(at, count)]) for at, count in rows
    ] + [(w1_in, w1_ref), (b1_in, b1_ref), (w2_in, w2_ref)]
    copies = [pltpu.make_async_copy(*pair, sems.at[index]) for index, pair in enumerate(copies)]
    for index in (2, 0, 3, 4, 1):
        copies[index].start()
    for index in (2, 0, 3):
        copies[index].wait()
    for at in range(0, hs.shape[0], D2):
        hs[at : at + D2, :] = hidden_rows(near_ref, first + at, D2, w1_ref, b1_ref)
    copies[4].wait()
    out_ref[...] = feature_rows(hs, 0, half, w2_ref)
    copies[1].wait()


def head_kernel(near_ref, halo_ref, w1_ref, b1_ref, w2_ref, out_ref, xs, hs):
    halo_rows = halo_ref.shape[0]
    xs[:halo_rows, :] = halo_ref[...]
    xs[halo_rows:, :] = near_ref[: LAG // 2, :]
    before = hidden_rows(xs, 0, D2, w1_ref, b1_ref)
    hs[:D2, :] = jnp.where(lax.axis_index("tm") > 0, before, jnp.zeros_like(before))
    for at in range(D2, hs.shape[0], D2):
        hs[at : at + D2, :] = hidden_rows(xs, at, D2, w1_ref, b1_ref)
    out_ref[...] = feature_rows(hs, 0, out_ref.shape[0], w2_ref)


def feature_scratch(rows, channels, hid):
    return [
        pltpu.VMEM((rows + D1 + D2, channels), BF16),
        pltpu.VMEM((rows + D2, hid), BF16),
    ]


def early_rows(frames, w1, b1, w2):
    vmem = pl.BlockSpec(memory_space=pltpu.VMEM)
    hbm = pl.BlockSpec(memory_space=pltpu.HBM)
    half, channels, hid = LAG // 2, frames.shape[1], w1.shape[1]
    shapes = [((half, w2.shape[1]), BF16), ((LAG, channels), BF16), (w1.shape, BF16), (b1.shape, F32), (w2.shape, BF16)]
    return pl.pallas_call(
        early_kernel,
        in_specs=[hbm] * 4,
        out_specs=(vmem,) * 5,
        out_shape=tuple(jax.ShapeDtypeStruct(*shape) for shape in shapes),
        scratch_shapes=[pltpu.VMEM((half + D2, hid), BF16), pltpu.SemaphoreType.DMA((5,))],
        compiler_params=pltpu.CompilerParams(vmem_limit_bytes=12 * MIB),
    )(frames, w1, b1, w2)


def head_rows(near, halo, w1, b1, w2):
    vmem = pl.BlockSpec(memory_space=pltpu.VMEM)
    half = LAG // 2
    return pl.pallas_call(
        head_kernel,
        in_specs=[vmem] * 5,
        out_specs=vmem,
        out_shape=jax.ShapeDtypeStruct((half, w2.shape[1]), BF16),
        scratch_shapes=feature_scratch(half, near.shape[1], w1.shape[1]),
        compiler_params=pltpu.CompilerParams(vmem_limit_bytes=12 * MIB),
    )(near, halo, w1, b1, w2)


def column_sum(rows):
    ones = jnp.ones((8, rows.shape[0]), BF16)
    return jnp.dot(ones, rows, preferred_element_type=F32)


def body_kernel(frames_ref, near_ref, head_ref, early_ref, w1_ref, b1_ref, w2_ref, out_ref, inst, lag, total, xs, hs, sems):
    rows, feat = out_ref.shape
    first = LAG - D1 - D2
    steps = (rows - LAG) // CHUNK

    def arriving(step):
        start = step * CHUNK + D1 + D2
        return pltpu.make_async_copy(
            frames_ref.at[pl.ds(first + start, CHUNK)], xs.at[pl.ds(start, CHUNK)], sems.at[step]
        )

    for step in range(steps):
        arriving(step).start()
    xs[: D1 + D2, :] = near_ref[first:, :]
    half = LAG // 2
    out_ref[:half, :] = head_ref[...]
    out_ref[half:LAG, :] = early_ref[...]
    tm_index, tm_last = lax.axis_index("tm"), lax.axis_size("tm") - 1
    first_weight = jnp.where(tm_index == 0, 1.0, 2.0)
    last_weight = jnp.where(tm_index == tm_last, 1.0, 2.0)
    start = out_ref[:LAG, :]
    inst[...] = first_weight * gram(start, start)
    total[...] = first_weight * column_sum(start)
    lag[...] = jnp.zeros_like(lag)
    hs[:D2, :] = hidden_rows(xs, 0, D2, w1_ref, b1_ref)
    arriving(0).wait()
    hs[D2 : D2 + CHUNK, :] = hidden_rows(xs, D2, CHUNK, w1_ref, b1_ref)

    def finish(step):
        value = feature_rows(hs, step * CHUNK, CHUNK, w2_ref)
        out_ref[pl.ds(LAG + step * CHUNK, CHUNK), :] = value
        weight = jnp.where(step >= steps - LAG // CHUNK, last_weight, 2.0)
        both = gram(value, jnp.concatenate([value, out_ref[pl.ds(step * CHUNK, CHUNK), :]], 1))
        inst[...] += weight * both[:, :feat]
        lag[...] += both[:, feat:]
        total[...] += weight * column_sum(value)

    def loop(step, carry):
        arriving(step + 1).wait()
        at = pl.multiple_of((step + 1) * CHUNK + D2, D2)
        fresh = hidden_rows(xs, at, CHUNK, w1_ref, b1_ref)
        finish(step)
        hs[pl.ds(at, CHUNK), :] = fresh
        return carry

    lax.fori_loop(0, steps - 1, loop, 0)
    finish(steps - 1)


def body(frames, near, head, early, w1, b1, w2):
    rows, channels = frames.shape
    hid, feat = w1.shape[1], w2.shape[1]
    vmem = pl.BlockSpec(memory_space=pltpu.VMEM)
    square = jax.ShapeDtypeStruct((feat, feat), F32)
    return pl.pallas_call(
        body_kernel,
        in_specs=[pl.BlockSpec(memory_space=pltpu.HBM)] + [vmem] * 6,
        out_specs=(vmem,) * 4,
        out_shape=(
            jax.ShapeDtypeStruct((rows, feat), BF16),
            square,
            square,
            jax.ShapeDtypeStruct((8, feat), F32),
        ),
        scratch_shapes=feature_scratch(rows - LAG, channels, hid)
        + [pltpu.SemaphoreType.DMA((rows // CHUNK,))],
        compiler_params=pltpu.CompilerParams(vmem_limit_bytes=24 * MIB),
    )(frames, near, head, early, w1, b1, w2)


def pack_kernel(feature_ref, ahead_head_ref, ahead_early_ref, inst, lag, total, kept_ref, sent_ref, packed):
    feat = inst.shape[0]
    half = LAG // 2
    edge = feature_ref.shape[0] - LAG
    cross = lag[...] + gram(ahead_head_ref[...], feature_ref[edge : edge + half, :])
    cross += gram(ahead_early_ref[...], feature_ref[edge + half :, :])
    both = cross + cross.T
    row = lax.broadcasted_iota(jnp.int32, (feat, feat), 0)
    column = lax.broadcasted_iota(jnp.int32, (feat, feat), 1)
    packed[...] = jnp.where(column >= row, inst[...], both)
    sums = total[0:1, :]
    diagonal = jnp.sum(jnp.where(column == row, both, 0.0), 0, keepdims=True)
    core = lax.axis_index("core")
    for ref, owner in ((kept_ref, core), (sent_ref, 1 - core)):
        extra = jnp.where(owner == 0, sums, diagonal)
        for chunk, _, share_row, lanes in slots(ref.shape, feat):
            source = pl.ds(owner * (feat // 2) + share_row, 1)
            ref[chunk, 0:1, lanes] = packed[source, :]
        for chunk in range(ref.shape[0]):
            part = extra[:, chunk * 128 : chunk * 128 + 128] if chunk < feat // 128 else jnp.zeros((1, 128), F32)
            ref[chunk, 0:1, ref.shape[2] - 128 :] = part


def slots(shape, feat):
    rows = (shape[2] - 128) // feat
    for chunk in range(shape[0]):
        for row in range(rows):
            yield chunk, row, chunk * rows + row, slice(row * feat, (row + 1) * feat)


def pack(feature, ahead_head, ahead_early, inst, lag, total, chips):
    vmem = pl.BlockSpec(memory_space=pltpu.VMEM)
    feat = inst.shape[0]
    share = jax.ShapeDtypeStruct((chips, 1, feat // 2 // chips * feat + 128), F32)
    return pl.pallas_call(
        pack_kernel,
        in_specs=[vmem] * 6,
        out_specs=(vmem, vmem),
        out_shape=(share, share),
        scratch_shapes=[pltpu.VMEM((feat, feat), F32)],
        compiler_params=pltpu.CompilerParams(vmem_limit_bytes=8 * MIB),
    )(feature, ahead_head, ahead_early, inst, lag, total)


def three_parts(x):
    high = x.astype(BF16)
    rest = x - high.astype(F32)
    middle = rest.astype(BF16)
    low = (rest - middle.astype(F32)).astype(BF16)
    return high, middle, low


def repeated_parts(block, offset):
    lane = lax.broadcasted_iota(jnp.int32, block.shape, 1)
    base = jnp.where((lane >= offset) & (lane < offset + PANEL), block, 0.0)
    if offset:
        base = pltpu.roll(base, 128 - offset, 1)
    two = base + pltpu.roll(base, PANEL, 1)
    six = two + pltpu.roll(two, 2 * PANEL, 1) + pltpu.roll(two, 4 * PANEL, 1)
    high, middle, low = (part.astype(F32) for part in three_parts(six))
    place = lane // PANEL
    chosen = jnp.where((place == 2) | (place == 5), middle, jnp.where(place == 4, low, high))
    return chosen.astype(BF16)


def stacked_parts(rows):
    high, middle, low = three_parts(rows)
    rest = jnp.zeros((128 - 6 * PANEL, rows.shape[1]), BF16)
    return jnp.concatenate([high, middle, high, low, high, middle, rest], 0)


def inverse_factor(work):
    size = work.shape[0]
    lane = lax.broadcasted_iota(jnp.int32, (PANEL, size), 1)
    sub = lax.broadcasted_iota(jnp.int32, (PANEL, size), 0)
    sub_narrow = lax.broadcasted_iota(jnp.int32, (PANEL, 128), 0)

    def wide(x):
        return jnp.concatenate([x] * (size // 128), 1)

    for start in range(0, size, PANEL):
        stop = start + PANEL
        panel = work[start:stop, :]
        columns = [
            jnp.broadcast_to(panel[:, start + k : start + k + 1], (PANEL, 128)) for k in range(PANEL)
        ]
        panel = jnp.where(
            (lane >= start) & (lane < stop), jnp.where(lane - start == sub, 1.0, 0.0), panel
        )
        solved = panel
        slab = start // 128 * 128
        if stop < size:
            left = repeated_parts(work[stop:, slab : slab + 128], start - slab)
        pivots = jnp.ones((PANEL, 128), F32)
        pivot = columns[0][0:1, :]
        for j in range(PANEL):
            inverse = pl.reciprocal(pivot, approx=True)
            pivots = jnp.where(sub_narrow == j, pivot, pivots)
            factor = jnp.where(sub_narrow == j, 0.0, columns[j]) * inverse
            if j + 1 < PANEL:
                beside = columns[j + 1][j : j + 1, :]
                pivot = columns[j + 1][j + 1 : j + 2, :] - beside * beside * inverse
            for k in range(j + 1, PANEL):
                columns[k] = columns[k] - factor * columns[k][j : j + 1, :]
            if j + 1 < PANEL:
                below = jnp.where(sub_narrow > j, factor, 0.0)
                panel = panel - wide(below) * panel[j : j + 1, :]
            solved = solved - wide(factor) * solved[j : j + 1, :]
        if stop < size:
            right = stacked_parts(solved * wide(1.0 / pivots))
            update = jnp.dot(left, right, preferred_element_type=F32)
            kept = lax.broadcasted_iota(jnp.int32, (size - stop, size), 1)
            kept = (kept < start) | (kept >= stop)
            work[stop:, :] = jnp.where(kept, work[stop:, :], 0.0) - update
        work[start:stop, :] = panel * wide(lax.rsqrt(pivots))
    row = lax.broadcasted_iota(jnp.int32, (size, size), 0)
    column = lax.broadcasted_iota(jnp.int32, (size, size), 1)
    return jnp.where(column <= row, work[...], 0.0)


def koopman_kernel(scale_ref, mine_ref, other_ref, split_ref, shift_ref, work, packed_ref):
    feat = packed_ref.shape[1]
    scale = scale_ref[0]
    core = lax.axis_index("core")
    extras = []
    for ref, owner in ((mine_ref, core), (other_ref, 1 - core)):
        for chunk, _, share_row, lanes in slots(ref.shape, feat):
            packed_ref[pl.ds(owner * (feat // 2) + share_row, 1), :] = ref[chunk, 0:1, lanes]
        parts = [ref[chunk, 0:1, ref.shape[2] - 128 :] for chunk in range(feat // 128)]
        extras.append(jnp.concatenate(parts, 1))
    packed = packed_ref[...]
    mean = jnp.where(core == 0, extras[0], extras[1]) * scale
    diagonal = jnp.where(core == 0, extras[1], extras[0])
    row = lax.broadcasted_iota(jnp.int32, (feat, feat), 0)
    column = lax.broadcasted_iota(jnp.int32, (feat, feat), 1)
    turned = packed.T
    centre = jnp.broadcast_to(mean, (feat, feat))
    centre = centre * centre.T
    inst = jnp.where(column >= row, packed, turned)
    lag = jnp.where(column < row, packed, turned)
    lag = jnp.where(column == row, jnp.broadcast_to(diagonal, (feat, feat)), lag)
    work[...] = inst * scale - centre + jnp.where(column == row, RIDGE, 0.0)
    lag = lag * scale - centre
    inverse = inverse_factor(work)
    half_step = jnp.dot(inverse, lag, precision=HIGHEST, preferred_element_type=F32)
    koopman = across(half_step, inverse, HIGHEST)
    moved = jnp.dot(koopman, inverse, precision=HIGHEST, preferred_element_type=F32)
    for index, matrix in enumerate((inverse, moved)):
        turned = matrix.T
        high = turned.astype(BF16)
        split_ref[index, :feat, :] = high
        split_ref[index, feat:, :] = (turned - high.astype(F32)).astype(BF16)
        rows = jnp.broadcast_to(mean, (8, feat))
        shift_ref[index] = jnp.dot(rows, turned, precision=HIGHEST, preferred_element_type=F32)


def koopman_parts(scale, mine, other, feat):
    vmem = pl.BlockSpec(memory_space=pltpu.VMEM)
    return pl.pallas_call(
        koopman_kernel,
        in_specs=[pl.BlockSpec(memory_space=pltpu.SMEM), vmem, vmem],
        out_specs=(vmem, vmem),
        out_shape=(
            jax.ShapeDtypeStruct((2, 2 * feat, feat), BF16),
            jax.ShapeDtypeStruct((2, 8, feat), F32),
        ),
        scratch_shapes=[pltpu.VMEM((feat, feat), F32), pltpu.VMEM((feat, feat), F32)],
        compiler_params=pltpu.CompilerParams(vmem_limit_bytes=12 * MIB),
    )(scale, mine, other)


def project_kernel(
    feature_ref, ahead_head_ref, ahead_early_ref, split_ref, shift_ref, moved_ref, residual_ref
):
    step = pl.program_id(0)
    inside = feature_ref.shape[0] // CHUNK - 2

    def product(block, index):
        twice = jnp.concatenate([block, block], 1)
        return jnp.dot(twice, split_ref[index], preferred_element_type=F32) - shift_ref[index][0:1]

    def moved():
        value = product(feature_ref[pl.ds(pl.multiple_of(step * CHUNK, CHUNK), CHUNK), :], 1)
        moved_ref[...] = value
        return value

    @pl.when(step < inside)
    def _():
        later = feature_ref[pl.ds(pl.multiple_of(step * CHUNK + LAG, CHUNK), CHUNK), :]
        residual_ref[...] = product(later, 0) - moved()

    for index, ahead_ref in enumerate((ahead_head_ref, ahead_early_ref)):

        @pl.when(step == inside + index)
        def _():
            value = product(ahead_ref[...], 0) - moved()
            at_end = lax.axis_index("tm") == lax.axis_size("tm") - 1
            residual_ref[...] = jnp.where(at_end, 0.0, value)


def project(feature, ahead_head, ahead_early, split, shift):
    rows, feat = feature.shape
    vmem = pl.BlockSpec(memory_space=pltpu.VMEM)
    out = jax.ShapeDtypeStruct((rows, feat), F32)
    block = pl.BlockSpec((CHUNK, feat), lambda i: (i, 0))
    return pl.pallas_call(
        project_kernel,
        grid=(rows // CHUNK,),
        in_specs=[vmem] * 5,
        out_specs=(block, block),
        out_shape=(out, out),
        compiler_params=pltpu.CompilerParams(vmem_limit_bytes=16 * MIB),
    )(feature, ahead_head, ahead_early, split, shift)


def summed(kept, sent):
    swap = [(0, 1), (1, 0)]
    chips = ("x", "tm")
    parts = kept + lax.ppermute(sent, "core", swap)
    mine = jnp.sum(lax.all_to_all(parts, chips, 0, 0, tiled=True), 0, keepdims=True)
    mine = lax.all_to_all(jnp.broadcast_to(mine, parts.shape), chips, 0, 0, tiled=True)
    return mine, lax.ppermute(mine, "core", swap)


def on_device(frames, first_weight, first_bias, second_weight):
    frame_block = frames[0]
    row_count, channels = frame_block.shape
    hid, feat = second_weight.shape[1:]
    weights = (
        first_weight.reshape(2 * channels, hid),
        first_bias.reshape(1, hid),
        second_weight.reshape(2 * hid, feat),
    )
    halo = passed_along(frame_block[row_count - D1 - D2 :], "tm", 1)
    early, near, *weights = early_rows(frame_block, *weights)
    ahead_early = passed_along(early, "tm", -1)
    head = head_rows(near, halo, *weights)
    ahead_head = passed_along(head, "tm", -1)
    feature, inst, lag, total = body(frame_block, near, head, early, *weights)
    chips = lax.axis_size("x") * lax.axis_size("tm")
    mine, other = summed(*pack(feature, ahead_head, ahead_early, inst, lag, total, chips))
    replicas = lax.axis_size("x") * lax.axis_size("core")
    pair_count = replicas * (row_count * lax.axis_size("tm") - LAG)
    scale = jnp.full((1,), 1.0 / (2.0 * pair_count), F32)
    split, shift = koopman_parts(scale, mine, other, feat)
    propagated, residual = project(feature, ahead_head, ahead_early, split, shift)
    return (propagated[None], residual[None])


def solution(mesh):
    replicas, blocks = mesh.devices.shape
    chips = Mesh(mesh.devices.reshape(replicas // 2, 2, blocks), ("x", "core", "tm"))
    split = P(("x", "core"), "tm", None)
    return jax.shard_map(
        on_device,
        mesh=chips,
        in_specs=(split, P(), P(), P()),
        out_specs=(split, split),
        check_vma=False,
    )
```

time: 78.4 us -> 78.5 us (level)
  Pallas kernels: 30.5 us -> 32.2 us
  blocking collectives: 29.9 us -> 28.4 us
    all_to_all x2, blocking collectives: 29.9 us -> 28.4 us  [the longest x1 17.7 us: summed(): lax.all_to_all(parts, chips, 0, 0, tiled=True)]
    pallas_call x1, Pallas kernels: 9.03 us -> 10.3 us  [koopman_parts(): pl.pallas_call(koopman_kernel, in_specs=[pl.BlockSpec(memory_space=pltpu....]
    unnamed x16 -> x10, local copies, waits for them, and re-layouts: 5.15 us -> 5.13 us
where the time goes in v4:
time: 78.5 us; the launch traced here: 78.1 us
  Pallas kernels  32.2 us (41%)
  blocking collectives  28.4 us (36%)
  starting transfers between devices  7.55 us (10%)
  local copies, waits for them, and re-layouts  6.19 us (8%)
  waiting for transfers between devices  2.71 us (3%)
    all_to_all x1, blocking collectives, summed(): lax.all_to_all(parts, chips, 0, 0, tiled=True)  17.7 us
    pallas_call x1, Pallas kernels, body(): pl.pallas_call(body_kernel, in_specs=[pl.BlockSpec(memory_space=pltpu.HBM...  11.5 us
    all_to_all x1, blocking collectives, summed(): lax.all_to_all(jnp.broadcast_to(mine, parts.shape), chips, 0, 0, tiled=True)  10.8 us
    pallas_call x1, Pallas kernels, koopman_parts(): pl.pallas_call(koopman_kernel, in_specs=[pl.BlockSpec(memory_space=pltpu....  10.3 us
    ppermute x3, starting transfers between devices, passed_along(): lax.ppermute(value, axis, [(source, source + steps) for source in range(f...  7.47 us
    pallas_call x1, Pallas kernels, project(): pl.pallas_call(project_kernel, grid=(rows // CHUNK,), in_specs=[vmem] * 5...  6.1 us
    unnamed x10, local copies, waits for them, and re-layouts  5.13 us
    pallas_call x1, Pallas kernels, early_rows(): pl.pallas_call(early_kernel, in_specs=[hbm] * 4, out_specs=(vmem,) * 5, o...  2.08 us
  transfers between devices with their start and end apart: 5, of which 2 were waited for; matrix products, arithmetic and copies ran while one was open for 0% of the time, Pallas kernels for 19%

profile of v4, /device:TPU:0, one launch (start us, length us, event | category | flops | bytes accessed | tf_op | source)
XLA Modules:
  0.0 78.1 jit_solution(16946460688271235415)
XLA Ops:
  0.6 1.0 %slice_bitcast_fusion = bf16[288,512]{1,0:T(8,128)(2,1)S(1)} fusion(bf16[1,4096,512]{2,1,0:T(8,128)(2,1)} %param.4), kind=kLoop, calls=%fused_computation | loop fusion | bytes 589824 | tf_op jit(solution)/shard_map/slice | solution.py:427
  1.6 4.9 %collective-permute-start = (bf16[288,512]{1,0:T(8,128)(2,1)S(1)}, bf16[288,512]{1,0:T(8,128)(2,1)S(1)}, u32[]{:S(2)}, u32[]{:S(2)}) collective-permute-start(bf16[288,512]{1,0:T(8,128)(2,1)S(1)} %slice_bitcast_fusion), channel_id=1, source_target_pairs={{0,1},{1,2},{2,3},{3,4},{4,5},{5,6},{6,7},{8,9},{9,10},{10,11},{11... | collective-permute-start | bytes 884744 | tf_op jit(solution)/shard_map/ppermute | solution.py:24
  6.5 0.0 copy-start
  6.5 2.2 %copy-done = bf16[1,4096,512]{2,1,0:T(8,128)(2,1)S(1)} copy-done((bf16[1,4096,512]{2,1,0:T(8,128)(2,1)S(1)}, bf16[1,4096,512]{2,1,0:T(8,128)(2,1)}, u32[]{:S(2)}) %copy-start) | copy-done | bytes 4194328
  8.7 0.0 copy-start.2
  8.7 1.2 %copy-done.2 = bf16[2,512,512]{2,1,0:T(8,128)(2,1)S(1)} copy-done((bf16[2,512,512]{2,1,0:T(8,128)(2,1)S(1)}, bf16[2,512,512]{2,1,0:T(8,128)(2,1)}, u32[]{:S(2)}) %copy-start.2) | copy-done | bytes 1048600
  9.9 0.0 copy-start.3
  9.9 1.0 %copy-done.3 = bf16[2,512,256]{2,1,0:T(8,128)(2,1)S(1)} copy-done((bf16[2,512,256]{2,1,0:T(8,128)(2,1)S(1)}, bf16[2,512,256]{2,1,0:T(8,128)(2,1)}, u32[]{:S(2)}) %copy-start.3) | copy-done | bytes 524312
  11.0 0.0 copy-start.4
  11.0 0.7 copy-done.4
  11.7 0.0 copy-start.1
  11.7 2.1 %shard_map.59 = (bf16[512,256]{1,0:T(8,128)(2,1)S(1)}, bf16[1024,512]{1,0:T(8,128)(2,1)S(1)}, bf16[1024,512]{1,0:T(8,128)(2,1)S(1)}, f32[1,512]{1,0:T(1,128)S(1)}, bf16[1024,256]{1,0:T(8,128)(2,1)S(1)}) custom-call(bf16[4096,512]{1,0:T(8,128)(2,1)S(1)} %bitcast.8, bf16[1024,512]{1,0:T(8,128)(2,1)S(1)} %bitcast.10, f32[1,512]{1,0:T(1,128)S(1)} %bitcast.12, ...), custom_call_target="tpu_custom_call" | custom-call | tf_op jit(solution)/shard_map/pallas_call | solution.py:96
  13.7 1.3 %collective-permute-start.2 = (bf16[512,256]{1,0:T(8,128)(2,1)S(1)}, bf16[512,256]{1,0:T(8,128)(2,1)S(1)}, u32[]{:S(2)}, u32[]{:S(2)}) collective-permute-start(bf16[512,256]{1,0:T(8,128)(2,1)S(1)} %get-tuple-element.21.early_ref), channel_id=1, source_target_pairs={{1,0},{2,1},{3,2},{4,3},{5,4},{6,5},{7,6},{9,8},{10,9},{11,10},{12... | collective-permute-start | bytes 786440 | tf_op jit(solution)/shard_map/ppermute | solution.py:24
  15.0 0.0 collective-permute-done.halo_ref
  15.1 1.4 %shard_map.60.head_ref = bf16[512,256]{1,0:T(8,128)(2,1)S(1)} custom-call(bf16[1024,512]{1,0:T(8,128)(2,1)S(1)} %get-tuple-element.17.near_ref, bf16[288,512]{1,0:T(8,128)(2,1)S(1)} %collective-permute-done.halo_ref, bf16[1024,512]{1,0:T(8,128)(2,1)S(1)} %get-tuple-element.18.w1_ref, f32[1,512]{1,0:T(1,128)S(1)} %get-tuple-element.19.b1_ref, ...), custom_call_target="tpu_custom_call" | custom-call | tf_op jit(solution)/shard_map/pallas_call | solution.py:109
  16.5 1.3 %collective-permute-start.1 = (bf16[512,256]{1,0:T(8,128)(2,1)S(1)}, bf16[512,256]{1,0:T(8,128)(2,1)S(1)}, u32[]{:S(2)}, u32[]{:S(2)}) collective-permute-start(bf16[512,256]{1,0:T(8,128)(2,1)S(1)} %shard_map.60.head_ref), channel_id=1, source_target_pairs={{1,0},{2,1},{3,2},{4,3},{5,4},{6,5},{7,6},{9,8},{10,9},{11,10},{12... | collective-permute-start | bytes 786440 | tf_op jit(solution)/shard_map/ppermute | solution.py:24
  17.8 0.0 copy-done.1
  17.8 11.5 %shard_map.61 = (bf16[4096,256]{1,0:T(8,128)(2,1)S(1)}, f32[256,256]{1,0:T(8,128)S(1)}, f32[256,256]{1,0:T(8,128)S(1)}, f32[8,256]{1,0:T(8,128)S(1)}) custom-call(bf16[4096,512]{1,0:T(8,128)(2,1)S(1)} %bitcast.9, bf16[1024,512]{1,0:T(8,128)(2,1)S(1)} %get-tuple-element.17.near_ref, bf16[512,256]{1,0:T(8,128)(2,1)S(1)} %shard_map.60.head_ref, ...), custom_call_target="tpu_custom_call" | custom-call | tf_op jit(solution)/shard_map/pallas_call | solution.py:178
  29.3 0.0 collective-permute-done.2.ahead_early_ref
  29.3 0.0 collective-permute-done.1.ahead_head_ref
  29.3 0.8 %shard_map.62 = (f32[16,1,2176]{2,1,0:T(1,128)S(1)}, f32[16,1,2176]{2,1,0:T(1,128)S(1)}) custom-call(bf16[4096,256]{1,0:T(8,128)(2,1)S(1)} %get-tuple-element.22.feature_ref, bf16[512,256]{1,0:T(8,128)(2,1)S(1)} %collective-permute-done.1.ahead_head_ref, bf16[512,256]{1,0:T(8,128)(2,1)S(1)} %collective-permute-done.2.ahead_early_ref, ...), custom_call_target="tpu_custom_call" | custom-call | tf_op jit(solution)/shard_map/pallas_call | solution.py:228
  30.1 0.1 collective-permute-start.3
  30.2 1.3 %collective-permute-done.3 = f32[16,1,2176]{2,1,0:T(1,128)S(1)} collective-permute-done((f32[16,1,2176]{2,1,0:T(1,128)S(1)}, f32[16,1,2176]{2,1,0:T(1,128)S(1)}, u32[]{:S(2)}, u32[]{:S(2)}) %collective-permute-start.3) | collective-permute-done | bytes 139296 | tf_op jit(solution)/shard_map/ppermute | solution.py:412
  31.6 0.1 add.3
  31.7 17.7 %all_to_all.10 = f32[16,1,2176]{2,1,0:T(1,128)S(1)} all-to-all(f32[16,1,2176]{2,1,0:T(1,128)S(1)} %add.3), channel_id=1, replica_groups=mesh['x'=2,'core'=2,'tm'=8] {'x','tm'}, dimensions={0} | all-to-all | bytes 278528 | tf_op jit(solution)/shard_map/all_to_all | solution.py:413
  49.4 0.1 reduce_sum.9
  49.5 0.1 broadcast_in_dim.12
  49.5 10.8 %all_to_all.11.mine_ref = f32[16,1,2176]{2,1,0:T(1,128)S(1)} all-to-all(f32[16,1,2176]{2,1,0:T(1,128)S(1)} %broadcast_in_dim.12), channel_id=1, replica_groups=mesh['x'=2,'core'=2,'tm'=8] {'x','tm'}, dimensions={0} | all-to-all | bytes 278528 | tf_op jit(solution)/shard_map/all_to_all | solution.py:414
  60.3 0.0 collective-permute-start.4
  60.3 1.4 %collective-permute-done.4.other_ref = f32[16,1,2176]{2,1,0:T(1,128)S(1)} collective-permute-done((f32[16,1,2176]{2,1,0:T(1,128)S(1)}, f32[16,1,2176]{2,1,0:T(1,128)S(1)}, u32[]{:S(2)}, u32[]{:S(2)}) %collective-permute-start.4) | collective-permute-done | bytes 139296 | tf_op jit(solution)/shard_map/ppermute | solution.py:415
  61.7 10.3 %shard_map.63 = (bf16[2,512,256]{2,1,0:T(8,128)(2,1)S(1)}, f32[2,8,256]{2,1,0:T(8,128)S(1)}) custom-call(f32[1]{0:T(128)} %constant.0.clone.1.scale_ref, f32[16,1,2176]{2,1,0:T(1,128)S(1)} %all_to_all.11.mine_ref, f32[16,1,2176]{2,1,0:T(1,128)S(1)} %collective-permute-done.4.other_ref), custom_call_target="tpu_custom_call" | custom-call | tf_op jit(solution)/shard_map/pallas_call | solution.py:352
  72.0 6.1 %shard_map.64 = (f32[4096,256]{1,0:T(8,128)}, f32[4096,256]{1,0:T(8,128)}) custom-call(bf16[4096,256]{1,0:T(8,128)(2,1)S(1)} %get-tuple-element.22.feature_ref, bf16[512,256]{1,0:T(8,128)(2,1)S(1)} %collective-permute-done.1.ahead_head_ref, bf16[512,256]{1,0:T(8,128)(2,1)S(1)} %collective-permute-done.2.ahead_early_ref, ...), custom_call_target="tpu_custom_call" | custom-call | tf_op jit(solution)/shard_map/pallas_call | solution.py:399
Async XLA Ops:
  1.6 13.4 %collective-permute-start = (bf16[288,512]{1,0:T(8,128)(2,1)S(1)}, bf16[288,512]{1,0:T(8,128)(2,1)S(1)}, u32[]{:S(2)}, u32[]{:S(2)}) collective-permute-start(bf16[288,512]{1,0:T(8,128)(2,1)S(1)} %slice_bitcast_fusion), channel_id=1, source_target_pairs={{0,1},{1,2},{2,3},{3,4},{4,5},{5,6},{6,7},{8,9},{9,10},{10,11},{11... | collective-permute-start | bytes 884744 | tf_op jit(solution)/shard_map/ppermute | solution.py:24
  6.5 2.2 %copy-start = (bf16[1,4096,512]{2,1,0:T(8,128)(2,1)S(1)}, bf16[1,4096,512]{2,1,0:T(8,128)(2,1)}, u32[]{:S(2)}) copy-start(bf16[1,4096,512]{2,1,0:T(8,128)(2,1)} %param.4) | copy-start | bytes 12582916
  8.7 1.2 %copy-start.2 = (bf16[2,512,512]{2,1,0:T(8,128)(2,1)S(1)}, bf16[2,512,512]{2,1,0:T(8,128)(2,1)}, u32[]{:S(2)}) copy-start(bf16[2,512,512]{2,1,0:T(8,128)(2,1)} %param.5) | copy-start | bytes 3145732
  9.9 1.0 %copy-start.3 = (bf16[2,512,256]{2,1,0:T(8,128)(2,1)S(1)}, bf16[2,512,256]{2,1,0:T(8,128)(2,1)}, u32[]{:S(2)}) copy-start(bf16[2,512,256]{2,1,0:T(8,128)(2,1)} %param.7) | copy-start | bytes 1572868
  11.0 0.7 copy-start.4
  11.7 6.1 %copy-start.1 = (bf16[1,4096,512]{2,1,0:T(8,128)(2,1)S(1)}, bf16[1,4096,512]{2,1,0:T(8,128)(2,1)}, u32[]{:S(2)}) copy-start(bf16[1,4096,512]{2,1,0:T(8,128)(2,1)} %param.4) | copy-start | bytes 12582916
  13.7 15.5 %collective-permute-start.2 = (bf16[512,256]{1,0:T(8,128)(2,1)S(1)}, bf16[512,256]{1,0:T(8,128)(2,1)S(1)}, u32[]{:S(2)}, u32[]{:S(2)}) collective-permute-start(bf16[512,256]{1,0:T(8,128)(2,1)S(1)} %get-tuple-element.21.early_ref), channel_id=1, source_target_pairs={{1,0},{2,1},{3,2},{4,3},{5,4},{6,5},{7,6},{9,8},{10,9},{11,10},{12... | collective-permute-start | bytes 786440 | tf_op jit(solution)/shard_map/ppermute | solution.py:24
  16.5 12.8 %collective-permute-start.1 = (bf16[512,256]{1,0:T(8,128)(2,1)S(1)}, bf16[512,256]{1,0:T(8,128)(2,1)S(1)}, u32[]{:S(2)}, u32[]{:S(2)}) collective-permute-start(bf16[512,256]{1,0:T(8,128)(2,1)S(1)} %shard_map.60.head_ref), channel_id=1, source_target_pairs={{1,0},{2,1},{3,2},{4,3},{5,4},{6,5},{7,6},{9,8},{10,9},{11,10},{12... | collective-permute-start | bytes 786440 | tf_op jit(solution)/shard_map/ppermute | solution.py:24
  30.1 1.4 %collective-permute-start.3 = (f32[16,1,2176]{2,1,0:T(1,128)S(1)}, f32[16,1,2176]{2,1,0:T(1,128)S(1)}, u32[]{:S(2)}, u32[]{:S(2)}) collective-permute-start(f32[16,1,2176]{2,1,0:T(1,128)S(1)} %get-tuple-element.27), channel_id=1, source_target_pairs={{0,8},{8,0},{1,9},{9,1},{2,10},{10,2},{3,11},{11,3},{4,12},{12,4},... | collective-permute-start | bytes 417800 | tf_op jit(solution)/shard_map/ppermute | solution.py:412
  60.3 1.4 %collective-permute-start.4 = (f32[16,1,2176]{2,1,0:T(1,128)S(1)}, f32[16,1,2176]{2,1,0:T(1,128)S(1)}, u32[]{:S(2)}, u32[]{:S(2)}) collective-permute-start(f32[16,1,2176]{2,1,0:T(1,128)S(1)} %all_to_all.11.mine_ref), channel_id=1, source_target_pairs={{0,8},{8,0},{1,9},{9,1},{2,10},{10,2},{3,11},{11,3},{4,12},{12,4},... | collective-permute-start | bytes 417800 | tf_op jit(solution)/shard_map/ppermute | solution.py:415

commit v5 on v4

--- a/solution.py
+++ b/solution.py
@@ -30,6 +30,10 @@
 
 def gram(a, b):
     return lax.dot_general(a, b, (((0,), (0,)), ((), ())), preferred_element_type=F32)
+
+
+def in_hbm(value):
+    return pltpu.with_memory_space_constraint(value, pltpu.HBM)
 
 
 def silu(x):
@@ -100,7 +104,7 @@
         out_shape=tuple(jax.ShapeDtypeStruct(*shape) for shape in shapes),
         scratch_shapes=[pltpu.VMEM((half + D2, hid), BF16), pltpu.SemaphoreType.DMA((5,))],
         compiler_params=pltpu.CompilerParams(vmem_limit_bytes=12 * MIB),
-    )(frames, w1, b1, w2)
+    )(*(in_hbm(value) for value in (frames, w1, b1, w2)))
 
 
 def head_rows(near, halo, w1, b1, w2):
@@ -117,8 +121,7 @@
 
 
 def column_sum(rows):
-    ones = jnp.ones((8, rows.shape[0]), BF16)
-    return jnp.dot(ones, rows, preferred_element_type=F32)
+    return jnp.sum(rows.astype(F32).reshape(-1, 8, rows.shape[1]), 0)
 
 
 def body_kernel(frames_ref, near_ref, head_ref, early_ref, w1_ref, b1_ref, w2_ref, out_ref, inst, lag, total, xs, hs, sems):
@@ -151,22 +154,19 @@
 
     def finish(step):
         value = feature_rows(hs, step * CHUNK, CHUNK, w2_ref)
-        out_ref[pl.ds(LAG + step * CHUNK, CHUNK), :] = value
-        weight = jnp.where(step >= steps - LAG // CHUNK, last_weight, 2.0)
-        both = gram(value, jnp.concatenate([value, out_ref[pl.ds(step * CHUNK, CHUNK), :]], 1))
+        at = step * CHUNK
+        out_ref[LAG + at : LAG + at + CHUNK, :] = value
+        weight = last_weight if step >= steps - LAG // CHUNK else 2.0
+        both = gram(value, jnp.concatenate([value, out_ref[at : at + CHUNK, :]], 1))
         inst[...] += weight * both[:, :feat]
         lag[...] += both[:, feat:]
         total[...] += weight * column_sum(value)
 
-    def loop(step, carry):
+    for step in range(steps - 1):
         arriving(step + 1).wait()
-        at = pl.multiple_of((step + 1) * CHUNK + D2, D2)
-        fresh = hidden_rows(xs, at, CHUNK, w1_ref, b1_ref)
+        at = (step + 1) * CHUNK + D2
+        hs[at : at + CHUNK, :] = hidden_rows(xs, at, CHUNK, w1_ref, b1_ref)
         finish(step)
-        hs[pl.ds(at, CHUNK), :] = fresh
-        return carry
-
-    lax.fori_loop(0, steps - 1, loop, 0)
     finish(steps - 1)
 
 
@@ -188,7 +188,7 @@
         scratch_shapes=feature_scratch(rows - LAG, channels, hid)
         + [pltpu.SemaphoreType.DMA((rows // CHUNK,))],
         compiler_params=pltpu.CompilerParams(vmem_limit_bytes=24 * MIB),
-    )(frames, near, head, early, w1, b1, w2)
+    )(in_hbm(frames), near, head, early, w1, b1, w2)
 
 
 def pack_kernel(feature_ref, ahead_head_ref, ahead_early_ref, inst, lag, total, kept_ref, sent_ref, packed):
@@ -201,7 +201,7 @@
     row = lax.broadcasted_iota(jnp.int32, (feat, feat), 0)
     column = lax.broadcasted_iota(jnp.int32, (feat, feat), 1)
     packed[...] = jnp.where(column >= row, inst[...], both)
-    sums = total[0:1, :]
+    sums = jnp.sum(total[...], 0, keepdims=True)
     diagonal = jnp.sum(jnp.where(column == row, both, 0.0), 0, keepdims=True)
     core = lax.axis_index("core")
     for ref, owner in ((kept_ref, core), (sent_ref, 1 - core)):
@@ -270,6 +270,9 @@
 
     def wide(x):
         return jnp.concatenate([x] * (size // 128), 1)
+
+    def spread(x, j):
+        return jnp.broadcast_to(x[j : j + 1, :], x.shape)
 
     for start in range(0, size, PANEL):
         stop = start + PANEL
@@ -285,20 +288,20 @@
         if stop < size:
             left = repeated_parts(work[stop:, slab : slab + 128], start - slab)
         pivots = jnp.ones((PANEL, 128), F32)
-        pivot = columns[0][0:1, :]
+        pivot = spread(columns[0], 0)
         for j in range(PANEL):
             inverse = pl.reciprocal(pivot, approx=True)
             pivots = jnp.where(sub_narrow == j, pivot, pivots)
             factor = jnp.where(sub_narrow == j, 0.0, columns[j]) * inverse
+            beside = [spread(columns[k], j) for k in range(j + 1, PANEL)]
             if j + 1 < PANEL:
-                beside = columns[j + 1][j : j + 1, :]
-                pivot = columns[j + 1][j + 1 : j + 2, :] - beside * beside * inverse
+                pivot = spread(columns[j + 1], j + 1) - beside[0] * beside[0] * inverse
             for k in range(j + 1, PANEL):
-                columns[k] = columns[k] - factor * columns[k][j : j + 1, :]
+                columns[k] = columns[k] - factor * beside[k - j - 1]
             if j + 1 < PANEL:
                 below = jnp.where(sub_narrow > j, factor, 0.0)
-                panel = panel - wide(below) * panel[j : j + 1, :]
-            solved = solved - wide(factor) * solved[j : j + 1, :]
+                panel = panel - wide(below) * spread(panel, j)
+            solved = solved - wide(factor) * spread(solved, j)
         if stop < size:
             right = stacked_parts(solved * wide(1.0 / pivots))
             update = jnp.dot(left, right, preferred_element_type=F32)
@@ -363,46 +366,52 @@
 
 
 def project_kernel(
-    feature_ref, ahead_head_ref, ahead_early_ref, split_ref, shift_ref, moved_ref, residual_ref
+    feature_ref, ahead_head_ref, ahead_early_ref, split_ref, shift_ref, moved_out, residual_out, moved, residual, sems
 ):
-    step = pl.program_id(0)
-    inside = feature_ref.shape[0] // CHUNK - 2
+    rows = feature_ref.shape[0]
+    half = LAG // 2
+    at_end = lax.axis_index("tm") == lax.axis_size("tm") - 1
 
     def product(block, index):
         twice = jnp.concatenate([block, block], 1)
         return jnp.dot(twice, split_ref[index], preferred_element_type=F32) - shift_ref[index][0:1]
 
-    def moved():
-        value = product(feature_ref[pl.ds(pl.multiple_of(step * CHUNK, CHUNK), CHUNK), :], 1)
-        moved_ref[...] = value
-        return value
-
-    @pl.when(step < inside)
-    def _():
-        later = feature_ref[pl.ds(pl.multiple_of(step * CHUNK + LAG, CHUNK), CHUNK), :]
-        residual_ref[...] = product(later, 0) - moved()
-
-    for index, ahead_ref in enumerate((ahead_head_ref, ahead_early_ref)):
-
-        @pl.when(step == inside + index)
-        def _():
-            value = product(ahead_ref[...], 0) - moved()
-            at_end = lax.axis_index("tm") == lax.axis_size("tm") - 1
-            residual_ref[...] = jnp.where(at_end, 0.0, value)
+    copies = []
+    for step in range(rows // CHUNK):
+        here = slice(step * CHUNK, (step + 1) * CHUNK)
+        start = step * CHUNK + LAG
+        if start < rows:
+            later = feature_ref[start : start + CHUNK, :]
+        else:
+            later = (ahead_head_ref if start == rows else ahead_early_ref)[...]
+        now = product(feature_ref[here, :], 1)
+        moved[here, :] = now
+        gap = product(later, 0) - now
+        residual[here, :] = gap if start < rows else jnp.where(at_end, 0.0, gap)
+        for index, (source, target) in enumerate(((moved, moved_out), (residual, residual_out))):
+            copy = pltpu.make_async_copy(source.at[here], target.at[here], sems.at[index, step])
+            copy.start()
+            copies.append(copy)
+    for copy in copies:
+        copy.wait()
 
 
 def project(feature, ahead_head, ahead_early, split, shift):
     rows, feat = feature.shape
     vmem = pl.BlockSpec(memory_space=pltpu.VMEM)
+    hbm = pl.BlockSpec(memory_space=pltpu.HBM)
     out = jax.ShapeDtypeStruct((rows, feat), F32)
-    block = pl.BlockSpec((CHUNK, feat), lambda i: (i, 0))
     return pl.pallas_call(
         project_kernel,
-        grid=(rows // CHUNK,),
         in_specs=[vmem] * 5,
-        out_specs=(block, block),
+        out_specs=(hbm, hbm),
         out_shape=(out, out),
-        compiler_params=pltpu.CompilerParams(vmem_limit_bytes=16 * MIB),
+        scratch_shapes=[
+            pltpu.VMEM((rows, feat), F32),
+            pltpu.VMEM((rows, feat), F32),
+            pltpu.SemaphoreType.DMA((2, rows // CHUNK)),
+        ],
+        compiler_params=pltpu.CompilerParams(vmem_limit_bytes=24 * MIB),
     )(feature, ahead_head, ahead_early, split, shift)
 
 

time: 78.5 us -> 72.7 us (0.926)
  local copies, waits for them, and re-layouts: 6.19 us -> 1.06 us
  Pallas kernels: 32.2 us -> 29.7 us
  waiting for transfers between devices: 2.71 us -> 4.57 us
    unnamed x10 -> x0, local copies, waits for them, and re-layouts: 5.13 us -> none
    pallas_call x1, Pallas kernels: 6.1 us -> 3.87 us  [project(): pl.pallas_call(project_kernel, in_specs=[vmem] * 5, out_specs=(hbm, hbm),...]
    ppermute x3, waiting for transfers between devices: 0.01 us -> 1.87 us  [passed_along(): lax.ppermute(value, axis, [(source, source + steps) for source in range(f...]
    pallas_call x1, Pallas kernels: 11.5 us -> 10.3 us  [body(): pl.pallas_call(body_kernel, in_specs=[pl.BlockSpec(memory_space=pltpu.HBM...]
    pallas_call x1, Pallas kernels: 2.08 us -> 3.06 us  [early_rows(): pl.pallas_call(early_kernel, in_specs=[hbm] * 4, out_specs=(vmem,) * 5, o...]
  transfers between devices with their start and end apart: 5 -> 5, of which waited for: 2 -> 3; matrix products, arithmetic and copies ran while one was open for 0% -> 0% of each run, Pallas kernels for 19% -> 20%
where the time goes in v5:
time: 72.7 us; the launch traced here: 72.4 us
  Pallas kernels  29.7 us (41%)
  blocking collectives  28.4 us (39%)
  starting transfers between devices  7.55 us (10%)
  waiting for transfers between devices  4.57 us (6%)
  local copies, waits for them, and re-layouts  1.06 us (1%)
  between operations  0.89 us (1%)
    all_to_all x1, blocking collectives, summed(): lax.all_to_all(parts, chips, 0, 0, tiled=True)  17.6 us
    all_to_all x1, blocking collectives, summed(): lax.all_to_all(jnp.broadcast_to(mine, parts.shape), chips, 0, 0, tiled=True)  10.8 us
    pallas_call x1, Pallas kernels, koopman_parts(): pl.pallas_call(koopman_kernel, in_specs=[pl.BlockSpec(memory_space=pltpu....  10.3 us
    pallas_call x1, Pallas kernels, body(): pl.pallas_call(body_kernel, in_specs=[pl.BlockSpec(memory_space=pltpu.HBM...  10.3 us
    ppermute x3, starting transfers between devices, passed_along(): lax.ppermute(value, axis, [(source, source + steps) for source in range(f...  7.47 us
    pallas_call x1, Pallas kernels, project(): pl.pallas_call(project_kernel, in_specs=[vmem] * 5, out_specs=(hbm, hbm),...  3.87 us
    pallas_call x1, Pallas kernels, early_rows(): pl.pallas_call(early_kernel, in_specs=[hbm] * 4, out_specs=(vmem,) * 5, o...  3.06 us
    ppermute x3, waiting for transfers between devices, passed_along(): lax.ppermute(value, axis, [(source, source + steps) for source in range(f...  1.87 us
  transfers between devices with their start and end apart: 5, of which 3 were waited for; matrix products, arithmetic and copies ran while one was open for 0% of the time, Pallas kernels for 20%

profile of v5, /device:TPU:0, one launch (start us, length us, event | category | flops | bytes accessed | tf_op | source)
XLA Modules:
  0.0 72.4 jit_solution(16659664718559851989)
XLA Ops:
  0.6 1.0 %slice_bitcast_fusion = bf16[288,512]{1,0:T(8,128)(2,1)S(1)} fusion(bf16[1,4096,512]{2,1,0:T(8,128)(2,1)} %param.4), kind=kLoop, calls=%fused_computation | loop fusion | bytes 589824 | tf_op jit(solution)/shard_map/slice | solution.py:436
  1.6 4.9 %collective-permute-start = (bf16[288,512]{1,0:T(8,128)(2,1)S(1)}, bf16[288,512]{1,0:T(8,128)(2,1)S(1)}, u32[]{:S(2)}, u32[]{:S(2)}) collective-permute-start(bf16[288,512]{1,0:T(8,128)(2,1)S(1)} %slice_bitcast_fusion), channel_id=1, source_target_pairs={{0,1},{1,2},{2,3},{3,4},{4,5},{5,6},{6,7},{8,9},{9,10},{10,11},{11... | collective-permute-start | bytes 884744 | tf_op jit(solution)/shard_map/ppermute | solution.py:24
  6.5 3.1 %shard_map.59 = (bf16[512,256]{1,0:T(8,128)(2,1)S(1)}, bf16[1024,512]{1,0:T(8,128)(2,1)S(1)}, bf16[1024,512]{1,0:T(8,128)(2,1)S(1)}, f32[1,512]{1,0:T(1,128)S(1)}, bf16[1024,256]{1,0:T(8,128)(2,1)S(1)}) custom-call(bf16[4096,512]{1,0:T(8,128)(2,1)} %bitcast.8, bf16[1024,512]{1,0:T(8,128)(2,1)} %bitcast.10, f32[1,512]{1,0:T(1,128)} %bitcast.12, ...), custom_call_target="tpu_custom_call" | custom-call | tf_op jit(solution)/shard_map/pallas_call | solution.py:100
  9.6 1.3 %collective-permute-start.2 = (bf16[512,256]{1,0:T(8,128)(2,1)S(1)}, bf16[512,256]{1,0:T(8,128)(2,1)S(1)}, u32[]{:S(2)}, u32[]{:S(2)}) collective-permute-start(bf16[512,256]{1,0:T(8,128)(2,1)S(1)} %get-tuple-element.21.early_ref), channel_id=1, source_target_pairs={{1,0},{2,1},{3,2},{4,3},{5,4},{6,5},{7,6},{9,8},{10,9},{11,10},{12... | collective-permute-start | bytes 786440 | tf_op jit(solution)/shard_map/ppermute | solution.py:24
  10.9 1.9 %collective-permute-done.halo_ref = bf16[288,512]{1,0:T(8,128)(2,1)S(1)} collective-permute-done((bf16[288,512]{1,0:T(8,128)(2,1)S(1)}, bf16[288,512]{1,0:T(8,128)(2,1)S(1)}, u32[]{:S(2)}, u32[]{:S(2)}) %collective-permute-start) | collective-permute-done | bytes 294944 | tf_op jit(solution)/shard_map/ppermute | solution.py:24
  12.7 1.4 %shard_map.60.head_ref = bf16[512,256]{1,0:T(8,128)(2,1)S(1)} custom-call(bf16[1024,512]{1,0:T(8,128)(2,1)S(1)} %get-tuple-element.17.near_ref, bf16[288,512]{1,0:T(8,128)(2,1)S(1)} %collective-permute-done.halo_ref, bf16[1024,512]{1,0:T(8,128)(2,1)S(1)} %get-tuple-element.18.w1_ref, f32[1,512]{1,0:T(1,128)S(1)} %get-tuple-element.19.b1_ref, ...), custom_call_target="tpu_custom_call" | custom-call | tf_op jit(solution)/shard_map/pallas_call | solution.py:113
  14.2 1.3 %collective-permute-start.1 = (bf16[512,256]{1,0:T(8,128)(2,1)S(1)}, bf16[512,256]{1,0:T(8,128)(2,1)S(1)}, u32[]{:S(2)}, u32[]{:S(2)}) collective-permute-start(bf16[512,256]{1,0:T(8,128)(2,1)S(1)} %shard_map.60.head_ref), channel_id=1, source_target_pairs={{1,0},{2,1},{3,2},{4,3},{5,4},{6,5},{7,6},{9,8},{10,9},{11,10},{12... | collective-permute-start | bytes 786440 | tf_op jit(solution)/shard_map/ppermute | solution.py:24
  15.5 10.3 %shard_map.61 = (bf16[4096,256]{1,0:T(8,128)(2,1)S(1)}, f32[256,256]{1,0:T(8,128)S(1)}, f32[256,256]{1,0:T(8,128)S(1)}, f32[8,256]{1,0:T(8,128)S(1)}) custom-call(bf16[4096,512]{1,0:T(8,128)(2,1)} %bitcast.9, bf16[1024,512]{1,0:T(8,128)(2,1)S(1)} %get-tuple-element.17.near_ref, bf16[512,256]{1,0:T(8,128)(2,1)S(1)} %shard_map.60.head_ref, ...), custom_call_target="tpu_custom_call" | custom-call | tf_op jit(solution)/shard_map/pallas_call | solution.py:178
  25.8 0.0 collective-permute-done.2.ahead_early_ref
  25.8 0.0 collective-permute-done.1.ahead_head_ref
  25.8 0.8 %shard_map.62 = (f32[16,1,2176]{2,1,0:T(1,128)S(1)}, f32[16,1,2176]{2,1,0:T(1,128)S(1)}) custom-call(bf16[4096,256]{1,0:T(8,128)(2,1)S(1)} %get-tuple-element.22.feature_ref, bf16[512,256]{1,0:T(8,128)(2,1)S(1)} %collective-permute-done.1.ahead_head_ref, bf16[512,256]{1,0:T(8,128)(2,1)S(1)} %collective-permute-done.2.ahead_early_ref, ...), custom_call_target="tpu_custom_call" | custom-call | tf_op jit(solution)/shard_map/pallas_call | solution.py:228
  26.6 0.1 collective-permute-start.3
  26.7 1.3 %collective-permute-done.3 = f32[16,1,2176]{2,1,0:T(1,128)S(1)} collective-permute-done((f32[16,1,2176]{2,1,0:T(1,128)S(1)}, f32[16,1,2176]{2,1,0:T(1,128)S(1)}, u32[]{:S(2)}, u32[]{:S(2)}) %collective-permute-start.3) | collective-permute-done | bytes 139296 | tf_op jit(solution)/shard_map/ppermute | solution.py:421
  28.0 0.1 add.3
  28.2 17.6 %all_to_all.10 = f32[16,1,2176]{2,1,0:T(1,128)S(1)} all-to-all(f32[16,1,2176]{2,1,0:T(1,128)S(1)} %add.3), channel_id=1, replica_groups=mesh['x'=2,'core'=2,'tm'=8] {'x','tm'}, dimensions={0} | all-to-all | bytes 278528 | tf_op jit(solution)/shard_map/all_to_all | solution.py:422
  45.8 0.1 reduce_sum.9
  45.9 0.1 broadcast_in_dim.12
  45.9 10.8 %all_to_all.11.mine_ref = f32[16,1,2176]{2,1,0:T(1,128)S(1)} all-to-all(f32[16,1,2176]{2,1,0:T(1,128)S(1)} %broadcast_in_dim.12), channel_id=1, replica_groups=mesh['x'=2,'core'=2,'tm'=8] {'x','tm'}, dimensions={0} | all-to-all | bytes 278528 | tf_op jit(solution)/shard_map/all_to_all | solution.py:423
  56.7 0.0 collective-permute-start.4
  56.7 1.4 %collective-permute-done.4.other_ref = f32[16,1,2176]{2,1,0:T(1,128)S(1)} collective-permute-done((f32[16,1,2176]{2,1,0:T(1,128)S(1)}, f32[16,1,2176]{2,1,0:T(1,128)S(1)}, u32[]{:S(2)}, u32[]{:S(2)}) %collective-permute-start.4) | collective-permute-done | bytes 139296 | tf_op jit(solution)/shard_map/ppermute | solution.py:424
  58.1 10.3 %shard_map.63 = (bf16[2,512,256]{2,1,0:T(8,128)(2,1)S(1)}, f32[2,8,256]{2,1,0:T(8,128)S(1)}) custom-call(f32[1]{0:T(128)} %constant.0.clone.1.scale_ref, f32[16,1,2176]{2,1,0:T(1,128)S(1)} %all_to_all.11.mine_ref, f32[16,1,2176]{2,1,0:T(1,128)S(1)} %collective-permute-done.4.other_ref), custom_call_target="tpu_custom_call" | custom-call | tf_op jit(solution)/shard_map/pallas_call | solution.py:355
  68.4 3.9 %shard_map.64 = (f32[4096,256]{1,0:T(8,128)}, f32[4096,256]{1,0:T(8,128)}) custom-call(bf16[4096,256]{1,0:T(8,128)(2,1)S(1)} %get-tuple-element.22.feature_ref, bf16[512,256]{1,0:T(8,128)(2,1)S(1)} %collective-permute-done.1.ahead_head_ref, bf16[512,256]{1,0:T(8,128)(2,1)S(1)} %collective-permute-done.2.ahead_early_ref, ...), custom_call_target="tpu_custom_call" | custom-call | tf_op jit(solution)/shard_map/pallas_call | solution.py:404
Async XLA Ops:
  1.6 11.1 %collective-permute-start = (bf16[288,512]{1,0:T(8,128)(2,1)S(1)}, bf16[288,512]{1,0:T(8,128)(2,1)S(1)}, u32[]{:S(2)}, u32[]{:S(2)}) collective-permute-start(bf16[288,512]{1,0:T(8,128)(2,1)S(1)} %slice_bitcast_fusion), channel_id=1, source_target_pairs={{0,1},{1,2},{2,3},{3,4},{4,5},{5,6},{6,7},{8,9},{9,10},{10,11},{11... | collective-permute-start | bytes 884744 | tf_op jit(solution)/shard_map/ppermute | solution.py:24
  9.6 16.2 %collective-permute-start.2 = (bf16[512,256]{1,0:T(8,128)(2,1)S(1)}, bf16[512,256]{1,0:T(8,128)(2,1)S(1)}, u32[]{:S(2)}, u32[]{:S(2)}) collective-permute-start(bf16[512,256]{1,0:T(8,128)(2,1)S(1)} %get-tuple-element.21.early_ref), channel_id=1, source_target_pairs={{1,0},{2,1},{3,2},{4,3},{5,4},{6,5},{7,6},{9,8},{10,9},{11,10},{12... | collective-permute-start | bytes 786440 | tf_op jit(solution)/shard_map/ppermute | solution.py:24
  14.2 11.6 %collective-permute-start.1 = (bf16[512,256]{1,0:T(8,128)(2,1)S(1)}, bf16[512,256]{1,0:T(8,128)(2,1)S(1)}, u32[]{:S(2)}, u32[]{:S(2)}) collective-permute-start(bf16[512,256]{1,0:T(8,128)(2,1)S(1)} %shard_map.60.head_ref), channel_id=1, source_target_pairs={{1,0},{2,1},{3,2},{4,3},{5,4},{6,5},{7,6},{9,8},{10,9},{11,10},{12... | collective-permute-start | bytes 786440 | tf_op jit(solution)/shard_map/ppermute | solution.py:24
  26.6 1.4 %collective-permute-start.3 = (f32[16,1,2176]{2,1,0:T(1,128)S(1)}, f32[16,1,2176]{2,1,0:T(1,128)S(1)}, u32[]{:S(2)}, u32[]{:S(2)}) collective-permute-start(f32[16,1,2176]{2,1,0:T(1,128)S(1)} %get-tuple-element.27), channel_id=1, source_target_pairs={{0,8},{8,0},{1,9},{9,1},{2,10},{10,2},{3,11},{11,3},{4,12},{12,4},... | collective-permute-start | bytes 417800 | tf_op jit(solution)/shard_map/ppermute | solution.py:421
  56.7 1.4 %collective-permute-start.4 = (f32[16,1,2176]{2,1,0:T(1,128)S(1)}, f32[16,1,2176]{2,1,0:T(1,128)S(1)}, u32[]{:S(2)}, u32[]{:S(2)}) collective-permute-start(f32[16,1,2176]{2,1,0:T(1,128)S(1)} %all_to_all.11.mine_ref), channel_id=1, source_target_pairs={{0,8},{8,0},{1,9},{9,1},{2,10},{10,2},{3,11},{11,3},{4,12},{12,4},... | collective-permute-start | bytes 417800 | tf_op jit(solution)/shard_map/ppermute | solution.py:424

commit v6 on v5

--- a/solution.py
+++ b/solution.py
@@ -42,36 +42,52 @@
 
 
 def hidden_rows(xs, at, rows, w1_ref, b1_ref):
-    channels = xs.shape[1]
-    z = jnp.dot(xs[pl.ds(at + D1, rows), :], w1_ref[:channels, :], preferred_element_type=F32)
-    z += jnp.dot(xs[pl.ds(at, rows), :], w1_ref[channels:, :], preferred_element_type=F32)
+    both = jnp.concatenate([xs[pl.ds(at + D1, rows), :], xs[pl.ds(at, rows), :]], 1)
+    z = jnp.dot(both, w1_ref[...], preferred_element_type=F32)
     return silu(z + b1_ref[...]).astype(BF16)
 
 
 def feature_rows(hs, at, rows, w2_ref):
-    hid = hs.shape[1]
-    value = jnp.dot(hs[pl.ds(at + D2, rows), :], w2_ref[:hid, :], preferred_element_type=F32)
-    value += jnp.dot(hs[pl.ds(at, rows), :], w2_ref[hid:, :], preferred_element_type=F32)
-    return value.astype(BF16)
-
-
-def early_kernel(frames_ref, w1_in, b1_in, w2_in, out_ref, near_ref, w1_ref, b1_ref, w2_ref, hs, sems):
-    half = LAG // 2
-    first = half - D1 - D2
-    rows = [(first, LAG - first), (0, first)]
-    copies = [
-        (frames_ref.at[pl.ds(at, count)], near_ref.at[pl.ds(at, count)]) for at, count in rows
-    ] + [(w1_in, w1_ref), (b1_in, b1_ref), (w2_in, w2_ref)]
-    copies = [pltpu.make_async_copy(*pair, sems.at[index]) for index, pair in enumerate(copies)]
-    for index in (2, 0, 3, 4, 1):
-        copies[index].start()
-    for index in (2, 0, 3):
-        copies[index].wait()
+    both = jnp.concatenate([hs[pl.ds(at + D2, rows), :], hs[pl.ds(at, rows), :]], 1)
+    return jnp.dot(both, w2_ref[...], preferred_element_type=F32).astype(BF16)
+
+
+def fetch_kernel(frames_ref, w1_in, b1_in, w2_in, last_ref, near_ref, w1_ref, b1_ref, w2_ref, sems):
+    rows = frames_ref.shape[0]
+    pairs = (
+        (frames_ref.at[pl.ds(rows - D1 - D2, D1 + D2)], last_ref),
+        (frames_ref.at[pl.ds(0, LAG)], near_ref),
+        (w1_in, w1_ref),
+        (b1_in, b1_ref),
+        (w2_in, w2_ref),
+    )
+    copies = [pltpu.make_async_copy(*pair, sems.at[index]) for index, pair in enumerate(pairs)]
+    for copy in copies:
+        copy.start()
+    for copy in copies:
+        copy.wait()
+
+
+def fetch(frames, w1, b1, w2):
+    vmem = pl.BlockSpec(memory_space=pltpu.VMEM)
+    hbm = pl.BlockSpec(memory_space=pltpu.HBM)
+    channels = frames.shape[1]
+    shapes = (((D1 + D2, channels), BF16), ((LAG, channels), BF16), (w1.shape, BF16), (b1.shape, F32), (w2.shape, BF16))
+    return pl.pallas_call(
+        fetch_kernel,
+        in_specs=[hbm] * 4,
+        out_specs=(vmem,) * 5,
+        out_shape=tuple(jax.ShapeDtypeStruct(*shape) for shape in shapes),
+        scratch_shapes=[pltpu.SemaphoreType.DMA((5,))],
+        compiler_params=pltpu.CompilerParams(vmem_limit_bytes=8 * MIB),
+    )(*(in_hbm(value) for value in (frames, w1, b1, w2)))
+
+
+def early_kernel(near_ref, w1_ref, b1_ref, w2_ref, out_ref, hs):
+    half = LAG // 2
     for at in range(0, hs.shape[0], D2):
-        hs[at : at + D2, :] = hidden_rows(near_ref, first + at, D2, w1_ref, b1_ref)
-    copies[4].wait()
+        hs[at : at + D2, :] = hidden_rows(near_ref, half - D1 - D2 + at, D2, w1_ref, b1_ref)
     out_ref[...] = feature_rows(hs, 0, half, w2_ref)
-    copies[1].wait()
 
 
 def head_kernel(near_ref, halo_ref, w1_ref, b1_ref, w2_ref, out_ref, xs, hs):
@@ -92,19 +108,17 @@
     ]
 
 
-def early_rows(frames, w1, b1, w2):
-    vmem = pl.BlockSpec(memory_space=pltpu.VMEM)
-    hbm = pl.BlockSpec(memory_space=pltpu.HBM)
-    half, channels, hid = LAG // 2, frames.shape[1], w1.shape[1]
-    shapes = [((half, w2.shape[1]), BF16), ((LAG, channels), BF16), (w1.shape, BF16), (b1.shape, F32), (w2.shape, BF16)]
+def early_rows(near, w1, b1, w2):
+    vmem = pl.BlockSpec(memory_space=pltpu.VMEM)
+    half = LAG // 2
     return pl.pallas_call(
         early_kernel,
-        in_specs=[hbm] * 4,
-        out_specs=(vmem,) * 5,
-        out_shape=tuple(jax.ShapeDtypeStruct(*shape) for shape in shapes),
-        scratch_shapes=[pltpu.VMEM((half + D2, hid), BF16), pltpu.SemaphoreType.DMA((5,))],
-        compiler_params=pltpu.CompilerParams(vmem_limit_bytes=12 * MIB),
-    )(*(in_hbm(value) for value in (frames, w1, b1, w2)))
+        in_specs=[vmem] * 4,
+        out_specs=vmem,
+        out_shape=jax.ShapeDtypeStruct((half, w2.shape[1]), BF16),
+        scratch_shapes=[pltpu.VMEM((half + D2, w1.shape[1]), BF16)],
+        compiler_params=pltpu.CompilerParams(vmem_limit_bytes=8 * MIB),
+    )(near, w1, b1, w2)
 
 
 def head_rows(near, halo, w1, b1, w2):
@@ -243,25 +257,6 @@
     return high, middle, low
 
 
-def repeated_parts(block, offset):
-    lane = lax.broadcasted_iota(jnp.int32, block.shape, 1)
-    base = jnp.where((lane >= offset) & (lane < offset + PANEL), block, 0.0)
-    if offset:
-        base = pltpu.roll(base, 128 - offset, 1)
-    two = base + pltpu.roll(base, PANEL, 1)
-    six = two + pltpu.roll(two, 2 * PANEL, 1) + pltpu.roll(two, 4 * PANEL, 1)
-    high, middle, low = (part.astype(F32) for part in three_parts(six))
-    place = lane // PANEL
-    chosen = jnp.where((place == 2) | (place == 5), middle, jnp.where(place == 4, low, high))
-    return chosen.astype(BF16)
-
-
-def stacked_parts(rows):
-    high, middle, low = three_parts(rows)
-    rest = jnp.zeros((128 - 6 * PANEL, rows.shape[1]), BF16)
-    return jnp.concatenate([high, middle, high, low, high, middle, rest], 0)
-
-
 def inverse_factor(work):
     size = work.shape[0]
     lane = lax.broadcasted_iota(jnp.int32, (PANEL, size), 1)
@@ -283,32 +278,30 @@
         panel = jnp.where(
             (lane >= start) & (lane < stop), jnp.where(lane - start == sub, 1.0, 0.0), panel
         )
-        solved = panel
-        slab = start // 128 * 128
-        if stop < size:
-            left = repeated_parts(work[stop:, slab : slab + 128], start - slab)
         pivots = jnp.ones((PANEL, 128), F32)
         pivot = spread(columns[0], 0)
         for j in range(PANEL):
             inverse = pl.reciprocal(pivot, approx=True)
             pivots = jnp.where(sub_narrow == j, pivot, pivots)
-            factor = jnp.where(sub_narrow == j, 0.0, columns[j]) * inverse
+            if j + 1 == PANEL:
+                break
+            factor = jnp.where(sub_narrow > j, columns[j], 0.0) * inverse
             beside = [spread(columns[k], j) for k in range(j + 1, PANEL)]
-            if j + 1 < PANEL:
-                pivot = spread(columns[j + 1], j + 1) - beside[0] * beside[0] * inverse
+            pivot = spread(columns[j + 1], j + 1) - beside[0] * beside[0] * inverse
             for k in range(j + 1, PANEL):
                 columns[k] = columns[k] - factor * beside[k - j - 1]
-            if j + 1 < PANEL:
-                below = jnp.where(sub_narrow > j, factor, 0.0)
-                panel = panel - wide(below) * spread(panel, j)
-            solved = solved - wide(factor) * spread(solved, j)
+            panel = panel - wide(factor) * spread(panel, j)
+        panel = panel * wide(lax.rsqrt(pivots))
+        work[start:stop, :] = panel
         if stop < size:
-            right = stacked_parts(solved * wide(1.0 / pivots))
-            update = jnp.dot(left, right, preferred_element_type=F32)
+            high, middle, low = three_parts(panel)
+            left = jnp.concatenate([high, high, middle, high, low, middle], 0)
+            right = jnp.concatenate([high, middle, high, low, high, middle], 0)
+            first = stop // 128 * 128
+            update = gram(left[:, first:], right)
             kept = lax.broadcasted_iota(jnp.int32, (size - stop, size), 1)
             kept = (kept < start) | (kept >= stop)
-            work[stop:, :] = jnp.where(kept, work[stop:, :], 0.0) - update
-        work[start:stop, :] = panel * wide(lax.rsqrt(pivots))
+            work[stop:, :] = jnp.where(kept, work[stop:, :], 0.0) - update[stop - first :]
     row = lax.broadcasted_iota(jnp.int32, (size, size), 0)
     column = lax.broadcasted_iota(jnp.int32, (size, size), 1)
     return jnp.where(column <= row, work[...], 0.0)
@@ -415,13 +408,30 @@
     )(feature, ahead_head, ahead_early, split, shift)
 
 
+def swapped(value, axis, bit):
+    return lax.ppermute(value, axis, [(i, i ^ bit) for i in range(lax.axis_size(axis))])
+
+
+def upper(axis, bit):
+    return lax.axis_index(axis) // bit % 2
+
+
 def summed(kept, sent):
-    swap = [(0, 1), (1, 0)]
-    chips = ("x", "tm")
-    parts = kept + lax.ppermute(sent, "core", swap)
-    mine = jnp.sum(lax.all_to_all(parts, chips, 0, 0, tiled=True), 0, keepdims=True)
-    mine = lax.all_to_all(jnp.broadcast_to(mine, parts.shape), chips, 0, 0, tiled=True)
-    return mine, lax.ppermute(mine, "core", swap)
+    bits = lambda axis: [1 << k for k in range(lax.axis_size(axis).bit_length() - 1)]
+    halved = [("x", bit) for bit in bits("x")] + [("tm", bit) for bit in bits("tm")[:1]]
+    mine = kept + swapped(sent, "core", 1)
+    for axis, bit in halved:
+        half = mine.shape[0] // 2
+        up = upper(axis, bit)
+        away = lax.dynamic_slice_in_dim(mine, (1 - up) * half, half)
+        mine = lax.dynamic_slice_in_dim(mine, up * half, half) + swapped(away, axis, bit)
+    for bit in bits("tm")[1:]:
+        mine = mine + swapped(mine, "tm", bit)
+    for axis, bit in reversed(halved):
+        other = swapped(mine, axis, bit)
+        in_upper = upper(axis, bit) == 1
+        mine = jnp.concatenate([jnp.where(in_upper, other, mine), jnp.where(in_upper, mine, other)], 0)
+    return mine, swapped(mine, "core", 1)
 
 
 def on_device(frames, first_weight, first_bias, second_weight):
@@ -433,8 +443,9 @@
         first_bias.reshape(1, hid),
         second_weight.reshape(2 * hid, feat),
     )
-    halo = passed_along(frame_block[row_count - D1 - D2 :], "tm", 1)
-    early, near, *weights = early_rows(frame_block, *weights)
+    last, near, *weights = fetch(frame_block, *weights)
+    halo = passed_along(last, "tm", 1)
+    early = early_rows(near, *weights)
     ahead_early = passed_along(early, "tm", -1)
     head = head_rows(near, halo, *weights)
     ahead_head = passed_along(head, "tm", -1)

time: 72.7 us -> 79 us (1.087)
  blocking collectives: 28.4 us -> 0 us
  waiting for transfers between devices: 4.57 us -> 26.7 us
  starting transfers between devices: 7.55 us -> 21.2 us
  local copies, waits for them, and re-layouts: 1.06 us -> 0.03 us
    all_to_all x2 -> x0, blocking collectives: 28.4 us -> none  [the longest x1 17.6 us: summed(): lax.all_to_all(parts, chips, 0, 0, tiled=True)]
    ppermute x2 -> x8, waiting for transfers between devices: 2.7 us -> 17.6 us  [swapped(): lax.ppermute(value, axis, [(i, i ^ bit) for i in range(lax.axis_size(axis...]
    ppermute x2 -> x8, starting transfers between devices: 0.07 us -> 13.6 us  [swapped(): lax.ppermute(value, axis, [(i, i ^ bit) for i in range(lax.axis_size(axis...]
    ppermute x3, waiting for transfers between devices: 1.87 us -> 9.15 us  [passed_along(): lax.ppermute(value, axis, [(source, source + steps) for source in range(f...]
    slice x1 -> x0, local copies, waits for them, and re-layouts: 0.98 us -> none  [on_device(): halo = passed_along(frame_block[row_count - D1 - D2:], 'tm', 1)]
    pallas_call x1 -> x2, Pallas kernels: 3.06 us -> 3.23 us  [the longest x1 1.83 us: fetch(): pl.pallas_call(fetch_kernel, in_specs=[hbm] * 4, out_specs=(vmem,) * 5, o...]
  transfers between devices with their start and end apart: 5 -> 11, of which waited for: 3 -> 9; matrix products, arithmetic and copies ran while one was open for 0% -> 0% of each run, Pallas kernels for 20% -> 17%
where the time goes in v6:
time: 79 us; the launch traced here: 78.8 us
  Pallas kernels  29.2 us (37%)
  waiting for transfers between devices  26.7 us (34%)
  starting transfers between devices  21.2 us (27%)
  between operations  0.98 us (1%)
    ppermute x8, waiting for transfers between devices, swapped(): lax.ppermute(value, axis, [(i, i ^ bit) for i in range(lax.axis_size(axis...  17.6 us
    ppermute x8, starting transfers between devices, swapped(): lax.ppermute(value, axis, [(i, i ^ bit) for i in range(lax.axis_size(axis...  13.6 us
    pallas_call x1, Pallas kernels, body(): pl.pallas_call(body_kernel, in_specs=[pl.BlockSpec(memory_space=pltpu.HBM...  10.3 us
    pallas_call x1, Pallas kernels, koopman_parts(): pl.pallas_call(koopman_kernel, in_specs=[pl.BlockSpec(memory_space=pltpu....  9.53 us
    ppermute x3, waiting for transfers between devices, passed_along(): lax.ppermute(value, axis, [(source, source + steps) for source in range(f...  9.15 us
    ppermute x3, starting transfers between devices, passed_along(): lax.ppermute(value, axis, [(source, source + steps) for source in range(f...  7.65 us
    pallas_call x1, Pallas kernels, project(): pl.pallas_call(project_kernel, in_specs=[vmem] * 5, out_specs=(hbm, hbm),...  3.87 us
    pallas_call x1, Pallas kernels, fetch(): pl.pallas_call(fetch_kernel, in_specs=[hbm] * 4, out_specs=(vmem,) * 5, o...  1.83 us
  transfers between devices with their start and end apart: 11, of which 9 were waited for; matrix products, arithmetic and copies ran while one was open for 0% of the time, Pallas kernels for 17%

profile of v6, /device:TPU:0, one launch (start us, length us, event | category | flops | bytes accessed | tf_op | source)
XLA Modules:
  0.0 78.8 jit_solution(12905543029658202137)
XLA Ops:
  0.6 1.8 %shard_map.59 = (bf16[288,512]{1,0:T(8,128)(2,1)S(1)}, bf16[1024,512]{1,0:T(8,128)(2,1)S(1)}, bf16[1024,512]{1,0:T(8,128)(2,1)S(1)}, f32[1,512]{1,0:T(1,128)S(1)}, bf16[1024,256]{1,0:T(8,128)(2,1)S(1)}) custom-call(bf16[4096,512]{1,0:T(8,128)(2,1)} %bitcast.6, bf16[1024,512]{1,0:T(8,128)(2,1)} %bitcast.8, f32[1,512]{1,0:T(1,128)} %bitcast.10, ...), custom_call_target="tpu_custom_call" | custom-call | tf_op jit(solution)/shard_map/pallas_call | solution.py:76
  2.5 4.9 %collective-permute-start = (bf16[288,512]{1,0:T(8,128)(2,1)S(1)}, bf16[288,512]{1,0:T(8,128)(2,1)S(1)}, u32[]{:S(2)}, u32[]{:S(2)}) collective-permute-start(bf16[288,512]{1,0:T(8,128)(2,1)S(1)} %get-tuple-element.18), channel_id=1, source_target_pairs={{0,1},{1,2},{2,3},{3,4},{4,5},{5,6},{6,7},{8,9},{9,10},{10,11},{11... | collective-permute-start | bytes 884744 | tf_op jit(solution)/shard_map/ppermute | solution.py:24
  7.4 1.4 %shard_map.61.early_ref = bf16[512,256]{1,0:T(8,128)(2,1)S(1)} custom-call(bf16[1024,512]{1,0:T(8,128)(2,1)S(1)} %get-tuple-element.17.near_ref, bf16[1024,512]{1,0:T(8,128)(2,1)S(1)} %get-tuple-element.19.w1_ref, f32[1,512]{1,0:T(1,128)S(1)} %get-tuple-element.20.b1_ref, bf16[1024,256]{1,0:T(8,128)(2,1)S(1)} %get-tuple-element.21.w2_ref), custom_call_target="tpu_custom_call" | custom-call | tf_op jit(solution)/shard_map/pallas_call | solution.py:114
  8.8 1.3 %collective-permute-start.2 = (bf16[512,256]{1,0:T(8,128)(2,1)S(1)}, bf16[512,256]{1,0:T(8,128)(2,1)S(1)}, u32[]{:S(2)}, u32[]{:S(2)}) collective-permute-start(bf16[512,256]{1,0:T(8,128)(2,1)S(1)} %shard_map.61.early_ref), channel_id=1, source_target_pairs={{1,0},{2,1},{3,2},{4,3},{5,4},{6,5},{7,6},{9,8},{10,9},{11,10},{12... | collective-permute-start | bytes 786440 | tf_op jit(solution)/shard_map/ppermute | solution.py:24
  10.1 9.1 %collective-permute-done.halo_ref = bf16[288,512]{1,0:T(8,128)(2,1)S(1)} collective-permute-done((bf16[288,512]{1,0:T(8,128)(2,1)S(1)}, bf16[288,512]{1,0:T(8,128)(2,1)S(1)}, u32[]{:S(2)}, u32[]{:S(2)}) %collective-permute-start) | collective-permute-done | bytes 294944 | tf_op jit(solution)/shard_map/ppermute | solution.py:24
  19.2 1.4 %shard_map.60.head_ref = bf16[512,256]{1,0:T(8,128)(2,1)S(1)} custom-call(bf16[1024,512]{1,0:T(8,128)(2,1)S(1)} %get-tuple-element.17.near_ref, bf16[288,512]{1,0:T(8,128)(2,1)S(1)} %collective-permute-done.halo_ref, bf16[1024,512]{1,0:T(8,128)(2,1)S(1)} %get-tuple-element.19.w1_ref, f32[1,512]{1,0:T(1,128)S(1)} %get-tuple-element.20.b1_ref, ...), custom_call_target="tpu_custom_call" | custom-call | tf_op jit(solution)/shard_map/pallas_call | solution.py:127
  20.7 1.5 %collective-permute-start.1 = (bf16[512,256]{1,0:T(8,128)(2,1)S(1)}, bf16[512,256]{1,0:T(8,128)(2,1)S(1)}, u32[]{:S(2)}, u32[]{:S(2)}) collective-permute-start(bf16[512,256]{1,0:T(8,128)(2,1)S(1)} %shard_map.60.head_ref), channel_id=1, source_target_pairs={{1,0},{2,1},{3,2},{4,3},{5,4},{6,5},{7,6},{9,8},{10,9},{11,10},{12... | collective-permute-start | bytes 786440 | tf_op jit(solution)/shard_map/ppermute | solution.py:24
  22.1 10.3 %shard_map.62 = (bf16[4096,256]{1,0:T(8,128)(2,1)S(1)}, f32[256,256]{1,0:T(8,128)S(1)}, f32[256,256]{1,0:T(8,128)S(1)}, f32[8,256]{1,0:T(8,128)S(1)}) custom-call(bf16[4096,512]{1,0:T(8,128)(2,1)} %bitcast.7, bf16[1024,512]{1,0:T(8,128)(2,1)S(1)} %get-tuple-element.17.near_ref, bf16[512,256]{1,0:T(8,128)(2,1)S(1)} %shard_map.60.head_ref, ...), custom_call_target="tpu_custom_call" | custom-call | tf_op jit(solution)/shard_map/pallas_call | solution.py:192
  32.5 0.8 shard_map.63
  33.3 0.1 collective-permute-start.3
  33.4 1.3 %collective-permute-done.3 = f32[16,1,2176]{2,1,0:T(1,128)S(1)} collective-permute-done((f32[16,1,2176]{2,1,0:T(1,128)S(1)}, f32[16,1,2176]{2,1,0:T(1,128)S(1)}, u32[]{:S(2)}, u32[]{:S(2)}) %collective-permute-start.3) | collective-permute-done | bytes 139296 | tf_op jit(solution)/shard_map/ppermute | solution.py:412
  34.7 0.1 add.40
  34.9 1.6 %collective-permute-start.4 = (f32[8,1,2176]{2,1,0:T(1,128)S(1)}, f32[8,1,2176]{2,1,0:T(1,128)S(1)}, u32[]{:S(2)}, u32[]{:S(2)}) collective-permute-start(f32[8,1,2176]{2,1,0:T(1,128)S(1)} %constant_dynamic-slice_fusion.1), channel_id=1, source_target_pairs={{0,16},{16,0},{1,17},{17,1},{2,18},{18,2},{3,19},{19,3},{4,20},{20... | collective-permute-start | bytes 208904 | tf_op jit(solution)/shard_map/ppermute | solution.py:412
  36.4 2.8 %collective-permute-done.4 = f32[8,1,2176]{2,1,0:T(1,128)S(1)} collective-permute-done((f32[8,1,2176]{2,1,0:T(1,128)S(1)}, f32[8,1,2176]{2,1,0:T(1,128)S(1)}, u32[]{:S(2)}, u32[]{:S(2)}) %collective-permute-start.4) | collective-permute-done | bytes 69664 | tf_op jit(solution)/shard_map/ppermute | solution.py:412
  39.2 0.1 dynamic-slice_add_fusion
  39.3 3.2 %collective-permute-start.5 = (f32[4,1,2176]{2,1,0:T(1,128)S(1)}, f32[4,1,2176]{2,1,0:T(1,128)S(1)}, u32[]{:S(2)}, u32[]{:S(2)}) collective-permute-start(f32[4,1,2176]{2,1,0:T(1,128)S(1)} %constant_dynamic-slice_fusion), channel_id=1, source_target_pairs={{0,1},{1,0},{2,3},{3,2},{4,5},{5,4},{6,7},{7,6},{8,9},{9,8},{10,11... | collective-permute-start | bytes 104456 | tf_op jit(solution)/shard_map/ppermute | solution.py:412
  42.5 1.9 %collective-permute-done.5 = f32[4,1,2176]{2,1,0:T(1,128)S(1)} collective-permute-done((f32[4,1,2176]{2,1,0:T(1,128)S(1)}, f32[4,1,2176]{2,1,0:T(1,128)S(1)}, u32[]{:S(2)}, u32[]{:S(2)}) %collective-permute-start.5) | collective-permute-done | bytes 34848 | tf_op jit(solution)/shard_map/ppermute | solution.py:412
  44.5 3.5 %collective-permute-start.6 = (f32[4,1,2176]{2,1,0:T(1,128)S(1)}, f32[4,1,2176]{2,1,0:T(1,128)S(1)}, u32[]{:S(2)}, u32[]{:S(2)}) collective-permute-start(f32[4,1,2176]{2,1,0:T(1,128)S(1)} %dynamic-slice_add_fusion.1), channel_id=1, source_target_pairs={{0,2},{1,3},{2,0},{3,1},{4,6},{5,7},{6,4},{7,5},{8,10},{9,11},{10,... | collective-permute-start | bytes 104456 | tf_op jit(solution)/shard_map/ppermute | solution.py:412
  48.0 1.9 %collective-permute-done.6 = f32[4,1,2176]{2,1,0:T(1,128)S(1)} collective-permute-done((f32[4,1,2176]{2,1,0:T(1,128)S(1)}, f32[4,1,2176]{2,1,0:T(1,128)S(1)}, u32[]{:S(2)}, u32[]{:S(2)}) %collective-permute-start.6) | collective-permute-done | bytes 34848 | tf_op jit(solution)/shard_map/ppermute | solution.py:412
  50.0 3.1 %collective-permute-start.7 = (f32[4,1,2176]{2,1,0:T(1,128)S(1)}, f32[4,1,2176]{2,1,0:T(1,128)S(1)}, u32[]{:S(2)}, u32[]{:S(2)}) collective-permute-start(f32[4,1,2176]{2,1,0:T(1,128)S(1)} %add.47), channel_id=1, source_target_pairs={{0,4},{1,5},{2,6},{3,7},{4,0},{5,1},{6,2},{7,3},{8,12},{9,13},{10,... | collective-permute-start | bytes 104456 | tf_op jit(solution)/shard_map/ppermute | solution.py:412
  53.1 1.9 %collective-permute-done.7 = f32[4,1,2176]{2,1,0:T(1,128)S(1)} collective-permute-done((f32[4,1,2176]{2,1,0:T(1,128)S(1)}, f32[4,1,2176]{2,1,0:T(1,128)S(1)}, u32[]{:S(2)}, u32[]{:S(2)}) %collective-permute-start.7) | collective-permute-done | bytes 34848 | tf_op jit(solution)/shard_map/ppermute | solution.py:412
  55.1 0.5 collective-permute-start.8
  55.5 3.5 %collective-permute-done.8 = f32[4,1,2176]{2,1,0:T(1,128)S(1)} collective-permute-done((f32[4,1,2176]{2,1,0:T(1,128)S(1)}, f32[4,1,2176]{2,1,0:T(1,128)S(1)}, u32[]{:S(2)}, u32[]{:S(2)}) %collective-permute-start.8) | collective-permute-done | bytes 34848 | tf_op jit(solution)/shard_map/ppermute | solution.py:412
  59.1 0.1 pad_maximum_fusion.1
  59.2 1.6 %collective-permute-start.9 = (f32[8,1,2176]{2,1,0:T(1,128)S(1)}, f32[8,1,2176]{2,1,0:T(1,128)S(1)}, u32[]{:S(2)}, u32[]{:S(2)}) collective-permute-start(f32[8,1,2176]{2,1,0:T(1,128)S(1)} %pad_maximum_fusion.1), channel_id=1, source_target_pairs={{0,16},{16,0},{1,17},{17,1},{2,18},{18,2},{3,19},{19,3},{4,20},{20... | collective-permute-start | bytes 208904 | tf_op jit(solution)/shard_map/ppermute | solution.py:412
  60.7 2.8 %collective-permute-done.9 = f32[8,1,2176]{2,1,0:T(1,128)S(1)} collective-permute-done((f32[8,1,2176]{2,1,0:T(1,128)S(1)}, f32[8,1,2176]{2,1,0:T(1,128)S(1)}, u32[]{:S(2)}, u32[]{:S(2)}) %collective-permute-start.9) | collective-permute-done | bytes 69664 | tf_op jit(solution)/shard_map/ppermute | solution.py:412
  63.6 0.1 broadcast_select_fusion.1
  63.7 0.1 pad_maximum_fusion.mine_ref
  63.8 0.1 collective-permute-start.10
  63.9 1.3 %collective-permute-done.10.other_ref = f32[16,1,2176]{2,1,0:T(1,128)S(1)} collective-permute-done((f32[16,1,2176]{2,1,0:T(1,128)S(1)}, f32[16,1,2176]{2,1,0:T(1,128)S(1)}, u32[]{:S(2)}, u32[]{:S(2)}) %collective-permute-start.10) | collective-permute-done | bytes 139296 | tf_op jit(solution)/shard_map/ppermute | solution.py:412
  65.2 9.5 %shard_map.64 = (bf16[2,512,256]{2,1,0:T(8,128)(2,1)S(1)}, f32[2,8,256]{2,1,0:T(8,128)S(1)}) custom-call(f32[1]{0:T(128)} %constant.52.clone.1.scale_ref, f32[16,1,2176]{2,1,0:T(1,128)S(1)} %pad_maximum_fusion.mine_ref, f32[16,1,2176]{2,1,0:T(1,128)S(1)} %collective-permute-done.10.other_ref), custom_call_target="tpu_custom_call" | custom-call | tf_op jit(solution)/shard_map/pallas_call | solution.py:348
  74.8 3.9 %shard_map.65 = (f32[4096,256]{1,0:T(8,128)}, f32[4096,256]{1,0:T(8,128)}) custom-call(bf16[4096,256]{1,0:T(8,128)(2,1)S(1)} %get-tuple-element.22.feature_ref, bf16[512,256]{1,0:T(8,128)(2,1)S(1)} %collective-permute-done.1.ahead_head_ref, bf16[512,256]{1,0:T(8,128)(2,1)S(1)} %collective-permute-done.2.ahead_early_ref, ...), custom_call_target="tpu_custom_call" | custom-call | tf_op jit(solution)/shard_map/pallas_call | solution.py:397
  (8 shorter events, 0.2 us)
Async XLA Ops:
  2.5 16.7 %collective-permute-start = (bf16[288,512]{1,0:T(8,128)(2,1)S(1)}, bf16[288,512]{1,0:T(8,128)(2,1)S(1)}, u32[]{:S(2)}, u32[]{:S(2)}) collective-permute-start(bf16[288,512]{1,0:T(8,128)(2,1)S(1)} %get-tuple-element.18), channel_id=1, source_target_pairs={{0,1},{1,2},{2,3},{3,4},{4,5},{5,6},{6,7},{8,9},{9,10},{10,11},{11... | collective-permute-start | bytes 884744 | tf_op jit(solution)/shard_map/ppermute | solution.py:24
  8.8 23.7 %collective-permute-start.2 = (bf16[512,256]{1,0:T(8,128)(2,1)S(1)}, bf16[512,256]{1,0:T(8,128)(2,1)S(1)}, u32[]{:S(2)}, u32[]{:S(2)}) collective-permute-start(bf16[512,256]{1,0:T(8,128)(2,1)S(1)} %shard_map.61.early_ref), channel_id=1, source_target_pairs={{1,0},{2,1},{3,2},{4,3},{5,4},{6,5},{7,6},{9,8},{10,9},{11,10},{12... | collective-permute-start | bytes 786440 | tf_op jit(solution)/shard_map/ppermute | solution.py:24
  20.7 11.8 %collective-permute-start.1 = (bf16[512,256]{1,0:T(8,128)(2,1)S(1)}, bf16[512,256]{1,0:T(8,128)(2,1)S(1)}, u32[]{:S(2)}, u32[]{:S(2)}) collective-permute-start(bf16[512,256]{1,0:T(8,128)(2,1)S(1)} %shard_map.60.head_ref), channel_id=1, source_target_pairs={{1,0},{2,1},{3,2},{4,3},{5,4},{6,5},{7,6},{9,8},{10,9},{11,10},{12... | collective-permute-start | bytes 786440 | tf_op jit(solution)/shard_map/ppermute | solution.py:24
  33.3 1.4 %collective-permute-start.3 = (f32[16,1,2176]{2,1,0:T(1,128)S(1)}, f32[16,1,2176]{2,1,0:T(1,128)S(1)}, u32[]{:S(2)}, u32[]{:S(2)}) collective-permute-start(f32[16,1,2176]{2,1,0:T(1,128)S(1)} %get-tuple-element.27), channel_id=1, source_target_pairs={{0,8},{8,0},{1,9},{9,1},{2,10},{10,2},{3,11},{11,3},{4,12},{12,4},... | collective-permute-start | bytes 417800 | tf_op jit(solution)/shard_map/ppermute | solution.py:412
  34.9 4.4 %collective-permute-start.4 = (f32[8,1,2176]{2,1,0:T(1,128)S(1)}, f32[8,1,2176]{2,1,0:T(1,128)S(1)}, u32[]{:S(2)}, u32[]{:S(2)}) collective-permute-start(f32[8,1,2176]{2,1,0:T(1,128)S(1)} %constant_dynamic-slice_fusion.1), channel_id=1, source_target_pairs={{0,16},{16,0},{1,17},{17,1},{2,18},{18,2},{3,19},{19,3},{4,20},{20... | collective-permute-start | bytes 208904 | tf_op jit(solution)/shard_map/ppermute | solution.py:412
  39.3 5.1 %collective-permute-start.5 = (f32[4,1,2176]{2,1,0:T(1,128)S(1)}, f32[4,1,2176]{2,1,0:T(1,128)S(1)}, u32[]{:S(2)}, u32[]{:S(2)}) collective-permute-start(f32[4,1,2176]{2,1,0:T(1,128)S(1)} %constant_dynamic-slice_fusion), channel_id=1, source_target_pairs={{0,1},{1,0},{2,3},{3,2},{4,5},{5,4},{6,7},{7,6},{8,9},{9,8},{10,11... | collective-permute-start | bytes 104456 | tf_op jit(solution)/shard_map/ppermute | solution.py:412
  44.5 5.5 %collective-permute-start.6 = (f32[4,1,2176]{2,1,0:T(1,128)S(1)}, f32[4,1,2176]{2,1,0:T(1,128)S(1)}, u32[]{:S(2)}, u32[]{:S(2)}) collective-permute-start(f32[4,1,2176]{2,1,0:T(1,128)S(1)} %dynamic-slice_add_fusion.1), channel_id=1, source_target_pairs={{0,2},{1,3},{2,0},{3,1},{4,6},{5,7},{6,4},{7,5},{8,10},{9,11},{10,... | collective-permute-start | bytes 104456 | tf_op jit(solution)/shard_map/ppermute | solution.py:412
  50.0 5.0 %collective-permute-start.7 = (f32[4,1,2176]{2,1,0:T(1,128)S(1)}, f32[4,1,2176]{2,1,0:T(1,128)S(1)}, u32[]{:S(2)}, u32[]{:S(2)}) collective-permute-start(f32[4,1,2176]{2,1,0:T(1,128)S(1)} %add.47), channel_id=1, source_target_pairs={{0,4},{1,5},{2,6},{3,7},{4,0},{5,1},{6,2},{7,3},{8,12},{9,13},{10,... | collective-permute-start | bytes 104456 | tf_op jit(solution)/shard_map/ppermute | solution.py:412
  55.1 4.0 %collective-permute-start.8 = (f32[4,1,2176]{2,1,0:T(1,128)S(1)}, f32[4,1,2176]{2,1,0:T(1,128)S(1)}, u32[]{:S(2)}, u32[]{:S(2)}) collective-permute-start(f32[4,1,2176]{2,1,0:T(1,128)S(1)} %add.48), channel_id=1, source_target_pairs={{0,1},{1,0},{2,3},{3,2},{4,5},{5,4},{6,7},{7,6},{8,9},{9,8},{10,11... | collective-permute-start | bytes 104456 | tf_op jit(solution)/shard_map/ppermute | solution.py:412
  59.2 4.4 %collective-permute-start.9 = (f32[8,1,2176]{2,1,0:T(1,128)S(1)}, f32[8,1,2176]{2,1,0:T(1,128)S(1)}, u32[]{:S(2)}, u32[]{:S(2)}) collective-permute-start(f32[8,1,2176]{2,1,0:T(1,128)S(1)} %pad_maximum_fusion.1), channel_id=1, source_target_pairs={{0,16},{16,0},{1,17},{17,1},{2,18},{18,2},{3,19},{19,3},{4,20},{20... | collective-permute-start | bytes 208904 | tf_op jit(solution)/shard_map/ppermute | solution.py:412
  63.8 1.4 %collective-permute-start.10 = (f32[16,1,2176]{2,1,0:T(1,128)S(1)}, f32[16,1,2176]{2,1,0:T(1,128)S(1)}, u32[]{:S(2)}, u32[]{:S(2)}) collective-permute-start(f32[16,1,2176]{2,1,0:T(1,128)S(1)} %pad_maximum_fusion.mine_ref), channel_id=1, source_target_pairs={{0,8},{8,0},{1,9},{9,1},{2,10},{10,2},{3,11},{11,3},{4,12},{12,4},... | collective-permute-start | bytes 417800 | tf_op jit(solution)/shard_map/ppermute | solution.py:412

commit v7 on v6

--- a/solution.py
+++ b/solution.py
@@ -43,8 +43,12 @@
 
 def hidden_rows(xs, at, rows, w1_ref, b1_ref):
     both = jnp.concatenate([xs[pl.ds(at + D1, rows), :], xs[pl.ds(at, rows), :]], 1)
-    z = jnp.dot(both, w1_ref[...], preferred_element_type=F32)
-    return silu(z + b1_ref[...]).astype(BF16)
+    hid = w1_ref.shape[1]
+    parts = []
+    for lanes in (slice(0, hid // 2), slice(hid // 2, hid)):
+        z = jnp.dot(both, w1_ref[:, lanes], preferred_element_type=F32)
+        parts.append(silu(z + b1_ref[:, lanes]).astype(BF16))
+    return jnp.concatenate(parts, 1)
 
 
 def feature_rows(hs, at, rows, w2_ref):
@@ -83,11 +87,44 @@
     )(*(in_hbm(value) for value in (frames, w1, b1, w2)))
 
 
-def early_kernel(near_ref, w1_ref, b1_ref, w2_ref, out_ref, hs):
+def first_weight():
+    return jnp.where(lax.axis_index("tm") == 0, 1.0, 2.0)
+
+
+def last_weight():
+    return jnp.where(lax.axis_index("tm") == lax.axis_size("tm") - 1, 1.0, 2.0)
+
+
+def early_kernel(
+    frames_ref, near_ref, w1_ref, b1_ref, w2_ref, early_ref, middle_ref, hidden_ref, inst, total, xs, hs, sems
+):
     half = LAG // 2
-    for at in range(0, hs.shape[0], D2):
-        hs[at : at + D2, :] = hidden_rows(near_ref, half - D1 - D2 + at, D2, w1_ref, b1_ref)
-    out_ref[...] = feature_rows(hs, 0, half, w2_ref)
+    first = half - D1 - D2
+
+    def arriving(step):
+        at = LAG + step * CHUNK
+        return pltpu.make_async_copy(
+            frames_ref.at[pl.ds(at, CHUNK)], xs.at[pl.ds(at - first, CHUNK)], sems.at[step]
+        )
+
+    steps = LAG // CHUNK
+    for step in range(steps):
+        arriving(step).start()
+    xs[: LAG - first, :] = near_ref[first:, :]
+    hs[: D2 + half, :] = hidden_rows(xs, 0, D2 + half, w1_ref, b1_ref)
+    value = feature_rows(hs, 0, half, w2_ref)
+    early_ref[...] = value
+    inst[...] = first_weight() * gram(value, value)
+    total[...] = first_weight() * column_sum(value)
+    for step in range(steps):
+        arriving(step).wait()
+        at = half + step * CHUNK
+        hs[at + D2 : at + D2 + CHUNK, :] = hidden_rows(xs, at + D2, CHUNK, w1_ref, b1_ref)
+        value = feature_rows(hs, at, CHUNK, w2_ref)
+        middle_ref[step * CHUNK : (step + 1) * CHUNK, :] = value
+        inst[...] += 2.0 * gram(value, value)
+        total[...] += 2.0 * column_sum(value)
+    hidden_ref[...] = hs[hs.shape[0] - D2 :, :]
 
 
 def head_kernel(near_ref, halo_ref, w1_ref, b1_ref, w2_ref, out_ref, xs, hs):
@@ -108,17 +145,19 @@
     ]
 
 
-def early_rows(near, w1, b1, w2):
-    vmem = pl.BlockSpec(memory_space=pltpu.VMEM)
-    half = LAG // 2
+def early_rows(frames, near, w1, b1, w2):
+    vmem = pl.BlockSpec(memory_space=pltpu.VMEM)
+    hbm = pl.BlockSpec(memory_space=pltpu.HBM)
+    half, hid, feat = LAG // 2, w1.shape[1], w2.shape[1]
+    shapes = (((half, feat), BF16), ((LAG, feat), BF16), ((D2, hid), BF16), ((feat, feat), F32), ((8, feat), F32))
     return pl.pallas_call(
         early_kernel,
-        in_specs=[vmem] * 4,
-        out_specs=vmem,
-        out_shape=jax.ShapeDtypeStruct((half, w2.shape[1]), BF16),
-        scratch_shapes=[pltpu.VMEM((half + D2, w1.shape[1]), BF16)],
-        compiler_params=pltpu.CompilerParams(vmem_limit_bytes=8 * MIB),
-    )(near, w1, b1, w2)
+        in_specs=[hbm] + [vmem] * 4,
+        out_specs=(vmem,) * 5,
+        out_shape=tuple(jax.ShapeDtypeStruct(*shape) for shape in shapes),
+        scratch_shapes=feature_scratch(half + LAG, near.shape[1], hid) + [pltpu.SemaphoreType.DMA((LAG // CHUNK,))],
+        compiler_params=pltpu.CompilerParams(vmem_limit_bytes=16 * MIB),
+    )(in_hbm(frames), near, w1, b1, w2)
 
 
 def head_rows(near, halo, w1, b1, w2):
@@ -138,60 +177,66 @@
     return jnp.sum(rows.astype(F32).reshape(-1, 8, rows.shape[1]), 0)
 
 
-def body_kernel(frames_ref, near_ref, head_ref, early_ref, w1_ref, b1_ref, w2_ref, out_ref, inst, lag, total, xs, hs, sems):
+def body_kernel(
+    frames_ref, head_ref, early_ref, middle_ref, hidden_ref, inst_in, total_in, w1_ref, b1_ref, w2_ref,
+    out_ref, inst, lag, total, xs, hs, sems
+):
     rows, feat = out_ref.shape
-    first = LAG - D1 - D2
-    steps = (rows - LAG) // CHUNK
+    done = 2 * LAG
+    steps = (rows - done) // CHUNK
 
     def arriving(step):
-        start = step * CHUNK + D1 + D2
+        more = D1 if step == 0 else 0
+        at = step * CHUNK + D1 - more
         return pltpu.make_async_copy(
-            frames_ref.at[pl.ds(first + start, CHUNK)], xs.at[pl.ds(start, CHUNK)], sems.at[step]
+            frames_ref.at[pl.ds(done - D1 + at, CHUNK + more)], xs.at[pl.ds(at, CHUNK + more)], sems.at[step]
         )
 
     for step in range(steps):
         arriving(step).start()
-    xs[: D1 + D2, :] = near_ref[first:, :]
     half = LAG // 2
+    hs[:D2, :] = hidden_ref[...]
     out_ref[:half, :] = head_ref[...]
     out_ref[half:LAG, :] = early_ref[...]
-    tm_index, tm_last = lax.axis_index("tm"), lax.axis_size("tm") - 1
-    first_weight = jnp.where(tm_index == 0, 1.0, 2.0)
-    last_weight = jnp.where(tm_index == tm_last, 1.0, 2.0)
-    start = out_ref[:LAG, :]
-    inst[...] = first_weight * gram(start, start)
-    total[...] = first_weight * column_sum(start)
-    lag[...] = jnp.zeros_like(lag)
-    hs[:D2, :] = hidden_rows(xs, 0, D2, w1_ref, b1_ref)
-    arriving(0).wait()
-    hs[D2 : D2 + CHUNK, :] = hidden_rows(xs, D2, CHUNK, w1_ref, b1_ref)
+    out_ref[LAG:done, :] = middle_ref[...]
+    start = out_ref[:half, :]
+    inst[...] = inst_in[...] + first_weight() * gram(start, start)
+    total[...] = total_in[...] + first_weight() * column_sum(start)
+    lag[...] = gram(out_ref[LAG : LAG + CHUNK, :], out_ref[:CHUNK, :])
+    for at in range(CHUNK, LAG, CHUNK):
+        lag[...] += gram(out_ref[LAG + at : LAG + at + CHUNK, :], out_ref[at : at + CHUNK, :])
+
+    def hidden(step):
+        arriving(step).wait()
+        at = step * CHUNK
+        hs[D2 + at : D2 + at + CHUNK, :] = hidden_rows(xs, at, CHUNK, w1_ref, b1_ref)
 
     def finish(step):
         value = feature_rows(hs, step * CHUNK, CHUNK, w2_ref)
-        at = step * CHUNK
-        out_ref[LAG + at : LAG + at + CHUNK, :] = value
-        weight = last_weight if step >= steps - LAG // CHUNK else 2.0
-        both = gram(value, jnp.concatenate([value, out_ref[at : at + CHUNK, :]], 1))
+        at = done + step * CHUNK
+        out_ref[at : at + CHUNK, :] = value
+        weight = last_weight() if at >= rows - LAG else 2.0
+        both = gram(value, jnp.concatenate([value, out_ref[at - LAG : at - LAG + CHUNK, :]], 1))
         inst[...] += weight * both[:, :feat]
         lag[...] += both[:, feat:]
         total[...] += weight * column_sum(value)
 
+    hidden(0)
     for step in range(steps - 1):
-        arriving(step + 1).wait()
-        at = (step + 1) * CHUNK + D2
-        hs[at : at + CHUNK, :] = hidden_rows(xs, at, CHUNK, w1_ref, b1_ref)
+        hidden(step + 1)
         finish(step)
     finish(steps - 1)
 
 
-def body(frames, near, head, early, w1, b1, w2):
+def body(frames, head, early, middle, hidden, inst, total, w1, b1, w2):
     rows, channels = frames.shape
     hid, feat = w1.shape[1], w2.shape[1]
     vmem = pl.BlockSpec(memory_space=pltpu.VMEM)
     square = jax.ShapeDtypeStruct((feat, feat), F32)
+    left = rows - 2 * LAG
     return pl.pallas_call(
         body_kernel,
-        in_specs=[pl.BlockSpec(memory_space=pltpu.HBM)] + [vmem] * 6,
+        in_specs=[pl.BlockSpec(memory_space=pltpu.HBM)] + [vmem] * 9,
         out_specs=(vmem,) * 4,
         out_shape=(
             jax.ShapeDtypeStruct((rows, feat), BF16),
@@ -199,10 +244,13 @@
             square,
             jax.ShapeDtypeStruct((8, feat), F32),
         ),
-        scratch_shapes=feature_scratch(rows - LAG, channels, hid)
-        + [pltpu.SemaphoreType.DMA((rows // CHUNK,))],
+        scratch_shapes=[
+            pltpu.VMEM((left + D1, channels), BF16),
+            pltpu.VMEM((left + D2, hid), BF16),
+            pltpu.SemaphoreType.DMA((left // CHUNK,)),
+        ],
         compiler_params=pltpu.CompilerParams(vmem_limit_bytes=24 * MIB),
-    )(in_hbm(frames), near, head, early, w1, b1, w2)
+    )(in_hbm(frames), head, early, middle, hidden, inst, total, w1, b1, w2)
 
 
 def pack_kernel(feature_ref, ahead_head_ref, ahead_early_ref, inst, lag, total, kept_ref, sent_ref, packed):
@@ -408,30 +456,13 @@
     )(feature, ahead_head, ahead_early, split, shift)
 
 
-def swapped(value, axis, bit):
-    return lax.ppermute(value, axis, [(i, i ^ bit) for i in range(lax.axis_size(axis))])
-
-
-def upper(axis, bit):
-    return lax.axis_index(axis) // bit % 2
-
-
 def summed(kept, sent):
-    bits = lambda axis: [1 << k for k in range(lax.axis_size(axis).bit_length() - 1)]
-    halved = [("x", bit) for bit in bits("x")] + [("tm", bit) for bit in bits("tm")[:1]]
-    mine = kept + swapped(sent, "core", 1)
-    for axis, bit in halved:
-        half = mine.shape[0] // 2
-        up = upper(axis, bit)
-        away = lax.dynamic_slice_in_dim(mine, (1 - up) * half, half)
-        mine = lax.dynamic_slice_in_dim(mine, up * half, half) + swapped(away, axis, bit)
-    for bit in bits("tm")[1:]:
-        mine = mine + swapped(mine, "tm", bit)
-    for axis, bit in reversed(halved):
-        other = swapped(mine, axis, bit)
-        in_upper = upper(axis, bit) == 1
-        mine = jnp.concatenate([jnp.where(in_upper, other, mine), jnp.where(in_upper, mine, other)], 0)
-    return mine, swapped(mine, "core", 1)
+    swap = [(0, 1), (1, 0)]
+    chips = ("x", "tm")
+    parts = kept + lax.ppermute(sent, "core", swap)
+    mine = jnp.sum(lax.all_to_all(parts, chips, 0, 0, tiled=True), 0, keepdims=True)
+    mine = lax.all_to_all(jnp.broadcast_to(mine, parts.shape), chips, 0, 0, tiled=True)
+    return mine, lax.ppermute(mine, "core", swap)
 
 
 def on_device(frames, first_weight, first_bias, second_weight):
@@ -445,11 +476,13 @@
     )
     last, near, *weights = fetch(frame_block, *weights)
     halo = passed_along(last, "tm", 1)
-    early = early_rows(near, *weights)
+    early, middle, hidden, inst, total = early_rows(frame_block, near, *weights)
     ahead_early = passed_along(early, "tm", -1)
     head = head_rows(near, halo, *weights)
     ahead_head = passed_along(head, "tm", -1)
-    feature, inst, lag, total = body(frame_block, near, head, early, *weights)
+    feature, inst, lag, total = body(
+        frame_block, head, early, middle, hidden, inst, total, *weights
+    )
     chips = lax.axis_size("x") * lax.axis_size("tm")
     mine, other = summed(*pack(feature, ahead_head, ahead_early, inst, lag, total, chips))
     replicas = lax.axis_size("x") * lax.axis_size("core")

time: 79 us -> 70.4 us (0.89)
  blocking collectives: 0 us -> 25.2 us
  waiting for transfers between devices: 26.7 us -> 6.82 us
  starting transfers between devices: 21.2 us -> 7.55 us
    all_to_all x0 -> x2, blocking collectives: none -> 25.2 us  [the longest x1 14.4 us: summed(): lax.all_to_all(parts, chips, 0, 0, tiled=True)]
    ppermute x8 -> x2, waiting for transfers between devices: 17.6 us -> 2.7 us  [the longest x1 1.36 us: summed(): return (mine, lax.ppermute(mine, 'core', swap))]
    ppermute x8 -> x2, starting transfers between devices: 13.6 us -> 0.07 us  [the longest x1 0.07 us: summed(): parts = kept + lax.ppermute(sent, 'core', swap)]
    ppermute x3, waiting for transfers between devices: 9.15 us -> 4.12 us  [passed_along(): lax.ppermute(value, axis, [(source, source + steps) for source in range(f...]
    pallas_call x1, Pallas kernels: 1.4 us -> 5 us  [early_rows(): pl.pallas_call(early_kernel, in_specs=[hbm] + [vmem] * 4, out_specs=(vmem...]
    pallas_call x1, Pallas kernels: 10.3 us -> 7.1 us  [body(): pl.pallas_call(body_kernel, in_specs=[pl.BlockSpec(memory_space=pltpu.HBM...]
  transfers between devices with their start and end apart: 11 -> 5, of which waited for: 9 -> 3; matrix products, arithmetic and copies ran while one was open for 0% -> 0% of each run, Pallas kernels for 17% -> 19%
where the time goes in v7:
time: 70.4 us; the launch traced here: 70.1 us
  Pallas kernels  29.3 us (42%)
  blocking collectives  25.2 us (36%)
  starting transfers between devices  7.55 us (11%)
  waiting for transfers between devices  6.82 us (10%)
  between operations  0.89 us (1%)
    all_to_all x1, blocking collectives, summed(): lax.all_to_all(parts, chips, 0, 0, tiled=True)  14.4 us
    all_to_all x1, blocking collectives, summed(): lax.all_to_all(jnp.broadcast_to(mine, parts.shape), chips, 0, 0, tiled=True)  10.8 us
    pallas_call x1, Pallas kernels, koopman_parts(): pl.pallas_call(koopman_kernel, in_specs=[pl.BlockSpec(memory_space=pltpu....  9.32 us
    ppermute x3, starting transfers between devices, passed_along(): lax.ppermute(value, axis, [(source, source + steps) for source in range(f...  7.47 us
    pallas_call x1, Pallas kernels, body(): pl.pallas_call(body_kernel, in_specs=[pl.BlockSpec(memory_space=pltpu.HBM...  7.1 us
    pallas_call x1, Pallas kernels, early_rows(): pl.pallas_call(early_kernel, in_specs=[hbm] + [vmem] * 4, out_specs=(vmem...  5 us
    ppermute x3, waiting for transfers between devices, passed_along(): lax.ppermute(value, axis, [(source, source + steps) for source in range(f...  4.12 us
    pallas_call x1, Pallas kernels, project(): pl.pallas_call(project_kernel, in_specs=[vmem] * 5, out_specs=(hbm, hbm),...  3.87 us
  transfers between devices with their start and end apart: 5, of which 3 were waited for; matrix products, arithmetic and copies ran while one was open for 0% of the time, Pallas kernels for 19%

profile of v7, /device:TPU:0, one launch (start us, length us, event | category | flops | bytes accessed | tf_op | source)
XLA Modules:
  0.0 70.1 jit_solution(2380035307803381766)
XLA Ops:
  0.6 1.8 %shard_map.59 = (bf16[288,512]{1,0:T(8,128)(2,1)S(1)}, bf16[1024,512]{1,0:T(8,128)(2,1)S(1)}, bf16[1024,512]{1,0:T(8,128)(2,1)S(1)}, f32[1,512]{1,0:T(1,128)S(1)}, bf16[1024,256]{1,0:T(8,128)(2,1)S(1)}) custom-call(bf16[4096,512]{1,0:T(8,128)(2,1)} %bitcast.6, bf16[1024,512]{1,0:T(8,128)(2,1)} %bitcast.9, f32[1,512]{1,0:T(1,128)} %bitcast.11, ...), custom_call_target="tpu_custom_call" | custom-call | tf_op jit(solution)/shard_map/pallas_call | solution.py:80
  2.5 4.9 %collective-permute-start = (bf16[288,512]{1,0:T(8,128)(2,1)S(1)}, bf16[288,512]{1,0:T(8,128)(2,1)S(1)}, u32[]{:S(2)}, u32[]{:S(2)}) collective-permute-start(bf16[288,512]{1,0:T(8,128)(2,1)S(1)} %get-tuple-element.23), channel_id=1, source_target_pairs={{0,1},{1,2},{2,3},{3,4},{4,5},{5,6},{6,7},{8,9},{9,10},{10,11},{11... | collective-permute-start | bytes 884744 | tf_op jit(solution)/shard_map/ppermute | solution.py:24
  7.4 5.0 %shard_map.61 = (bf16[512,256]{1,0:T(8,128)(2,1)S(1)}, bf16[1024,256]{1,0:T(8,128)(2,1)S(1)}, bf16[256,512]{1,0:T(8,128)(2,1)S(1)}, f32[256,256]{1,0:T(8,128)S(1)}, f32[8,256]{1,0:T(8,128)S(1)}) custom-call(bf16[4096,512]{1,0:T(8,128)(2,1)} %bitcast.7, bf16[1024,512]{1,0:T(8,128)(2,1)S(1)} %get-tuple-element.22.near_ref, ...), custom_call_target="tpu_custom_call" | custom-call | tf_op jit(solution)/shard_map/pallas_call | solution.py:153
  12.4 1.3 %collective-permute-start.2 = (bf16[512,256]{1,0:T(8,128)(2,1)S(1)}, bf16[512,256]{1,0:T(8,128)(2,1)S(1)}, u32[]{:S(2)}, u32[]{:S(2)}) collective-permute-start(bf16[512,256]{1,0:T(8,128)(2,1)S(1)} %get-tuple-element.27.early_ref), channel_id=1, source_target_pairs={{1,0},{2,1},{3,2},{4,3},{5,4},{6,5},{7,6},{9,8},{10,9},{11,10},{12... | collective-permute-start | bytes 786440 | tf_op jit(solution)/shard_map/ppermute | solution.py:24
  13.7 0.0 collective-permute-done.halo_ref
  13.7 1.4 %shard_map.60.head_ref = bf16[512,256]{1,0:T(8,128)(2,1)S(1)} custom-call(bf16[1024,512]{1,0:T(8,128)(2,1)S(1)} %get-tuple-element.22.near_ref, bf16[288,512]{1,0:T(8,128)(2,1)S(1)} %collective-permute-done.halo_ref, bf16[1024,512]{1,0:T(8,128)(2,1)S(1)} %get-tuple-element.24.w1_ref, f32[1,512]{1,0:T(1,128)S(1)} %get-tuple-element.25.b1_ref, ...), custom_call_target="tpu_custom_call" | custom-call | tf_op jit(solution)/shard_map/pallas_call | solution.py:166
  15.1 1.3 %collective-permute-start.1 = (bf16[512,256]{1,0:T(8,128)(2,1)S(1)}, bf16[512,256]{1,0:T(8,128)(2,1)S(1)}, u32[]{:S(2)}, u32[]{:S(2)}) collective-permute-start(bf16[512,256]{1,0:T(8,128)(2,1)S(1)} %shard_map.60.head_ref), channel_id=1, source_target_pairs={{1,0},{2,1},{3,2},{4,3},{5,4},{6,5},{7,6},{9,8},{10,9},{11,10},{12... | collective-permute-start | bytes 786440 | tf_op jit(solution)/shard_map/ppermute | solution.py:24
  16.4 7.1 %shard_map.62 = (bf16[4096,256]{1,0:T(8,128)(2,1)S(1)}, f32[256,256]{1,0:T(8,128)S(1)}, f32[256,256]{1,0:T(8,128)S(1)}, f32[8,256]{1,0:T(8,128)S(1)}) custom-call(bf16[4096,512]{1,0:T(8,128)(2,1)} %bitcast.8, bf16[512,256]{1,0:T(8,128)(2,1)S(1)} %shard_map.60.head_ref, bf16[512,256]{1,0:T(8,128)(2,1)S(1)} %get-tuple-element.27.early_ref, ...), custom_call_target="tpu_custom_call" | custom-call | tf_op jit(solution)/shard_map/pallas_call | solution.py:237
  23.5 0.0 collective-permute-done.2.ahead_early_ref
  23.5 4.1 %collective-permute-done.1.ahead_head_ref = bf16[512,256]{1,0:T(8,128)(2,1)S(1)} collective-permute-done((bf16[512,256]{1,0:T(8,128)(2,1)S(1)}, bf16[512,256]{1,0:T(8,128)(2,1)S(1)}, u32[]{:S(2)}, u32[]{:S(2)}) %collective-permute-start.1) | collective-permute-done | bytes 262176 | tf_op jit(solution)/shard_map/ppermute | solution.py:24
  27.6 0.8 %shard_map.63 = (f32[16,1,2176]{2,1,0:T(1,128)S(1)}, f32[16,1,2176]{2,1,0:T(1,128)S(1)}) custom-call(bf16[4096,256]{1,0:T(8,128)(2,1)S(1)} %get-tuple-element.32.feature_ref, bf16[512,256]{1,0:T(8,128)(2,1)S(1)} %collective-permute-done.1.ahead_head_ref, bf16[512,256]{1,0:T(8,128)(2,1)S(1)} %collective-permute-done.2.ahead_early_ref, ...), custom_call_target="tpu_custom_call" | custom-call | tf_op jit(solution)/shard_map/pallas_call | solution.py:290
  28.4 0.1 collective-permute-start.3
  28.5 1.3 %collective-permute-done.3 = f32[16,1,2176]{2,1,0:T(1,128)S(1)} collective-permute-done((f32[16,1,2176]{2,1,0:T(1,128)S(1)}, f32[16,1,2176]{2,1,0:T(1,128)S(1)}, u32[]{:S(2)}, u32[]{:S(2)}) %collective-permute-start.3) | collective-permute-done | bytes 139296 | tf_op jit(solution)/shard_map/ppermute | solution.py:462
  29.9 0.1 add.3
  30.0 14.4 %all_to_all.10 = f32[16,1,2176]{2,1,0:T(1,128)S(1)} all-to-all(f32[16,1,2176]{2,1,0:T(1,128)S(1)} %add.3), channel_id=1, replica_groups=mesh['x'=2,'core'=2,'tm'=8] {'x','tm'}, dimensions={0} | all-to-all | bytes 278528 | tf_op jit(solution)/shard_map/all_to_all | solution.py:463
  44.4 0.1 reduce_sum.9
  44.5 0.1 broadcast_in_dim.12
  44.6 10.8 %all_to_all.11.mine_ref = f32[16,1,2176]{2,1,0:T(1,128)S(1)} all-to-all(f32[16,1,2176]{2,1,0:T(1,128)S(1)} %broadcast_in_dim.12), channel_id=1, replica_groups=mesh['x'=2,'core'=2,'tm'=8] {'x','tm'}, dimensions={0} | all-to-all | bytes 278528 | tf_op jit(solution)/shard_map/all_to_all | solution.py:464
  55.4 0.0 collective-permute-start.4
  55.4 1.4 %collective-permute-done.4.other_ref = f32[16,1,2176]{2,1,0:T(1,128)S(1)} collective-permute-done((f32[16,1,2176]{2,1,0:T(1,128)S(1)}, f32[16,1,2176]{2,1,0:T(1,128)S(1)}, u32[]{:S(2)}, u32[]{:S(2)}) %collective-permute-start.4) | collective-permute-done | bytes 139296 | tf_op jit(solution)/shard_map/ppermute | solution.py:465
  56.7 9.3 %shard_map.64 = (bf16[2,512,256]{2,1,0:T(8,128)(2,1)S(1)}, f32[2,8,256]{2,1,0:T(8,128)S(1)}) custom-call(f32[1]{0:T(128)} %constant.0.clone.1.scale_ref, f32[16,1,2176]{2,1,0:T(1,128)S(1)} %all_to_all.11.mine_ref, f32[16,1,2176]{2,1,0:T(1,128)S(1)} %collective-permute-done.4.other_ref), custom_call_target="tpu_custom_call" | custom-call | tf_op jit(solution)/shard_map/pallas_call | solution.py:396
  66.0 3.9 %shard_map.65 = (f32[4096,256]{1,0:T(8,128)}, f32[4096,256]{1,0:T(8,128)}) custom-call(bf16[4096,256]{1,0:T(8,128)(2,1)S(1)} %get-tuple-element.32.feature_ref, bf16[512,256]{1,0:T(8,128)(2,1)S(1)} %collective-permute-done.1.ahead_head_ref, bf16[512,256]{1,0:T(8,128)(2,1)S(1)} %collective-permute-done.2.ahead_early_ref, ...), custom_call_target="tpu_custom_call" | custom-call | tf_op jit(solution)/shard_map/pallas_call | solution.py:445
Async XLA Ops:
  2.5 11.2 %collective-permute-start = (bf16[288,512]{1,0:T(8,128)(2,1)S(1)}, bf16[288,512]{1,0:T(8,128)(2,1)S(1)}, u32[]{:S(2)}, u32[]{:S(2)}) collective-permute-start(bf16[288,512]{1,0:T(8,128)(2,1)S(1)} %get-tuple-element.23), channel_id=1, source_target_pairs={{0,1},{1,2},{2,3},{3,4},{4,5},{5,6},{6,7},{8,9},{9,10},{10,11},{11... | collective-permute-start | bytes 884744 | tf_op jit(solution)/shard_map/ppermute | solution.py:24
  12.4 11.2 %collective-permute-start.2 = (bf16[512,256]{1,0:T(8,128)(2,1)S(1)}, bf16[512,256]{1,0:T(8,128)(2,1)S(1)}, u32[]{:S(2)}, u32[]{:S(2)}) collective-permute-start(bf16[512,256]{1,0:T(8,128)(2,1)S(1)} %get-tuple-element.27.early_ref), channel_id=1, source_target_pairs={{1,0},{2,1},{3,2},{4,3},{5,4},{6,5},{7,6},{9,8},{10,9},{11,10},{12... | collective-permute-start | bytes 786440 | tf_op jit(solution)/shard_map/ppermute | solution.py:24
  15.1 12.5 %collective-permute-start.1 = (bf16[512,256]{1,0:T(8,128)(2,1)S(1)}, bf16[512,256]{1,0:T(8,128)(2,1)S(1)}, u32[]{:S(2)}, u32[]{:S(2)}) collective-permute-start(bf16[512,256]{1,0:T(8,128)(2,1)S(1)} %shard_map.60.head_ref), channel_id=1, source_target_pairs={{1,0},{2,1},{3,2},{4,3},{5,4},{6,5},{7,6},{9,8},{10,9},{11,10},{12... | collective-permute-start | bytes 786440 | tf_op jit(solution)/shard_map/ppermute | solution.py:24
  28.4 1.4 %collective-permute-start.3 = (f32[16,1,2176]{2,1,0:T(1,128)S(1)}, f32[16,1,2176]{2,1,0:T(1,128)S(1)}, u32[]{:S(2)}, u32[]{:S(2)}) collective-permute-start(f32[16,1,2176]{2,1,0:T(1,128)S(1)} %get-tuple-element.37), channel_id=1, source_target_pairs={{0,8},{8,0},{1,9},{9,1},{2,10},{10,2},{3,11},{11,3},{4,12},{12,4},... | collective-permute-start | bytes 417800 | tf_op jit(solution)/shard_map/ppermute | solution.py:462
  55.4 1.4 %collective-permute-start.4 = (f32[16,1,2176]{2,1,0:T(1,128)S(1)}, f32[16,1,2176]{2,1,0:T(1,128)S(1)}, u32[]{:S(2)}, u32[]{:S(2)}) collective-permute-start(f32[16,1,2176]{2,1,0:T(1,128)S(1)} %all_to_all.11.mine_ref), channel_id=1, source_target_pairs={{0,8},{8,0},{1,9},{9,1},{2,10},{10,2},{3,11},{11,3},{4,12},{12,4},... | collective-permute-start | bytes 417800 | tf_op jit(solution)/shard_map/ppermute | solution.py:465

commit v8 on v7

--- a/solution.py
+++ b/solution.py
@@ -30,6 +30,15 @@
 
 def gram(a, b):
     return lax.dot_general(a, b, (((0,), (0,)), ((), ())), preferred_element_type=F32)
+
+
+def feature_gram(a, b):
+    size = a.shape[1]
+    row = lax.broadcasted_iota(jnp.int32, (size, size), 0)
+    column = lax.broadcasted_iota(jnp.int32, (size, size), 1)
+    identity = jnp.where(row == column, 1.0, 0.0).astype(BF16)
+    turned = across(identity, a).astype(BF16)
+    return jnp.dot(turned, b, preferred_element_type=F32)
 
 
 def in_hbm(value):
@@ -56,10 +65,8 @@
     return jnp.dot(both, w2_ref[...], preferred_element_type=F32).astype(BF16)
 
 
-def fetch_kernel(frames_ref, w1_in, b1_in, w2_in, last_ref, near_ref, w1_ref, b1_ref, w2_ref, sems):
-    rows = frames_ref.shape[0]
+def fetch_kernel(frames_ref, w1_in, b1_in, w2_in, near_ref, w1_ref, b1_ref, w2_ref, sems):
     pairs = (
-        (frames_ref.at[pl.ds(rows - D1 - D2, D1 + D2)], last_ref),
         (frames_ref.at[pl.ds(0, LAG)], near_ref),
         (w1_in, w1_ref),
         (b1_in, b1_ref),
@@ -76,13 +83,13 @@
     vmem = pl.BlockSpec(memory_space=pltpu.VMEM)
     hbm = pl.BlockSpec(memory_space=pltpu.HBM)
     channels = frames.shape[1]
-    shapes = (((D1 + D2, channels), BF16), ((LAG, channels), BF16), (w1.shape, BF16), (b1.shape, F32), (w2.shape, BF16))
+    shapes = (((LAG, channels), BF16), (w1.shape, BF16), (b1.shape, F32), (w2.shape, BF16))
     return pl.pallas_call(
         fetch_kernel,
         in_specs=[hbm] * 4,
-        out_specs=(vmem,) * 5,
+        out_specs=(vmem,) * 4,
         out_shape=tuple(jax.ShapeDtypeStruct(*shape) for shape in shapes),
-        scratch_shapes=[pltpu.SemaphoreType.DMA((5,))],
+        scratch_shapes=[pltpu.SemaphoreType.DMA((4,))],
         compiler_params=pltpu.CompilerParams(vmem_limit_bytes=8 * MIB),
     )(*(in_hbm(value) for value in (frames, w1, b1, w2)))
 
@@ -114,7 +121,7 @@
     hs[: D2 + half, :] = hidden_rows(xs, 0, D2 + half, w1_ref, b1_ref)
     value = feature_rows(hs, 0, half, w2_ref)
     early_ref[...] = value
-    inst[...] = first_weight() * gram(value, value)
+    inst[...] = first_weight() * feature_gram(value, value)
     total[...] = first_weight() * column_sum(value)
     for step in range(steps):
         arriving(step).wait()
@@ -122,7 +129,7 @@
         hs[at + D2 : at + D2 + CHUNK, :] = hidden_rows(xs, at + D2, CHUNK, w1_ref, b1_ref)
         value = feature_rows(hs, at, CHUNK, w2_ref)
         middle_ref[step * CHUNK : (step + 1) * CHUNK, :] = value
-        inst[...] += 2.0 * gram(value, value)
+        inst[...] += 2.0 * feature_gram(value, value)
         total[...] += 2.0 * column_sum(value)
     hidden_ref[...] = hs[hs.shape[0] - D2 :, :]
 
@@ -200,11 +207,11 @@
     out_ref[half:LAG, :] = early_ref[...]
     out_ref[LAG:done, :] = middle_ref[...]
     start = out_ref[:half, :]
-    inst[...] = inst_in[...] + first_weight() * gram(start, start)
+    inst[...] = inst_in[...] + first_weight() * feature_gram(start, start)
     total[...] = total_in[...] + first_weight() * column_sum(start)
-    lag[...] = gram(out_ref[LAG : LAG + CHUNK, :], out_ref[:CHUNK, :])
+    lag[...] = feature_gram(out_ref[LAG : LAG + CHUNK, :], out_ref[:CHUNK, :])
     for at in range(CHUNK, LAG, CHUNK):
-        lag[...] += gram(out_ref[LAG + at : LAG + at + CHUNK, :], out_ref[at : at + CHUNK, :])
+        lag[...] += feature_gram(out_ref[LAG + at : LAG + at + CHUNK, :], out_ref[at : at + CHUNK, :])
 
     def hidden(step):
         arriving(step).wait()
@@ -216,7 +223,7 @@
         at = done + step * CHUNK
         out_ref[at : at + CHUNK, :] = value
         weight = last_weight() if at >= rows - LAG else 2.0
-        both = gram(value, jnp.concatenate([value, out_ref[at - LAG : at - LAG + CHUNK, :]], 1))
+        both = feature_gram(value, jnp.concatenate([value, out_ref[at - LAG : at - LAG + CHUNK, :]], 1))
         inst[...] += weight * both[:, :feat]
         lag[...] += both[:, feat:]
         total[...] += weight * column_sum(value)
@@ -257,8 +264,8 @@
     feat = inst.shape[0]
     half = LAG // 2
     edge = feature_ref.shape[0] - LAG
-    cross = lag[...] + gram(ahead_head_ref[...], feature_ref[edge : edge + half, :])
-    cross += gram(ahead_early_ref[...], feature_ref[edge + half :, :])
+    cross = lag[...] + feature_gram(ahead_head_ref[...], feature_ref[edge : edge + half, :])
+    cross += feature_gram(ahead_early_ref[...], feature_ref[edge + half :, :])
     both = cross + cross.T
     row = lax.broadcasted_iota(jnp.int32, (feat, feat), 0)
     column = lax.broadcasted_iota(jnp.int32, (feat, feat), 1)
@@ -474,8 +481,8 @@
         first_bias.reshape(1, hid),
         second_weight.reshape(2 * hid, feat),
     )
-    last, near, *weights = fetch(frame_block, *weights)
-    halo = passed_along(last, "tm", 1)
+    halo = passed_along(frame_block[row_count - D1 - D2 :], "tm", 1)
+    near, *weights = fetch(frame_block, *weights)
     early, middle, hidden, inst, total = early_rows(frame_block, near, *weights)
     ahead_early = passed_along(early, "tm", -1)
     head = head_rows(near, halo, *weights)

time: 70.4 us -> 71.7 us (1.018)
  Pallas kernels: 29.3 us -> 30.4 us
  local copies, waits for them, and re-layouts: 0.07 us -> 1.06 us
    slice x0 -> x1, local copies, waits for them, and re-layouts: none -> 0.98 us  [on_device(): halo = passed_along(frame_block[row_count - D1 - D2:], 'tm', 1)]
  transfers between devices with their start and end apart: 5 -> 5, of which waited for: 3 -> 3; matrix products, arithmetic and copies ran while one was open for 0% -> 0% of each run, Pallas kernels for 19% -> 23%
where the time goes in v8:
time: 71.7 us; the launch traced here: 71.4 us
  Pallas kernels  30.4 us (42%)
  blocking collectives  25.2 us (35%)
  starting transfers between devices  7.55 us (11%)
  waiting for transfers between devices  6.11 us (9%)
  local copies, waits for them, and re-layouts  1.06 us (1%)
  between operations  0.9 us (1%)
    all_to_all x1, blocking collectives, summed(): lax.all_to_all(parts, chips, 0, 0, tiled=True)  14.4 us
    all_to_all x1, blocking collectives, summed(): lax.all_to_all(jnp.broadcast_to(mine, parts.shape), chips, 0, 0, tiled=True)  10.8 us
    pallas_call x1, Pallas kernels, koopman_parts(): pl.pallas_call(koopman_kernel, in_specs=[pl.BlockSpec(memory_space=pltpu....  9.32 us
    pallas_call x1, Pallas kernels, body(): pl.pallas_call(body_kernel, in_specs=[pl.BlockSpec(memory_space=pltpu.HBM...  7.81 us
    ppermute x3, starting transfers between devices, passed_along(): lax.ppermute(value, axis, [(source, source + steps) for source in range(f...  7.47 us
    pallas_call x1, Pallas kernels, early_rows(): pl.pallas_call(early_kernel, in_specs=[hbm] + [vmem] * 4, out_specs=(vmem...  5.2 us
    pallas_call x1, Pallas kernels, project(): pl.pallas_call(project_kernel, in_specs=[vmem] * 5, out_specs=(hbm, hbm),...  3.87 us
    ppermute x3, waiting for transfers between devices, passed_along(): lax.ppermute(value, axis, [(source, source + steps) for source in range(f...  3.41 us
  transfers between devices with their start and end apart: 5, of which 3 were waited for; matrix products, arithmetic and copies ran while one was open for 0% of the time, Pallas kernels for 23%

profile of v8, /device:TPU:0, one launch (start us, length us, event | category | flops | bytes accessed | tf_op | source)
XLA Modules:
  0.0 71.4 jit_solution(14039626874342967887)
XLA Ops:
  0.6 1.0 %slice_bitcast_fusion = bf16[288,512]{1,0:T(8,128)(2,1)S(1)} fusion(bf16[1,4096,512]{2,1,0:T(8,128)(2,1)} %param.4), kind=kLoop, calls=%fused_computation | loop fusion | bytes 589824 | tf_op jit(solution)/shard_map/slice | solution.py:484
  1.6 4.9 %collective-permute-start = (bf16[288,512]{1,0:T(8,128)(2,1)S(1)}, bf16[288,512]{1,0:T(8,128)(2,1)S(1)}, u32[]{:S(2)}, u32[]{:S(2)}) collective-permute-start(bf16[288,512]{1,0:T(8,128)(2,1)S(1)} %slice_bitcast_fusion), channel_id=1, source_target_pairs={{0,1},{1,2},{2,3},{3,4},{4,5},{5,6},{6,7},{8,9},{9,10},{10,11},{11... | collective-permute-start | bytes 884744 | tf_op jit(solution)/shard_map/ppermute | solution.py:24
  6.5 1.7 %shard_map.59 = (bf16[1024,512]{1,0:T(8,128)(2,1)S(1)}, bf16[1024,512]{1,0:T(8,128)(2,1)S(1)}, f32[1,512]{1,0:T(1,128)S(1)}, bf16[1024,256]{1,0:T(8,128)(2,1)S(1)}) custom-call(bf16[4096,512]{1,0:T(8,128)(2,1)} %bitcast.8, bf16[1024,512]{1,0:T(8,128)(2,1)} %bitcast.11, f32[1,512]{1,0:T(1,128)} %bitcast.13, bf16[1024,256]{1,0:T(8,128)(2,1)} %bitcast.12), custom_call_target="tpu_custom_call" | custom-call | tf_op jit(solution)/shard_map/pallas_call | solution.py:87
  8.2 5.2 %shard_map.61 = (bf16[512,256]{1,0:T(8,128)(2,1)S(1)}, bf16[1024,256]{1,0:T(8,128)(2,1)S(1)}, bf16[256,512]{1,0:T(8,128)(2,1)S(1)}, f32[256,256]{1,0:T(8,128)S(1)}, f32[8,256]{1,0:T(8,128)S(1)}) custom-call(bf16[4096,512]{1,0:T(8,128)(2,1)} %bitcast.9, bf16[1024,512]{1,0:T(8,128)(2,1)S(1)} %get-tuple-element.21.near_ref, ...), custom_call_target="tpu_custom_call" | custom-call | tf_op jit(solution)/shard_map/pallas_call | solution.py:160
  13.5 1.3 %collective-permute-start.2 = (bf16[512,256]{1,0:T(8,128)(2,1)S(1)}, bf16[512,256]{1,0:T(8,128)(2,1)S(1)}, u32[]{:S(2)}, u32[]{:S(2)}) collective-permute-start(bf16[512,256]{1,0:T(8,128)(2,1)S(1)} %get-tuple-element.25.early_ref), channel_id=1, source_target_pairs={{1,0},{2,1},{3,2},{4,3},{5,4},{6,5},{7,6},{9,8},{10,9},{11,10},{12... | collective-permute-start | bytes 786440 | tf_op jit(solution)/shard_map/ppermute | solution.py:24
  14.8 0.0 collective-permute-done.halo_ref
  14.8 1.4 %shard_map.60.head_ref = bf16[512,256]{1,0:T(8,128)(2,1)S(1)} custom-call(bf16[1024,512]{1,0:T(8,128)(2,1)S(1)} %get-tuple-element.21.near_ref, bf16[288,512]{1,0:T(8,128)(2,1)S(1)} %collective-permute-done.halo_ref, bf16[1024,512]{1,0:T(8,128)(2,1)S(1)} %get-tuple-element.22.w1_ref, f32[1,512]{1,0:T(1,128)S(1)} %get-tuple-element.23.b1_ref, ...), custom_call_target="tpu_custom_call" | custom-call | tf_op jit(solution)/shard_map/pallas_call | solution.py:173
  16.2 1.3 %collective-permute-start.1 = (bf16[512,256]{1,0:T(8,128)(2,1)S(1)}, bf16[512,256]{1,0:T(8,128)(2,1)S(1)}, u32[]{:S(2)}, u32[]{:S(2)}) collective-permute-start(bf16[512,256]{1,0:T(8,128)(2,1)S(1)} %shard_map.60.head_ref), channel_id=1, source_target_pairs={{1,0},{2,1},{3,2},{4,3},{5,4},{6,5},{7,6},{9,8},{10,9},{11,10},{12... | collective-permute-start | bytes 786440 | tf_op jit(solution)/shard_map/ppermute | solution.py:24
  17.5 7.8 %shard_map.62 = (bf16[4096,256]{1,0:T(8,128)(2,1)S(1)}, f32[256,256]{1,0:T(8,128)S(1)}, f32[256,256]{1,0:T(8,128)S(1)}, f32[8,256]{1,0:T(8,128)S(1)}) custom-call(bf16[4096,512]{1,0:T(8,128)(2,1)} %bitcast.10, bf16[512,256]{1,0:T(8,128)(2,1)S(1)} %shard_map.60.head_ref, bf16[512,256]{1,0:T(8,128)(2,1)S(1)} %get-tuple-element.25.early_ref, ...), custom_call_target="tpu_custom_call" | custom-call | tf_op jit(solution)/shard_map/pallas_call | solution.py:244
  25.3 0.0 collective-permute-done.2.ahead_early_ref
  25.3 3.4 %collective-permute-done.1.ahead_head_ref = bf16[512,256]{1,0:T(8,128)(2,1)S(1)} collective-permute-done((bf16[512,256]{1,0:T(8,128)(2,1)S(1)}, bf16[512,256]{1,0:T(8,128)(2,1)S(1)}, u32[]{:S(2)}, u32[]{:S(2)}) %collective-permute-start.1) | collective-permute-done | bytes 262176 | tf_op jit(solution)/shard_map/ppermute | solution.py:24
  28.7 1.0 %shard_map.63 = (f32[16,1,2176]{2,1,0:T(1,128)S(1)}, f32[16,1,2176]{2,1,0:T(1,128)S(1)}) custom-call(bf16[4096,256]{1,0:T(8,128)(2,1)S(1)} %get-tuple-element.30.feature_ref, bf16[512,256]{1,0:T(8,128)(2,1)S(1)} %collective-permute-done.1.ahead_head_ref, bf16[512,256]{1,0:T(8,128)(2,1)S(1)} %collective-permute-done.2.ahead_early_ref, ...), custom_call_target="tpu_custom_call" | custom-call | tf_op jit(solution)/shard_map/pallas_call | solution.py:297
  29.7 0.1 collective-permute-start.3
  29.8 1.3 %collective-permute-done.3 = f32[16,1,2176]{2,1,0:T(1,128)S(1)} collective-permute-done((f32[16,1,2176]{2,1,0:T(1,128)S(1)}, f32[16,1,2176]{2,1,0:T(1,128)S(1)}, u32[]{:S(2)}, u32[]{:S(2)}) %collective-permute-start.3) | collective-permute-done | bytes 139296 | tf_op jit(solution)/shard_map/ppermute | solution.py:469
  31.2 0.1 add.3
  31.3 14.4 %all_to_all.10 = f32[16,1,2176]{2,1,0:T(1,128)S(1)} all-to-all(f32[16,1,2176]{2,1,0:T(1,128)S(1)} %add.3), channel_id=1, replica_groups=mesh['x'=2,'core'=2,'tm'=8] {'x','tm'}, dimensions={0} | all-to-all | bytes 278528 | tf_op jit(solution)/shard_map/all_to_all | solution.py:470
  45.7 0.1 reduce_sum.9
  45.8 0.1 broadcast_in_dim.12
  45.9 10.8 %all_to_all.11.mine_ref = f32[16,1,2176]{2,1,0:T(1,128)S(1)} all-to-all(f32[16,1,2176]{2,1,0:T(1,128)S(1)} %broadcast_in_dim.12), channel_id=1, replica_groups=mesh['x'=2,'core'=2,'tm'=8] {'x','tm'}, dimensions={0} | all-to-all | bytes 278528 | tf_op jit(solution)/shard_map/all_to_all | solution.py:471
  56.7 0.0 collective-permute-start.4
  56.7 1.4 %collective-permute-done.4.other_ref = f32[16,1,2176]{2,1,0:T(1,128)S(1)} collective-permute-done((f32[16,1,2176]{2,1,0:T(1,128)S(1)}, f32[16,1,2176]{2,1,0:T(1,128)S(1)}, u32[]{:S(2)}, u32[]{:S(2)}) %collective-permute-start.4) | collective-permute-done | bytes 139296 | tf_op jit(solution)/shard_map/ppermute | solution.py:472
  58.0 9.3 %shard_map.64 = (bf16[2,512,256]{2,1,0:T(8,128)(2,1)S(1)}, f32[2,8,256]{2,1,0:T(8,128)S(1)}) custom-call(f32[1]{0:T(128)} %constant.0.clone.1.scale_ref, f32[16,1,2176]{2,1,0:T(1,128)S(1)} %all_to_all.11.mine_ref, f32[16,1,2176]{2,1,0:T(1,128)S(1)} %collective-permute-done.4.other_ref), custom_call_target="tpu_custom_call" | custom-call | tf_op jit(solution)/shard_map/pallas_call | solution.py:403
  67.3 3.9 %shard_map.65 = (f32[4096,256]{1,0:T(8,128)}, f32[4096,256]{1,0:T(8,128)}) custom-call(bf16[4096,256]{1,0:T(8,128)(2,1)S(1)} %get-tuple-element.30.feature_ref, bf16[512,256]{1,0:T(8,128)(2,1)S(1)} %collective-permute-done.1.ahead_head_ref, bf16[512,256]{1,0:T(8,128)(2,1)S(1)} %collective-permute-done.2.ahead_early_ref, ...), custom_call_target="tpu_custom_call" | custom-call | tf_op jit(solution)/shard_map/pallas_call | solution.py:452
Async XLA Ops:
  1.6 13.1 %collective-permute-start = (bf16[288,512]{1,0:T(8,128)(2,1)S(1)}, bf16[288,512]{1,0:T(8,128)(2,1)S(1)}, u32[]{:S(2)}, u32[]{:S(2)}) collective-permute-start(bf16[288,512]{1,0:T(8,128)(2,1)S(1)} %slice_bitcast_fusion), channel_id=1, source_target_pairs={{0,1},{1,2},{2,3},{3,4},{4,5},{5,6},{6,7},{8,9},{9,10},{10,11},{11... | collective-permute-start | bytes 884744 | tf_op jit(solution)/shard_map/ppermute | solution.py:24
  13.5 11.9 %collective-permute-start.2 = (bf16[512,256]{1,0:T(8,128)(2,1)S(1)}, bf16[512,256]{1,0:T(8,128)(2,1)S(1)}, u32[]{:S(2)}, u32[]{:S(2)}) collective-permute-start(bf16[512,256]{1,0:T(8,128)(2,1)S(1)} %get-tuple-element.25.early_ref), channel_id=1, source_target_pairs={{1,0},{2,1},{3,2},{4,3},{5,4},{6,5},{7,6},{9,8},{10,9},{11,10},{12... | collective-permute-start | bytes 786440 | tf_op jit(solution)/shard_map/ppermute | solution.py:24
  16.2 12.5 %collective-permute-start.1 = (bf16[512,256]{1,0:T(8,128)(2,1)S(1)}, bf16[512,256]{1,0:T(8,128)(2,1)S(1)}, u32[]{:S(2)}, u32[]{:S(2)}) collective-permute-start(bf16[512,256]{1,0:T(8,128)(2,1)S(1)} %shard_map.60.head_ref), channel_id=1, source_target_pairs={{1,0},{2,1},{3,2},{4,3},{5,4},{6,5},{7,6},{9,8},{10,9},{11,10},{12... | collective-permute-start | bytes 786440 | tf_op jit(solution)/shard_map/ppermute | solution.py:24
  29.7 1.4 %collective-permute-start.3 = (f32[16,1,2176]{2,1,0:T(1,128)S(1)}, f32[16,1,2176]{2,1,0:T(1,128)S(1)}, u32[]{:S(2)}, u32[]{:S(2)}) collective-permute-start(f32[16,1,2176]{2,1,0:T(1,128)S(1)} %get-tuple-element.35), channel_id=1, source_target_pairs={{0,8},{8,0},{1,9},{9,1},{2,10},{10,2},{3,11},{11,3},{4,12},{12,4},... | collective-permute-start | bytes 417800 | tf_op jit(solution)/shard_map/ppermute | solution.py:469
  56.7 1.4 %collective-permute-start.4 = (f32[16,1,2176]{2,1,0:T(1,128)S(1)}, f32[16,1,2176]{2,1,0:T(1,128)S(1)}, u32[]{:S(2)}, u32[]{:S(2)}) collective-permute-start(f32[16,1,2176]{2,1,0:T(1,128)S(1)} %all_to_all.11.mine_ref), channel_id=1, source_target_pairs={{0,8},{8,0},{1,9},{9,1},{2,10},{10,2},{3,11},{11,3},{4,12},{12,4},... | collective-permute-start | bytes 417800 | tf_op jit(solution)/shard_map/ppermute | solution.py:472

commit v9 on v8

--- a/solution.py
+++ b/solution.py
@@ -15,7 +15,6 @@
 
 F32 = jnp.float32
 BF16 = jnp.bfloat16
-HIGHEST = lax.Precision.HIGHEST
 
 
 def passed_along(value, axis, steps):
@@ -24,21 +23,8 @@
     return lax.ppermute(value, axis, [(source, source + steps) for source in range(first, last)])
 
 
-def across(a, b, precision=None):
-    return lax.dot_general(a, b, (((1,), (1,)), ((), ())), precision=precision, preferred_element_type=F32)
-
-
 def gram(a, b):
     return lax.dot_general(a, b, (((0,), (0,)), ((), ())), preferred_element_type=F32)
-
-
-def feature_gram(a, b):
-    size = a.shape[1]
-    row = lax.broadcasted_iota(jnp.int32, (size, size), 0)
-    column = lax.broadcasted_iota(jnp.int32, (size, size), 1)
-    identity = jnp.where(row == column, 1.0, 0.0).astype(BF16)
-    turned = across(identity, a).astype(BF16)
-    return jnp.dot(turned, b, preferred_element_type=F32)
 
 
 def in_hbm(value):
@@ -94,17 +80,7 @@
     )(*(in_hbm(value) for value in (frames, w1, b1, w2)))
 
 
-def first_weight():
-    return jnp.where(lax.axis_index("tm") == 0, 1.0, 2.0)
-
-
-def last_weight():
-    return jnp.where(lax.axis_index("tm") == lax.axis_size("tm") - 1, 1.0, 2.0)
-
-
-def early_kernel(
-    frames_ref, near_ref, w1_ref, b1_ref, w2_ref, early_ref, middle_ref, hidden_ref, inst, total, xs, hs, sems
-):
+def early_kernel(frames_ref, near_ref, w1_ref, b1_ref, w2_ref, early_ref, middle_ref, hidden_ref, xs, hs, sems):
     half = LAG // 2
     first = half - D1 - D2
 
@@ -119,18 +95,15 @@
         arriving(step).start()
     xs[: LAG - first, :] = near_ref[first:, :]
     hs[: D2 + half, :] = hidden_rows(xs, 0, D2 + half, w1_ref, b1_ref)
-    value = feature_rows(hs, 0, half, w2_ref)
-    early_ref[...] = value
-    inst[...] = first_weight() * feature_gram(value, value)
-    total[...] = first_weight() * column_sum(value)
     for step in range(steps):
         arriving(step).wait()
         at = half + step * CHUNK
         hs[at + D2 : at + D2 + CHUNK, :] = hidden_rows(xs, at + D2, CHUNK, w1_ref, b1_ref)
-        value = feature_rows(hs, at, CHUNK, w2_ref)
-        middle_ref[step * CHUNK : (step + 1) * CHUNK, :] = value
-        inst[...] += 2.0 * feature_gram(value, value)
-        total[...] += 2.0 * column_sum(value)
+        if step == 0:
+            early_ref[...] = feature_rows(hs, 0, half, w2_ref)
+        else:
+            middle_ref[(step - 1) * CHUNK : step * CHUNK, :] = feature_rows(hs, at - CHUNK, CHUNK, w2_ref)
+    middle_ref[LAG - CHUNK :, :] = feature_rows(hs, half + LAG - CHUNK, CHUNK, w2_ref)
     hidden_ref[...] = hs[hs.shape[0] - D2 :, :]
 
 
@@ -156,11 +129,11 @@
     vmem = pl.BlockSpec(memory_space=pltpu.VMEM)
     hbm = pl.BlockSpec(memory_space=pltpu.HBM)
     half, hid, feat = LAG // 2, w1.shape[1], w2.shape[1]
-    shapes = (((half, feat), BF16), ((LAG, feat), BF16), ((D2, hid), BF16), ((feat, feat), F32), ((8, feat), F32))
+    shapes = (((half, feat), BF16), ((LAG, feat), BF16), ((D2, hid), BF16))
     return pl.pallas_call(
         early_kernel,
         in_specs=[hbm] + [vmem] * 4,
-        out_specs=(vmem,) * 5,
+        out_specs=(vmem,) * 3,
         out_shape=tuple(jax.ShapeDtypeStruct(*shape) for shape in shapes),
         scratch_shapes=feature_scratch(half + LAG, near.shape[1], hid) + [pltpu.SemaphoreType.DMA((LAG // CHUNK,))],
         compiler_params=pltpu.CompilerParams(vmem_limit_bytes=16 * MIB),
@@ -180,15 +153,10 @@
     )(near, halo, w1, b1, w2)
 
 
-def column_sum(rows):
-    return jnp.sum(rows.astype(F32).reshape(-1, 8, rows.shape[1]), 0)
-
-
 def body_kernel(
-    frames_ref, head_ref, early_ref, middle_ref, hidden_ref, inst_in, total_in, w1_ref, b1_ref, w2_ref,
-    out_ref, inst, lag, total, xs, hs, sems
+    frames_ref, head_ref, early_ref, middle_ref, hidden_ref, w1_ref, b1_ref, w2_ref, out_ref, xs, hs, sems
 ):
-    rows, feat = out_ref.shape
+    rows = out_ref.shape[0]
     done = 2 * LAG
     steps = (rows - done) // CHUNK
 
@@ -206,66 +174,78 @@
     out_ref[:half, :] = head_ref[...]
     out_ref[half:LAG, :] = early_ref[...]
     out_ref[LAG:done, :] = middle_ref[...]
-    start = out_ref[:half, :]
-    inst[...] = inst_in[...] + first_weight() * feature_gram(start, start)
-    total[...] = total_in[...] + first_weight() * column_sum(start)
-    lag[...] = feature_gram(out_ref[LAG : LAG + CHUNK, :], out_ref[:CHUNK, :])
-    for at in range(CHUNK, LAG, CHUNK):
-        lag[...] += feature_gram(out_ref[LAG + at : LAG + at + CHUNK, :], out_ref[at : at + CHUNK, :])
-
-    def hidden(step):
-        arriving(step).wait()
+    for step in range(steps + 1):
         at = step * CHUNK
-        hs[D2 + at : D2 + at + CHUNK, :] = hidden_rows(xs, at, CHUNK, w1_ref, b1_ref)
-
-    def finish(step):
-        value = feature_rows(hs, step * CHUNK, CHUNK, w2_ref)
-        at = done + step * CHUNK
-        out_ref[at : at + CHUNK, :] = value
-        weight = last_weight() if at >= rows - LAG else 2.0
-        both = feature_gram(value, jnp.concatenate([value, out_ref[at - LAG : at - LAG + CHUNK, :]], 1))
-        inst[...] += weight * both[:, :feat]
-        lag[...] += both[:, feat:]
-        total[...] += weight * column_sum(value)
-
-    hidden(0)
-    for step in range(steps - 1):
-        hidden(step + 1)
-        finish(step)
-    finish(steps - 1)
-
-
-def body(frames, head, early, middle, hidden, inst, total, w1, b1, w2):
+        if step < steps:
+            arriving(step).wait()
+            hs[D2 + at : D2 + at + CHUNK, :] = hidden_rows(xs, at, CHUNK, w1_ref, b1_ref)
+        if step:
+            out_ref[done + at - CHUNK : done + at, :] = feature_rows(hs, at - CHUNK, CHUNK, w2_ref)
+
+
+def body(frames, head, early, middle, hidden, w1, b1, w2):
     rows, channels = frames.shape
     hid, feat = w1.shape[1], w2.shape[1]
     vmem = pl.BlockSpec(memory_space=pltpu.VMEM)
-    square = jax.ShapeDtypeStruct((feat, feat), F32)
     left = rows - 2 * LAG
     return pl.pallas_call(
         body_kernel,
-        in_specs=[pl.BlockSpec(memory_space=pltpu.HBM)] + [vmem] * 9,
-        out_specs=(vmem,) * 4,
-        out_shape=(
-            jax.ShapeDtypeStruct((rows, feat), BF16),
-            square,
-            square,
-            jax.ShapeDtypeStruct((8, feat), F32),
-        ),
+        in_specs=[pl.BlockSpec(memory_space=pltpu.HBM)] + [vmem] * 7,
+        out_specs=vmem,
+        out_shape=jax.ShapeDtypeStruct((rows, feat), BF16),
         scratch_shapes=[
             pltpu.VMEM((left + D1, channels), BF16),
             pltpu.VMEM((left + D2, hid), BF16),
             pltpu.SemaphoreType.DMA((left // CHUNK,)),
         ],
-        compiler_params=pltpu.CompilerParams(vmem_limit_bytes=24 * MIB),
-    )(in_hbm(frames), head, early, middle, hidden, inst, total, w1, b1, w2)
+        compiler_params=pltpu.CompilerParams(vmem_limit_bytes=16 * MIB),
+    )(in_hbm(frames), head, early, middle, hidden, w1, b1, w2)
+
+
+def column_sum(rows):
+    parts = rows.astype(F32).reshape(4, -1, 8, rows.shape[1])
+    return jnp.sum(jnp.sum(parts, 1), 0)
+
+
+def moment_kernel(feature_ref, inst, lag, total):
+    rows, feat = feature_ref.shape
+    tm_index, tm_last = lax.axis_index("tm"), lax.axis_size("tm") - 1
+    for at in range(0, rows, LAG):
+        weight = 2.0
+        if at == 0:
+            weight = jnp.where(tm_index == 0, 1.0, 2.0)
+        elif at == rows - LAG:
+            weight = jnp.where(tm_index == tm_last, 1.0, 2.0)
+        now = feature_ref[at : at + LAG, :]
+        if at == 0:
+            inst[...] = weight * gram(now, now)
+            total[...] = weight * column_sum(now)
+            continue
+        both = gram(now, jnp.concatenate([now, feature_ref[at - LAG : at, :]], 1))
+        inst[...] += weight * both[:, :feat]
+        lag[...] = both[:, feat:] if at == LAG else lag[...] + both[:, feat:]
+        total[...] += weight * column_sum(now)
+
+
+def moments(feature):
+    feat = feature.shape[1]
+    vmem = pl.BlockSpec(memory_space=pltpu.VMEM)
+    square = jax.ShapeDtypeStruct((feat, feat), F32)
+    return pl.pallas_call(
+        moment_kernel,
+        in_specs=[vmem],
+        out_specs=(vmem,) * 3,
+        out_shape=(square, square, jax.ShapeDtypeStruct((8, feat), F32)),
+        compiler_params=pltpu.CompilerParams(vmem_limit_bytes=12 * MIB),
+    )(feature)
 
 
 def pack_kernel(feature_ref, ahead_head_ref, ahead_early_ref, inst, lag, total, kept_ref, sent_ref, packed):
     feat = inst.shape[0]
     half = LAG // 2
     edge = feature_ref.shape[0] - LAG
-    cross = lag[...] + feature_gram(ahead_head_ref[...], feature_ref[edge : edge + half, :])
-    cross += feature_gram(ahead_early_ref[...], feature_ref[edge + half :, :])
+    cross = lag[...] + gram(ahead_head_ref[...], feature_ref[edge : edge + half, :])
+    cross += gram(ahead_early_ref[...], feature_ref[edge + half :, :])
     both = cross + cross.T
     row = lax.broadcasted_iota(jnp.int32, (feat, feat), 0)
     column = lax.broadcasted_iota(jnp.int32, (feat, feat), 1)
@@ -310,6 +290,14 @@
     middle = rest.astype(BF16)
     low = (rest - middle.astype(F32)).astype(BF16)
     return high, middle, low
+
+
+def product(a, b):
+    high, middle, low = three_parts(a)
+    left = jnp.concatenate([high, high, middle, high, low, middle], 1)
+    high, middle, low = three_parts(b)
+    right = jnp.concatenate([high, middle, high, low, high, middle], 0)
+    return jnp.dot(left, right, preferred_element_type=F32)
 
 
 def inverse_factor(work):
@@ -378,24 +366,23 @@
     row = lax.broadcasted_iota(jnp.int32, (feat, feat), 0)
     column = lax.broadcasted_iota(jnp.int32, (feat, feat), 1)
     turned = packed.T
-    centre = jnp.broadcast_to(mean, (feat, feat))
-    centre = centre * centre.T
+    mean_column = jnp.broadcast_to(mean, (feat, feat)).T
+    centre = mean_column * mean
     inst = jnp.where(column >= row, packed, turned)
     lag = jnp.where(column < row, packed, turned)
     lag = jnp.where(column == row, jnp.broadcast_to(diagonal, (feat, feat)), lag)
     work[...] = inst * scale - centre + jnp.where(column == row, RIDGE, 0.0)
     lag = lag * scale - centre
     inverse = inverse_factor(work)
-    half_step = jnp.dot(inverse, lag, precision=HIGHEST, preferred_element_type=F32)
-    koopman = across(half_step, inverse, HIGHEST)
-    moved = jnp.dot(koopman, inverse, precision=HIGHEST, preferred_element_type=F32)
-    for index, matrix in enumerate((inverse, moved)):
-        turned = matrix.T
-        high = turned.astype(BF16)
+    inverse_turned = inverse.T
+    koopman = product(product(inverse, lag), inverse_turned)
+    moved_turned = product(inverse_turned, koopman)
+    for index, matrix in enumerate((inverse_turned, moved_turned)):
+        high = matrix.astype(BF16)
         split_ref[index, :feat, :] = high
-        split_ref[index, feat:, :] = (turned - high.astype(F32)).astype(BF16)
-        rows = jnp.broadcast_to(mean, (8, feat))
-        shift_ref[index] = jnp.dot(rows, turned, precision=HIGHEST, preferred_element_type=F32)
+        split_ref[index, feat:, :] = (matrix - high.astype(F32)).astype(BF16)
+        shift = jnp.sum(mean_column * matrix, 0, keepdims=True)
+        shift_ref[index] = jnp.broadcast_to(shift, (8, feat))
 
 
 def koopman_parts(scale, mine, other, feat):
@@ -483,13 +470,12 @@
     )
     halo = passed_along(frame_block[row_count - D1 - D2 :], "tm", 1)
     near, *weights = fetch(frame_block, *weights)
-    early, middle, hidden, inst, total = early_rows(frame_block, near, *weights)
+    early, middle, hidden = early_rows(frame_block, near, *weights)
     ahead_early = passed_along(early, "tm", -1)
     head = head_rows(near, halo, *weights)
     ahead_head = passed_along(head, "tm", -1)
-    feature, inst, lag, total = body(
-        frame_block, head, early, middle, hidden, inst, total, *weights
-    )
+    feature = body(frame_block, head, early, middle, hidden, *weights)
+    inst, lag, total = moments(feature)
     chips = lax.axis_size("x") * lax.axis_size("tm")
     mine, other = summed(*pack(feature, ahead_head, ahead_early, inst, lag, total, chips))
     replicas = lax.axis_size("x") * lax.axis_size("core")

time: 71.7 us -> 70.1 us (0.978)
  Pallas kernels: 30.4 us -> 27.9 us
  waiting for transfers between devices: 6.11 us -> 6.89 us
    pallas_call x1, Pallas kernels: 7.81 us -> 5.88 us  [body(): pl.pallas_call(body_kernel, in_specs=[pl.BlockSpec(memory_space=pltpu.HBM...]
    pallas_call x1, Pallas kernels: 5.2 us -> 4 us  [early_rows(): pl.pallas_call(early_kernel, in_specs=[hbm] + [vmem] * 4, out_specs=(vmem...]
    pallas_call x0 -> x1, Pallas kernels: none -> 1.15 us  [moments(): pl.pallas_call(moment_kernel, in_specs=[vmem], out_specs=(vmem,) * 3, out...]
    ppermute x3, waiting for transfers between devices: 3.41 us -> 4.19 us  [passed_along(): lax.ppermute(value, axis, [(source, source + steps) for source in range(f...]
  transfers between devices with their start and end apart: 5 -> 5, of which waited for: 3 -> 3; matrix products, arithmetic and copies ran while one was open for 0% -> 0% of each run, Pallas kernels for 23% -> 20%
where the time goes in v9:
time: 70.1 us; the launch traced here: 69.7 us
  Pallas kernels  27.9 us (40%)
  blocking collectives  25.2 us (36%)
  starting transfers between devices  7.55 us (11%)
  waiting for transfers between devices  6.89 us (10%)
  local copies, waits for them, and re-layouts  1.06 us (2%)
  between operations  0.9 us (1%)
    all_to_all x1, blocking collectives, summed(): lax.all_to_all(parts, chips, 0, 0, tiled=True)  14.4 us
    all_to_all x1, blocking collectives, summed(): lax.all_to_all(jnp.broadcast_to(mine, parts.shape), chips, 0, 0, tiled=True)  10.8 us
    pallas_call x1, Pallas kernels, koopman_parts(): pl.pallas_call(koopman_kernel, in_specs=[pl.BlockSpec(memory_space=pltpu....  9.1 us
    ppermute x3, starting transfers between devices, passed_along(): lax.ppermute(value, axis, [(source, source + steps) for source in range(f...  7.47 us
    pallas_call x1, Pallas kernels, body(): pl.pallas_call(body_kernel, in_specs=[pl.BlockSpec(memory_space=pltpu.HBM...  5.88 us
    ppermute x3, waiting for transfers between devices, passed_along(): lax.ppermute(value, axis, [(source, source + steps) for source in range(f...  4.19 us
    pallas_call x1, Pallas kernels, early_rows(): pl.pallas_call(early_kernel, in_specs=[hbm] + [vmem] * 4, out_specs=(vmem...  4 us
    pallas_call x1, Pallas kernels, project(): pl.pallas_call(project_kernel, in_specs=[vmem] * 5, out_specs=(hbm, hbm),...  3.86 us
  transfers between devices with their start and end apart: 5, of which 3 were waited for; matrix products, arithmetic and copies ran while one was open for 0% of the time, Pallas kernels for 20%

profile of v9, /device:TPU:0, one launch (start us, length us, event | category | flops | bytes accessed | tf_op | source)
XLA Modules:
  0.0 69.7 jit_solution(14948352656039788001)
XLA Ops:
  0.6 1.0 %slice_bitcast_fusion = bf16[288,512]{1,0:T(8,128)(2,1)S(1)} fusion(bf16[1,4096,512]{2,1,0:T(8,128)(2,1)} %param.4), kind=kLoop, calls=%fused_computation | loop fusion | bytes 589824 | tf_op jit(solution)/shard_map/slice | solution.py:471
  1.6 4.9 %collective-permute-start = (bf16[288,512]{1,0:T(8,128)(2,1)S(1)}, bf16[288,512]{1,0:T(8,128)(2,1)S(1)}, u32[]{:S(2)}, u32[]{:S(2)}) collective-permute-start(bf16[288,512]{1,0:T(8,128)(2,1)S(1)} %slice_bitcast_fusion), channel_id=1, source_target_pairs={{0,1},{1,2},{2,3},{3,4},{4,5},{5,6},{6,7},{8,9},{9,10},{10,11},{11... | collective-permute-start | bytes 884744 | tf_op jit(solution)/shard_map/ppermute | solution.py:23
  6.5 1.7 %shard_map.59 = (bf16[1024,512]{1,0:T(8,128)(2,1)S(1)}, bf16[1024,512]{1,0:T(8,128)(2,1)S(1)}, f32[1,512]{1,0:T(1,128)S(1)}, bf16[1024,256]{1,0:T(8,128)(2,1)S(1)}) custom-call(bf16[4096,512]{1,0:T(8,128)(2,1)} %bitcast.8, bf16[1024,512]{1,0:T(8,128)(2,1)} %bitcast.11, f32[1,512]{1,0:T(1,128)} %bitcast.13, bf16[1024,256]{1,0:T(8,128)(2,1)} %bitcast.12), custom_call_target="tpu_custom_call" | custom-call | tf_op jit(solution)/shard_map/pallas_call | solution.py:73
  8.2 4.0 %shard_map.61 = (bf16[512,256]{1,0:T(8,128)(2,1)S(1)}, bf16[1024,256]{1,0:T(8,128)(2,1)S(1)}, bf16[256,512]{1,0:T(8,128)(2,1)S(1)}) custom-call(bf16[4096,512]{1,0:T(8,128)(2,1)} %bitcast.9, bf16[1024,512]{1,0:T(8,128)(2,1)S(1)} %get-tuple-element.18.near_ref, bf16[1024,512]{1,0:T(8,128)(2,1)S(1)} %get-tuple-element.19.w1_ref, ...), custom_call_target="tpu_custom_call" | custom-call | tf_op jit(solution)/shard_map/pallas_call | solution.py:133
  12.3 1.3 %collective-permute-start.2 = (bf16[512,256]{1,0:T(8,128)(2,1)S(1)}, bf16[512,256]{1,0:T(8,128)(2,1)S(1)}, u32[]{:S(2)}, u32[]{:S(2)}) collective-permute-start(bf16[512,256]{1,0:T(8,128)(2,1)S(1)} %get-tuple-element.22.early_ref), channel_id=1, source_target_pairs={{1,0},{2,1},{3,2},{4,3},{5,4},{6,5},{7,6},{9,8},{10,9},{11,10},{12... | collective-permute-start | bytes 786440 | tf_op jit(solution)/shard_map/ppermute | solution.py:23
  13.6 0.0 collective-permute-done.halo_ref
  13.6 1.4 %shard_map.60.head_ref = bf16[512,256]{1,0:T(8,128)(2,1)S(1)} custom-call(bf16[1024,512]{1,0:T(8,128)(2,1)S(1)} %get-tuple-element.18.near_ref, bf16[288,512]{1,0:T(8,128)(2,1)S(1)} %collective-permute-done.halo_ref, bf16[1024,512]{1,0:T(8,128)(2,1)S(1)} %get-tuple-element.19.w1_ref, f32[1,512]{1,0:T(1,128)S(1)} %get-tuple-element.20.b1_ref, ...), custom_call_target="tpu_custom_call" | custom-call | tf_op jit(solution)/shard_map/pallas_call | solution.py:146
  15.0 1.3 %collective-permute-start.1 = (bf16[512,256]{1,0:T(8,128)(2,1)S(1)}, bf16[512,256]{1,0:T(8,128)(2,1)S(1)}, u32[]{:S(2)}, u32[]{:S(2)}) collective-permute-start(bf16[512,256]{1,0:T(8,128)(2,1)S(1)} %shard_map.60.head_ref), channel_id=1, source_target_pairs={{1,0},{2,1},{3,2},{4,3},{5,4},{6,5},{7,6},{9,8},{10,9},{11,10},{12... | collective-permute-start | bytes 786440 | tf_op jit(solution)/shard_map/ppermute | solution.py:23
  16.3 5.9 %shard_map.62.feature_ref = bf16[4096,256]{1,0:T(8,128)(2,1)S(1)} custom-call(bf16[4096,512]{1,0:T(8,128)(2,1)} %bitcast.10, bf16[512,256]{1,0:T(8,128)(2,1)S(1)} %shard_map.60.head_ref, bf16[512,256]{1,0:T(8,128)(2,1)S(1)} %get-tuple-element.22.early_ref, bf16[1024,256]{1,0:T(8,128)(2,1)S(1)} %get-tuple-element.23.middle_ref, ...), custom_call_target="tpu_custom_call" | custom-call | tf_op jit(solution)/shard_map/pallas_call | solution.py:191
  22.2 1.2 %shard_map.63 = (f32[256,256]{1,0:T(8,128)S(1)}, f32[256,256]{1,0:T(8,128)S(1)}, f32[8,256]{1,0:T(8,128)S(1)}) custom-call(bf16[4096,256]{1,0:T(8,128)(2,1)S(1)} %shard_map.62.feature_ref), custom_call_target="tpu_custom_call" | custom-call | tf_op jit(solution)/shard_map/pallas_call | solution.py:234
  23.3 0.0 collective-permute-done.2.ahead_early_ref
  23.4 4.2 %collective-permute-done.1.ahead_head_ref = bf16[512,256]{1,0:T(8,128)(2,1)S(1)} collective-permute-done((bf16[512,256]{1,0:T(8,128)(2,1)S(1)}, bf16[512,256]{1,0:T(8,128)(2,1)S(1)}, u32[]{:S(2)}, u32[]{:S(2)}) %collective-permute-start.1) | collective-permute-done | bytes 262176 | tf_op jit(solution)/shard_map/ppermute | solution.py:23
  27.5 0.8 %shard_map.64 = (f32[16,1,2176]{2,1,0:T(1,128)S(1)}, f32[16,1,2176]{2,1,0:T(1,128)S(1)}) custom-call(bf16[4096,256]{1,0:T(8,128)(2,1)S(1)} %shard_map.62.feature_ref, bf16[512,256]{1,0:T(8,128)(2,1)S(1)} %collective-permute-done.1.ahead_head_ref, bf16[512,256]{1,0:T(8,128)(2,1)S(1)} %collective-permute-done.2.ahead_early_ref, ...), custom_call_target="tpu_custom_call" | custom-call | tf_op jit(solution)/shard_map/pallas_call | solution.py:277
  28.3 0.1 collective-permute-start.3
  28.4 1.3 %collective-permute-done.3 = f32[16,1,2176]{2,1,0:T(1,128)S(1)} collective-permute-done((f32[16,1,2176]{2,1,0:T(1,128)S(1)}, f32[16,1,2176]{2,1,0:T(1,128)S(1)}, u32[]{:S(2)}, u32[]{:S(2)}) %collective-permute-start.3) | collective-permute-done | bytes 139296 | tf_op jit(solution)/shard_map/ppermute | solution.py:456
  29.8 0.1 add.3
  29.9 14.4 %all_to_all.10 = f32[16,1,2176]{2,1,0:T(1,128)S(1)} all-to-all(f32[16,1,2176]{2,1,0:T(1,128)S(1)} %add.3), channel_id=1, replica_groups=mesh['x'=2,'core'=2,'tm'=8] {'x','tm'}, dimensions={0} | all-to-all | bytes 278528 | tf_op jit(solution)/shard_map/all_to_all | solution.py:457
  44.3 0.1 reduce_sum.9
  44.4 0.1 broadcast_in_dim.12
  44.5 10.8 %all_to_all.11.mine_ref = f32[16,1,2176]{2,1,0:T(1,128)S(1)} all-to-all(f32[16,1,2176]{2,1,0:T(1,128)S(1)} %broadcast_in_dim.12), channel_id=1, replica_groups=mesh['x'=2,'core'=2,'tm'=8] {'x','tm'}, dimensions={0} | all-to-all | bytes 278528 | tf_op jit(solution)/shard_map/all_to_all | solution.py:458
  55.2 0.0 collective-permute-start.4
  55.2 1.4 %collective-permute-done.4.other_ref = f32[16,1,2176]{2,1,0:T(1,128)S(1)} collective-permute-done((f32[16,1,2176]{2,1,0:T(1,128)S(1)}, f32[16,1,2176]{2,1,0:T(1,128)S(1)}, u32[]{:S(2)}, u32[]{:S(2)}) %collective-permute-start.4) | collective-permute-done | bytes 139296 | tf_op jit(solution)/shard_map/ppermute | solution.py:459
  56.6 9.1 %shard_map.65 = (bf16[2,512,256]{2,1,0:T(8,128)(2,1)S(1)}, f32[2,8,256]{2,1,0:T(8,128)S(1)}) custom-call(f32[1]{0:T(128)} %constant.0.clone.1.scale_ref, f32[16,1,2176]{2,1,0:T(1,128)S(1)} %all_to_all.11.mine_ref, f32[16,1,2176]{2,1,0:T(1,128)S(1)} %collective-permute-done.4.other_ref), custom_call_target="tpu_custom_call" | custom-call | tf_op jit(solution)/shard_map/pallas_call | solution.py:390
  65.7 3.9 %shard_map.66 = (f32[4096,256]{1,0:T(8,128)}, f32[4096,256]{1,0:T(8,128)}) custom-call(bf16[4096,256]{1,0:T(8,128)(2,1)S(1)} %shard_map.62.feature_ref, bf16[512,256]{1,0:T(8,128)(2,1)S(1)} %collective-permute-done.1.ahead_head_ref, bf16[512,256]{1,0:T(8,128)(2,1)S(1)} %collective-permute-done.2.ahead_early_ref, ...), custom_call_target="tpu_custom_call" | custom-call | tf_op jit(solution)/shard_map/pallas_call | solution.py:439
Async XLA Ops:
  1.6 11.9 %collective-permute-start = (bf16[288,512]{1,0:T(8,128)(2,1)S(1)}, bf16[288,512]{1,0:T(8,128)(2,1)S(1)}, u32[]{:S(2)}, u32[]{:S(2)}) collective-permute-start(bf16[288,512]{1,0:T(8,128)(2,1)S(1)} %slice_bitcast_fusion), channel_id=1, source_target_pairs={{0,1},{1,2},{2,3},{3,4},{4,5},{5,6},{6,7},{8,9},{9,10},{10,11},{11... | collective-permute-start | bytes 884744 | tf_op jit(solution)/shard_map/ppermute | solution.py:23
  12.3 11.1 %collective-permute-start.2 = (bf16[512,256]{1,0:T(8,128)(2,1)S(1)}, bf16[512,256]{1,0:T(8,128)(2,1)S(1)}, u32[]{:S(2)}, u32[]{:S(2)}) collective-permute-start(bf16[512,256]{1,0:T(8,128)(2,1)S(1)} %get-tuple-element.22.early_ref), channel_id=1, source_target_pairs={{1,0},{2,1},{3,2},{4,3},{5,4},{6,5},{7,6},{9,8},{10,9},{11,10},{12... | collective-permute-start | bytes 786440 | tf_op jit(solution)/shard_map/ppermute | solution.py:23
  15.0 12.5 %collective-permute-start.1 = (bf16[512,256]{1,0:T(8,128)(2,1)S(1)}, bf16[512,256]{1,0:T(8,128)(2,1)S(1)}, u32[]{:S(2)}, u32[]{:S(2)}) collective-permute-start(bf16[512,256]{1,0:T(8,128)(2,1)S(1)} %shard_map.60.head_ref), channel_id=1, source_target_pairs={{1,0},{2,1},{3,2},{4,3},{5,4},{6,5},{7,6},{9,8},{10,9},{11,10},{12... | collective-permute-start | bytes 786440 | tf_op jit(solution)/shard_map/ppermute | solution.py:23
  28.3 1.4 %collective-permute-start.3 = (f32[16,1,2176]{2,1,0:T(1,128)S(1)}, f32[16,1,2176]{2,1,0:T(1,128)S(1)}, u32[]{:S(2)}, u32[]{:S(2)}) collective-permute-start(f32[16,1,2176]{2,1,0:T(1,128)S(1)} %get-tuple-element.29), channel_id=1, source_target_pairs={{0,8},{8,0},{1,9},{9,1},{2,10},{10,2},{3,11},{11,3},{4,12},{12,4},... | collective-permute-start | bytes 417800 | tf_op jit(solution)/shard_map/ppermute | solution.py:456
  55.2 1.4 %collective-permute-start.4 = (f32[16,1,2176]{2,1,0:T(1,128)S(1)}, f32[16,1,2176]{2,1,0:T(1,128)S(1)}, u32[]{:S(2)}, u32[]{:S(2)}) collective-permute-start(f32[16,1,2176]{2,1,0:T(1,128)S(1)} %all_to_all.11.mine_ref), channel_id=1, source_target_pairs={{0,8},{8,0},{1,9},{9,1},{2,10},{10,2},{3,11},{11,3},{4,12},{12,4},... | collective-permute-start | bytes 417800 | tf_op jit(solution)/shard_map/ppermute | solution.py:459

commit v10 on v9

--- a/solution.py
+++ b/solution.py
@@ -10,6 +10,7 @@
 LAG = 1024
 RIDGE = 0.001
 CHUNK = 512
+EARLY = 1536
 PANEL = 16
 MIB = 1024 * 1024
 
@@ -51,38 +52,52 @@
     return jnp.dot(both, w2_ref[...], preferred_element_type=F32).astype(BF16)
 
 
-def fetch_kernel(frames_ref, w1_in, b1_in, w2_in, near_ref, w1_ref, b1_ref, w2_ref, sems):
+def tail_kernel(frames_ref, w1_in, b1_in, w2_in, sent_ref, near_ref, w1_ref, b1_ref, w2_ref, xs, sems):
+    rows = frames_ref.shape[0]
     pairs = (
-        (frames_ref.at[pl.ds(0, LAG)], near_ref),
+        (frames_ref.at[pl.ds(rows - D1 - D2, D1 + D2)], xs),
         (w1_in, w1_ref),
         (b1_in, b1_ref),
         (w2_in, w2_ref),
+        (frames_ref.at[pl.ds(0, LAG)], near_ref),
     )
     copies = [pltpu.make_async_copy(*pair, sems.at[index]) for index, pair in enumerate(pairs)]
     for copy in copies:
         copy.start()
-    for copy in copies:
+    for copy in copies[:3]:
         copy.wait()
-
-
-def fetch(frames, w1, b1, w2):
+    hidden = hidden_rows(xs, 0, D2, w1_ref, b1_ref)
+    copies[3].wait()
+    hid, feat = hidden.shape[1], w2_ref.shape[1]
+    sent_ref[:D2, :] = jnp.dot(hidden, w2_ref[hid:, :], preferred_element_type=F32).astype(BF16)
+    for index in range(xs.shape[1] // feat):
+        part = slice(D2 + index * D1, D2 + (index + 1) * D1)
+        sent_ref[part, :] = xs[D2:, index * feat : (index + 1) * feat]
+    copies[4].wait()
+
+
+def tail_rows(frames, w1, b1, w2):
     vmem = pl.BlockSpec(memory_space=pltpu.VMEM)
     hbm = pl.BlockSpec(memory_space=pltpu.HBM)
-    channels = frames.shape[1]
-    shapes = (((LAG, channels), BF16), (w1.shape, BF16), (b1.shape, F32), (w2.shape, BF16))
-    return pl.pallas_call(
-        fetch_kernel,
+    channels, feat = frames.shape[1], w2.shape[1]
+    sent = (D2 + D1 * channels // feat, feat)
+    shapes = ((sent, BF16), ((LAG, channels), BF16), (w1.shape, BF16), (b1.shape, F32), (w2.shape, BF16))
+    return pl.pallas_call(
+        tail_kernel,
         in_specs=[hbm] * 4,
-        out_specs=(vmem,) * 4,
+        out_specs=(vmem,) * 5,
         out_shape=tuple(jax.ShapeDtypeStruct(*shape) for shape in shapes),
-        scratch_shapes=[pltpu.SemaphoreType.DMA((4,))],
-        compiler_params=pltpu.CompilerParams(vmem_limit_bytes=8 * MIB),
+        scratch_shapes=[pltpu.VMEM((D1 + D2, channels), BF16), pltpu.SemaphoreType.DMA((5,))],
+        compiler_params=pltpu.CompilerParams(vmem_limit_bytes=12 * MIB),
     )(*(in_hbm(value) for value in (frames, w1, b1, w2)))
 
 
-def early_kernel(frames_ref, near_ref, w1_ref, b1_ref, w2_ref, early_ref, middle_ref, hidden_ref, xs, hs, sems):
+def early_kernel(
+    frames_ref, near_ref, w1_ref, b1_ref, w2_ref, early_ref, middle_ref, hidden_ref, far_ref, xs, hs, sems
+):
     half = LAG // 2
     first = half - D1 - D2
+    steps = (EARLY - LAG) // CHUNK
 
     def arriving(step):
         at = LAG + step * CHUNK
@@ -90,9 +105,12 @@
             frames_ref.at[pl.ds(at, CHUNK)], xs.at[pl.ds(at - first, CHUNK)], sems.at[step]
         )
 
-    steps = LAG // CHUNK
     for step in range(steps):
         arriving(step).start()
+    later = pltpu.make_async_copy(
+        frames_ref.at[pl.ds(EARLY - D1, far_ref.shape[0])], far_ref, sems.at[steps]
+    )
+    later.start()
     xs[: LAG - first, :] = near_ref[first:, :]
     hs[: D2 + half, :] = hidden_rows(xs, 0, D2 + half, w1_ref, b1_ref)
     for step in range(steps):
@@ -103,103 +121,86 @@
             early_ref[...] = feature_rows(hs, 0, half, w2_ref)
         else:
             middle_ref[(step - 1) * CHUNK : step * CHUNK, :] = feature_rows(hs, at - CHUNK, CHUNK, w2_ref)
-    middle_ref[LAG - CHUNK :, :] = feature_rows(hs, half + LAG - CHUNK, CHUNK, w2_ref)
+    middle_ref[(steps - 1) * CHUNK :, :] = feature_rows(hs, half + (steps - 1) * CHUNK, CHUNK, w2_ref)
     hidden_ref[...] = hs[hs.shape[0] - D2 :, :]
-
-
-def head_kernel(near_ref, halo_ref, w1_ref, b1_ref, w2_ref, out_ref, xs, hs):
-    halo_rows = halo_ref.shape[0]
-    xs[:halo_rows, :] = halo_ref[...]
-    xs[halo_rows:, :] = near_ref[: LAG // 2, :]
-    before = hidden_rows(xs, 0, D2, w1_ref, b1_ref)
-    hs[:D2, :] = jnp.where(lax.axis_index("tm") > 0, before, jnp.zeros_like(before))
-    for at in range(D2, hs.shape[0], D2):
-        hs[at : at + D2, :] = hidden_rows(xs, at, D2, w1_ref, b1_ref)
-    out_ref[...] = feature_rows(hs, 0, out_ref.shape[0], w2_ref)
-
-
-def feature_scratch(rows, channels, hid):
-    return [
-        pltpu.VMEM((rows + D1 + D2, channels), BF16),
-        pltpu.VMEM((rows + D2, hid), BF16),
-    ]
+    later.wait()
 
 
 def early_rows(frames, near, w1, b1, w2):
     vmem = pl.BlockSpec(memory_space=pltpu.VMEM)
     hbm = pl.BlockSpec(memory_space=pltpu.HBM)
+    rows, channels = frames.shape
     half, hid, feat = LAG // 2, w1.shape[1], w2.shape[1]
-    shapes = (((half, feat), BF16), ((LAG, feat), BF16), ((D2, hid), BF16))
+    shapes = ((half, feat), (EARLY - LAG, feat), (D2, hid), (rows - EARLY + D1, channels))
+    done = EARLY - half
     return pl.pallas_call(
         early_kernel,
         in_specs=[hbm] + [vmem] * 4,
-        out_specs=(vmem,) * 3,
-        out_shape=tuple(jax.ShapeDtypeStruct(*shape) for shape in shapes),
-        scratch_shapes=feature_scratch(half + LAG, near.shape[1], hid) + [pltpu.SemaphoreType.DMA((LAG // CHUNK,))],
+        out_specs=(vmem,) * 4,
+        out_shape=tuple(jax.ShapeDtypeStruct(shape, BF16) for shape in shapes),
+        scratch_shapes=[
+            pltpu.VMEM((done + D1 + D2, channels), BF16),
+            pltpu.VMEM((done + D2, hid), BF16),
+            pltpu.SemaphoreType.DMA(((EARLY - LAG) // CHUNK + 1,)),
+        ],
         compiler_params=pltpu.CompilerParams(vmem_limit_bytes=16 * MIB),
     )(in_hbm(frames), near, w1, b1, w2)
 
 
+def head_kernel(near_ref, halo_ref, w1_ref, b1_ref, w2_ref, out_ref, xs, hs):
+    half = LAG // 2
+    hid, feat = w1_ref.shape[1], w2_ref.shape[1]
+    for index in range(xs.shape[1] // feat):
+        part = slice(D2 + index * D1, D2 + (index + 1) * D1)
+        xs[:D1, index * feat : (index + 1) * feat] = halo_ref[part, :]
+    xs[D1:, :] = near_ref[:half, :]
+    for at in range(0, half, D2):
+        hs[at : at + D2, :] = hidden_rows(xs, at, D2, w1_ref, b1_ref)
+    value = jnp.dot(hs[:D2, :], w2_ref[:hid, :], preferred_element_type=F32)
+    out_ref[:D2, :] = (value + halo_ref[:D2, :].astype(F32)).astype(BF16)
+    out_ref[D2:, :] = feature_rows(hs, 0, half - D2, w2_ref)
+
+
 def head_rows(near, halo, w1, b1, w2):
     vmem = pl.BlockSpec(memory_space=pltpu.VMEM)
-    half = LAG // 2
+    half, channels, hid = LAG // 2, near.shape[1], w1.shape[1]
     return pl.pallas_call(
         head_kernel,
         in_specs=[vmem] * 5,
         out_specs=vmem,
         out_shape=jax.ShapeDtypeStruct((half, w2.shape[1]), BF16),
-        scratch_shapes=feature_scratch(half, near.shape[1], w1.shape[1]),
-        compiler_params=pltpu.CompilerParams(vmem_limit_bytes=12 * MIB),
+        scratch_shapes=[pltpu.VMEM((half + D1, channels), BF16), pltpu.VMEM((half, hid), BF16)],
+        compiler_params=pltpu.CompilerParams(vmem_limit_bytes=8 * MIB),
     )(near, halo, w1, b1, w2)
 
 
-def body_kernel(
-    frames_ref, head_ref, early_ref, middle_ref, hidden_ref, w1_ref, b1_ref, w2_ref, out_ref, xs, hs, sems
-):
+def body_kernel(far_ref, head_ref, early_ref, middle_ref, hidden_ref, w1_ref, b1_ref, w2_ref, out_ref, hs):
     rows = out_ref.shape[0]
-    done = 2 * LAG
-    steps = (rows - done) // CHUNK
-
-    def arriving(step):
-        more = D1 if step == 0 else 0
-        at = step * CHUNK + D1 - more
-        return pltpu.make_async_copy(
-            frames_ref.at[pl.ds(done - D1 + at, CHUNK + more)], xs.at[pl.ds(at, CHUNK + more)], sems.at[step]
-        )
-
-    for step in range(steps):
-        arriving(step).start()
+    steps = (rows - EARLY) // CHUNK
     half = LAG // 2
     hs[:D2, :] = hidden_ref[...]
     out_ref[:half, :] = head_ref[...]
     out_ref[half:LAG, :] = early_ref[...]
-    out_ref[LAG:done, :] = middle_ref[...]
+    out_ref[LAG:EARLY, :] = middle_ref[...]
     for step in range(steps + 1):
         at = step * CHUNK
         if step < steps:
-            arriving(step).wait()
-            hs[D2 + at : D2 + at + CHUNK, :] = hidden_rows(xs, at, CHUNK, w1_ref, b1_ref)
+            hs[D2 + at : D2 + at + CHUNK, :] = hidden_rows(far_ref, at, CHUNK, w1_ref, b1_ref)
         if step:
-            out_ref[done + at - CHUNK : done + at, :] = feature_rows(hs, at - CHUNK, CHUNK, w2_ref)
-
-
-def body(frames, head, early, middle, hidden, w1, b1, w2):
-    rows, channels = frames.shape
-    hid, feat = w1.shape[1], w2.shape[1]
-    vmem = pl.BlockSpec(memory_space=pltpu.VMEM)
-    left = rows - 2 * LAG
+            out_ref[EARLY + at - CHUNK : EARLY + at, :] = feature_rows(hs, at - CHUNK, CHUNK, w2_ref)
+
+
+def body(far, head, early, middle, hidden, w1, b1, w2):
+    rows, hid, feat = far.shape[0] - D1 + EARLY, w1.shape[1], w2.shape[1]
+    vmem = pl.BlockSpec(memory_space=pltpu.VMEM)
     return pl.pallas_call(
         body_kernel,
-        in_specs=[pl.BlockSpec(memory_space=pltpu.HBM)] + [vmem] * 7,
+        in_specs=[vmem] * 8,
         out_specs=vmem,
         out_shape=jax.ShapeDtypeStruct((rows, feat), BF16),
-        scratch_shapes=[
-            pltpu.VMEM((left + D1, channels), BF16),
-            pltpu.VMEM((left + D2, hid), BF16),
-            pltpu.SemaphoreType.DMA((left // CHUNK,)),
-        ],
+        scratch_shapes=[pltpu.VMEM((rows - EARLY + D2, hid), BF16)],
         compiler_params=pltpu.CompilerParams(vmem_limit_bytes=16 * MIB),
-    )(in_hbm(frames), head, early, middle, hidden, w1, b1, w2)
+    )(far, head, early, middle, hidden, w1, b1, w2)
 
 
 def column_sum(rows):
@@ -468,13 +469,13 @@
         first_bias.reshape(1, hid),
         second_weight.reshape(2 * hid, feat),
     )
-    halo = passed_along(frame_block[row_count - D1 - D2 :], "tm", 1)
-    near, *weights = fetch(frame_block, *weights)
-    early, middle, hidden = early_rows(frame_block, near, *weights)
+    sent, near, *weights = tail_rows(frame_block, *weights)
+    halo = passed_along(sent, "tm", 1)
+    early, middle, hidden, far = early_rows(frame_block, near, *weights)
     ahead_early = passed_along(early, "tm", -1)
     head = head_rows(near, halo, *weights)
     ahead_head = passed_along(head, "tm", -1)
-    feature = body(frame_block, head, early, middle, hidden, *weights)
+    feature = body(far, head, early, middle, hidden, *weights)
     inst, lag, total = moments(feature)
     chips = lax.axis_size("x") * lax.axis_size("tm")
     mine, other = summed(*pack(feature, ahead_head, ahead_early, inst, lag, total, chips))

time: 70.1 us -> 68 us (0.970)
  Pallas kernels: 27.9 us -> 25.3 us
  waiting for transfers between devices: 6.89 us -> 8.56 us
  local copies, waits for them, and re-layouts: 1.06 us -> 0.07 us
    ppermute x3, waiting for transfers between devices: 4.19 us -> 5.86 us  [passed_along(): lax.ppermute(value, axis, [(source, source + steps) for source in range(f...]
    pallas_call x1, Pallas kernels: 4 us -> 2.56 us  [early_rows(): pl.pallas_call(early_kernel, in_specs=[hbm] + [vmem] * 4, out_specs=(vmem...]
    slice x1 -> x0, local copies, waits for them, and re-layouts: 0.98 us -> none  [on_device(): halo = passed_along(frame_block[row_count - D1 - D2:], 'tm', 1)]
    pallas_call x2, Pallas kernels: 7.61 us -> 6.72 us  [the longest x1 4.53 us: body(): pl.pallas_call(body_kernel, in_specs=[vmem] * 8, out_specs=vmem, out_shap...]
  transfers between devices with their start and end apart: 5 -> 5, of which waited for: 3 -> 4; matrix products, arithmetic and copies ran while one was open for 0% -> 0% of each run, Pallas kernels for 20% -> 14%
where the time goes in v10:
time: 68 us; the launch traced here: 67.8 us
  Pallas kernels  25.3 us (37%)
  blocking collectives  25.2 us (37%)
  waiting for transfers between devices  8.56 us (13%)
  starting transfers between devices  7.54 us (11%)
  between operations  0.89 us (1%)
    all_to_all x1, blocking collectives, summed(): lax.all_to_all(parts, chips, 0, 0, tiled=True)  14.4 us
    all_to_all x1, blocking collectives, summed(): lax.all_to_all(jnp.broadcast_to(mine, parts.shape), chips, 0, 0, tiled=True)  10.8 us
    pallas_call x1, Pallas kernels, koopman_parts(): pl.pallas_call(koopman_kernel, in_specs=[pl.BlockSpec(memory_space=pltpu....  9.1 us
    ppermute x3, starting transfers between devices, passed_along(): lax.ppermute(value, axis, [(source, source + steps) for source in range(f...  7.46 us
    ppermute x3, waiting for transfers between devices, passed_along(): lax.ppermute(value, axis, [(source, source + steps) for source in range(f...  5.86 us
    pallas_call x1, Pallas kernels, body(): pl.pallas_call(body_kernel, in_specs=[vmem] * 8, out_specs=vmem, out_shap...  4.53 us
    pallas_call x1, Pallas kernels, project(): pl.pallas_call(project_kernel, in_specs=[vmem] * 5, out_specs=(hbm, hbm),...  3.86 us
    pallas_call x1, Pallas kernels, early_rows(): pl.pallas_call(early_kernel, in_specs=[hbm] + [vmem] * 4, out_specs=(vmem...  2.56 us
  transfers between devices with their start and end apart: 5, of which 4 were waited for; matrix products, arithmetic and copies ran while one was open for 0% of the time, Pallas kernels for 14%

profile of v10, /device:TPU:0, one launch (start us, length us, event | category | flops | bytes accessed | tf_op | source)
XLA Modules:
  0.0 67.8 jit_solution(17679627620370638787)
XLA Ops:
  0.6 2.2 %shard_map.59 = (bf16[320,256]{1,0:T(8,128)(2,1)S(1)}, bf16[1024,512]{1,0:T(8,128)(2,1)S(1)}, bf16[1024,512]{1,0:T(8,128)(2,1)S(1)}, f32[1,512]{1,0:T(1,128)S(1)}, bf16[1024,256]{1,0:T(8,128)(2,1)S(1)}) custom-call(bf16[4096,512]{1,0:T(8,128)(2,1)} %bitcast.6, bf16[1024,512]{1,0:T(8,128)(2,1)} %bitcast.8, f32[1,512]{1,0:T(1,128)} %bitcast.10, ...), custom_call_target="tpu_custom_call" | custom-call | tf_op jit(solution)/shard_map/pallas_call | solution.py:85
  2.8 4.9 %collective-permute-start = (bf16[320,256]{1,0:T(8,128)(2,1)S(1)}, bf16[320,256]{1,0:T(8,128)(2,1)S(1)}, u32[]{:S(2)}, u32[]{:S(2)}) collective-permute-start(bf16[320,256]{1,0:T(8,128)(2,1)S(1)} %get-tuple-element.25), channel_id=1, source_target_pairs={{0,1},{1,2},{2,3},{3,4},{4,5},{5,6},{6,7},{8,9},{9,10},{10,11},{11... | collective-permute-start | bytes 491528 | tf_op jit(solution)/shard_map/ppermute | solution.py:24
  7.7 2.6 %shard_map.60 = (bf16[512,256]{1,0:T(8,128)(2,1)S(1)}, bf16[512,256]{1,0:T(8,128)(2,1)S(1)}, bf16[256,512]{1,0:T(8,128)(2,1)S(1)}, bf16[2592,512]{1,0:T(8,128)(2,1)S(1)}) custom-call(bf16[4096,512]{1,0:T(8,128)(2,1)} %bitcast.7, bf16[1024,512]{1,0:T(8,128)(2,1)S(1)} %get-tuple-element.20.near_ref, bf16[1024,512]{1,0:T(8,128)(2,1)S(1)} %get-tuple-element.21.w1_ref, ...), custom_call_target="tpu_custom_call" | custom-call | tf_op jit(solution)/shard_map/pallas_call | solution.py:136
  10.3 1.3 %collective-permute-start.2 = (bf16[512,256]{1,0:T(8,128)(2,1)S(1)}, bf16[512,256]{1,0:T(8,128)(2,1)S(1)}, u32[]{:S(2)}, u32[]{:S(2)}) collective-permute-start(bf16[512,256]{1,0:T(8,128)(2,1)S(1)} %get-tuple-element.26.early_ref), channel_id=1, source_target_pairs={{1,0},{2,1},{3,2},{4,3},{5,4},{6,5},{7,6},{9,8},{10,9},{11,10},{12... | collective-permute-start | bytes 786440 | tf_op jit(solution)/shard_map/ppermute | solution.py:24
  11.6 0.0 collective-permute-done.halo_ref
  11.6 1.1 %shard_map.61.head_ref = bf16[512,256]{1,0:T(8,128)(2,1)S(1)} custom-call(bf16[1024,512]{1,0:T(8,128)(2,1)S(1)} %get-tuple-element.20.near_ref, bf16[320,256]{1,0:T(8,128)(2,1)S(1)} %collective-permute-done.halo_ref, bf16[1024,512]{1,0:T(8,128)(2,1)S(1)} %get-tuple-element.21.w1_ref, f32[1,512]{1,0:T(1,128)S(1)} %get-tuple-element.22.b1_ref, ...), custom_call_target="tpu_custom_call" | custom-call | tf_op jit(solution)/shard_map/pallas_call | solution.py:167
  12.7 1.3 %collective-permute-start.1 = (bf16[512,256]{1,0:T(8,128)(2,1)S(1)}, bf16[512,256]{1,0:T(8,128)(2,1)S(1)}, u32[]{:S(2)}, u32[]{:S(2)}) collective-permute-start(bf16[512,256]{1,0:T(8,128)(2,1)S(1)} %shard_map.61.head_ref), channel_id=1, source_target_pairs={{1,0},{2,1},{3,2},{4,3},{5,4},{6,5},{7,6},{9,8},{10,9},{11,10},{12... | collective-permute-start | bytes 786440 | tf_op jit(solution)/shard_map/ppermute | solution.py:24
  14.0 4.5 %shard_map.62.feature_ref = bf16[4096,256]{1,0:T(8,128)(2,1)S(1)} custom-call(bf16[2592,512]{1,0:T(8,128)(2,1)S(1)} %get-tuple-element.24.far_ref, bf16[512,256]{1,0:T(8,128)(2,1)S(1)} %shard_map.61.head_ref, bf16[512,256]{1,0:T(8,128)(2,1)S(1)} %get-tuple-element.26.early_ref, bf16[512,256]{1,0:T(8,128)(2,1)S(1)} %get-tuple-element.27.middle_ref, ...), custom_call_target="tpu_custom_call" | custom-call | tf_op jit(solution)/shard_map/pallas_call | solution.py:196
  18.6 1.1 %shard_map.63 = (f32[256,256]{1,0:T(8,128)S(1)}, f32[256,256]{1,0:T(8,128)S(1)}, f32[8,256]{1,0:T(8,128)S(1)}) custom-call(bf16[4096,256]{1,0:T(8,128)(2,1)S(1)} %shard_map.62.feature_ref), custom_call_target="tpu_custom_call" | custom-call | tf_op jit(solution)/shard_map/pallas_call | solution.py:235
  19.7 1.7 %collective-permute-done.2.ahead_early_ref = bf16[512,256]{1,0:T(8,128)(2,1)S(1)} collective-permute-done((bf16[512,256]{1,0:T(8,128)(2,1)S(1)}, bf16[512,256]{1,0:T(8,128)(2,1)S(1)}, u32[]{:S(2)}, u32[]{:S(2)}) %collective-permute-start.2) | collective-permute-done | bytes 262176 | tf_op jit(solution)/shard_map/ppermute | solution.py:24
  21.4 4.2 %collective-permute-done.1.ahead_head_ref = bf16[512,256]{1,0:T(8,128)(2,1)S(1)} collective-permute-done((bf16[512,256]{1,0:T(8,128)(2,1)S(1)}, bf16[512,256]{1,0:T(8,128)(2,1)S(1)}, u32[]{:S(2)}, u32[]{:S(2)}) %collective-permute-start.1) | collective-permute-done | bytes 262176 | tf_op jit(solution)/shard_map/ppermute | solution.py:24
  25.6 0.8 %shard_map.64 = (f32[16,1,2176]{2,1,0:T(1,128)S(1)}, f32[16,1,2176]{2,1,0:T(1,128)S(1)}) custom-call(bf16[4096,256]{1,0:T(8,128)(2,1)S(1)} %shard_map.62.feature_ref, bf16[512,256]{1,0:T(8,128)(2,1)S(1)} %collective-permute-done.1.ahead_head_ref, bf16[512,256]{1,0:T(8,128)(2,1)S(1)} %collective-permute-done.2.ahead_early_ref, ...), custom_call_target="tpu_custom_call" | custom-call | tf_op jit(solution)/shard_map/pallas_call | solution.py:278
  26.4 0.1 collective-permute-start.3
  26.4 1.3 %collective-permute-done.3 = f32[16,1,2176]{2,1,0:T(1,128)S(1)} collective-permute-done((f32[16,1,2176]{2,1,0:T(1,128)S(1)}, f32[16,1,2176]{2,1,0:T(1,128)S(1)}, u32[]{:S(2)}, u32[]{:S(2)}) %collective-permute-start.3) | collective-permute-done | bytes 139296 | tf_op jit(solution)/shard_map/ppermute | solution.py:457
  27.8 0.1 add.3
  27.9 14.4 %all_to_all.10 = f32[16,1,2176]{2,1,0:T(1,128)S(1)} all-to-all(f32[16,1,2176]{2,1,0:T(1,128)S(1)} %add.3), channel_id=1, replica_groups=mesh['x'=2,'core'=2,'tm'=8] {'x','tm'}, dimensions={0} | all-to-all | bytes 278528 | tf_op jit(solution)/shard_map/all_to_all | solution.py:458
  42.3 0.1 reduce_sum.9
  42.4 0.1 broadcast_in_dim.12
  42.5 10.8 %all_to_all.11.mine_ref = f32[16,1,2176]{2,1,0:T(1,128)S(1)} all-to-all(f32[16,1,2176]{2,1,0:T(1,128)S(1)} %broadcast_in_dim.12), channel_id=1, replica_groups=mesh['x'=2,'core'=2,'tm'=8] {'x','tm'}, dimensions={0} | all-to-all | bytes 278528 | tf_op jit(solution)/shard_map/all_to_all | solution.py:459
  53.3 0.0 collective-permute-start.4
  53.3 1.4 %collective-permute-done.4.other_ref = f32[16,1,2176]{2,1,0:T(1,128)S(1)} collective-permute-done((f32[16,1,2176]{2,1,0:T(1,128)S(1)}, f32[16,1,2176]{2,1,0:T(1,128)S(1)}, u32[]{:S(2)}, u32[]{:S(2)}) %collective-permute-start.4) | collective-permute-done | bytes 139296 | tf_op jit(solution)/shard_map/ppermute | solution.py:460
  54.6 9.1 %shard_map.65 = (bf16[2,512,256]{2,1,0:T(8,128)(2,1)S(1)}, f32[2,8,256]{2,1,0:T(8,128)S(1)}) custom-call(f32[1]{0:T(128)} %constant.0.clone.1.scale_ref, f32[16,1,2176]{2,1,0:T(1,128)S(1)} %all_to_all.11.mine_ref, f32[16,1,2176]{2,1,0:T(1,128)S(1)} %collective-permute-done.4.other_ref), custom_call_target="tpu_custom_call" | custom-call | tf_op jit(solution)/shard_map/pallas_call | solution.py:391
  63.7 3.9 %shard_map.66 = (f32[4096,256]{1,0:T(8,128)}, f32[4096,256]{1,0:T(8,128)}) custom-call(bf16[4096,256]{1,0:T(8,128)(2,1)S(1)} %shard_map.62.feature_ref, bf16[512,256]{1,0:T(8,128)(2,1)S(1)} %collective-permute-done.1.ahead_head_ref, bf16[512,256]{1,0:T(8,128)(2,1)S(1)} %collective-permute-done.2.ahead_early_ref, ...), custom_call_target="tpu_custom_call" | custom-call | tf_op jit(solution)/shard_map/pallas_call | solution.py:440
Async XLA Ops:
  2.8 8.8 %collective-permute-start = (bf16[320,256]{1,0:T(8,128)(2,1)S(1)}, bf16[320,256]{1,0:T(8,128)(2,1)S(1)}, u32[]{:S(2)}, u32[]{:S(2)}) collective-permute-start(bf16[320,256]{1,0:T(8,128)(2,1)S(1)} %get-tuple-element.25), channel_id=1, source_target_pairs={{0,1},{1,2},{2,3},{3,4},{4,5},{5,6},{6,7},{8,9},{9,10},{10,11},{11... | collective-permute-start | bytes 491528 | tf_op jit(solution)/shard_map/ppermute | solution.py:24
  10.3 11.1 %collective-permute-start.2 = (bf16[512,256]{1,0:T(8,128)(2,1)S(1)}, bf16[512,256]{1,0:T(8,128)(2,1)S(1)}, u32[]{:S(2)}, u32[]{:S(2)}) collective-permute-start(bf16[512,256]{1,0:T(8,128)(2,1)S(1)} %get-tuple-element.26.early_ref), channel_id=1, source_target_pairs={{1,0},{2,1},{3,2},{4,3},{5,4},{6,5},{7,6},{9,8},{10,9},{11,10},{12... | collective-permute-start | bytes 786440 | tf_op jit(solution)/shard_map/ppermute | solution.py:24
  12.7 12.8 %collective-permute-start.1 = (bf16[512,256]{1,0:T(8,128)(2,1)S(1)}, bf16[512,256]{1,0:T(8,128)(2,1)S(1)}, u32[]{:S(2)}, u32[]{:S(2)}) collective-permute-start(bf16[512,256]{1,0:T(8,128)(2,1)S(1)} %shard_map.61.head_ref), channel_id=1, source_target_pairs={{1,0},{2,1},{3,2},{4,3},{5,4},{6,5},{7,6},{9,8},{10,9},{11,10},{12... | collective-permute-start | bytes 786440 | tf_op jit(solution)/shard_map/ppermute | solution.py:24
  26.4 1.4 %collective-permute-start.3 = (f32[16,1,2176]{2,1,0:T(1,128)S(1)}, f32[16,1,2176]{2,1,0:T(1,128)S(1)}, u32[]{:S(2)}, u32[]{:S(2)}) collective-permute-start(f32[16,1,2176]{2,1,0:T(1,128)S(1)} %get-tuple-element.33), channel_id=1, source_target_pairs={{0,8},{8,0},{1,9},{9,1},{2,10},{10,2},{3,11},{11,3},{4,12},{12,4},... | collective-permute-start | bytes 417800 | tf_op jit(solution)/shard_map/ppermute | solution.py:457
  53.3 1.4 %collective-permute-start.4 = (f32[16,1,2176]{2,1,0:T(1,128)S(1)}, f32[16,1,2176]{2,1,0:T(1,128)S(1)}, u32[]{:S(2)}, u32[]{:S(2)}) collective-permute-start(f32[16,1,2176]{2,1,0:T(1,128)S(1)} %all_to_all.11.mine_ref), channel_id=1, source_target_pairs={{0,8},{8,0},{1,9},{9,1},{2,10},{10,2},{3,11},{11,3},{4,12},{12,4},... | collective-permute-start | bytes 417800 | tf_op jit(solution)/shard_map/ppermute | solution.py:460

commit v11 on v10

--- a/solution.py
+++ b/solution.py
@@ -92,59 +92,68 @@
     )(*(in_hbm(value) for value in (frames, w1, b1, w2)))
 
 
-def early_kernel(
-    frames_ref, near_ref, w1_ref, b1_ref, w2_ref, early_ref, middle_ref, hidden_ref, far_ref, xs, hs, sems
+def early_kernel(near_ref, w1_ref, b1_ref, w2_ref, out_ref, hidden_ref, hs):
+    half = LAG // 2
+    for at in range(0, hs.shape[0], D2):
+        hs[at : at + D2, :] = hidden_rows(near_ref, half - D1 - D2 + at, D2, w1_ref, b1_ref)
+    out_ref[...] = feature_rows(hs, 0, half, w2_ref)
+    hidden_ref[...] = hs[half:, :]
+
+
+def early_rows(near, w1, b1, w2):
+    vmem = pl.BlockSpec(memory_space=pltpu.VMEM)
+    half, hid = LAG // 2, w1.shape[1]
+    return pl.pallas_call(
+        early_kernel,
+        in_specs=[vmem] * 4,
+        out_specs=(vmem, vmem),
+        out_shape=(
+            jax.ShapeDtypeStruct((half, w2.shape[1]), BF16),
+            jax.ShapeDtypeStruct((D2, hid), BF16),
+        ),
+        scratch_shapes=[pltpu.VMEM((half + D2, hid), BF16)],
+        compiler_params=pltpu.CompilerParams(vmem_limit_bytes=8 * MIB),
+    )(near, w1, b1, w2)
+
+
+def middle_kernel(
+    frames_ref, near_ref, before_ref, w1_ref, b1_ref, w2_ref, middle_ref, hidden_ref, far_ref, xs, hs, sems
 ):
-    half = LAG // 2
-    first = half - D1 - D2
-    steps = (EARLY - LAG) // CHUNK
-
-    def arriving(step):
-        at = LAG + step * CHUNK
-        return pltpu.make_async_copy(
-            frames_ref.at[pl.ds(at, CHUNK)], xs.at[pl.ds(at - first, CHUNK)], sems.at[step]
-        )
-
-    for step in range(steps):
-        arriving(step).start()
+    rows = EARLY - LAG
+    now = pltpu.make_async_copy(frames_ref.at[pl.ds(LAG, rows)], xs.at[pl.ds(D1, rows)], sems.at[0])
     later = pltpu.make_async_copy(
-        frames_ref.at[pl.ds(EARLY - D1, far_ref.shape[0])], far_ref, sems.at[steps]
+        frames_ref.at[pl.ds(EARLY - D1, far_ref.shape[0])], far_ref, sems.at[1]
     )
+    now.start()
     later.start()
-    xs[: LAG - first, :] = near_ref[first:, :]
-    hs[: D2 + half, :] = hidden_rows(xs, 0, D2 + half, w1_ref, b1_ref)
-    for step in range(steps):
-        arriving(step).wait()
-        at = half + step * CHUNK
-        hs[at + D2 : at + D2 + CHUNK, :] = hidden_rows(xs, at + D2, CHUNK, w1_ref, b1_ref)
-        if step == 0:
-            early_ref[...] = feature_rows(hs, 0, half, w2_ref)
-        else:
-            middle_ref[(step - 1) * CHUNK : step * CHUNK, :] = feature_rows(hs, at - CHUNK, CHUNK, w2_ref)
-    middle_ref[(steps - 1) * CHUNK :, :] = feature_rows(hs, half + (steps - 1) * CHUNK, CHUNK, w2_ref)
-    hidden_ref[...] = hs[hs.shape[0] - D2 :, :]
+    xs[:D1, :] = near_ref[LAG - D1 :, :]
+    hs[:D2, :] = before_ref[...]
+    now.wait()
+    for at in range(0, rows, D2):
+        hs[D2 + at : 2 * D2 + at, :] = hidden_rows(xs, at, D2, w1_ref, b1_ref)
+    middle_ref[...] = feature_rows(hs, 0, rows, w2_ref)
+    hidden_ref[...] = hs[rows:, :]
     later.wait()
 
 
-def early_rows(frames, near, w1, b1, w2):
+def middle_rows(frames, near, before, w1, b1, w2):
     vmem = pl.BlockSpec(memory_space=pltpu.VMEM)
     hbm = pl.BlockSpec(memory_space=pltpu.HBM)
     rows, channels = frames.shape
-    half, hid, feat = LAG // 2, w1.shape[1], w2.shape[1]
-    shapes = ((half, feat), (EARLY - LAG, feat), (D2, hid), (rows - EARLY + D1, channels))
-    done = EARLY - half
-    return pl.pallas_call(
-        early_kernel,
-        in_specs=[hbm] + [vmem] * 4,
-        out_specs=(vmem,) * 4,
+    hid, feat = w1.shape[1], w2.shape[1]
+    shapes = ((EARLY - LAG, feat), (D2, hid), (rows - EARLY + D1, channels))
+    return pl.pallas_call(
+        middle_kernel,
+        in_specs=[hbm] + [vmem] * 5,
+        out_specs=(vmem,) * 3,
         out_shape=tuple(jax.ShapeDtypeStruct(shape, BF16) for shape in shapes),
         scratch_shapes=[
-            pltpu.VMEM((done + D1 + D2, channels), BF16),
-            pltpu.VMEM((done + D2, hid), BF16),
-            pltpu.SemaphoreType.DMA(((EARLY - LAG) // CHUNK + 1,)),
+            pltpu.VMEM((EARLY - LAG + D1, channels), BF16),
+            pltpu.VMEM((EARLY - LAG + D2, hid), BF16),
+            pltpu.SemaphoreType.DMA((2,)),
         ],
-        compiler_params=pltpu.CompilerParams(vmem_limit_bytes=16 * MIB),
-    )(in_hbm(frames), near, w1, b1, w2)
+        compiler_params=pltpu.CompilerParams(vmem_limit_bytes=12 * MIB),
+    )(in_hbm(frames), near, before, w1, b1, w2)
 
 
 def head_kernel(near_ref, halo_ref, w1_ref, b1_ref, w2_ref, out_ref, xs, hs):
@@ -256,19 +265,18 @@
     core = lax.axis_index("core")
     for ref, owner in ((kept_ref, core), (sent_ref, 1 - core)):
         extra = jnp.where(owner == 0, sums, diagonal)
-        for chunk, _, share_row, lanes in slots(ref.shape, feat):
-            source = pl.ds(owner * (feat // 2) + share_row, 1)
-            ref[chunk, 0:1, lanes] = packed[source, :]
-        for chunk in range(ref.shape[0]):
+        chunks = ref.shape[0]
+        for index, lanes in slots(ref.shape, feat):
+            at = pl.multiple_of(owner * (feat // 2) + index * chunks, 8)
+            ref[:, 0, lanes] = packed[pl.ds(at, chunks), :]
+        for chunk in range(chunks):
             part = extra[:, chunk * 128 : chunk * 128 + 128] if chunk < feat // 128 else jnp.zeros((1, 128), F32)
             ref[chunk, 0:1, ref.shape[2] - 128 :] = part
 
 
 def slots(shape, feat):
-    rows = (shape[2] - 128) // feat
-    for chunk in range(shape[0]):
-        for row in range(rows):
-            yield chunk, row, chunk * rows + row, slice(row * feat, (row + 1) * feat)
+    for index in range((shape[2] - 128) // feat):
+        yield index, slice(index * feat, (index + 1) * feat)
 
 
 def pack(feature, ahead_head, ahead_early, inst, lag, total, chips):
@@ -303,9 +311,10 @@
 
 def inverse_factor(work):
     size = work.shape[0]
+    parts = range(PANEL // 8)
     lane = lax.broadcasted_iota(jnp.int32, (PANEL, size), 1)
     sub = lax.broadcasted_iota(jnp.int32, (PANEL, size), 0)
-    sub_narrow = lax.broadcasted_iota(jnp.int32, (PANEL, 128), 0)
+    sub_narrow = lax.broadcasted_iota(jnp.int32, (8, 128), 0)
 
     def wide(x):
         return jnp.concatenate([x] * (size // 128), 1)
@@ -317,25 +326,42 @@
         stop = start + PANEL
         panel = work[start:stop, :]
         columns = [
-            jnp.broadcast_to(panel[:, start + k : start + k + 1], (PANEL, 128)) for k in range(PANEL)
+            [
+                jnp.broadcast_to(panel[8 * h : 8 * h + 8, start + k : start + k + 1], (8, 128))
+                for h in parts
+            ]
+            for k in range(PANEL)
         ]
         panel = jnp.where(
             (lane >= start) & (lane < stop), jnp.where(lane - start == sub, 1.0, 0.0), panel
         )
-        pivots = jnp.ones((PANEL, 128), F32)
-        pivot = spread(columns[0], 0)
+        rows = [panel[8 * h : 8 * h + 8, :] for h in parts]
+        pivots = [jnp.ones((8, 128), F32) for _ in parts]
+        pivot_row = {k: spread(columns[k][0], 0) for k in range(PANEL)}
+        panel_row = spread(rows[0], 0)
         for j in range(PANEL):
-            inverse = pl.reciprocal(pivot, approx=True)
-            pivots = jnp.where(sub_narrow == j, pivot, pivots)
+            inverse = pl.reciprocal(pivot_row[j], approx=True)
+            here, at = divmod(j, 8)
+            pivots[here] = jnp.where(sub_narrow == at, pivot_row[j], pivots[here])
             if j + 1 == PANEL:
                 break
-            factor = jnp.where(sub_narrow > j, columns[j], 0.0) * inverse
-            beside = [spread(columns[k], j) for k in range(j + 1, PANEL)]
-            pivot = spread(columns[j + 1], j + 1) - beside[0] * beside[0] * inverse
-            for k in range(j + 1, PANEL):
-                columns[k] = columns[k] - factor * beside[k - j - 1]
-            panel = panel - wide(factor) * spread(panel, j)
-        panel = panel * wide(lax.rsqrt(pivots))
+            there, after = divmod(j + 1, 8)
+            share = pivot_row[j + 1] * inverse
+            next_row = {
+                k: spread(columns[k][there], after) - share * pivot_row[k] for k in range(j + 1, PANEL)
+            }
+            next_panel_row = spread(rows[there], after) - wide(share) * panel_row
+            for h in parts:
+                if 8 * h + 7 <= j:
+                    continue
+                factor = columns[j][h] * inverse
+                if h == here:
+                    factor = jnp.where(sub_narrow > at, factor, 0.0)
+                for k in range(j + 1, PANEL):
+                    columns[k][h] = columns[k][h] - factor * pivot_row[k]
+                rows[h] = rows[h] - wide(factor) * panel_row
+            pivot_row, panel_row = next_row, next_panel_row
+        panel = jnp.concatenate([rows[h] * wide(lax.rsqrt(pivots[h])) for h in parts], 0)
         work[start:stop, :] = panel
         if stop < size:
             high, middle, low = three_parts(panel)
@@ -357,8 +383,10 @@
     core = lax.axis_index("core")
     extras = []
     for ref, owner in ((mine_ref, core), (other_ref, 1 - core)):
-        for chunk, _, share_row, lanes in slots(ref.shape, feat):
-            packed_ref[pl.ds(owner * (feat // 2) + share_row, 1), :] = ref[chunk, 0:1, lanes]
+        chunks = ref.shape[0]
+        for index, lanes in slots(ref.shape, feat):
+            at = pl.multiple_of(owner * (feat // 2) + index * chunks, 8)
+            packed_ref[pl.ds(at, chunks), :] = ref[:, 0, lanes]
         parts = [ref[chunk, 0:1, ref.shape[2] - 128 :] for chunk in range(feat // 128)]
         extras.append(jnp.concatenate(parts, 1))
     packed = packed_ref[...]
@@ -471,8 +499,9 @@
     )
     sent, near, *weights = tail_rows(frame_block, *weights)
     halo = passed_along(sent, "tm", 1)
-    early, middle, hidden, far = early_rows(frame_block, near, *weights)
+    early, before = early_rows(near, *weights)
     ahead_early = passed_along(early, "tm", -1)
+    middle, hidden, far = middle_rows(frame_block, near, before, *weights)
     head = head_rows(near, halo, *weights)
     ahead_head = passed_along(head, "tm", -1)
     feature = body(far, head, early, middle, hidden, *weights)

time: 68 us -> 66.9 us (0.984)
  waiting for transfers between devices: 8.56 us -> 6.37 us
  Pallas kernels: 25.3 us -> 26.2 us
    ppermute x3, waiting for transfers between devices: 5.86 us -> 3.67 us  [passed_along(): lax.ppermute(value, axis, [(source, source + steps) for source in range(f...]
    pallas_call x1 -> x2, Pallas kernels: 2.56 us -> 3.59 us  [the longest x1 2.17 us: middle_rows(): pl.pallas_call(middle_kernel, in_specs=[hbm] + [vmem] * 5, out_specs=(vme...]
  transfers between devices with their start and end apart: 5 -> 5, of which waited for: 4 -> 4; matrix products, arithmetic and copies ran while one was open for 0% -> 0% of each run, Pallas kernels for 14% -> 16%
where the time goes in v11:
time: 66.9 us; the launch traced here: 66.6 us
  Pallas kernels  26.2 us (39%)
  blocking collectives  25.3 us (38%)
  starting transfers between devices  7.54 us (11%)
  waiting for transfers between devices  6.37 us (10%)
  between operations  0.9 us (1%)
    all_to_all x1, blocking collectives, summed(): lax.all_to_all(parts, chips, 0, 0, tiled=True)  14.6 us
    all_to_all x1, blocking collectives, summed(): lax.all_to_all(jnp.broadcast_to(mine, parts.shape), chips, 0, 0, tiled=True)  10.8 us
    pallas_call x1, Pallas kernels, koopman_parts(): pl.pallas_call(koopman_kernel, in_specs=[pl.BlockSpec(memory_space=pltpu....  9.25 us
    ppermute x3, starting transfers between devices, passed_along(): lax.ppermute(value, axis, [(source, source + steps) for source in range(f...  7.46 us
    pallas_call x1, Pallas kernels, body(): pl.pallas_call(body_kernel, in_specs=[vmem] * 8, out_specs=vmem, out_shap...  4.53 us
    pallas_call x1, Pallas kernels, project(): pl.pallas_call(project_kernel, in_specs=[vmem] * 5, out_specs=(hbm, hbm),...  3.86 us
    ppermute x3, waiting for transfers between devices, passed_along(): lax.ppermute(value, axis, [(source, source + steps) for source in range(f...  3.67 us
    pallas_call x1, Pallas kernels, tail_rows(): pl.pallas_call(tail_kernel, in_specs=[hbm] * 4, out_specs=(vmem,) * 5, ou...  2.19 us
  transfers between devices with their start and end apart: 5, of which 4 were waited for; matrix products, arithmetic and copies ran while one was open for 0% of the time, Pallas kernels for 16%

profile of v11, /device:TPU:0, one launch (start us, length us, event | category | flops | bytes accessed | tf_op | source)
XLA Modules:
  0.0 66.6 jit_solution(11968480059889698247)
XLA Ops:
  0.6 2.2 %shard_map.59 = (bf16[320,256]{1,0:T(8,128)(2,1)S(1)}, bf16[1024,512]{1,0:T(8,128)(2,1)S(1)}, bf16[1024,512]{1,0:T(8,128)(2,1)S(1)}, f32[1,512]{1,0:T(1,128)S(1)}, bf16[1024,256]{1,0:T(8,128)(2,1)S(1)}) custom-call(bf16[4096,512]{1,0:T(8,128)(2,1)} %bitcast.6, bf16[1024,512]{1,0:T(8,128)(2,1)} %bitcast.8, f32[1,512]{1,0:T(1,128)} %bitcast.10, ...), custom_call_target="tpu_custom_call" | custom-call | tf_op jit(solution)/shard_map/pallas_call | solution.py:85
  2.8 4.9 %collective-permute-start = (bf16[320,256]{1,0:T(8,128)(2,1)S(1)}, bf16[320,256]{1,0:T(8,128)(2,1)S(1)}, u32[]{:S(2)}, u32[]{:S(2)}) collective-permute-start(bf16[320,256]{1,0:T(8,128)(2,1)S(1)} %get-tuple-element.27), channel_id=1, source_target_pairs={{0,1},{1,2},{2,3},{3,4},{4,5},{5,6},{6,7},{8,9},{9,10},{10,11},{11... | collective-permute-start | bytes 491528 | tf_op jit(solution)/shard_map/ppermute | solution.py:24
  7.7 1.4 %shard_map.60 = (bf16[512,256]{1,0:T(8,128)(2,1)S(1)}, bf16[256,512]{1,0:T(8,128)(2,1)S(1)}) custom-call(bf16[1024,512]{1,0:T(8,128)(2,1)S(1)} %get-tuple-element.21.near_ref, bf16[1024,512]{1,0:T(8,128)(2,1)S(1)} %get-tuple-element.22.w1_ref, f32[1,512]{1,0:T(1,128)S(1)} %get-tuple-element.23.b1_ref, bf16[1024,256]{1,0:T(8,128)(2,1)S(1)} %get-tuple-element.24.w2_ref), custom_call_target="tpu_custom_call" | custom-call | tf_op jit(solution)/shard_map/pallas_call | solution.py:106
  9.1 1.3 %collective-permute-start.2 = (bf16[512,256]{1,0:T(8,128)(2,1)S(1)}, bf16[512,256]{1,0:T(8,128)(2,1)S(1)}, u32[]{:S(2)}, u32[]{:S(2)}) collective-permute-start(bf16[512,256]{1,0:T(8,128)(2,1)S(1)} %get-tuple-element.28.early_ref), channel_id=1, source_target_pairs={{1,0},{2,1},{3,2},{4,3},{5,4},{6,5},{7,6},{9,8},{10,9},{11,10},{12... | collective-permute-start | bytes 786440 | tf_op jit(solution)/shard_map/ppermute | solution.py:24
  10.4 0.7 %collective-permute-done.halo_ref = bf16[320,256]{1,0:T(8,128)(2,1)S(1)} collective-permute-done((bf16[320,256]{1,0:T(8,128)(2,1)S(1)}, bf16[320,256]{1,0:T(8,128)(2,1)S(1)}, u32[]{:S(2)}, u32[]{:S(2)}) %collective-permute-start) | collective-permute-done | bytes 163872 | tf_op jit(solution)/shard_map/ppermute | solution.py:24
  11.1 1.1 %shard_map.62.head_ref = bf16[512,256]{1,0:T(8,128)(2,1)S(1)} custom-call(bf16[1024,512]{1,0:T(8,128)(2,1)S(1)} %get-tuple-element.21.near_ref, bf16[320,256]{1,0:T(8,128)(2,1)S(1)} %collective-permute-done.halo_ref, bf16[1024,512]{1,0:T(8,128)(2,1)S(1)} %get-tuple-element.22.w1_ref, f32[1,512]{1,0:T(1,128)S(1)} %get-tuple-element.23.b1_ref, ...), custom_call_target="tpu_custom_call" | custom-call | tf_op jit(solution)/shard_map/pallas_call | solution.py:176
  12.3 1.3 %collective-permute-start.1 = (bf16[512,256]{1,0:T(8,128)(2,1)S(1)}, bf16[512,256]{1,0:T(8,128)(2,1)S(1)}, u32[]{:S(2)}, u32[]{:S(2)}) collective-permute-start(bf16[512,256]{1,0:T(8,128)(2,1)S(1)} %shard_map.62.head_ref), channel_id=1, source_target_pairs={{1,0},{2,1},{3,2},{4,3},{5,4},{6,5},{7,6},{9,8},{10,9},{11,10},{12... | collective-permute-start | bytes 786440 | tf_op jit(solution)/shard_map/ppermute | solution.py:24
  13.6 2.2 %shard_map.61 = (bf16[512,256]{1,0:T(8,128)(2,1)S(1)}, bf16[256,512]{1,0:T(8,128)(2,1)S(1)}, bf16[2592,512]{1,0:T(8,128)(2,1)S(1)}) custom-call(bf16[4096,512]{1,0:T(8,128)(2,1)} %bitcast.7, bf16[1024,512]{1,0:T(8,128)(2,1)S(1)} %get-tuple-element.21.near_ref, bf16[256,512]{1,0:T(8,128)(2,1)S(1)} %get-tuple-element.25.before_ref, ...), custom_call_target="tpu_custom_call" | custom-call | tf_op jit(solution)/shard_map/pallas_call | solution.py:145
  15.8 4.5 %shard_map.63.feature_ref = bf16[4096,256]{1,0:T(8,128)(2,1)S(1)} custom-call(bf16[2592,512]{1,0:T(8,128)(2,1)S(1)} %get-tuple-element.26.far_ref, bf16[512,256]{1,0:T(8,128)(2,1)S(1)} %shard_map.62.head_ref, bf16[512,256]{1,0:T(8,128)(2,1)S(1)} %get-tuple-element.28.early_ref, bf16[512,256]{1,0:T(8,128)(2,1)S(1)} %get-tuple-element.29.middle_ref, ...), custom_call_target="tpu_custom_call" | custom-call | tf_op jit(solution)/shard_map/pallas_call | solution.py:205
  20.3 1.1 %shard_map.64 = (f32[256,256]{1,0:T(8,128)S(1)}, f32[256,256]{1,0:T(8,128)S(1)}, f32[8,256]{1,0:T(8,128)S(1)}) custom-call(bf16[4096,256]{1,0:T(8,128)(2,1)S(1)} %shard_map.63.feature_ref), custom_call_target="tpu_custom_call" | custom-call | tf_op jit(solution)/shard_map/pallas_call | solution.py:244
  21.4 0.0 collective-permute-done.2.ahead_early_ref
  21.5 3.0 %collective-permute-done.1.ahead_head_ref = bf16[512,256]{1,0:T(8,128)(2,1)S(1)} collective-permute-done((bf16[512,256]{1,0:T(8,128)(2,1)S(1)}, bf16[512,256]{1,0:T(8,128)(2,1)S(1)}, u32[]{:S(2)}, u32[]{:S(2)}) %collective-permute-start.1) | collective-permute-done | bytes 262176 | tf_op jit(solution)/shard_map/ppermute | solution.py:24
  24.4 0.5 shard_map.65
  24.9 0.1 collective-permute-start.3
  25.0 1.3 %collective-permute-done.3 = f32[16,1,2176]{2,1,0:T(1,128)S(1)} collective-permute-done((f32[16,1,2176]{2,1,0:T(1,128)S(1)}, f32[16,1,2176]{2,1,0:T(1,128)S(1)}, u32[]{:S(2)}, u32[]{:S(2)}) %collective-permute-start.3) | collective-permute-done | bytes 139296 | tf_op jit(solution)/shard_map/ppermute | solution.py:485
  26.3 0.1 add.3
  26.5 14.6 %all_to_all.10 = f32[16,1,2176]{2,1,0:T(1,128)S(1)} all-to-all(f32[16,1,2176]{2,1,0:T(1,128)S(1)} %add.3), channel_id=1, replica_groups=mesh['x'=2,'core'=2,'tm'=8] {'x','tm'}, dimensions={0} | all-to-all | bytes 278528 | tf_op jit(solution)/shard_map/all_to_all | solution.py:486
  41.0 0.1 reduce_sum.9
  41.1 0.1 broadcast_in_dim.12
  41.2 10.8 %all_to_all.11.mine_ref = f32[16,1,2176]{2,1,0:T(1,128)S(1)} all-to-all(f32[16,1,2176]{2,1,0:T(1,128)S(1)} %broadcast_in_dim.12), channel_id=1, replica_groups=mesh['x'=2,'core'=2,'tm'=8] {'x','tm'}, dimensions={0} | all-to-all | bytes 278528 | tf_op jit(solution)/shard_map/all_to_all | solution.py:487
  52.0 0.0 collective-permute-start.4
  52.0 1.4 %collective-permute-done.4.other_ref = f32[16,1,2176]{2,1,0:T(1,128)S(1)} collective-permute-done((f32[16,1,2176]{2,1,0:T(1,128)S(1)}, f32[16,1,2176]{2,1,0:T(1,128)S(1)}, u32[]{:S(2)}, u32[]{:S(2)}) %collective-permute-start.4) | collective-permute-done | bytes 139296 | tf_op jit(solution)/shard_map/ppermute | solution.py:488
  53.4 9.2 %shard_map.66 = (bf16[2,512,256]{2,1,0:T(8,128)(2,1)S(1)}, f32[2,8,256]{2,1,0:T(8,128)S(1)}) custom-call(f32[1]{0:T(128)} %constant.0.clone.1.scale_ref, f32[16,1,2176]{2,1,0:T(1,128)S(1)} %all_to_all.11.mine_ref, f32[16,1,2176]{2,1,0:T(1,128)S(1)} %collective-permute-done.4.other_ref), custom_call_target="tpu_custom_call" | custom-call | tf_op jit(solution)/shard_map/pallas_call | solution.py:419
  62.6 3.9 %shard_map.67 = (f32[4096,256]{1,0:T(8,128)}, f32[4096,256]{1,0:T(8,128)}) custom-call(bf16[4096,256]{1,0:T(8,128)(2,1)S(1)} %shard_map.63.feature_ref, bf16[512,256]{1,0:T(8,128)(2,1)S(1)} %collective-permute-done.1.ahead_head_ref, bf16[512,256]{1,0:T(8,128)(2,1)S(1)} %collective-permute-done.2.ahead_early_ref, ...), custom_call_target="tpu_custom_call" | custom-call | tf_op jit(solution)/shard_map/pallas_call | solution.py:468
Async XLA Ops:
  2.8 8.3 %collective-permute-start = (bf16[320,256]{1,0:T(8,128)(2,1)S(1)}, bf16[320,256]{1,0:T(8,128)(2,1)S(1)}, u32[]{:S(2)}, u32[]{:S(2)}) collective-permute-start(bf16[320,256]{1,0:T(8,128)(2,1)S(1)} %get-tuple-element.27), channel_id=1, source_target_pairs={{0,1},{1,2},{2,3},{3,4},{4,5},{5,6},{6,7},{8,9},{9,10},{10,11},{11... | collective-permute-start | bytes 491528 | tf_op jit(solution)/shard_map/ppermute | solution.py:24
  9.1 12.3 %collective-permute-start.2 = (bf16[512,256]{1,0:T(8,128)(2,1)S(1)}, bf16[512,256]{1,0:T(8,128)(2,1)S(1)}, u32[]{:S(2)}, u32[]{:S(2)}) collective-permute-start(bf16[512,256]{1,0:T(8,128)(2,1)S(1)} %get-tuple-element.28.early_ref), channel_id=1, source_target_pairs={{1,0},{2,1},{3,2},{4,3},{5,4},{6,5},{7,6},{9,8},{10,9},{11,10},{12... | collective-permute-start | bytes 786440 | tf_op jit(solution)/shard_map/ppermute | solution.py:24
  12.3 12.1 %collective-permute-start.1 = (bf16[512,256]{1,0:T(8,128)(2,1)S(1)}, bf16[512,256]{1,0:T(8,128)(2,1)S(1)}, u32[]{:S(2)}, u32[]{:S(2)}) collective-permute-start(bf16[512,256]{1,0:T(8,128)(2,1)S(1)} %shard_map.62.head_ref), channel_id=1, source_target_pairs={{1,0},{2,1},{3,2},{4,3},{5,4},{6,5},{7,6},{9,8},{10,9},{11,10},{12... | collective-permute-start | bytes 786440 | tf_op jit(solution)/shard_map/ppermute | solution.py:24
  24.9 1.4 %collective-permute-start.3 = (f32[16,1,2176]{2,1,0:T(1,128)S(1)}, f32[16,1,2176]{2,1,0:T(1,128)S(1)}, u32[]{:S(2)}, u32[]{:S(2)}) collective-permute-start(f32[16,1,2176]{2,1,0:T(1,128)S(1)} %get-tuple-element.35), channel_id=1, source_target_pairs={{0,8},{8,0},{1,9},{9,1},{2,10},{10,2},{3,11},{11,3},{4,12},{12,4},... | collective-permute-start | bytes 417800 | tf_op jit(solution)/shard_map/ppermute | solution.py:485
  52.0 1.4 %collective-permute-start.4 = (f32[16,1,2176]{2,1,0:T(1,128)S(1)}, f32[16,1,2176]{2,1,0:T(1,128)S(1)}, u32[]{:S(2)}, u32[]{:S(2)}) collective-permute-start(f32[16,1,2176]{2,1,0:T(1,128)S(1)} %all_to_all.11.mine_ref), channel_id=1, source_target_pairs={{0,8},{8,0},{1,9},{9,1},{2,10},{10,2},{3,11},{11,3},{4,12},{12,4},... | collective-permute-start | bytes 417800 | tf_op jit(solution)/shard_map/ppermute | solution.py:488

commit v12 on v11

--- a/solution.py
+++ b/solution.py
@@ -12,6 +12,7 @@
 CHUNK = 512
 EARLY = 1536
 PANEL = 16
+SUPER = 32
 MIB = 1024 * 1024
 
 F32 = jnp.float32
@@ -309,12 +310,11 @@
     return jnp.dot(left, right, preferred_element_type=F32)
 
 
-def inverse_factor(work):
-    size = work.shape[0]
-    parts = range(PANEL // 8)
-    lane = lax.broadcasted_iota(jnp.int32, (PANEL, size), 1)
-    sub = lax.broadcasted_iota(jnp.int32, (PANEL, size), 0)
+def eliminate(rows, start, size):
+    lane = lax.broadcasted_iota(jnp.int32, (8, size), 1) - start
+    sub = lax.broadcasted_iota(jnp.int32, (8, size), 0)
     sub_narrow = lax.broadcasted_iota(jnp.int32, (8, 128), 0)
+    tiles = range(len(rows))
 
     def wide(x):
         return jnp.concatenate([x] * (size // 128), 1)
@@ -322,46 +322,51 @@
     def spread(x, j):
         return jnp.broadcast_to(x[j : j + 1, :], x.shape)
 
-    for start in range(0, size, PANEL):
-        stop = start + PANEL
-        panel = work[start:stop, :]
-        columns = [
-            [
-                jnp.broadcast_to(panel[8 * h : 8 * h + 8, start + k : start + k + 1], (8, 128))
-                for h in parts
-            ]
-            for k in range(PANEL)
-        ]
-        panel = jnp.where(
-            (lane >= start) & (lane < stop), jnp.where(lane - start == sub, 1.0, 0.0), panel
-        )
-        rows = [panel[8 * h : 8 * h + 8, :] for h in parts]
-        pivots = [jnp.ones((8, 128), F32) for _ in parts]
-        pivot_row = {k: spread(columns[k][0], 0) for k in range(PANEL)}
-        panel_row = spread(rows[0], 0)
-        for j in range(PANEL):
-            inverse = pl.reciprocal(pivot_row[j], approx=True)
-            here, at = divmod(j, 8)
-            pivots[here] = jnp.where(sub_narrow == at, pivot_row[j], pivots[here])
-            if j + 1 == PANEL:
-                break
+    columns = [
+        [jnp.broadcast_to(rows[h][:, start + k : start + k + 1], (8, 128)) for h in tiles]
+        for k in range(PANEL)
+    ]
+    inside = (lane >= 0) & (lane < PANEL)
+    rows = [jnp.where(inside, jnp.where(lane == sub + 8 * h, 1.0, 0.0), rows[h]) for h in tiles]
+    pivots = [jnp.ones((8, 128), F32) for _ in range(PANEL // 8)]
+    pivot_row = {k: spread(columns[k][0], 0) for k in range(PANEL)}
+    panel_row = spread(rows[0], 0)
+    for j in range(PANEL):
+        inverse = pl.reciprocal(pivot_row[j], approx=True)
+        here, at = divmod(j, 8)
+        pivots[here] = jnp.where(sub_narrow == at, pivot_row[j], pivots[here])
+        last = j + 1 == PANEL
+        if not last:
             there, after = divmod(j + 1, 8)
             share = pivot_row[j + 1] * inverse
             next_row = {
                 k: spread(columns[k][there], after) - share * pivot_row[k] for k in range(j + 1, PANEL)
             }
             next_panel_row = spread(rows[there], after) - wide(share) * panel_row
-            for h in parts:
-                if 8 * h + 7 <= j:
-                    continue
-                factor = columns[j][h] * inverse
-                if h == here:
-                    factor = jnp.where(sub_narrow > at, factor, 0.0)
-                for k in range(j + 1, PANEL):
-                    columns[k][h] = columns[k][h] - factor * pivot_row[k]
-                rows[h] = rows[h] - wide(factor) * panel_row
+        for h in tiles:
+            if 8 * h + 7 <= j:
+                continue
+            factor = columns[j][h] * inverse
+            if h == here:
+                factor = jnp.where(sub_narrow > at, factor, 0.0)
+            for k in range(j + 1, PANEL):
+                columns[k][h] = columns[k][h] - factor * pivot_row[k]
+            rows[h] = rows[h] - wide(factor) * panel_row
+        if not last:
             pivot_row, panel_row = next_row, next_panel_row
-        panel = jnp.concatenate([rows[h] * wide(lax.rsqrt(pivots[h])) for h in parts], 0)
+    return [rows[h] * wide(lax.rsqrt(pivots[h])) if h < len(pivots) else rows[h] for h in tiles]
+
+
+def inverse_factor(work):
+    size = work.shape[0]
+    for start in range(0, size, SUPER):
+        stop = start + SUPER
+        rows = [work[at : at + 8, :] for at in range(start, stop, 8)]
+        for at in range(0, SUPER, PANEL):
+            rows[at // 8 :] = eliminate(rows[at // 8 :], start + at, size)
+        row = lax.broadcasted_iota(jnp.int32, (SUPER, size), 0)
+        column = lax.broadcasted_iota(jnp.int32, (SUPER, size), 1) - start
+        panel = jnp.where((column > row) & (column < SUPER), 0.0, jnp.concatenate(rows, 0))
         work[start:stop, :] = panel
         if stop < size:
             high, middle, low = three_parts(panel)
@@ -377,7 +382,10 @@
     return jnp.where(column <= row, work[...], 0.0)
 
 
-def koopman_kernel(scale_ref, mine_ref, other_ref, split_ref, shift_ref, work, packed_ref):
+def koopman_kernel(
+    scale_ref, mine_ref, other_ref, feature_ref, ahead_head_ref, ahead_early_ref, moved_out, residual_out,
+    work, packed_ref, split_ref, shift_ref, moved, residual, sems,
+):
     feat = packed_ref.shape[1]
     scale = scale_ref[0]
     core = lax.axis_index("core")
@@ -412,31 +420,18 @@
         split_ref[index, feat:, :] = (matrix - high.astype(F32)).astype(BF16)
         shift = jnp.sum(mean_column * matrix, 0, keepdims=True)
         shift_ref[index] = jnp.broadcast_to(shift, (8, feat))
-
-
-def koopman_parts(scale, mine, other, feat):
-    vmem = pl.BlockSpec(memory_space=pltpu.VMEM)
-    return pl.pallas_call(
-        koopman_kernel,
-        in_specs=[pl.BlockSpec(memory_space=pltpu.SMEM), vmem, vmem],
-        out_specs=(vmem, vmem),
-        out_shape=(
-            jax.ShapeDtypeStruct((2, 2 * feat, feat), BF16),
-            jax.ShapeDtypeStruct((2, 8, feat), F32),
-        ),
-        scratch_shapes=[pltpu.VMEM((feat, feat), F32), pltpu.VMEM((feat, feat), F32)],
-        compiler_params=pltpu.CompilerParams(vmem_limit_bytes=12 * MIB),
-    )(scale, mine, other)
-
-
-def project_kernel(
+    project_rows(
+        feature_ref, ahead_head_ref, ahead_early_ref, split_ref, shift_ref, moved_out, residual_out, moved, residual, sems
+    )
+
+
+def project_rows(
     feature_ref, ahead_head_ref, ahead_early_ref, split_ref, shift_ref, moved_out, residual_out, moved, residual, sems
 ):
     rows = feature_ref.shape[0]
-    half = LAG // 2
     at_end = lax.axis_index("tm") == lax.axis_size("tm") - 1
 
-    def product(block, index):
+    def image(block, index):
         twice = jnp.concatenate([block, block], 1)
         return jnp.dot(twice, split_ref[index], preferred_element_type=F32) - shift_ref[index][0:1]
 
@@ -448,9 +443,9 @@
             later = feature_ref[start : start + CHUNK, :]
         else:
             later = (ahead_head_ref if start == rows else ahead_early_ref)[...]
-        now = product(feature_ref[here, :], 1)
+        now = image(feature_ref[here, :], 1)
         moved[here, :] = now
-        gap = product(later, 0) - now
+        gap = image(later, 0) - now
         residual[here, :] = gap if start < rows else jnp.where(at_end, 0.0, gap)
         for index, (source, target) in enumerate(((moved, moved_out), (residual, residual_out))):
             copy = pltpu.make_async_copy(source.at[here], target.at[here], sems.at[index, step])
@@ -460,23 +455,27 @@
         copy.wait()
 
 
-def project(feature, ahead_head, ahead_early, split, shift):
+def project(scale, mine, other, feature, ahead_head, ahead_early):
     rows, feat = feature.shape
     vmem = pl.BlockSpec(memory_space=pltpu.VMEM)
     hbm = pl.BlockSpec(memory_space=pltpu.HBM)
     out = jax.ShapeDtypeStruct((rows, feat), F32)
     return pl.pallas_call(
-        project_kernel,
-        in_specs=[vmem] * 5,
+        koopman_kernel,
+        in_specs=[pl.BlockSpec(memory_space=pltpu.SMEM)] + [vmem] * 5,
         out_specs=(hbm, hbm),
         out_shape=(out, out),
         scratch_shapes=[
+            pltpu.VMEM((feat, feat), F32),
+            pltpu.VMEM((feat, feat), F32),
+            pltpu.VMEM((2, 2 * feat, feat), BF16),
+            pltpu.VMEM((2, 8, feat), F32),
             pltpu.VMEM((rows, feat), F32),
             pltpu.VMEM((rows, feat), F32),
             pltpu.SemaphoreType.DMA((2, rows // CHUNK)),
         ],
-        compiler_params=pltpu.CompilerParams(vmem_limit_bytes=24 * MIB),
-    )(feature, ahead_head, ahead_early, split, shift)
+        compiler_params=pltpu.CompilerParams(vmem_limit_bytes=32 * MIB),
+    )(scale, mine, other, feature, ahead_head, ahead_early)
 
 
 def summed(kept, sent):
@@ -511,8 +510,7 @@
     replicas = lax.axis_size("x") * lax.axis_size("core")
     pair_count = replicas * (row_count * lax.axis_size("tm") - LAG)
     scale = jnp.full((1,), 1.0 / (2.0 * pair_count), F32)
-    split, shift = koopman_parts(scale, mine, other, feat)
-    propagated, residual = project(feature, ahead_head, ahead_early, split, shift)
+    propagated, residual = project(scale, mine, other, feature, ahead_head, ahead_early)
     return (propagated[None], residual[None])
 
 

time: 66.9 us -> 66.3 us (level)
  Pallas kernels: 26.2 us -> 25.5 us
    pallas_call x2 -> x1, Pallas kernels: 13.1 us -> 12.5 us  [project(): pl.pallas_call(koopman_kernel, in_specs=[pl.BlockSpec(memory_space=pltpu....]
where the time goes in v12:
time: 66.3 us; the launch traced here: 66 us
  Pallas kernels  25.5 us (38%)
  blocking collectives  25.3 us (38%)
  starting transfers between devices  7.54 us (11%)
  waiting for transfers between devices  6.37 us (10%)
  between operations  0.89 us (1%)
    all_to_all x1, blocking collectives, summed(): lax.all_to_all(parts, chips, 0, 0, tiled=True)  14.6 us
    pallas_call x1, Pallas kernels, project(): pl.pallas_call(koopman_kernel, in_specs=[pl.BlockSpec(memory_space=pltpu....  12.5 us
    all_to_all x1, blocking collectives, summed(): lax.all_to_all(jnp.broadcast_to(mine, parts.shape), chips, 0, 0, tiled=True)  10.8 us
    ppermute x3, starting transfers between devices, passed_along(): lax.ppermute(value, axis, [(source, source + steps) for source in range(f...  7.46 us
    pallas_call x1, Pallas kernels, body(): pl.pallas_call(body_kernel, in_specs=[vmem] * 8, out_specs=vmem, out_shap...  4.53 us
    ppermute x3, waiting for transfers between devices, passed_along(): lax.ppermute(value, axis, [(source, source + steps) for source in range(f...  3.67 us
    pallas_call x1, Pallas kernels, tail_rows(): pl.pallas_call(tail_kernel, in_specs=[hbm] * 4, out_specs=(vmem,) * 5, ou...  2.19 us
    pallas_call x1, Pallas kernels, middle_rows(): pl.pallas_call(middle_kernel, in_specs=[hbm] + [vmem] * 5, out_specs=(vme...  2.17 us
  transfers between devices with their start and end apart: 5, of which 4 were waited for; matrix products, arithmetic and copies ran while one was open for 0% of the time, Pallas kernels for 16%

profile of v12, /device:TPU:0, one launch (start us, length us, event | category | flops | bytes accessed | tf_op | source)
XLA Modules:
  0.0 66.0 jit_solution(13345210622184759757)
XLA Ops:
  0.6 2.2 %shard_map.59 = (bf16[320,256]{1,0:T(8,128)(2,1)S(1)}, bf16[1024,512]{1,0:T(8,128)(2,1)S(1)}, bf16[1024,512]{1,0:T(8,128)(2,1)S(1)}, f32[1,512]{1,0:T(1,128)S(1)}, bf16[1024,256]{1,0:T(8,128)(2,1)S(1)}) custom-call(bf16[4096,512]{1,0:T(8,128)(2,1)} %bitcast.6, bf16[1024,512]{1,0:T(8,128)(2,1)} %bitcast.8, f32[1,512]{1,0:T(1,128)} %bitcast.10, ...), custom_call_target="tpu_custom_call" | custom-call | tf_op jit(solution)/shard_map/pallas_call | solution.py:86
  2.8 4.9 %collective-permute-start = (bf16[320,256]{1,0:T(8,128)(2,1)S(1)}, bf16[320,256]{1,0:T(8,128)(2,1)S(1)}, u32[]{:S(2)}, u32[]{:S(2)}) collective-permute-start(bf16[320,256]{1,0:T(8,128)(2,1)S(1)} %get-tuple-element.25), channel_id=1, source_target_pairs={{0,1},{1,2},{2,3},{3,4},{4,5},{5,6},{6,7},{8,9},{9,10},{10,11},{11... | collective-permute-start | bytes 491528 | tf_op jit(solution)/shard_map/ppermute | solution.py:25
  7.7 1.4 %shard_map.60 = (bf16[512,256]{1,0:T(8,128)(2,1)S(1)}, bf16[256,512]{1,0:T(8,128)(2,1)S(1)}) custom-call(bf16[1024,512]{1,0:T(8,128)(2,1)S(1)} %get-tuple-element.19.near_ref, bf16[1024,512]{1,0:T(8,128)(2,1)S(1)} %get-tuple-element.20.w1_ref, f32[1,512]{1,0:T(1,128)S(1)} %get-tuple-element.21.b1_ref, bf16[1024,256]{1,0:T(8,128)(2,1)S(1)} %get-tuple-element.22.w2_ref), custom_call_target="tpu_custom_call" | custom-call | tf_op jit(solution)/shard_map/pallas_call | solution.py:107
  9.1 1.3 %collective-permute-start.2 = (bf16[512,256]{1,0:T(8,128)(2,1)S(1)}, bf16[512,256]{1,0:T(8,128)(2,1)S(1)}, u32[]{:S(2)}, u32[]{:S(2)}) collective-permute-start(bf16[512,256]{1,0:T(8,128)(2,1)S(1)} %get-tuple-element.26.early_ref), channel_id=1, source_target_pairs={{1,0},{2,1},{3,2},{4,3},{5,4},{6,5},{7,6},{9,8},{10,9},{11,10},{12... | collective-permute-start | bytes 786440 | tf_op jit(solution)/shard_map/ppermute | solution.py:25
  10.4 0.7 %collective-permute-done.halo_ref = bf16[320,256]{1,0:T(8,128)(2,1)S(1)} collective-permute-done((bf16[320,256]{1,0:T(8,128)(2,1)S(1)}, bf16[320,256]{1,0:T(8,128)(2,1)S(1)}, u32[]{:S(2)}, u32[]{:S(2)}) %collective-permute-start) | collective-permute-done | bytes 163872 | tf_op jit(solution)/shard_map/ppermute | solution.py:25
  11.1 1.1 %shard_map.62.head_ref = bf16[512,256]{1,0:T(8,128)(2,1)S(1)} custom-call(bf16[1024,512]{1,0:T(8,128)(2,1)S(1)} %get-tuple-element.19.near_ref, bf16[320,256]{1,0:T(8,128)(2,1)S(1)} %collective-permute-done.halo_ref, bf16[1024,512]{1,0:T(8,128)(2,1)S(1)} %get-tuple-element.20.w1_ref, f32[1,512]{1,0:T(1,128)S(1)} %get-tuple-element.21.b1_ref, ...), custom_call_target="tpu_custom_call" | custom-call | tf_op jit(solution)/shard_map/pallas_call | solution.py:177
  12.3 1.3 %collective-permute-start.1 = (bf16[512,256]{1,0:T(8,128)(2,1)S(1)}, bf16[512,256]{1,0:T(8,128)(2,1)S(1)}, u32[]{:S(2)}, u32[]{:S(2)}) collective-permute-start(bf16[512,256]{1,0:T(8,128)(2,1)S(1)} %shard_map.62.head_ref), channel_id=1, source_target_pairs={{1,0},{2,1},{3,2},{4,3},{5,4},{6,5},{7,6},{9,8},{10,9},{11,10},{12... | collective-permute-start | bytes 786440 | tf_op jit(solution)/shard_map/ppermute | solution.py:25
  13.6 2.2 %shard_map.61 = (bf16[512,256]{1,0:T(8,128)(2,1)S(1)}, bf16[256,512]{1,0:T(8,128)(2,1)S(1)}, bf16[2592,512]{1,0:T(8,128)(2,1)S(1)}) custom-call(bf16[4096,512]{1,0:T(8,128)(2,1)} %bitcast.7, bf16[1024,512]{1,0:T(8,128)(2,1)S(1)} %get-tuple-element.19.near_ref, bf16[256,512]{1,0:T(8,128)(2,1)S(1)} %get-tuple-element.23.before_ref, ...), custom_call_target="tpu_custom_call" | custom-call | tf_op jit(solution)/shard_map/pallas_call | solution.py:146
  15.8 4.5 %shard_map.63.feature_ref = bf16[4096,256]{1,0:T(8,128)(2,1)S(1)} custom-call(bf16[2592,512]{1,0:T(8,128)(2,1)S(1)} %get-tuple-element.24.far_ref, bf16[512,256]{1,0:T(8,128)(2,1)S(1)} %shard_map.62.head_ref, bf16[512,256]{1,0:T(8,128)(2,1)S(1)} %get-tuple-element.26.early_ref, bf16[512,256]{1,0:T(8,128)(2,1)S(1)} %get-tuple-element.27.middle_ref, ...), custom_call_target="tpu_custom_call" | custom-call | tf_op jit(solution)/shard_map/pallas_call | solution.py:206
  20.3 1.1 %shard_map.64 = (f32[256,256]{1,0:T(8,128)S(1)}, f32[256,256]{1,0:T(8,128)S(1)}, f32[8,256]{1,0:T(8,128)S(1)}) custom-call(bf16[4096,256]{1,0:T(8,128)(2,1)S(1)} %shard_map.63.feature_ref), custom_call_target="tpu_custom_call" | custom-call | tf_op jit(solution)/shard_map/pallas_call | solution.py:245
  21.4 0.0 collective-permute-done.2.ahead_early_ref
  21.5 3.0 %collective-permute-done.1.ahead_head_ref = bf16[512,256]{1,0:T(8,128)(2,1)S(1)} collective-permute-done((bf16[512,256]{1,0:T(8,128)(2,1)S(1)}, bf16[512,256]{1,0:T(8,128)(2,1)S(1)}, u32[]{:S(2)}, u32[]{:S(2)}) %collective-permute-start.1) | collective-permute-done | bytes 262176 | tf_op jit(solution)/shard_map/ppermute | solution.py:25
  24.4 0.5 shard_map.65
  24.9 0.1 collective-permute-start.3
  25.0 1.3 %collective-permute-done.3 = f32[16,1,2176]{2,1,0:T(1,128)S(1)} collective-permute-done((f32[16,1,2176]{2,1,0:T(1,128)S(1)}, f32[16,1,2176]{2,1,0:T(1,128)S(1)}, u32[]{:S(2)}, u32[]{:S(2)}) %collective-permute-start.3) | collective-permute-done | bytes 139296 | tf_op jit(solution)/shard_map/ppermute | solution.py:484
  26.3 0.1 add.3
  26.5 14.6 %all_to_all.10 = f32[16,1,2176]{2,1,0:T(1,128)S(1)} all-to-all(f32[16,1,2176]{2,1,0:T(1,128)S(1)} %add.3), channel_id=1, replica_groups=mesh['x'=2,'core'=2,'tm'=8] {'x','tm'}, dimensions={0} | all-to-all | bytes 278528 | tf_op jit(solution)/shard_map/all_to_all | solution.py:485
  41.0 0.1 reduce_sum.9
  41.1 0.1 broadcast_in_dim.12
  41.2 10.8 %all_to_all.11.mine_ref = f32[16,1,2176]{2,1,0:T(1,128)S(1)} all-to-all(f32[16,1,2176]{2,1,0:T(1,128)S(1)} %broadcast_in_dim.12), channel_id=1, replica_groups=mesh['x'=2,'core'=2,'tm'=8] {'x','tm'}, dimensions={0} | all-to-all | bytes 278528 | tf_op jit(solution)/shard_map/all_to_all | solution.py:486
  52.0 0.0 collective-permute-start.4
  52.0 1.4 %collective-permute-done.4.other_ref = f32[16,1,2176]{2,1,0:T(1,128)S(1)} collective-permute-done((f32[16,1,2176]{2,1,0:T(1,128)S(1)}, f32[16,1,2176]{2,1,0:T(1,128)S(1)}, u32[]{:S(2)}, u32[]{:S(2)}) %collective-permute-start.4) | collective-permute-done | bytes 139296 | tf_op jit(solution)/shard_map/ppermute | solution.py:487
  53.4 12.5 %shard_map.66 = (f32[4096,256]{1,0:T(8,128)}, f32[4096,256]{1,0:T(8,128)}) custom-call(f32[1]{0:T(128)} %constant.0.clone.1.scale_ref, f32[16,1,2176]{2,1,0:T(1,128)S(1)} %all_to_all.11.mine_ref, f32[16,1,2176]{2,1,0:T(1,128)S(1)} %collective-permute-done.4.other_ref, bf16[4096,256]{1,0:T(8,128)(2,1)S(1)} %shard_map.63.feature_ref, ...), custom_call_target="tpu_custom_call" | custom-call | tf_op jit(solution)/shard_map/pallas_call | solution.py:463
Async XLA Ops:
  2.8 8.3 %collective-permute-start = (bf16[320,256]{1,0:T(8,128)(2,1)S(1)}, bf16[320,256]{1,0:T(8,128)(2,1)S(1)}, u32[]{:S(2)}, u32[]{:S(2)}) collective-permute-start(bf16[320,256]{1,0:T(8,128)(2,1)S(1)} %get-tuple-element.25), channel_id=1, source_target_pairs={{0,1},{1,2},{2,3},{3,4},{4,5},{5,6},{6,7},{8,9},{9,10},{10,11},{11... | collective-permute-start | bytes 491528 | tf_op jit(solution)/shard_map/ppermute | solution.py:25
  9.1 12.3 %collective-permute-start.2 = (bf16[512,256]{1,0:T(8,128)(2,1)S(1)}, bf16[512,256]{1,0:T(8,128)(2,1)S(1)}, u32[]{:S(2)}, u32[]{:S(2)}) collective-permute-start(bf16[512,256]{1,0:T(8,128)(2,1)S(1)} %get-tuple-element.26.early_ref), channel_id=1, source_target_pairs={{1,0},{2,1},{3,2},{4,3},{5,4},{6,5},{7,6},{9,8},{10,9},{11,10},{12... | collective-permute-start | bytes 786440 | tf_op jit(solution)/shard_map/ppermute | solution.py:25
  12.3 12.1 %collective-permute-start.1 = (bf16[512,256]{1,0:T(8,128)(2,1)S(1)}, bf16[512,256]{1,0:T(8,128)(2,1)S(1)}, u32[]{:S(2)}, u32[]{:S(2)}) collective-permute-start(bf16[512,256]{1,0:T(8,128)(2,1)S(1)} %shard_map.62.head_ref), channel_id=1, source_target_pairs={{1,0},{2,1},{3,2},{4,3},{5,4},{6,5},{7,6},{9,8},{10,9},{11,10},{12... | collective-permute-start | bytes 786440 | tf_op jit(solution)/shard_map/ppermute | solution.py:25
  24.9 1.4 %collective-permute-start.3 = (f32[16,1,2176]{2,1,0:T(1,128)S(1)}, f32[16,1,2176]{2,1,0:T(1,128)S(1)}, u32[]{:S(2)}, u32[]{:S(2)}) collective-permute-start(f32[16,1,2176]{2,1,0:T(1,128)S(1)} %get-tuple-element.33), channel_id=1, source_target_pairs={{0,8},{8,0},{1,9},{9,1},{2,10},{10,2},{3,11},{11,3},{4,12},{12,4},... | collective-permute-start | bytes 417800 | tf_op jit(solution)/shard_map/ppermute | solution.py:484
  52.0 1.4 %collective-permute-start.4 = (f32[16,1,2176]{2,1,0:T(1,128)S(1)}, f32[16,1,2176]{2,1,0:T(1,128)S(1)}, u32[]{:S(2)}, u32[]{:S(2)}) collective-permute-start(f32[16,1,2176]{2,1,0:T(1,128)S(1)} %all_to_all.11.mine_ref), channel_id=1, source_target_pairs={{0,8},{8,0},{1,9},{9,1},{2,10},{10,2},{3,11},{11,3},{4,12},{12,4},... | collective-permute-start | bytes 417800 | tf_op jit(solution)/shard_map/ppermute | solution.py:487

commit v13 on v12

--- a/solution.py
+++ b/solution.py
@@ -328,33 +328,50 @@
     ]
     inside = (lane >= 0) & (lane < PANEL)
     rows = [jnp.where(inside, jnp.where(lane == sub + 8 * h, 1.0, 0.0), rows[h]) for h in tiles]
-    pivots = [jnp.ones((8, 128), F32) for _ in range(PANEL // 8)]
-    pivot_row = {k: spread(columns[k][0], 0) for k in range(PANEL)}
-    panel_row = spread(rows[0], 0)
-    for j in range(PANEL):
-        inverse = pl.reciprocal(pivot_row[j], approx=True)
+    inverses = [jnp.ones((8, 128), F32) for _ in range(PANEL // 8)]
+    first, second = ({k: spread(columns[k][0], r) for k in range(PANEL)} for r in (0, 1))
+    first_row, second_row = (spread(rows[0], r) for r in (0, 1))
+    for j in range(0, PANEL, 2):
         here, at = divmod(j, 8)
-        pivots[here] = jnp.where(sub_narrow == at, pivot_row[j], pivots[here])
-        last = j + 1 == PANEL
-        if not last:
-            there, after = divmod(j + 1, 8)
-            share = pivot_row[j + 1] * inverse
-            next_row = {
-                k: spread(columns[k][there], after) - share * pivot_row[k] for k in range(j + 1, PANEL)
-            }
-            next_panel_row = spread(rows[there], after) - wide(share) * panel_row
+        inverse = pl.reciprocal(first[j], approx=True)
+        determinant = first[j] * second[j + 1] - first[j + 1] * first[j + 1]
+        inverse_second = first[j] * pl.reciprocal(determinant, approx=True)
+        inverses[here] = jnp.where(sub_narrow == at, inverse, inverses[here])
+        inverses[here] = jnp.where(sub_narrow == at + 1, inverse_second, inverses[here])
+        share = first[j + 1] * inverse
+        second = {k: second[k] - share * first[k] for k in range(j + 1, PANEL)}
+        second_row = second_row - wide(share) * first_row
+        following = []
+        if j + 2 < PANEL:
+            there, after = divmod(j + 2, 8)
+            for r in (0, 1):
+                one = first[j + 2 + r] * inverse
+                two = second[j + 2 + r] * inverse_second
+                following.append(
+                    {
+                        k: spread(columns[k][there], after + r) - one * first[k] - two * second[k]
+                        for k in range(j + 2, PANEL)
+                    }
+                )
+                following.append(
+                    spread(rows[there], after + r) - wide(one) * first_row - wide(two) * second_row
+                )
         for h in tiles:
             if 8 * h + 7 <= j:
                 continue
-            factor = columns[j][h] * inverse
+            one = columns[j][h] * inverse
             if h == here:
-                factor = jnp.where(sub_narrow > at, factor, 0.0)
-            for k in range(j + 1, PANEL):
-                columns[k][h] = columns[k][h] - factor * pivot_row[k]
-            rows[h] = rows[h] - wide(factor) * panel_row
-        if not last:
-            pivot_row, panel_row = next_row, next_panel_row
-    return [rows[h] * wide(lax.rsqrt(pivots[h])) if h < len(pivots) else rows[h] for h in tiles]
+                one = jnp.where(sub_narrow > at, one, 0.0)
+            two = (columns[j + 1][h] - one * first[j + 1]) * inverse_second
+            if h == here:
+                two = jnp.where(sub_narrow > at + 1, two, 0.0)
+            for k in range(j + 2, PANEL):
+                columns[k][h] = columns[k][h] - one * first[k] - two * second[k]
+            rows[h] = rows[h] - wide(one) * first_row - wide(two) * second_row
+        if following:
+            first, first_row, second, second_row = following
+    scales = [x * lax.rsqrt(x) for x in inverses]
+    return [rows[h] * wide(scales[h]) if h < len(scales) else rows[h] for h in tiles]
 
 
 def inverse_factor(work):

time: 66.3 us -> 66.8 us (level)
  no operation moved by 1% of the time
where the time goes in v13:
time: 66.8 us; the launch traced here: 66.5 us
  Pallas kernels  26.1 us (39%)
  blocking collectives  25.3 us (38%)
  starting transfers between devices  7.54 us (11%)
  waiting for transfers between devices  6.37 us (10%)
  between operations  0.89 us (1%)
    all_to_all x1, blocking collectives, summed(): lax.all_to_all(parts, chips, 0, 0, tiled=True)  14.6 us
    pallas_call x1, Pallas kernels, project(): pl.pallas_call(koopman_kernel, in_specs=[pl.BlockSpec(memory_space=pltpu....  13 us
    all_to_all x1, blocking collectives, summed(): lax.all_to_all(jnp.broadcast_to(mine, parts.shape), chips, 0, 0, tiled=True)  10.8 us
    ppermute x3, starting transfers between devices, passed_along(): lax.ppermute(value, axis, [(source, source + steps) for source in range(f...  7.46 us
    pallas_call x1, Pallas kernels, body(): pl.pallas_call(body_kernel, in_specs=[vmem] * 8, out_specs=vmem, out_shap...  4.53 us
    ppermute x3, waiting for transfers between devices, passed_along(): lax.ppermute(value, axis, [(source, source + steps) for source in range(f...  3.67 us
    pallas_call x1, Pallas kernels, tail_rows(): pl.pallas_call(tail_kernel, in_specs=[hbm] * 4, out_specs=(vmem,) * 5, ou...  2.19 us
    pallas_call x1, Pallas kernels, middle_rows(): pl.pallas_call(middle_kernel, in_specs=[hbm] + [vmem] * 5, out_specs=(vme...  2.17 us
  transfers between devices with their start and end apart: 5, of which 4 were waited for; matrix products, arithmetic and copies ran while one was open for 0% of the time, Pallas kernels for 16%

profile of v13, /device:TPU:0, one launch (start us, length us, event | category | flops | bytes accessed | tf_op | source)
XLA Modules:
  0.0 66.5 jit_solution(9840229434058766626)
XLA Ops:
  0.6 2.2 %shard_map.59 = (bf16[320,256]{1,0:T(8,128)(2,1)S(1)}, bf16[1024,512]{1,0:T(8,128)(2,1)S(1)}, bf16[1024,512]{1,0:T(8,128)(2,1)S(1)}, f32[1,512]{1,0:T(1,128)S(1)}, bf16[1024,256]{1,0:T(8,128)(2,1)S(1)}) custom-call(bf16[4096,512]{1,0:T(8,128)(2,1)} %bitcast.6, bf16[1024,512]{1,0:T(8,128)(2,1)} %bitcast.8, f32[1,512]{1,0:T(1,128)} %bitcast.10, ...), custom_call_target="tpu_custom_call" | custom-call | tf_op jit(solution)/shard_map/pallas_call | solution.py:86
  2.8 4.9 %collective-permute-start = (bf16[320,256]{1,0:T(8,128)(2,1)S(1)}, bf16[320,256]{1,0:T(8,128)(2,1)S(1)}, u32[]{:S(2)}, u32[]{:S(2)}) collective-permute-start(bf16[320,256]{1,0:T(8,128)(2,1)S(1)} %get-tuple-element.25), channel_id=1, source_target_pairs={{0,1},{1,2},{2,3},{3,4},{4,5},{5,6},{6,7},{8,9},{9,10},{10,11},{11... | collective-permute-start | bytes 491528 | tf_op jit(solution)/shard_map/ppermute | solution.py:25
  7.7 1.4 %shard_map.60 = (bf16[512,256]{1,0:T(8,128)(2,1)S(1)}, bf16[256,512]{1,0:T(8,128)(2,1)S(1)}) custom-call(bf16[1024,512]{1,0:T(8,128)(2,1)S(1)} %get-tuple-element.19.near_ref, bf16[1024,512]{1,0:T(8,128)(2,1)S(1)} %get-tuple-element.20.w1_ref, f32[1,512]{1,0:T(1,128)S(1)} %get-tuple-element.21.b1_ref, bf16[1024,256]{1,0:T(8,128)(2,1)S(1)} %get-tuple-element.22.w2_ref), custom_call_target="tpu_custom_call" | custom-call | tf_op jit(solution)/shard_map/pallas_call | solution.py:107
  9.1 1.3 %collective-permute-start.2 = (bf16[512,256]{1,0:T(8,128)(2,1)S(1)}, bf16[512,256]{1,0:T(8,128)(2,1)S(1)}, u32[]{:S(2)}, u32[]{:S(2)}) collective-permute-start(bf16[512,256]{1,0:T(8,128)(2,1)S(1)} %get-tuple-element.26.early_ref), channel_id=1, source_target_pairs={{1,0},{2,1},{3,2},{4,3},{5,4},{6,5},{7,6},{9,8},{10,9},{11,10},{12... | collective-permute-start | bytes 786440 | tf_op jit(solution)/shard_map/ppermute | solution.py:25
  10.4 0.7 %collective-permute-done.halo_ref = bf16[320,256]{1,0:T(8,128)(2,1)S(1)} collective-permute-done((bf16[320,256]{1,0:T(8,128)(2,1)S(1)}, bf16[320,256]{1,0:T(8,128)(2,1)S(1)}, u32[]{:S(2)}, u32[]{:S(2)}) %collective-permute-start) | collective-permute-done | bytes 163872 | tf_op jit(solution)/shard_map/ppermute | solution.py:25
  11.1 1.1 %shard_map.62.head_ref = bf16[512,256]{1,0:T(8,128)(2,1)S(1)} custom-call(bf16[1024,512]{1,0:T(8,128)(2,1)S(1)} %get-tuple-element.19.near_ref, bf16[320,256]{1,0:T(8,128)(2,1)S(1)} %collective-permute-done.halo_ref, bf16[1024,512]{1,0:T(8,128)(2,1)S(1)} %get-tuple-element.20.w1_ref, f32[1,512]{1,0:T(1,128)S(1)} %get-tuple-element.21.b1_ref, ...), custom_call_target="tpu_custom_call" | custom-call | tf_op jit(solution)/shard_map/pallas_call | solution.py:177
  12.3 1.3 %collective-permute-start.1 = (bf16[512,256]{1,0:T(8,128)(2,1)S(1)}, bf16[512,256]{1,0:T(8,128)(2,1)S(1)}, u32[]{:S(2)}, u32[]{:S(2)}) collective-permute-start(bf16[512,256]{1,0:T(8,128)(2,1)S(1)} %shard_map.62.head_ref), channel_id=1, source_target_pairs={{1,0},{2,1},{3,2},{4,3},{5,4},{6,5},{7,6},{9,8},{10,9},{11,10},{12... | collective-permute-start | bytes 786440 | tf_op jit(solution)/shard_map/ppermute | solution.py:25
  13.6 2.2 %shard_map.61 = (bf16[512,256]{1,0:T(8,128)(2,1)S(1)}, bf16[256,512]{1,0:T(8,128)(2,1)S(1)}, bf16[2592,512]{1,0:T(8,128)(2,1)S(1)}) custom-call(bf16[4096,512]{1,0:T(8,128)(2,1)} %bitcast.7, bf16[1024,512]{1,0:T(8,128)(2,1)S(1)} %get-tuple-element.19.near_ref, bf16[256,512]{1,0:T(8,128)(2,1)S(1)} %get-tuple-element.23.before_ref, ...), custom_call_target="tpu_custom_call" | custom-call | tf_op jit(solution)/shard_map/pallas_call | solution.py:146
  15.8 4.5 %shard_map.63.feature_ref = bf16[4096,256]{1,0:T(8,128)(2,1)S(1)} custom-call(bf16[2592,512]{1,0:T(8,128)(2,1)S(1)} %get-tuple-element.24.far_ref, bf16[512,256]{1,0:T(8,128)(2,1)S(1)} %shard_map.62.head_ref, bf16[512,256]{1,0:T(8,128)(2,1)S(1)} %get-tuple-element.26.early_ref, bf16[512,256]{1,0:T(8,128)(2,1)S(1)} %get-tuple-element.27.middle_ref, ...), custom_call_target="tpu_custom_call" | custom-call | tf_op jit(solution)/shard_map/pallas_call | solution.py:206
  20.3 1.1 %shard_map.64 = (f32[256,256]{1,0:T(8,128)S(1)}, f32[256,256]{1,0:T(8,128)S(1)}, f32[8,256]{1,0:T(8,128)S(1)}) custom-call(bf16[4096,256]{1,0:T(8,128)(2,1)S(1)} %shard_map.63.feature_ref), custom_call_target="tpu_custom_call" | custom-call | tf_op jit(solution)/shard_map/pallas_call | solution.py:245
  21.4 0.0 collective-permute-done.2.ahead_early_ref
  21.5 3.0 %collective-permute-done.1.ahead_head_ref = bf16[512,256]{1,0:T(8,128)(2,1)S(1)} collective-permute-done((bf16[512,256]{1,0:T(8,128)(2,1)S(1)}, bf16[512,256]{1,0:T(8,128)(2,1)S(1)}, u32[]{:S(2)}, u32[]{:S(2)}) %collective-permute-start.1) | collective-permute-done | bytes 262176 | tf_op jit(solution)/shard_map/ppermute | solution.py:25
  24.4 0.5 shard_map.65
  24.9 0.1 collective-permute-start.3
  25.0 1.3 %collective-permute-done.3 = f32[16,1,2176]{2,1,0:T(1,128)S(1)} collective-permute-done((f32[16,1,2176]{2,1,0:T(1,128)S(1)}, f32[16,1,2176]{2,1,0:T(1,128)S(1)}, u32[]{:S(2)}, u32[]{:S(2)}) %collective-permute-start.3) | collective-permute-done | bytes 139296 | tf_op jit(solution)/shard_map/ppermute | solution.py:501
  26.3 0.1 add.3
  26.5 14.6 %all_to_all.10 = f32[16,1,2176]{2,1,0:T(1,128)S(1)} all-to-all(f32[16,1,2176]{2,1,0:T(1,128)S(1)} %add.3), channel_id=1, replica_groups=mesh['x'=2,'core'=2,'tm'=8] {'x','tm'}, dimensions={0} | all-to-all | bytes 278528 | tf_op jit(solution)/shard_map/all_to_all | solution.py:502
  41.0 0.1 reduce_sum.9
  41.1 0.1 broadcast_in_dim.12
  41.2 10.8 %all_to_all.11.mine_ref = f32[16,1,2176]{2,1,0:T(1,128)S(1)} all-to-all(f32[16,1,2176]{2,1,0:T(1,128)S(1)} %broadcast_in_dim.12), channel_id=1, replica_groups=mesh['x'=2,'core'=2,'tm'=8] {'x','tm'}, dimensions={0} | all-to-all | bytes 278528 | tf_op jit(solution)/shard_map/all_to_all | solution.py:503
  52.0 0.0 collective-permute-start.4
  52.0 1.4 %collective-permute-done.4.other_ref = f32[16,1,2176]{2,1,0:T(1,128)S(1)} collective-permute-done((f32[16,1,2176]{2,1,0:T(1,128)S(1)}, f32[16,1,2176]{2,1,0:T(1,128)S(1)}, u32[]{:S(2)}, u32[]{:S(2)}) %collective-permute-start.4) | collective-permute-done | bytes 139296 | tf_op jit(solution)/shard_map/ppermute | solution.py:504
  53.4 13.0 %shard_map.66 = (f32[4096,256]{1,0:T(8,128)}, f32[4096,256]{1,0:T(8,128)}) custom-call(f32[1]{0:T(128)} %constant.0.clone.1.scale_ref, f32[16,1,2176]{2,1,0:T(1,128)S(1)} %all_to_all.11.mine_ref, f32[16,1,2176]{2,1,0:T(1,128)S(1)} %collective-permute-done.4.other_ref, bf16[4096,256]{1,0:T(8,128)(2,1)S(1)} %shard_map.63.feature_ref, ...), custom_call_target="tpu_custom_call" | custom-call | tf_op jit(solution)/shard_map/pallas_call | solution.py:480
Async XLA Ops:
  2.8 8.3 %collective-permute-start = (bf16[320,256]{1,0:T(8,128)(2,1)S(1)}, bf16[320,256]{1,0:T(8,128)(2,1)S(1)}, u32[]{:S(2)}, u32[]{:S(2)}) collective-permute-start(bf16[320,256]{1,0:T(8,128)(2,1)S(1)} %get-tuple-element.25), channel_id=1, source_target_pairs={{0,1},{1,2},{2,3},{3,4},{4,5},{5,6},{6,7},{8,9},{9,10},{10,11},{11... | collective-permute-start | bytes 491528 | tf_op jit(solution)/shard_map/ppermute | solution.py:25
  9.1 12.3 %collective-permute-start.2 = (bf16[512,256]{1,0:T(8,128)(2,1)S(1)}, bf16[512,256]{1,0:T(8,128)(2,1)S(1)}, u32[]{:S(2)}, u32[]{:S(2)}) collective-permute-start(bf16[512,256]{1,0:T(8,128)(2,1)S(1)} %get-tuple-element.26.early_ref), channel_id=1, source_target_pairs={{1,0},{2,1},{3,2},{4,3},{5,4},{6,5},{7,6},{9,8},{10,9},{11,10},{12... | collective-permute-start | bytes 786440 | tf_op jit(solution)/shard_map/ppermute | solution.py:25
  12.3 12.1 %collective-permute-start.1 = (bf16[512,256]{1,0:T(8,128)(2,1)S(1)}, bf16[512,256]{1,0:T(8,128)(2,1)S(1)}, u32[]{:S(2)}, u32[]{:S(2)}) collective-permute-start(bf16[512,256]{1,0:T(8,128)(2,1)S(1)} %shard_map.62.head_ref), channel_id=1, source_target_pairs={{1,0},{2,1},{3,2},{4,3},{5,4},{6,5},{7,6},{9,8},{10,9},{11,10},{12... | collective-permute-start | bytes 786440 | tf_op jit(solution)/shard_map/ppermute | solution.py:25
  24.9 1.4 %collective-permute-start.3 = (f32[16,1,2176]{2,1,0:T(1,128)S(1)}, f32[16,1,2176]{2,1,0:T(1,128)S(1)}, u32[]{:S(2)}, u32[]{:S(2)}) collective-permute-start(f32[16,1,2176]{2,1,0:T(1,128)S(1)} %get-tuple-element.33), channel_id=1, source_target_pairs={{0,8},{8,0},{1,9},{9,1},{2,10},{10,2},{3,11},{11,3},{4,12},{12,4},... | collective-permute-start | bytes 417800 | tf_op jit(solution)/shard_map/ppermute | solution.py:501
  52.0 1.4 %collective-permute-start.4 = (f32[16,1,2176]{2,1,0:T(1,128)S(1)}, f32[16,1,2176]{2,1,0:T(1,128)S(1)}, u32[]{:S(2)}, u32[]{:S(2)}) collective-permute-start(f32[16,1,2176]{2,1,0:T(1,128)S(1)} %all_to_all.11.mine_ref), channel_id=1, source_target_pairs={{0,8},{8,0},{1,9},{9,1},{2,10},{10,2},{3,11},{11,3},{4,12},{12,4},... | collective-permute-start | bytes 417800 | tf_op jit(solution)/shard_map/ppermute | solution.py:504

commit v14 on v12

--- a/solution.py
+++ b/solution.py
@@ -12,7 +12,6 @@
 CHUNK = 512
 EARLY = 1536
 PANEL = 16
-SUPER = 32
 MIB = 1024 * 1024
 
 F32 = jnp.float32
@@ -310,7 +309,8 @@
     return jnp.dot(left, right, preferred_element_type=F32)
 
 
-def eliminate(rows, start, size):
+def eliminate(rows, columns, start):
+    size = rows[0].shape[1]
     lane = lax.broadcasted_iota(jnp.int32, (8, size), 1) - start
     sub = lax.broadcasted_iota(jnp.int32, (8, size), 0)
     sub_narrow = lax.broadcasted_iota(jnp.int32, (8, 128), 0)
@@ -322,27 +322,20 @@
     def spread(x, j):
         return jnp.broadcast_to(x[j : j + 1, :], x.shape)
 
-    columns = [
-        [jnp.broadcast_to(rows[h][:, start + k : start + k + 1], (8, 128)) for h in tiles]
-        for k in range(PANEL)
-    ]
     inside = (lane >= 0) & (lane < PANEL)
     rows = [jnp.where(inside, jnp.where(lane == sub + 8 * h, 1.0, 0.0), rows[h]) for h in tiles]
-    pivots = [jnp.ones((8, 128), F32) for _ in range(PANEL // 8)]
-    pivot_row = {k: spread(columns[k][0], 0) for k in range(PANEL)}
-    panel_row = spread(rows[0], 0)
+    pivots = [jnp.ones((8, 128), F32) for _ in tiles]
+    pivot = spread(columns[0][0], 0)
     for j in range(PANEL):
-        inverse = pl.reciprocal(pivot_row[j], approx=True)
+        inverse = pl.reciprocal(pivot, approx=True)
         here, at = divmod(j, 8)
-        pivots[here] = jnp.where(sub_narrow == at, pivot_row[j], pivots[here])
-        last = j + 1 == PANEL
-        if not last:
-            there, after = divmod(j + 1, 8)
-            share = pivot_row[j + 1] * inverse
-            next_row = {
-                k: spread(columns[k][there], after) - share * pivot_row[k] for k in range(j + 1, PANEL)
-            }
-            next_panel_row = spread(rows[there], after) - wide(share) * panel_row
+        pivots[here] = jnp.where(sub_narrow == at, pivot, pivots[here])
+        if j + 1 == PANEL:
+            break
+        beside = {k: spread(columns[k][here], at) for k in range(j + 1, PANEL)}
+        there, after = divmod(j + 1, 8)
+        pivot = spread(columns[j + 1][there], after) - beside[j + 1] * beside[j + 1] * inverse
+        panel_row = spread(rows[here], at)
         for h in tiles:
             if 8 * h + 7 <= j:
                 continue
@@ -350,33 +343,38 @@
             if h == here:
                 factor = jnp.where(sub_narrow > at, factor, 0.0)
             for k in range(j + 1, PANEL):
-                columns[k][h] = columns[k][h] - factor * pivot_row[k]
+                columns[k][h] = columns[k][h] - factor * beside[k]
             rows[h] = rows[h] - wide(factor) * panel_row
-        if not last:
-            pivot_row, panel_row = next_row, next_panel_row
-    return [rows[h] * wide(lax.rsqrt(pivots[h])) if h < len(pivots) else rows[h] for h in tiles]
+    return [rows[h] * wide(lax.rsqrt(pivots[h])) for h in tiles]
 
 
 def inverse_factor(work):
     size = work.shape[0]
-    for start in range(0, size, SUPER):
-        stop = start + SUPER
-        rows = [work[at : at + 8, :] for at in range(start, stop, 8)]
-        for at in range(0, SUPER, PANEL):
-            rows[at // 8 :] = eliminate(rows[at // 8 :], start + at, size)
-        row = lax.broadcasted_iota(jnp.int32, (SUPER, size), 0)
-        column = lax.broadcasted_iota(jnp.int32, (SUPER, size), 1) - start
-        panel = jnp.where((column > row) & (column < SUPER), 0.0, jnp.concatenate(rows, 0))
-        work[start:stop, :] = panel
-        if stop < size:
-            high, middle, low = three_parts(panel)
-            left = jnp.concatenate([high, high, middle, high, low, middle], 0)
-            right = jnp.concatenate([high, middle, high, low, high, middle], 0)
-            first = stop // 128 * 128
-            update = gram(left[:, first:], right)
-            kept = lax.broadcasted_iota(jnp.int32, (size - stop, size), 1)
-            kept = (kept < start) | (kept >= stop)
-            work[stop:, :] = jnp.where(kept, work[stop:, :], 0.0) - update[stop - first :]
+    tiles = range(PANEL // 8)
+
+    def step(index, carry):
+        start = pl.multiple_of(index * PANEL, PANEL)
+        panel = work[pl.ds(start, PANEL), :]
+        near = pltpu.roll(panel, lax.rem(size - start, size), 1)
+        columns = [
+            [jnp.broadcast_to(near[8 * h : 8 * h + 8, k : k + 1], (8, 128)) for h in tiles]
+            for k in range(PANEL)
+        ]
+        rows = eliminate([panel[8 * h : 8 * h + 8, :] for h in tiles], columns, start)
+        panel = jnp.concatenate(rows, 0)
+        high, middle, low = three_parts(panel)
+        left = jnp.concatenate([high, high, middle, high, low, middle], 0)
+        right = jnp.concatenate([high, middle, high, low, high, middle], 0)
+        update = gram(left, right)
+        row = lax.broadcasted_iota(jnp.int32, (size, size), 0)
+        column = lax.broadcasted_iota(jnp.int32, (size, size), 1) - start
+        old = work[...]
+        rest = jnp.where((column >= 0) & (column < PANEL), 0.0, old) - update
+        work[...] = jnp.where(row >= start + PANEL, rest, old)
+        work[pl.ds(start, PANEL), :] = panel
+        return carry
+
+    lax.fori_loop(0, size // PANEL, step, 0)
     row = lax.broadcasted_iota(jnp.int32, (size, size), 0)
     column = lax.broadcasted_iota(jnp.int32, (size, size), 1)
     return jnp.where(column <= row, work[...], 0.0)

time: 66.3 us -> 68.4 us (1.032)
  Pallas kernels: 25.5 us -> 27.7 us
    pallas_call x1, Pallas kernels: 12.5 us -> 14.6 us  [project(): pl.pallas_call(koopman_kernel, in_specs=[pl.BlockSpec(memory_space=pltpu....]
  transfers between devices with their start and end apart: 5 -> 5, of which waited for: 4 -> 4; matrix products, arithmetic and copies ran while one was open for 0% -> 0% of each run, Pallas kernels for 16% -> 15%
where the time goes in v14:
time: 68.4 us; the launch traced here: 68.1 us
  Pallas kernels  27.7 us (40%)
  blocking collectives  25.3 us (37%)
  starting transfers between devices  7.54 us (11%)
  waiting for transfers between devices  6.37 us (9%)
  between operations  0.89 us (1%)
    pallas_call x1, Pallas kernels, project(): pl.pallas_call(koopman_kernel, in_specs=[pl.BlockSpec(memory_space=pltpu....  14.6 us
    all_to_all x1, blocking collectives, summed(): lax.all_to_all(parts, chips, 0, 0, tiled=True)  14.6 us
    all_to_all x1, blocking collectives, summed(): lax.all_to_all(jnp.broadcast_to(mine, parts.shape), chips, 0, 0, tiled=True)  10.8 us
    ppermute x3, starting transfers between devices, passed_along(): lax.ppermute(value, axis, [(source, source + steps) for source in range(f...  7.46 us
    pallas_call x1, Pallas kernels, body(): pl.pallas_call(body_kernel, in_specs=[vmem] * 8, out_specs=vmem, out_shap...  4.53 us
    ppermute x3, waiting for transfers between devices, passed_along(): lax.ppermute(value, axis, [(source, source + steps) for source in range(f...  3.67 us
    pallas_call x1, Pallas kernels, tail_rows(): pl.pallas_call(tail_kernel, in_specs=[hbm] * 4, out_specs=(vmem,) * 5, ou...  2.19 us
    pallas_call x1, Pallas kernels, middle_rows(): pl.pallas_call(middle_kernel, in_specs=[hbm] + [vmem] * 5, out_specs=(vme...  2.17 us
  transfers between devices with their start and end apart: 5, of which 4 were waited for; matrix products, arithmetic and copies ran while one was open for 0% of the time, Pallas kernels for 15%

profile of v14, /device:TPU:0, one launch (start us, length us, event | category | flops | bytes accessed | tf_op | source)
XLA Modules:
  0.0 68.1 jit_solution(5117482523273107908)
XLA Ops:
  0.6 2.2 %shard_map.59 = (bf16[320,256]{1,0:T(8,128)(2,1)S(1)}, bf16[1024,512]{1,0:T(8,128)(2,1)S(1)}, bf16[1024,512]{1,0:T(8,128)(2,1)S(1)}, f32[1,512]{1,0:T(1,128)S(1)}, bf16[1024,256]{1,0:T(8,128)(2,1)S(1)}) custom-call(bf16[4096,512]{1,0:T(8,128)(2,1)} %bitcast.6, bf16[1024,512]{1,0:T(8,128)(2,1)} %bitcast.8, f32[1,512]{1,0:T(1,128)} %bitcast.10, ...), custom_call_target="tpu_custom_call" | custom-call | tf_op jit(solution)/shard_map/pallas_call | solution.py:85
  2.8 4.9 %collective-permute-start = (bf16[320,256]{1,0:T(8,128)(2,1)S(1)}, bf16[320,256]{1,0:T(8,128)(2,1)S(1)}, u32[]{:S(2)}, u32[]{:S(2)}) collective-permute-start(bf16[320,256]{1,0:T(8,128)(2,1)S(1)} %get-tuple-element.25), channel_id=1, source_target_pairs={{0,1},{1,2},{2,3},{3,4},{4,5},{5,6},{6,7},{8,9},{9,10},{10,11},{11... | collective-permute-start | bytes 491528 | tf_op jit(solution)/shard_map/ppermute | solution.py:24
  7.7 1.4 %shard_map.60 = (bf16[512,256]{1,0:T(8,128)(2,1)S(1)}, bf16[256,512]{1,0:T(8,128)(2,1)S(1)}) custom-call(bf16[1024,512]{1,0:T(8,128)(2,1)S(1)} %get-tuple-element.19.near_ref, bf16[1024,512]{1,0:T(8,128)(2,1)S(1)} %get-tuple-element.20.w1_ref, f32[1,512]{1,0:T(1,128)S(1)} %get-tuple-element.21.b1_ref, bf16[1024,256]{1,0:T(8,128)(2,1)S(1)} %get-tuple-element.22.w2_ref), custom_call_target="tpu_custom_call" | custom-call | tf_op jit(solution)/shard_map/pallas_call | solution.py:106
  9.1 1.3 %collective-permute-start.2 = (bf16[512,256]{1,0:T(8,128)(2,1)S(1)}, bf16[512,256]{1,0:T(8,128)(2,1)S(1)}, u32[]{:S(2)}, u32[]{:S(2)}) collective-permute-start(bf16[512,256]{1,0:T(8,128)(2,1)S(1)} %get-tuple-element.26.early_ref), channel_id=1, source_target_pairs={{1,0},{2,1},{3,2},{4,3},{5,4},{6,5},{7,6},{9,8},{10,9},{11,10},{12... | collective-permute-start | bytes 786440 | tf_op jit(solution)/shard_map/ppermute | solution.py:24
  10.4 0.7 %collective-permute-done.halo_ref = bf16[320,256]{1,0:T(8,128)(2,1)S(1)} collective-permute-done((bf16[320,256]{1,0:T(8,128)(2,1)S(1)}, bf16[320,256]{1,0:T(8,128)(2,1)S(1)}, u32[]{:S(2)}, u32[]{:S(2)}) %collective-permute-start) | collective-permute-done | bytes 163872 | tf_op jit(solution)/shard_map/ppermute | solution.py:24
  11.1 1.1 %shard_map.62.head_ref = bf16[512,256]{1,0:T(8,128)(2,1)S(1)} custom-call(bf16[1024,512]{1,0:T(8,128)(2,1)S(1)} %get-tuple-element.19.near_ref, bf16[320,256]{1,0:T(8,128)(2,1)S(1)} %collective-permute-done.halo_ref, bf16[1024,512]{1,0:T(8,128)(2,1)S(1)} %get-tuple-element.20.w1_ref, f32[1,512]{1,0:T(1,128)S(1)} %get-tuple-element.21.b1_ref, ...), custom_call_target="tpu_custom_call" | custom-call | tf_op jit(solution)/shard_map/pallas_call | solution.py:176
  12.3 1.3 %collective-permute-start.1 = (bf16[512,256]{1,0:T(8,128)(2,1)S(1)}, bf16[512,256]{1,0:T(8,128)(2,1)S(1)}, u32[]{:S(2)}, u32[]{:S(2)}) collective-permute-start(bf16[512,256]{1,0:T(8,128)(2,1)S(1)} %shard_map.62.head_ref), channel_id=1, source_target_pairs={{1,0},{2,1},{3,2},{4,3},{5,4},{6,5},{7,6},{9,8},{10,9},{11,10},{12... | collective-permute-start | bytes 786440 | tf_op jit(solution)/shard_map/ppermute | solution.py:24
  13.6 2.2 %shard_map.61 = (bf16[512,256]{1,0:T(8,128)(2,1)S(1)}, bf16[256,512]{1,0:T(8,128)(2,1)S(1)}, bf16[2592,512]{1,0:T(8,128)(2,1)S(1)}) custom-call(bf16[4096,512]{1,0:T(8,128)(2,1)} %bitcast.7, bf16[1024,512]{1,0:T(8,128)(2,1)S(1)} %get-tuple-element.19.near_ref, bf16[256,512]{1,0:T(8,128)(2,1)S(1)} %get-tuple-element.23.before_ref, ...), custom_call_target="tpu_custom_call" | custom-call | tf_op jit(solution)/shard_map/pallas_call | solution.py:145
  15.8 4.5 %shard_map.63.feature_ref = bf16[4096,256]{1,0:T(8,128)(2,1)S(1)} custom-call(bf16[2592,512]{1,0:T(8,128)(2,1)S(1)} %get-tuple-element.24.far_ref, bf16[512,256]{1,0:T(8,128)(2,1)S(1)} %shard_map.62.head_ref, bf16[512,256]{1,0:T(8,128)(2,1)S(1)} %get-tuple-element.26.early_ref, bf16[512,256]{1,0:T(8,128)(2,1)S(1)} %get-tuple-element.27.middle_ref, ...), custom_call_target="tpu_custom_call" | custom-call | tf_op jit(solution)/shard_map/pallas_call | solution.py:205
  20.3 1.1 %shard_map.64 = (f32[256,256]{1,0:T(8,128)S(1)}, f32[256,256]{1,0:T(8,128)S(1)}, f32[8,256]{1,0:T(8,128)S(1)}) custom-call(bf16[4096,256]{1,0:T(8,128)(2,1)S(1)} %shard_map.63.feature_ref), custom_call_target="tpu_custom_call" | custom-call | tf_op jit(solution)/shard_map/pallas_call | solution.py:244
  21.4 0.0 collective-permute-done.2.ahead_early_ref
  21.5 3.0 %collective-permute-done.1.ahead_head_ref = bf16[512,256]{1,0:T(8,128)(2,1)S(1)} collective-permute-done((bf16[512,256]{1,0:T(8,128)(2,1)S(1)}, bf16[512,256]{1,0:T(8,128)(2,1)S(1)}, u32[]{:S(2)}, u32[]{:S(2)}) %collective-permute-start.1) | collective-permute-done | bytes 262176 | tf_op jit(solution)/shard_map/ppermute | solution.py:24
  24.4 0.5 shard_map.65
  24.9 0.1 collective-permute-start.3
  25.0 1.3 %collective-permute-done.3 = f32[16,1,2176]{2,1,0:T(1,128)S(1)} collective-permute-done((f32[16,1,2176]{2,1,0:T(1,128)S(1)}, f32[16,1,2176]{2,1,0:T(1,128)S(1)}, u32[]{:S(2)}, u32[]{:S(2)}) %collective-permute-start.3) | collective-permute-done | bytes 139296 | tf_op jit(solution)/shard_map/ppermute | solution.py:482
  26.3 0.1 add.3
  26.5 14.6 %all_to_all.10 = f32[16,1,2176]{2,1,0:T(1,128)S(1)} all-to-all(f32[16,1,2176]{2,1,0:T(1,128)S(1)} %add.3), channel_id=1, replica_groups=mesh['x'=2,'core'=2,'tm'=8] {'x','tm'}, dimensions={0} | all-to-all | bytes 278528 | tf_op jit(solution)/shard_map/all_to_all | solution.py:483
  41.0 0.1 reduce_sum.9
  41.1 0.1 broadcast_in_dim.12
  41.2 10.8 %all_to_all.11.mine_ref = f32[16,1,2176]{2,1,0:T(1,128)S(1)} all-to-all(f32[16,1,2176]{2,1,0:T(1,128)S(1)} %broadcast_in_dim.12), channel_id=1, replica_groups=mesh['x'=2,'core'=2,'tm'=8] {'x','tm'}, dimensions={0} | all-to-all | bytes 278528 | tf_op jit(solution)/shard_map/all_to_all | solution.py:484
  52.0 0.0 collective-permute-start.4
  52.0 1.4 %collective-permute-done.4.other_ref = f32[16,1,2176]{2,1,0:T(1,128)S(1)} collective-permute-done((f32[16,1,2176]{2,1,0:T(1,128)S(1)}, f32[16,1,2176]{2,1,0:T(1,128)S(1)}, u32[]{:S(2)}, u32[]{:S(2)}) %collective-permute-start.4) | collective-permute-done | bytes 139296 | tf_op jit(solution)/shard_map/ppermute | solution.py:485
  53.4 14.6 %shard_map.66 = (f32[4096,256]{1,0:T(8,128)}, f32[4096,256]{1,0:T(8,128)}) custom-call(f32[1]{0:T(128)} %constant.0.clone.1.scale_ref, f32[16,1,2176]{2,1,0:T(1,128)S(1)} %all_to_all.11.mine_ref, f32[16,1,2176]{2,1,0:T(1,128)S(1)} %collective-permute-done.4.other_ref, bf16[4096,256]{1,0:T(8,128)(2,1)S(1)} %shard_map.63.feature_ref, ...), custom_call_target="tpu_custom_call" | custom-call | tf_op jit(solution)/shard_map/pallas_call | solution.py:461
Async XLA Ops:
  2.8 8.3 %collective-permute-start = (bf16[320,256]{1,0:T(8,128)(2,1)S(1)}, bf16[320,256]{1,0:T(8,128)(2,1)S(1)}, u32[]{:S(2)}, u32[]{:S(2)}) collective-permute-start(bf16[320,256]{1,0:T(8,128)(2,1)S(1)} %get-tuple-element.25), channel_id=1, source_target_pairs={{0,1},{1,2},{2,3},{3,4},{4,5},{5,6},{6,7},{8,9},{9,10},{10,11},{11... | collective-permute-start | bytes 491528 | tf_op jit(solution)/shard_map/ppermute | solution.py:24
  9.1 12.3 %collective-permute-start.2 = (bf16[512,256]{1,0:T(8,128)(2,1)S(1)}, bf16[512,256]{1,0:T(8,128)(2,1)S(1)}, u32[]{:S(2)}, u32[]{:S(2)}) collective-permute-start(bf16[512,256]{1,0:T(8,128)(2,1)S(1)} %get-tuple-element.26.early_ref), channel_id=1, source_target_pairs={{1,0},{2,1},{3,2},{4,3},{5,4},{6,5},{7,6},{9,8},{10,9},{11,10},{12... | collective-permute-start | bytes 786440 | tf_op jit(solution)/shard_map/ppermute | solution.py:24
  12.3 12.1 %collective-permute-start.1 = (bf16[512,256]{1,0:T(8,128)(2,1)S(1)}, bf16[512,256]{1,0:T(8,128)(2,1)S(1)}, u32[]{:S(2)}, u32[]{:S(2)}) collective-permute-start(bf16[512,256]{1,0:T(8,128)(2,1)S(1)} %shard_map.62.head_ref), channel_id=1, source_target_pairs={{1,0},{2,1},{3,2},{4,3},{5,4},{6,5},{7,6},{9,8},{10,9},{11,10},{12... | collective-permute-start | bytes 786440 | tf_op jit(solution)/shard_map/ppermute | solution.py:24
  24.9 1.4 %collective-permute-start.3 = (f32[16,1,2176]{2,1,0:T(1,128)S(1)}, f32[16,1,2176]{2,1,0:T(1,128)S(1)}, u32[]{:S(2)}, u32[]{:S(2)}) collective-permute-start(f32[16,1,2176]{2,1,0:T(1,128)S(1)} %get-tuple-element.33), channel_id=1, source_target_pairs={{0,8},{8,0},{1,9},{9,1},{2,10},{10,2},{3,11},{11,3},{4,12},{12,4},... | collective-permute-start | bytes 417800 | tf_op jit(solution)/shard_map/ppermute | solution.py:482
  52.0 1.4 %collective-permute-start.4 = (f32[16,1,2176]{2,1,0:T(1,128)S(1)}, f32[16,1,2176]{2,1,0:T(1,128)S(1)}, u32[]{:S(2)}, u32[]{:S(2)}) collective-permute-start(f32[16,1,2176]{2,1,0:T(1,128)S(1)} %all_to_all.11.mine_ref), channel_id=1, source_target_pairs={{0,8},{8,0},{1,9},{9,1},{2,10},{10,2},{3,11},{11,3},{4,12},{12,4},... | collective-permute-start | bytes 417800 | tf_op jit(solution)/shard_map/ppermute | solution.py:485

commit v15 on v12

--- a/solution.py
+++ b/solution.py
@@ -63,10 +63,11 @@
         (frames_ref.at[pl.ds(0, LAG)], near_ref),
     )
     copies = [pltpu.make_async_copy(*pair, sems.at[index]) for index, pair in enumerate(pairs)]
-    for copy in copies:
+    for copy in copies[:4]:
         copy.start()
     for copy in copies[:3]:
         copy.wait()
+    copies[4].start()
     hidden = hidden_rows(xs, 0, D2, w1_ref, b1_ref)
     copies[3].wait()
     hid, feat = hidden.shape[1], w2_ref.shape[1]
@@ -329,31 +330,25 @@
     inside = (lane >= 0) & (lane < PANEL)
     rows = [jnp.where(inside, jnp.where(lane == sub + 8 * h, 1.0, 0.0), rows[h]) for h in tiles]
     pivots = [jnp.ones((8, 128), F32) for _ in range(PANEL // 8)]
-    pivot_row = {k: spread(columns[k][0], 0) for k in range(PANEL)}
-    panel_row = spread(rows[0], 0)
+    pivot = spread(columns[0][0], 0)
     for j in range(PANEL):
-        inverse = pl.reciprocal(pivot_row[j], approx=True)
+        inverse = pl.reciprocal(pivot, approx=True)
         here, at = divmod(j, 8)
-        pivots[here] = jnp.where(sub_narrow == at, pivot_row[j], pivots[here])
-        last = j + 1 == PANEL
-        if not last:
+        pivots[here] = jnp.where(sub_narrow == at, pivot, pivots[here])
+        beside = {k: spread(columns[k][here], at) for k in range(j + 1, PANEL)}
+        if beside:
             there, after = divmod(j + 1, 8)
-            share = pivot_row[j + 1] * inverse
-            next_row = {
-                k: spread(columns[k][there], after) - share * pivot_row[k] for k in range(j + 1, PANEL)
-            }
-            next_panel_row = spread(rows[there], after) - wide(share) * panel_row
+            pivot = spread(columns[j + 1][there], after) - beside[j + 1] * beside[j + 1] * inverse
+        panel_row = spread(rows[here], at)
         for h in tiles:
             if 8 * h + 7 <= j:
                 continue
             factor = columns[j][h] * inverse
             if h == here:
                 factor = jnp.where(sub_narrow > at, factor, 0.0)
-            for k in range(j + 1, PANEL):
-                columns[k][h] = columns[k][h] - factor * pivot_row[k]
+            for k in beside:
+                columns[k][h] = columns[k][h] - factor * beside[k]
             rows[h] = rows[h] - wide(factor) * panel_row
-        if not last:
-            pivot_row, panel_row = next_row, next_panel_row
     return [rows[h] * wide(lax.rsqrt(pivots[h])) if h < len(pivots) else rows[h] for h in tiles]
 
 
@@ -403,7 +398,7 @@
     row = lax.broadcasted_iota(jnp.int32, (feat, feat), 0)
     column = lax.broadcasted_iota(jnp.int32, (feat, feat), 1)
     turned = packed.T
-    mean_column = jnp.broadcast_to(mean, (feat, feat)).T
+    mean_column = jnp.broadcast_to(jnp.broadcast_to(mean, (8, feat)).T[:, 0:1], (feat, feat))
     centre = mean_column * mean
     inst = jnp.where(column >= row, packed, turned)
     lag = jnp.where(column < row, packed, turned)

time: 66.3 us -> 66.1 us (level)
  no operation moved by 1% of the time
where the time goes in v15:
time: 66.1 us; the launch traced here: 65.8 us
  Pallas kernels  25.4 us (38%)
  blocking collectives  25.3 us (38%)
  starting transfers between devices  7.54 us (11%)
  waiting for transfers between devices  6.37 us (10%)
  between operations  0.89 us (1%)
    all_to_all x1, blocking collectives, summed(): lax.all_to_all(parts, chips, 0, 0, tiled=True)  14.6 us
    pallas_call x1, Pallas kernels, project(): pl.pallas_call(koopman_kernel, in_specs=[pl.BlockSpec(memory_space=pltpu....  11.9 us
    all_to_all x1, blocking collectives, summed(): lax.all_to_all(jnp.broadcast_to(mine, parts.shape), chips, 0, 0, tiled=True)  10.8 us
    ppermute x3, starting transfers between devices, passed_along(): lax.ppermute(value, axis, [(source, source + steps) for source in range(f...  7.46 us
    pallas_call x1, Pallas kernels, body(): pl.pallas_call(body_kernel, in_specs=[vmem] * 8, out_specs=vmem, out_shap...  4.53 us
    ppermute x3, waiting for transfers between devices, passed_along(): lax.ppermute(value, axis, [(source, source + steps) for source in range(f...  3.67 us
    pallas_call x1, Pallas kernels, tail_rows(): pl.pallas_call(tail_kernel, in_specs=[hbm] * 4, out_specs=(vmem,) * 5, ou...  2.64 us
    pallas_call x1, Pallas kernels, middle_rows(): pl.pallas_call(middle_kernel, in_specs=[hbm] + [vmem] * 5, out_specs=(vme...  2.17 us
  transfers between devices with their start and end apart: 5, of which 4 were waited for; matrix products, arithmetic and copies ran while one was open for 0% of the time, Pallas kernels for 16%

profile of v15, /device:TPU:0, one launch (start us, length us, event | category | flops | bytes accessed | tf_op | source)
XLA Modules:
  0.0 65.8 jit_solution(16764345649281826749)
XLA Ops:
  0.6 2.6 %shard_map.59 = (bf16[320,256]{1,0:T(8,128)(2,1)S(1)}, bf16[1024,512]{1,0:T(8,128)(2,1)S(1)}, bf16[1024,512]{1,0:T(8,128)(2,1)S(1)}, f32[1,512]{1,0:T(1,128)S(1)}, bf16[1024,256]{1,0:T(8,128)(2,1)S(1)}) custom-call(bf16[4096,512]{1,0:T(8,128)(2,1)} %bitcast.6, bf16[1024,512]{1,0:T(8,128)(2,1)} %bitcast.8, f32[1,512]{1,0:T(1,128)} %bitcast.10, ...), custom_call_target="tpu_custom_call" | custom-call | tf_op jit(solution)/shard_map/pallas_call | solution.py:87
  3.3 4.9 %collective-permute-start = (bf16[320,256]{1,0:T(8,128)(2,1)S(1)}, bf16[320,256]{1,0:T(8,128)(2,1)S(1)}, u32[]{:S(2)}, u32[]{:S(2)}) collective-permute-start(bf16[320,256]{1,0:T(8,128)(2,1)S(1)} %get-tuple-element.25), channel_id=1, source_target_pairs={{0,1},{1,2},{2,3},{3,4},{4,5},{5,6},{6,7},{8,9},{9,10},{10,11},{11... | collective-permute-start | bytes 491528 | tf_op jit(solution)/shard_map/ppermute | solution.py:25
  8.2 1.4 %shard_map.60 = (bf16[512,256]{1,0:T(8,128)(2,1)S(1)}, bf16[256,512]{1,0:T(8,128)(2,1)S(1)}) custom-call(bf16[1024,512]{1,0:T(8,128)(2,1)S(1)} %get-tuple-element.19.near_ref, bf16[1024,512]{1,0:T(8,128)(2,1)S(1)} %get-tuple-element.20.w1_ref, f32[1,512]{1,0:T(1,128)S(1)} %get-tuple-element.21.b1_ref, bf16[1024,256]{1,0:T(8,128)(2,1)S(1)} %get-tuple-element.22.w2_ref), custom_call_target="tpu_custom_call" | custom-call | tf_op jit(solution)/shard_map/pallas_call | solution.py:108
  9.6 1.3 %collective-permute-start.2 = (bf16[512,256]{1,0:T(8,128)(2,1)S(1)}, bf16[512,256]{1,0:T(8,128)(2,1)S(1)}, u32[]{:S(2)}, u32[]{:S(2)}) collective-permute-start(bf16[512,256]{1,0:T(8,128)(2,1)S(1)} %get-tuple-element.26.early_ref), channel_id=1, source_target_pairs={{1,0},{2,1},{3,2},{4,3},{5,4},{6,5},{7,6},{9,8},{10,9},{11,10},{12... | collective-permute-start | bytes 786440 | tf_op jit(solution)/shard_map/ppermute | solution.py:25
  10.9 0.7 %collective-permute-done.halo_ref = bf16[320,256]{1,0:T(8,128)(2,1)S(1)} collective-permute-done((bf16[320,256]{1,0:T(8,128)(2,1)S(1)}, bf16[320,256]{1,0:T(8,128)(2,1)S(1)}, u32[]{:S(2)}, u32[]{:S(2)}) %collective-permute-start) | collective-permute-done | bytes 163872 | tf_op jit(solution)/shard_map/ppermute | solution.py:25
  11.6 1.1 %shard_map.62.head_ref = bf16[512,256]{1,0:T(8,128)(2,1)S(1)} custom-call(bf16[1024,512]{1,0:T(8,128)(2,1)S(1)} %get-tuple-element.19.near_ref, bf16[320,256]{1,0:T(8,128)(2,1)S(1)} %collective-permute-done.halo_ref, bf16[1024,512]{1,0:T(8,128)(2,1)S(1)} %get-tuple-element.20.w1_ref, f32[1,512]{1,0:T(1,128)S(1)} %get-tuple-element.21.b1_ref, ...), custom_call_target="tpu_custom_call" | custom-call | tf_op jit(solution)/shard_map/pallas_call | solution.py:178
  12.7 1.3 %collective-permute-start.1 = (bf16[512,256]{1,0:T(8,128)(2,1)S(1)}, bf16[512,256]{1,0:T(8,128)(2,1)S(1)}, u32[]{:S(2)}, u32[]{:S(2)}) collective-permute-start(bf16[512,256]{1,0:T(8,128)(2,1)S(1)} %shard_map.62.head_ref), channel_id=1, source_target_pairs={{1,0},{2,1},{3,2},{4,3},{5,4},{6,5},{7,6},{9,8},{10,9},{11,10},{12... | collective-permute-start | bytes 786440 | tf_op jit(solution)/shard_map/ppermute | solution.py:25
  14.0 2.2 %shard_map.61 = (bf16[512,256]{1,0:T(8,128)(2,1)S(1)}, bf16[256,512]{1,0:T(8,128)(2,1)S(1)}, bf16[2592,512]{1,0:T(8,128)(2,1)S(1)}) custom-call(bf16[4096,512]{1,0:T(8,128)(2,1)} %bitcast.7, bf16[1024,512]{1,0:T(8,128)(2,1)S(1)} %get-tuple-element.19.near_ref, bf16[256,512]{1,0:T(8,128)(2,1)S(1)} %get-tuple-element.23.before_ref, ...), custom_call_target="tpu_custom_call" | custom-call | tf_op jit(solution)/shard_map/pallas_call | solution.py:147
  16.2 4.5 %shard_map.63.feature_ref = bf16[4096,256]{1,0:T(8,128)(2,1)S(1)} custom-call(bf16[2592,512]{1,0:T(8,128)(2,1)S(1)} %get-tuple-element.24.far_ref, bf16[512,256]{1,0:T(8,128)(2,1)S(1)} %shard_map.62.head_ref, bf16[512,256]{1,0:T(8,128)(2,1)S(1)} %get-tuple-element.26.early_ref, bf16[512,256]{1,0:T(8,128)(2,1)S(1)} %get-tuple-element.27.middle_ref, ...), custom_call_target="tpu_custom_call" | custom-call | tf_op jit(solution)/shard_map/pallas_call | solution.py:207
  20.7 1.1 %shard_map.64 = (f32[256,256]{1,0:T(8,128)S(1)}, f32[256,256]{1,0:T(8,128)S(1)}, f32[8,256]{1,0:T(8,128)S(1)}) custom-call(bf16[4096,256]{1,0:T(8,128)(2,1)S(1)} %shard_map.63.feature_ref), custom_call_target="tpu_custom_call" | custom-call | tf_op jit(solution)/shard_map/pallas_call | solution.py:246
  21.9 0.0 collective-permute-done.2.ahead_early_ref
  21.9 3.0 %collective-permute-done.1.ahead_head_ref = bf16[512,256]{1,0:T(8,128)(2,1)S(1)} collective-permute-done((bf16[512,256]{1,0:T(8,128)(2,1)S(1)}, bf16[512,256]{1,0:T(8,128)(2,1)S(1)}, u32[]{:S(2)}, u32[]{:S(2)}) %collective-permute-start.1) | collective-permute-done | bytes 262176 | tf_op jit(solution)/shard_map/ppermute | solution.py:25
  24.9 0.5 shard_map.65
  25.3 0.1 collective-permute-start.3
  25.4 1.3 %collective-permute-done.3 = f32[16,1,2176]{2,1,0:T(1,128)S(1)} collective-permute-done((f32[16,1,2176]{2,1,0:T(1,128)S(1)}, f32[16,1,2176]{2,1,0:T(1,128)S(1)}, u32[]{:S(2)}, u32[]{:S(2)}) %collective-permute-start.3) | collective-permute-done | bytes 139296 | tf_op jit(solution)/shard_map/ppermute | solution.py:479
  26.8 0.1 add.3
  26.9 14.6 %all_to_all.10 = f32[16,1,2176]{2,1,0:T(1,128)S(1)} all-to-all(f32[16,1,2176]{2,1,0:T(1,128)S(1)} %add.3), channel_id=1, replica_groups=mesh['x'=2,'core'=2,'tm'=8] {'x','tm'}, dimensions={0} | all-to-all | bytes 278528 | tf_op jit(solution)/shard_map/all_to_all | solution.py:480
  41.5 0.1 reduce_sum.9
  41.6 0.1 broadcast_in_dim.12
  41.7 10.8 %all_to_all.11.mine_ref = f32[16,1,2176]{2,1,0:T(1,128)S(1)} all-to-all(f32[16,1,2176]{2,1,0:T(1,128)S(1)} %broadcast_in_dim.12), channel_id=1, replica_groups=mesh['x'=2,'core'=2,'tm'=8] {'x','tm'}, dimensions={0} | all-to-all | bytes 278528 | tf_op jit(solution)/shard_map/all_to_all | solution.py:481
  52.4 0.0 collective-permute-start.4
  52.5 1.4 %collective-permute-done.4.other_ref = f32[16,1,2176]{2,1,0:T(1,128)S(1)} collective-permute-done((f32[16,1,2176]{2,1,0:T(1,128)S(1)}, f32[16,1,2176]{2,1,0:T(1,128)S(1)}, u32[]{:S(2)}, u32[]{:S(2)}) %collective-permute-start.4) | collective-permute-done | bytes 139296 | tf_op jit(solution)/shard_map/ppermute | solution.py:482
  53.8 11.9 %shard_map.66 = (f32[4096,256]{1,0:T(8,128)}, f32[4096,256]{1,0:T(8,128)}) custom-call(f32[1]{0:T(128)} %constant.0.clone.1.scale_ref, f32[16,1,2176]{2,1,0:T(1,128)S(1)} %all_to_all.11.mine_ref, f32[16,1,2176]{2,1,0:T(1,128)S(1)} %collective-permute-done.4.other_ref, bf16[4096,256]{1,0:T(8,128)(2,1)S(1)} %shard_map.63.feature_ref, ...), custom_call_target="tpu_custom_call" | custom-call | tf_op jit(solution)/shard_map/pallas_call | solution.py:458
Async XLA Ops:
  3.3 8.3 %collective-permute-start = (bf16[320,256]{1,0:T(8,128)(2,1)S(1)}, bf16[320,256]{1,0:T(8,128)(2,1)S(1)}, u32[]{:S(2)}, u32[]{:S(2)}) collective-permute-start(bf16[320,256]{1,0:T(8,128)(2,1)S(1)} %get-tuple-element.25), channel_id=1, source_target_pairs={{0,1},{1,2},{2,3},{3,4},{4,5},{5,6},{6,7},{8,9},{9,10},{10,11},{11... | collective-permute-start | bytes 491528 | tf_op jit(solution)/shard_map/ppermute | solution.py:25
  9.6 12.3 %collective-permute-start.2 = (bf16[512,256]{1,0:T(8,128)(2,1)S(1)}, bf16[512,256]{1,0:T(8,128)(2,1)S(1)}, u32[]{:S(2)}, u32[]{:S(2)}) collective-permute-start(bf16[512,256]{1,0:T(8,128)(2,1)S(1)} %get-tuple-element.26.early_ref), channel_id=1, source_target_pairs={{1,0},{2,1},{3,2},{4,3},{5,4},{6,5},{7,6},{9,8},{10,9},{11,10},{12... | collective-permute-start | bytes 786440 | tf_op jit(solution)/shard_map/ppermute | solution.py:25
  12.7 12.1 %collective-permute-start.1 = (bf16[512,256]{1,0:T(8,128)(2,1)S(1)}, bf16[512,256]{1,0:T(8,128)(2,1)S(1)}, u32[]{:S(2)}, u32[]{:S(2)}) collective-permute-start(bf16[512,256]{1,0:T(8,128)(2,1)S(1)} %shard_map.62.head_ref), channel_id=1, source_target_pairs={{1,0},{2,1},{3,2},{4,3},{5,4},{6,5},{7,6},{9,8},{10,9},{11,10},{12... | collective-permute-start | bytes 786440 | tf_op jit(solution)/shard_map/ppermute | solution.py:25
  25.3 1.4 %collective-permute-start.3 = (f32[16,1,2176]{2,1,0:T(1,128)S(1)}, f32[16,1,2176]{2,1,0:T(1,128)S(1)}, u32[]{:S(2)}, u32[]{:S(2)}) collective-permute-start(f32[16,1,2176]{2,1,0:T(1,128)S(1)} %get-tuple-element.33), channel_id=1, source_target_pairs={{0,8},{8,0},{1,9},{9,1},{2,10},{10,2},{3,11},{11,3},{4,12},{12,4},... | collective-permute-start | bytes 417800 | tf_op jit(solution)/shard_map/ppermute | solution.py:479
  52.4 1.4 %collective-permute-start.4 = (f32[16,1,2176]{2,1,0:T(1,128)S(1)}, f32[16,1,2176]{2,1,0:T(1,128)S(1)}, u32[]{:S(2)}, u32[]{:S(2)}) collective-permute-start(f32[16,1,2176]{2,1,0:T(1,128)S(1)} %all_to_all.11.mine_ref), channel_id=1, source_target_pairs={{0,8},{8,0},{1,9},{9,1},{2,10},{10,2},{3,11},{11,3},{4,12},{12,4},... | collective-permute-start | bytes 417800 | tf_op jit(solution)/shard_map/ppermute | solution.py:482

commit v16 on v15

--- a/solution.py
+++ b/solution.py
@@ -11,7 +11,7 @@
 RIDGE = 0.001
 CHUNK = 512
 EARLY = 1536
-PANEL = 16
+PANEL = 8
 SUPER = 32
 MIB = 1024 * 1024
 
@@ -55,27 +55,28 @@
 
 def tail_kernel(frames_ref, w1_in, b1_in, w2_in, sent_ref, near_ref, w1_ref, b1_ref, w2_ref, xs, sems):
     rows = frames_ref.shape[0]
+    taps = w1_in.shape[0] // 2
     pairs = (
         (frames_ref.at[pl.ds(rows - D1 - D2, D1 + D2)], xs),
-        (w1_in, w1_ref),
+        (w1_in.at[pl.ds(0, taps)], w1_ref.at[pl.ds(0, taps)]),
+        (w1_in.at[pl.ds(taps, taps)], w1_ref.at[pl.ds(taps, taps)]),
         (b1_in, b1_ref),
         (w2_in, w2_ref),
         (frames_ref.at[pl.ds(0, LAG)], near_ref),
     )
     copies = [pltpu.make_async_copy(*pair, sems.at[index]) for index, pair in enumerate(pairs)]
+    for copy in copies:
+        copy.start()
     for copy in copies[:4]:
-        copy.start()
-    for copy in copies[:3]:
         copy.wait()
-    copies[4].start()
     hidden = hidden_rows(xs, 0, D2, w1_ref, b1_ref)
-    copies[3].wait()
+    copies[4].wait()
     hid, feat = hidden.shape[1], w2_ref.shape[1]
     sent_ref[:D2, :] = jnp.dot(hidden, w2_ref[hid:, :], preferred_element_type=F32).astype(BF16)
     for index in range(xs.shape[1] // feat):
         part = slice(D2 + index * D1, D2 + (index + 1) * D1)
         sent_ref[part, :] = xs[D2:, index * feat : (index + 1) * feat]
-    copies[4].wait()
+    copies[5].wait()
 
 
 def tail_rows(frames, w1, b1, w2):
@@ -89,7 +90,7 @@
         in_specs=[hbm] * 4,
         out_specs=(vmem,) * 5,
         out_shape=tuple(jax.ShapeDtypeStruct(*shape) for shape in shapes),
-        scratch_shapes=[pltpu.VMEM((D1 + D2, channels), BF16), pltpu.SemaphoreType.DMA((5,))],
+        scratch_shapes=[pltpu.VMEM((D1 + D2, channels), BF16), pltpu.SemaphoreType.DMA((6,))],
         compiler_params=pltpu.CompilerParams(vmem_limit_bytes=12 * MIB),
     )(*(in_hbm(value) for value in (frames, w1, b1, w2)))
 
@@ -369,9 +370,13 @@
             right = jnp.concatenate([high, middle, high, low, high, middle], 0)
             first = stop // 128 * 128
             update = gram(left[:, first:], right)
-            kept = lax.broadcasted_iota(jnp.int32, (size - stop, size), 1)
-            kept = (kept < start) | (kept >= stop)
-            work[stop:, :] = jnp.where(kept, work[stop:, :], 0.0) - update[stop - first :]
+            for at in range(0, size, 128):
+                lanes = slice(at, at + 128)
+                old = work[stop:, lanes]
+                if at <= start < at + 128:
+                    place = lax.broadcasted_iota(jnp.int32, old.shape, 1) + at
+                    old = jnp.where((place < start) | (place >= stop), old, 0.0)
+                work[stop:, lanes] = old - update[stop - first :, lanes]
     row = lax.broadcasted_iota(jnp.int32, (size, size), 0)
     column = lax.broadcasted_iota(jnp.int32, (size, size), 1)
     return jnp.where(column <= row, work[...], 0.0)

time: 66.1 us -> 66.9 us (1.012)
  Pallas kernels: 25.4 us -> 26.1 us
    pallas_call x1, Pallas kernels: 11.9 us -> 13.1 us  [project(): pl.pallas_call(koopman_kernel, in_specs=[pl.BlockSpec(memory_space=pltpu....]
where the time goes in v16:
time: 66.9 us; the launch traced here: 66.6 us
  Pallas kernels  26.1 us (39%)
  blocking collectives  25.4 us (38%)
  starting transfers between devices  7.54 us (11%)
  waiting for transfers between devices  6.37 us (10%)
  between operations  0.89 us (1%)
    all_to_all x1, blocking collectives, summed(): lax.all_to_all(parts, chips, 0, 0, tiled=True)  14.6 us
    pallas_call x1, Pallas kernels, project(): pl.pallas_call(koopman_kernel, in_specs=[pl.BlockSpec(memory_space=pltpu....  13.1 us
    all_to_all x1, blocking collectives, summed(): lax.all_to_all(jnp.broadcast_to(mine, parts.shape), chips, 0, 0, tiled=True)  10.8 us
    ppermute x3, starting transfers between devices, passed_along(): lax.ppermute(value, axis, [(source, source + steps) for source in range(f...  7.46 us
    pallas_call x1, Pallas kernels, body(): pl.pallas_call(body_kernel, in_specs=[vmem] * 8, out_specs=vmem, out_shap...  4.53 us
    ppermute x3, waiting for transfers between devices, passed_along(): lax.ppermute(value, axis, [(source, source + steps) for source in range(f...  3.67 us
    pallas_call x1, Pallas kernels, middle_rows(): pl.pallas_call(middle_kernel, in_specs=[hbm] + [vmem] * 5, out_specs=(vme...  2.17 us
    pallas_call x1, Pallas kernels, tail_rows(): pl.pallas_call(tail_kernel, in_specs=[hbm] * 4, out_specs=(vmem,) * 5, ou...  2.16 us
  transfers between devices with their start and end apart: 5, of which 4 were waited for; matrix products, arithmetic and copies ran while one was open for 0% of the time, Pallas kernels for 16%

profile of v16, /device:TPU:0, one launch (start us, length us, event | category | flops | bytes accessed | tf_op | source)
XLA Modules:
  0.0 66.6 jit_solution(3977052201001946760)
XLA Ops:
  0.6 2.2 %shard_map.59 = (bf16[320,256]{1,0:T(8,128)(2,1)S(1)}, bf16[1024,512]{1,0:T(8,128)(2,1)S(1)}, bf16[1024,512]{1,0:T(8,128)(2,1)S(1)}, f32[1,512]{1,0:T(1,128)S(1)}, bf16[1024,256]{1,0:T(8,128)(2,1)S(1)}) custom-call(bf16[4096,512]{1,0:T(8,128)(2,1)} %bitcast.6, bf16[1024,512]{1,0:T(8,128)(2,1)} %bitcast.8, f32[1,512]{1,0:T(1,128)} %bitcast.10, ...), custom_call_target="tpu_custom_call" | custom-call | tf_op jit(solution)/shard_map/pallas_call | solution.py:88
  2.8 4.9 %collective-permute-start = (bf16[320,256]{1,0:T(8,128)(2,1)S(1)}, bf16[320,256]{1,0:T(8,128)(2,1)S(1)}, u32[]{:S(2)}, u32[]{:S(2)}) collective-permute-start(bf16[320,256]{1,0:T(8,128)(2,1)S(1)} %get-tuple-element.25), channel_id=1, source_target_pairs={{0,1},{1,2},{2,3},{3,4},{4,5},{5,6},{6,7},{8,9},{9,10},{10,11},{11... | collective-permute-start | bytes 491528 | tf_op jit(solution)/shard_map/ppermute | solution.py:25
  7.7 1.4 %shard_map.60 = (bf16[512,256]{1,0:T(8,128)(2,1)S(1)}, bf16[256,512]{1,0:T(8,128)(2,1)S(1)}) custom-call(bf16[1024,512]{1,0:T(8,128)(2,1)S(1)} %get-tuple-element.19.near_ref, bf16[1024,512]{1,0:T(8,128)(2,1)S(1)} %get-tuple-element.20.w1_ref, f32[1,512]{1,0:T(1,128)S(1)} %get-tuple-element.21.b1_ref, bf16[1024,256]{1,0:T(8,128)(2,1)S(1)} %get-tuple-element.22.w2_ref), custom_call_target="tpu_custom_call" | custom-call | tf_op jit(solution)/shard_map/pallas_call | solution.py:109
  9.1 1.3 %collective-permute-start.2 = (bf16[512,256]{1,0:T(8,128)(2,1)S(1)}, bf16[512,256]{1,0:T(8,128)(2,1)S(1)}, u32[]{:S(2)}, u32[]{:S(2)}) collective-permute-start(bf16[512,256]{1,0:T(8,128)(2,1)S(1)} %get-tuple-element.26.early_ref), channel_id=1, source_target_pairs={{1,0},{2,1},{3,2},{4,3},{5,4},{6,5},{7,6},{9,8},{10,9},{11,10},{12... | collective-permute-start | bytes 786440 | tf_op jit(solution)/shard_map/ppermute | solution.py:25
  10.4 0.7 %collective-permute-done.halo_ref = bf16[320,256]{1,0:T(8,128)(2,1)S(1)} collective-permute-done((bf16[320,256]{1,0:T(8,128)(2,1)S(1)}, bf16[320,256]{1,0:T(8,128)(2,1)S(1)}, u32[]{:S(2)}, u32[]{:S(2)}) %collective-permute-start) | collective-permute-done | bytes 163872 | tf_op jit(solution)/shard_map/ppermute | solution.py:25
  11.1 1.1 %shard_map.62.head_ref = bf16[512,256]{1,0:T(8,128)(2,1)S(1)} custom-call(bf16[1024,512]{1,0:T(8,128)(2,1)S(1)} %get-tuple-element.19.near_ref, bf16[320,256]{1,0:T(8,128)(2,1)S(1)} %collective-permute-done.halo_ref, bf16[1024,512]{1,0:T(8,128)(2,1)S(1)} %get-tuple-element.20.w1_ref, f32[1,512]{1,0:T(1,128)S(1)} %get-tuple-element.21.b1_ref, ...), custom_call_target="tpu_custom_call" | custom-call | tf_op jit(solution)/shard_map/pallas_call | solution.py:179
  12.2 1.3 %collective-permute-start.1 = (bf16[512,256]{1,0:T(8,128)(2,1)S(1)}, bf16[512,256]{1,0:T(8,128)(2,1)S(1)}, u32[]{:S(2)}, u32[]{:S(2)}) collective-permute-start(bf16[512,256]{1,0:T(8,128)(2,1)S(1)} %shard_map.62.head_ref), channel_id=1, source_target_pairs={{1,0},{2,1},{3,2},{4,3},{5,4},{6,5},{7,6},{9,8},{10,9},{11,10},{12... | collective-permute-start | bytes 786440 | tf_op jit(solution)/shard_map/ppermute | solution.py:25
  13.5 2.2 %shard_map.61 = (bf16[512,256]{1,0:T(8,128)(2,1)S(1)}, bf16[256,512]{1,0:T(8,128)(2,1)S(1)}, bf16[2592,512]{1,0:T(8,128)(2,1)S(1)}) custom-call(bf16[4096,512]{1,0:T(8,128)(2,1)} %bitcast.7, bf16[1024,512]{1,0:T(8,128)(2,1)S(1)} %get-tuple-element.19.near_ref, bf16[256,512]{1,0:T(8,128)(2,1)S(1)} %get-tuple-element.23.before_ref, ...), custom_call_target="tpu_custom_call" | custom-call | tf_op jit(solution)/shard_map/pallas_call | solution.py:148
  15.7 4.5 %shard_map.63.feature_ref = bf16[4096,256]{1,0:T(8,128)(2,1)S(1)} custom-call(bf16[2592,512]{1,0:T(8,128)(2,1)S(1)} %get-tuple-element.24.far_ref, bf16[512,256]{1,0:T(8,128)(2,1)S(1)} %shard_map.62.head_ref, bf16[512,256]{1,0:T(8,128)(2,1)S(1)} %get-tuple-element.26.early_ref, bf16[512,256]{1,0:T(8,128)(2,1)S(1)} %get-tuple-element.27.middle_ref, ...), custom_call_target="tpu_custom_call" | custom-call | tf_op jit(solution)/shard_map/pallas_call | solution.py:208
  20.3 1.1 %shard_map.64 = (f32[256,256]{1,0:T(8,128)S(1)}, f32[256,256]{1,0:T(8,128)S(1)}, f32[8,256]{1,0:T(8,128)S(1)}) custom-call(bf16[4096,256]{1,0:T(8,128)(2,1)S(1)} %shard_map.63.feature_ref), custom_call_target="tpu_custom_call" | custom-call | tf_op jit(solution)/shard_map/pallas_call | solution.py:247
  21.4 0.0 collective-permute-done.2.ahead_early_ref
  21.4 3.0 %collective-permute-done.1.ahead_head_ref = bf16[512,256]{1,0:T(8,128)(2,1)S(1)} collective-permute-done((bf16[512,256]{1,0:T(8,128)(2,1)S(1)}, bf16[512,256]{1,0:T(8,128)(2,1)S(1)}, u32[]{:S(2)}, u32[]{:S(2)}) %collective-permute-start.1) | collective-permute-done | bytes 262176 | tf_op jit(solution)/shard_map/ppermute | solution.py:25
  24.4 0.5 shard_map.65
  24.9 0.1 collective-permute-start.3
  24.9 1.3 %collective-permute-done.3 = f32[16,1,2176]{2,1,0:T(1,128)S(1)} collective-permute-done((f32[16,1,2176]{2,1,0:T(1,128)S(1)}, f32[16,1,2176]{2,1,0:T(1,128)S(1)}, u32[]{:S(2)}, u32[]{:S(2)}) %collective-permute-start.3) | collective-permute-done | bytes 139296 | tf_op jit(solution)/shard_map/ppermute | solution.py:484
  26.3 0.1 add.3
  26.4 14.6 %all_to_all.10 = f32[16,1,2176]{2,1,0:T(1,128)S(1)} all-to-all(f32[16,1,2176]{2,1,0:T(1,128)S(1)} %add.3), channel_id=1, replica_groups=mesh['x'=2,'core'=2,'tm'=8] {'x','tm'}, dimensions={0} | all-to-all | bytes 278528 | tf_op jit(solution)/shard_map/all_to_all | solution.py:485
  41.0 0.1 reduce_sum.9
  41.1 0.1 broadcast_in_dim.12
  41.2 10.8 %all_to_all.11.mine_ref = f32[16,1,2176]{2,1,0:T(1,128)S(1)} all-to-all(f32[16,1,2176]{2,1,0:T(1,128)S(1)} %broadcast_in_dim.12), channel_id=1, replica_groups=mesh['x'=2,'core'=2,'tm'=8] {'x','tm'}, dimensions={0} | all-to-all | bytes 278528 | tf_op jit(solution)/shard_map/all_to_all | solution.py:486
  52.0 0.0 collective-permute-start.4
  52.0 1.4 %collective-permute-done.4.other_ref = f32[16,1,2176]{2,1,0:T(1,128)S(1)} collective-permute-done((f32[16,1,2176]{2,1,0:T(1,128)S(1)}, f32[16,1,2176]{2,1,0:T(1,128)S(1)}, u32[]{:S(2)}, u32[]{:S(2)}) %collective-permute-start.4) | collective-permute-done | bytes 139296 | tf_op jit(solution)/shard_map/ppermute | solution.py:487
  53.3 13.1 %shard_map.66 = (f32[4096,256]{1,0:T(8,128)}, f32[4096,256]{1,0:T(8,128)}) custom-call(f32[1]{0:T(128)} %constant.0.clone.1.scale_ref, f32[16,1,2176]{2,1,0:T(1,128)S(1)} %all_to_all.11.mine_ref, f32[16,1,2176]{2,1,0:T(1,128)S(1)} %collective-permute-done.4.other_ref, bf16[4096,256]{1,0:T(8,128)(2,1)S(1)} %shard_map.63.feature_ref, ...), custom_call_target="tpu_custom_call" | custom-call | tf_op jit(solution)/shard_map/pallas_call | solution.py:463
Async XLA Ops:
  2.8 8.3 %collective-permute-start = (bf16[320,256]{1,0:T(8,128)(2,1)S(1)}, bf16[320,256]{1,0:T(8,128)(2,1)S(1)}, u32[]{:S(2)}, u32[]{:S(2)}) collective-permute-start(bf16[320,256]{1,0:T(8,128)(2,1)S(1)} %get-tuple-element.25), channel_id=1, source_target_pairs={{0,1},{1,2},{2,3},{3,4},{4,5},{5,6},{6,7},{8,9},{9,10},{10,11},{11... | collective-permute-start | bytes 491528 | tf_op jit(solution)/shard_map/ppermute | solution.py:25
  9.1 12.3 %collective-permute-start.2 = (bf16[512,256]{1,0:T(8,128)(2,1)S(1)}, bf16[512,256]{1,0:T(8,128)(2,1)S(1)}, u32[]{:S(2)}, u32[]{:S(2)}) collective-permute-start(bf16[512,256]{1,0:T(8,128)(2,1)S(1)} %get-tuple-element.26.early_ref), channel_id=1, source_target_pairs={{1,0},{2,1},{3,2},{4,3},{5,4},{6,5},{7,6},{9,8},{10,9},{11,10},{12... | collective-permute-start | bytes 786440 | tf_op jit(solution)/shard_map/ppermute | solution.py:25
  12.2 12.1 %collective-permute-start.1 = (bf16[512,256]{1,0:T(8,128)(2,1)S(1)}, bf16[512,256]{1,0:T(8,128)(2,1)S(1)}, u32[]{:S(2)}, u32[]{:S(2)}) collective-permute-start(bf16[512,256]{1,0:T(8,128)(2,1)S(1)} %shard_map.62.head_ref), channel_id=1, source_target_pairs={{1,0},{2,1},{3,2},{4,3},{5,4},{6,5},{7,6},{9,8},{10,9},{11,10},{12... | collective-permute-start | bytes 786440 | tf_op jit(solution)/shard_map/ppermute | solution.py:25
  24.9 1.4 %collective-permute-start.3 = (f32[16,1,2176]{2,1,0:T(1,128)S(1)}, f32[16,1,2176]{2,1,0:T(1,128)S(1)}, u32[]{:S(2)}, u32[]{:S(2)}) collective-permute-start(f32[16,1,2176]{2,1,0:T(1,128)S(1)} %get-tuple-element.33), channel_id=1, source_target_pairs={{0,8},{8,0},{1,9},{9,1},{2,10},{10,2},{3,11},{11,3},{4,12},{12,4},... | collective-permute-start | bytes 417800 | tf_op jit(solution)/shard_map/ppermute | solution.py:484
  52.0 1.4 %collective-permute-start.4 = (f32[16,1,2176]{2,1,0:T(1,128)S(1)}, f32[16,1,2176]{2,1,0:T(1,128)S(1)}, u32[]{:S(2)}, u32[]{:S(2)}) collective-permute-start(f32[16,1,2176]{2,1,0:T(1,128)S(1)} %all_to_all.11.mine_ref), channel_id=1, source_target_pairs={{0,8},{8,0},{1,9},{9,1},{2,10},{10,2},{3,11},{11,3},{4,12},{12,4},... | collective-permute-start | bytes 417800 | tf_op jit(solution)/shard_map/ppermute | solution.py:487

commit v17 on v16

--- a/solution.py
+++ b/solution.py
@@ -11,7 +11,7 @@
 RIDGE = 0.001
 CHUNK = 512
 EARLY = 1536
-PANEL = 8
+PANEL = 16
 SUPER = 32
 MIB = 1024 * 1024
 
@@ -336,7 +336,7 @@
         inverse = pl.reciprocal(pivot, approx=True)
         here, at = divmod(j, 8)
         pivots[here] = jnp.where(sub_narrow == at, pivot, pivots[here])
-        beside = {k: spread(columns[k][here], at) for k in range(j + 1, PANEL)}
+        beside = {k: spread(columns[j][k // 8], k % 8) for k in range(j + 1, PANEL)}
         if beside:
             there, after = divmod(j + 1, 8)
             pivot = spread(columns[j + 1][there], after) - beside[j + 1] * beside[j + 1] * inverse
@@ -348,7 +348,8 @@
             if h == here:
                 factor = jnp.where(sub_narrow > at, factor, 0.0)
             for k in beside:
-                columns[k][h] = columns[k][h] - factor * beside[k]
+                if 8 * h + 7 >= k:
+                    columns[k][h] = columns[k][h] - factor * beside[k]
             rows[h] = rows[h] - wide(factor) * panel_row
     return [rows[h] * wide(lax.rsqrt(pivots[h])) if h < len(pivots) else rows[h] for h in tiles]
 

time: 66.9 us -> 65.1 us (0.973)
  Pallas kernels: 26.1 us -> 24.4 us
    pallas_call x1, Pallas kernels: 13.1 us -> 11.4 us  [project(): pl.pallas_call(koopman_kernel, in_specs=[pl.BlockSpec(memory_space=pltpu....]
where the time goes in v17:
time: 65.1 us; the launch traced here: 64.9 us
  blocking collectives  25.4 us (39%)
  Pallas kernels  24.4 us (37%)
  starting transfers between devices  7.54 us (12%)
  waiting for transfers between devices  6.37 us (10%)
  between operations  0.89 us (1%)
    all_to_all x1, blocking collectives, summed(): lax.all_to_all(parts, chips, 0, 0, tiled=True)  14.6 us
    pallas_call x1, Pallas kernels, project(): pl.pallas_call(koopman_kernel, in_specs=[pl.BlockSpec(memory_space=pltpu....  11.4 us
    all_to_all x1, blocking collectives, summed(): lax.all_to_all(jnp.broadcast_to(mine, parts.shape), chips, 0, 0, tiled=True)  10.8 us
    ppermute x3, starting transfers between devices, passed_along(): lax.ppermute(value, axis, [(source, source + steps) for source in range(f...  7.46 us
    pallas_call x1, Pallas kernels, body(): pl.pallas_call(body_kernel, in_specs=[vmem] * 8, out_specs=vmem, out_shap...  4.53 us
    ppermute x3, waiting for transfers between devices, passed_along(): lax.ppermute(value, axis, [(source, source + steps) for source in range(f...  3.67 us
    pallas_call x1, Pallas kernels, middle_rows(): pl.pallas_call(middle_kernel, in_specs=[hbm] + [vmem] * 5, out_specs=(vme...  2.17 us
    pallas_call x1, Pallas kernels, tail_rows(): pl.pallas_call(tail_kernel, in_specs=[hbm] * 4, out_specs=(vmem,) * 5, ou...  2.16 us
  transfers between devices with their start and end apart: 5, of which 4 were waited for; matrix products, arithmetic and copies ran while one was open for 0% of the time, Pallas kernels for 16%

profile of v17, /device:TPU:0, one launch (start us, length us, event | category | flops | bytes accessed | tf_op | source)
XLA Modules:
  0.0 64.9 jit_solution(14162253546396710353)
XLA Ops:
  0.6 2.2 %shard_map.59 = (bf16[320,256]{1,0:T(8,128)(2,1)S(1)}, bf16[1024,512]{1,0:T(8,128)(2,1)S(1)}, bf16[1024,512]{1,0:T(8,128)(2,1)S(1)}, f32[1,512]{1,0:T(1,128)S(1)}, bf16[1024,256]{1,0:T(8,128)(2,1)S(1)}) custom-call(bf16[4096,512]{1,0:T(8,128)(2,1)} %bitcast.6, bf16[1024,512]{1,0:T(8,128)(2,1)} %bitcast.8, f32[1,512]{1,0:T(1,128)} %bitcast.10, ...), custom_call_target="tpu_custom_call" | custom-call | tf_op jit(solution)/shard_map/pallas_call | solution.py:88
  2.8 4.9 %collective-permute-start = (bf16[320,256]{1,0:T(8,128)(2,1)S(1)}, bf16[320,256]{1,0:T(8,128)(2,1)S(1)}, u32[]{:S(2)}, u32[]{:S(2)}) collective-permute-start(bf16[320,256]{1,0:T(8,128)(2,1)S(1)} %get-tuple-element.25), channel_id=1, source_target_pairs={{0,1},{1,2},{2,3},{3,4},{4,5},{5,6},{6,7},{8,9},{9,10},{10,11},{11... | collective-permute-start | bytes 491528 | tf_op jit(solution)/shard_map/ppermute | solution.py:25
  7.7 1.4 %shard_map.60 = (bf16[512,256]{1,0:T(8,128)(2,1)S(1)}, bf16[256,512]{1,0:T(8,128)(2,1)S(1)}) custom-call(bf16[1024,512]{1,0:T(8,128)(2,1)S(1)} %get-tuple-element.19.near_ref, bf16[1024,512]{1,0:T(8,128)(2,1)S(1)} %get-tuple-element.20.w1_ref, f32[1,512]{1,0:T(1,128)S(1)} %get-tuple-element.21.b1_ref, bf16[1024,256]{1,0:T(8,128)(2,1)S(1)} %get-tuple-element.22.w2_ref), custom_call_target="tpu_custom_call" | custom-call | tf_op jit(solution)/shard_map/pallas_call | solution.py:109
  9.1 1.3 %collective-permute-start.2 = (bf16[512,256]{1,0:T(8,128)(2,1)S(1)}, bf16[512,256]{1,0:T(8,128)(2,1)S(1)}, u32[]{:S(2)}, u32[]{:S(2)}) collective-permute-start(bf16[512,256]{1,0:T(8,128)(2,1)S(1)} %get-tuple-element.26.early_ref), channel_id=1, source_target_pairs={{1,0},{2,1},{3,2},{4,3},{5,4},{6,5},{7,6},{9,8},{10,9},{11,10},{12... | collective-permute-start | bytes 786440 | tf_op jit(solution)/shard_map/ppermute | solution.py:25
  10.4 0.7 %collective-permute-done.halo_ref = bf16[320,256]{1,0:T(8,128)(2,1)S(1)} collective-permute-done((bf16[320,256]{1,0:T(8,128)(2,1)S(1)}, bf16[320,256]{1,0:T(8,128)(2,1)S(1)}, u32[]{:S(2)}, u32[]{:S(2)}) %collective-permute-start) | collective-permute-done | bytes 163872 | tf_op jit(solution)/shard_map/ppermute | solution.py:25
  11.1 1.1 %shard_map.62.head_ref = bf16[512,256]{1,0:T(8,128)(2,1)S(1)} custom-call(bf16[1024,512]{1,0:T(8,128)(2,1)S(1)} %get-tuple-element.19.near_ref, bf16[320,256]{1,0:T(8,128)(2,1)S(1)} %collective-permute-done.halo_ref, bf16[1024,512]{1,0:T(8,128)(2,1)S(1)} %get-tuple-element.20.w1_ref, f32[1,512]{1,0:T(1,128)S(1)} %get-tuple-element.21.b1_ref, ...), custom_call_target="tpu_custom_call" | custom-call | tf_op jit(solution)/shard_map/pallas_call | solution.py:179
  12.2 1.3 %collective-permute-start.1 = (bf16[512,256]{1,0:T(8,128)(2,1)S(1)}, bf16[512,256]{1,0:T(8,128)(2,1)S(1)}, u32[]{:S(2)}, u32[]{:S(2)}) collective-permute-start(bf16[512,256]{1,0:T(8,128)(2,1)S(1)} %shard_map.62.head_ref), channel_id=1, source_target_pairs={{1,0},{2,1},{3,2},{4,3},{5,4},{6,5},{7,6},{9,8},{10,9},{11,10},{12... | collective-permute-start | bytes 786440 | tf_op jit(solution)/shard_map/ppermute | solution.py:25
  13.5 2.2 %shard_map.61 = (bf16[512,256]{1,0:T(8,128)(2,1)S(1)}, bf16[256,512]{1,0:T(8,128)(2,1)S(1)}, bf16[2592,512]{1,0:T(8,128)(2,1)S(1)}) custom-call(bf16[4096,512]{1,0:T(8,128)(2,1)} %bitcast.7, bf16[1024,512]{1,0:T(8,128)(2,1)S(1)} %get-tuple-element.19.near_ref, bf16[256,512]{1,0:T(8,128)(2,1)S(1)} %get-tuple-element.23.before_ref, ...), custom_call_target="tpu_custom_call" | custom-call | tf_op jit(solution)/shard_map/pallas_call | solution.py:148
  15.7 4.5 %shard_map.63.feature_ref = bf16[4096,256]{1,0:T(8,128)(2,1)S(1)} custom-call(bf16[2592,512]{1,0:T(8,128)(2,1)S(1)} %get-tuple-element.24.far_ref, bf16[512,256]{1,0:T(8,128)(2,1)S(1)} %shard_map.62.head_ref, bf16[512,256]{1,0:T(8,128)(2,1)S(1)} %get-tuple-element.26.early_ref, bf16[512,256]{1,0:T(8,128)(2,1)S(1)} %get-tuple-element.27.middle_ref, ...), custom_call_target="tpu_custom_call" | custom-call | tf_op jit(solution)/shard_map/pallas_call | solution.py:208
  20.3 1.1 %shard_map.64 = (f32[256,256]{1,0:T(8,128)S(1)}, f32[256,256]{1,0:T(8,128)S(1)}, f32[8,256]{1,0:T(8,128)S(1)}) custom-call(bf16[4096,256]{1,0:T(8,128)(2,1)S(1)} %shard_map.63.feature_ref), custom_call_target="tpu_custom_call" | custom-call | tf_op jit(solution)/shard_map/pallas_call | solution.py:247
  21.4 0.0 collective-permute-done.2.ahead_early_ref
  21.4 3.0 %collective-permute-done.1.ahead_head_ref = bf16[512,256]{1,0:T(8,128)(2,1)S(1)} collective-permute-done((bf16[512,256]{1,0:T(8,128)(2,1)S(1)}, bf16[512,256]{1,0:T(8,128)(2,1)S(1)}, u32[]{:S(2)}, u32[]{:S(2)}) %collective-permute-start.1) | collective-permute-done | bytes 262176 | tf_op jit(solution)/shard_map/ppermute | solution.py:25
  24.4 0.5 shard_map.65
  24.9 0.1 collective-permute-start.3
  24.9 1.3 %collective-permute-done.3 = f32[16,1,2176]{2,1,0:T(1,128)S(1)} collective-permute-done((f32[16,1,2176]{2,1,0:T(1,128)S(1)}, f32[16,1,2176]{2,1,0:T(1,128)S(1)}, u32[]{:S(2)}, u32[]{:S(2)}) %collective-permute-start.3) | collective-permute-done | bytes 139296 | tf_op jit(solution)/shard_map/ppermute | solution.py:485
  26.3 0.1 add.3
  26.4 14.6 %all_to_all.10 = f32[16,1,2176]{2,1,0:T(1,128)S(1)} all-to-all(f32[16,1,2176]{2,1,0:T(1,128)S(1)} %add.3), channel_id=1, replica_groups=mesh['x'=2,'core'=2,'tm'=8] {'x','tm'}, dimensions={0} | all-to-all | bytes 278528 | tf_op jit(solution)/shard_map/all_to_all | solution.py:486
  41.0 0.1 reduce_sum.9
  41.1 0.1 broadcast_in_dim.12
  41.2 10.8 %all_to_all.11.mine_ref = f32[16,1,2176]{2,1,0:T(1,128)S(1)} all-to-all(f32[16,1,2176]{2,1,0:T(1,128)S(1)} %broadcast_in_dim.12), channel_id=1, replica_groups=mesh['x'=2,'core'=2,'tm'=8] {'x','tm'}, dimensions={0} | all-to-all | bytes 278528 | tf_op jit(solution)/shard_map/all_to_all | solution.py:487
  52.0 0.0 collective-permute-start.4
  52.0 1.4 %collective-permute-done.4.other_ref = f32[16,1,2176]{2,1,0:T(1,128)S(1)} collective-permute-done((f32[16,1,2176]{2,1,0:T(1,128)S(1)}, f32[16,1,2176]{2,1,0:T(1,128)S(1)}, u32[]{:S(2)}, u32[]{:S(2)}) %collective-permute-start.4) | collective-permute-done | bytes 139296 | tf_op jit(solution)/shard_map/ppermute | solution.py:488
  53.3 11.4 %shard_map.66 = (f32[4096,256]{1,0:T(8,128)}, f32[4096,256]{1,0:T(8,128)}) custom-call(f32[1]{0:T(128)} %constant.0.clone.1.scale_ref, f32[16,1,2176]{2,1,0:T(1,128)S(1)} %all_to_all.11.mine_ref, f32[16,1,2176]{2,1,0:T(1,128)S(1)} %collective-permute-done.4.other_ref, bf16[4096,256]{1,0:T(8,128)(2,1)S(1)} %shard_map.63.feature_ref, ...), custom_call_target="tpu_custom_call" | custom-call | tf_op jit(solution)/shard_map/pallas_call | solution.py:464
Async XLA Ops:
  2.8 8.3 %collective-permute-start = (bf16[320,256]{1,0:T(8,128)(2,1)S(1)}, bf16[320,256]{1,0:T(8,128)(2,1)S(1)}, u32[]{:S(2)}, u32[]{:S(2)}) collective-permute-start(bf16[320,256]{1,0:T(8,128)(2,1)S(1)} %get-tuple-element.25), channel_id=1, source_target_pairs={{0,1},{1,2},{2,3},{3,4},{4,5},{5,6},{6,7},{8,9},{9,10},{10,11},{11... | collective-permute-start | bytes 491528 | tf_op jit(solution)/shard_map/ppermute | solution.py:25
  9.1 12.3 %collective-permute-start.2 = (bf16[512,256]{1,0:T(8,128)(2,1)S(1)}, bf16[512,256]{1,0:T(8,128)(2,1)S(1)}, u32[]{:S(2)}, u32[]{:S(2)}) collective-permute-start(bf16[512,256]{1,0:T(8,128)(2,1)S(1)} %get-tuple-element.26.early_ref), channel_id=1, source_target_pairs={{1,0},{2,1},{3,2},{4,3},{5,4},{6,5},{7,6},{9,8},{10,9},{11,10},{12... | collective-permute-start | bytes 786440 | tf_op jit(solution)/shard_map/ppermute | solution.py:25
  12.2 12.1 %collective-permute-start.1 = (bf16[512,256]{1,0:T(8,128)(2,1)S(1)}, bf16[512,256]{1,0:T(8,128)(2,1)S(1)}, u32[]{:S(2)}, u32[]{:S(2)}) collective-permute-start(bf16[512,256]{1,0:T(8,128)(2,1)S(1)} %shard_map.62.head_ref), channel_id=1, source_target_pairs={{1,0},{2,1},{3,2},{4,3},{5,4},{6,5},{7,6},{9,8},{10,9},{11,10},{12... | collective-permute-start | bytes 786440 | tf_op jit(solution)/shard_map/ppermute | solution.py:25
  24.9 1.4 %collective-permute-start.3 = (f32[16,1,2176]{2,1,0:T(1,128)S(1)}, f32[16,1,2176]{2,1,0:T(1,128)S(1)}, u32[]{:S(2)}, u32[]{:S(2)}) collective-permute-start(f32[16,1,2176]{2,1,0:T(1,128)S(1)} %get-tuple-element.33), channel_id=1, source_target_pairs={{0,8},{8,0},{1,9},{9,1},{2,10},{10,2},{3,11},{11,3},{4,12},{12,4},... | collective-permute-start | bytes 417800 | tf_op jit(solution)/shard_map/ppermute | solution.py:485
  52.0 1.4 %collective-permute-start.4 = (f32[16,1,2176]{2,1,0:T(1,128)S(1)}, f32[16,1,2176]{2,1,0:T(1,128)S(1)}, u32[]{:S(2)}, u32[]{:S(2)}) collective-permute-start(f32[16,1,2176]{2,1,0:T(1,128)S(1)} %all_to_all.11.mine_ref), channel_id=1, source_target_pairs={{0,8},{8,0},{1,9},{9,1},{2,10},{10,2},{3,11},{11,3},{4,12},{12,4},... | collective-permute-start | bytes 417800 | tf_op jit(solution)/shard_map/ppermute | solution.py:488

commit v18 on v17

--- a/solution.py
+++ b/solution.py
@@ -220,8 +220,9 @@
     return jnp.sum(jnp.sum(parts, 1), 0)
 
 
-def moment_kernel(feature_ref, inst, lag, total):
+def moment_kernel(feature_ref, inst, lag, total, turned_ref):
     rows, feat = feature_ref.shape
+    turned_ref[...] = feature_ref[rows - LAG :, :].T
     tm_index, tm_last = lax.axis_index("tm"), lax.axis_size("tm") - 1
     for at in range(0, rows, LAG):
         weight = 2.0
@@ -247,18 +248,22 @@
     return pl.pallas_call(
         moment_kernel,
         in_specs=[vmem],
-        out_specs=(vmem,) * 3,
-        out_shape=(square, square, jax.ShapeDtypeStruct((8, feat), F32)),
+        out_specs=(vmem,) * 4,
+        out_shape=(
+            square,
+            square,
+            jax.ShapeDtypeStruct((8, feat), F32),
+            jax.ShapeDtypeStruct((feat, LAG), BF16),
+        ),
         compiler_params=pltpu.CompilerParams(vmem_limit_bytes=12 * MIB),
     )(feature)
 
 
-def pack_kernel(feature_ref, ahead_head_ref, ahead_early_ref, inst, lag, total, kept_ref, sent_ref, packed):
+def pack_kernel(turned_ref, ahead_head_ref, ahead_early_ref, inst, lag, total, kept_ref, sent_ref, packed):
     feat = inst.shape[0]
     half = LAG // 2
-    edge = feature_ref.shape[0] - LAG
-    cross = lag[...] + gram(ahead_head_ref[...], feature_ref[edge : edge + half, :])
-    cross += gram(ahead_early_ref[...], feature_ref[edge + half :, :])
+    cross = lag[...] + jnp.dot(turned_ref[:, :half], ahead_head_ref[...], preferred_element_type=F32)
+    cross += jnp.dot(turned_ref[:, half:], ahead_early_ref[...], preferred_element_type=F32)
     both = cross + cross.T
     row = lax.broadcasted_iota(jnp.int32, (feat, feat), 0)
     column = lax.broadcasted_iota(jnp.int32, (feat, feat), 1)
@@ -282,7 +287,7 @@
         yield index, slice(index * feat, (index + 1) * feat)
 
 
-def pack(feature, ahead_head, ahead_early, inst, lag, total, chips):
+def pack(turned, ahead_head, ahead_early, inst, lag, total, chips):
     vmem = pl.BlockSpec(memory_space=pltpu.VMEM)
     feat = inst.shape[0]
     share = jax.ShapeDtypeStruct((chips, 1, feat // 2 // chips * feat + 128), F32)
@@ -293,7 +298,7 @@
         out_shape=(share, share),
         scratch_shapes=[pltpu.VMEM((feat, feat), F32)],
         compiler_params=pltpu.CompilerParams(vmem_limit_bytes=8 * MIB),
-    )(feature, ahead_head, ahead_early, inst, lag, total)
+    )(turned, ahead_head, ahead_early, inst, lag, total)
 
 
 def three_parts(x):
@@ -305,9 +310,9 @@
 
 
 def product(a, b):
-    high, middle, low = three_parts(a)
+    high, middle, low = a
     left = jnp.concatenate([high, high, middle, high, low, middle], 1)
-    high, middle, low = three_parts(b)
+    high, middle, low = b
     right = jnp.concatenate([high, middle, high, low, high, middle], 0)
     return jnp.dot(left, right, preferred_element_type=F32)
 
@@ -412,13 +417,14 @@
     work[...] = inst * scale - centre + jnp.where(column == row, RIDGE, 0.0)
     lag = lag * scale - centre
     inverse = inverse_factor(work)
-    inverse_turned = inverse.T
-    koopman = product(product(inverse, lag), inverse_turned)
-    moved_turned = product(inverse_turned, koopman)
-    for index, matrix in enumerate((inverse_turned, moved_turned)):
-        high = matrix.astype(BF16)
+    turned_parts = three_parts(inverse.T)
+    half_step = product(three_parts(inverse), three_parts(lag))
+    koopman_part = three_parts(product(three_parts(half_step), turned_parts))
+    moved_parts = three_parts(product(turned_parts, koopman_part))
+    for index, (high, middle, _) in enumerate((turned_parts, moved_parts)):
         split_ref[index, :feat, :] = high
-        split_ref[index, feat:, :] = (matrix - high.astype(F32)).astype(BF16)
+        split_ref[index, feat:, :] = middle
+        matrix = high.astype(F32) + middle.astype(F32)
         shift = jnp.sum(mean_column * matrix, 0, keepdims=True)
         shift_ref[index] = jnp.broadcast_to(shift, (8, feat))
     project_rows(
@@ -505,9 +511,9 @@
     head = head_rows(near, halo, *weights)
     ahead_head = passed_along(head, "tm", -1)
     feature = body(far, head, early, middle, hidden, *weights)
-    inst, lag, total = moments(feature)
+    inst, lag, total, turned = moments(feature)
     chips = lax.axis_size("x") * lax.axis_size("tm")
-    mine, other = summed(*pack(feature, ahead_head, ahead_early, inst, lag, total, chips))
+    mine, other = summed(*pack(turned, ahead_head, ahead_early, inst, lag, total, chips))
     replicas = lax.axis_size("x") * lax.axis_size("core")
     pair_count = replicas * (row_count * lax.axis_size("tm") - LAG)
     scale = jnp.full((1,), 1.0 / (2.0 * pair_count), F32)

time: 65.1 us -> 65.1 us (level)
  no operation moved by 1% of the time
where the time goes in v18:
time: 65.1 us; the launch traced here: 64.9 us
  blocking collectives  25.4 us (39%)
  Pallas kernels  24.4 us (37%)
  starting transfers between devices  7.54 us (12%)
  waiting for transfers between devices  6.36 us (10%)
  between operations  0.9 us (1%)
    all_to_all x1, blocking collectives, summed(): lax.all_to_all(parts, chips, 0, 0, tiled=True)  14.6 us
    pallas_call x1, Pallas kernels, project(): pl.pallas_call(koopman_kernel, in_specs=[pl.BlockSpec(memory_space=pltpu....  11.4 us
    all_to_all x1, blocking collectives, summed(): lax.all_to_all(jnp.broadcast_to(mine, parts.shape), chips, 0, 0, tiled=True)  10.8 us
    ppermute x3, starting transfers between devices, passed_along(): lax.ppermute(value, axis, [(source, source + steps) for source in range(f...  7.46 us
    pallas_call x1, Pallas kernels, body(): pl.pallas_call(body_kernel, in_specs=[vmem] * 8, out_specs=vmem, out_shap...  4.53 us
    ppermute x3, waiting for transfers between devices, passed_along(): lax.ppermute(value, axis, [(source, source + steps) for source in range(f...  3.66 us
    pallas_call x1, Pallas kernels, middle_rows(): pl.pallas_call(middle_kernel, in_specs=[hbm] + [vmem] * 5, out_specs=(vme...  2.17 us
    pallas_call x1, Pallas kernels, tail_rows(): pl.pallas_call(tail_kernel, in_specs=[hbm] * 4, out_specs=(vmem,) * 5, ou...  2.16 us
  transfers between devices with their start and end apart: 5, of which 4 were waited for; matrix products, arithmetic and copies ran while one was open for 0% of the time, Pallas kernels for 16%

profile of v18, /device:TPU:0, one launch (start us, length us, event | category | flops | bytes accessed | tf_op | source)
XLA Modules:
  0.0 64.9 jit_solution(17669643157689025729)
XLA Ops:
  0.6 2.2 %shard_map.59 = (bf16[320,256]{1,0:T(8,128)(2,1)S(1)}, bf16[1024,512]{1,0:T(8,128)(2,1)S(1)}, bf16[1024,512]{1,0:T(8,128)(2,1)S(1)}, f32[1,512]{1,0:T(1,128)S(1)}, bf16[1024,256]{1,0:T(8,128)(2,1)S(1)}) custom-call(bf16[4096,512]{1,0:T(8,128)(2,1)} %bitcast.6, bf16[1024,512]{1,0:T(8,128)(2,1)} %bitcast.8, f32[1,512]{1,0:T(1,128)} %bitcast.10, ...), custom_call_target="tpu_custom_call" | custom-call | tf_op jit(solution)/shard_map/pallas_call | solution.py:88
  2.8 4.9 %collective-permute-start = (bf16[320,256]{1,0:T(8,128)(2,1)S(1)}, bf16[320,256]{1,0:T(8,128)(2,1)S(1)}, u32[]{:S(2)}, u32[]{:S(2)}) collective-permute-start(bf16[320,256]{1,0:T(8,128)(2,1)S(1)} %get-tuple-element.26), channel_id=1, source_target_pairs={{0,1},{1,2},{2,3},{3,4},{4,5},{5,6},{6,7},{8,9},{9,10},{10,11},{11... | collective-permute-start | bytes 491528 | tf_op jit(solution)/shard_map/ppermute | solution.py:25
  7.7 1.4 %shard_map.60 = (bf16[512,256]{1,0:T(8,128)(2,1)S(1)}, bf16[256,512]{1,0:T(8,128)(2,1)S(1)}) custom-call(bf16[1024,512]{1,0:T(8,128)(2,1)S(1)} %get-tuple-element.20.near_ref, bf16[1024,512]{1,0:T(8,128)(2,1)S(1)} %get-tuple-element.21.w1_ref, f32[1,512]{1,0:T(1,128)S(1)} %get-tuple-element.22.b1_ref, bf16[1024,256]{1,0:T(8,128)(2,1)S(1)} %get-tuple-element.23.w2_ref), custom_call_target="tpu_custom_call" | custom-call | tf_op jit(solution)/shard_map/pallas_call | solution.py:109
  9.1 1.3 %collective-permute-start.2 = (bf16[512,256]{1,0:T(8,128)(2,1)S(1)}, bf16[512,256]{1,0:T(8,128)(2,1)S(1)}, u32[]{:S(2)}, u32[]{:S(2)}) collective-permute-start(bf16[512,256]{1,0:T(8,128)(2,1)S(1)} %get-tuple-element.27.early_ref), channel_id=1, source_target_pairs={{1,0},{2,1},{3,2},{4,3},{5,4},{6,5},{7,6},{9,8},{10,9},{11,10},{12... | collective-permute-start | bytes 786440 | tf_op jit(solution)/shard_map/ppermute | solution.py:25
  10.4 0.7 %collective-permute-done.halo_ref = bf16[320,256]{1,0:T(8,128)(2,1)S(1)} collective-permute-done((bf16[320,256]{1,0:T(8,128)(2,1)S(1)}, bf16[320,256]{1,0:T(8,128)(2,1)S(1)}, u32[]{:S(2)}, u32[]{:S(2)}) %collective-permute-start) | collective-permute-done | bytes 163872 | tf_op jit(solution)/shard_map/ppermute | solution.py:25
  11.1 1.1 %shard_map.62.head_ref = bf16[512,256]{1,0:T(8,128)(2,1)S(1)} custom-call(bf16[1024,512]{1,0:T(8,128)(2,1)S(1)} %get-tuple-element.20.near_ref, bf16[320,256]{1,0:T(8,128)(2,1)S(1)} %collective-permute-done.halo_ref, bf16[1024,512]{1,0:T(8,128)(2,1)S(1)} %get-tuple-element.21.w1_ref, f32[1,512]{1,0:T(1,128)S(1)} %get-tuple-element.22.b1_ref, ...), custom_call_target="tpu_custom_call" | custom-call | tf_op jit(solution)/shard_map/pallas_call | solution.py:179
  12.2 1.3 %collective-permute-start.1 = (bf16[512,256]{1,0:T(8,128)(2,1)S(1)}, bf16[512,256]{1,0:T(8,128)(2,1)S(1)}, u32[]{:S(2)}, u32[]{:S(2)}) collective-permute-start(bf16[512,256]{1,0:T(8,128)(2,1)S(1)} %shard_map.62.head_ref), channel_id=1, source_target_pairs={{1,0},{2,1},{3,2},{4,3},{5,4},{6,5},{7,6},{9,8},{10,9},{11,10},{12... | collective-permute-start | bytes 786440 | tf_op jit(solution)/shard_map/ppermute | solution.py:25
  13.5 2.2 %shard_map.61 = (bf16[512,256]{1,0:T(8,128)(2,1)S(1)}, bf16[256,512]{1,0:T(8,128)(2,1)S(1)}, bf16[2592,512]{1,0:T(8,128)(2,1)S(1)}) custom-call(bf16[4096,512]{1,0:T(8,128)(2,1)} %bitcast.7, bf16[1024,512]{1,0:T(8,128)(2,1)S(1)} %get-tuple-element.20.near_ref, bf16[256,512]{1,0:T(8,128)(2,1)S(1)} %get-tuple-element.24.before_ref, ...), custom_call_target="tpu_custom_call" | custom-call | tf_op jit(solution)/shard_map/pallas_call | solution.py:148
  15.7 4.5 %shard_map.63.feature_ref = bf16[4096,256]{1,0:T(8,128)(2,1)S(1)} custom-call(bf16[2592,512]{1,0:T(8,128)(2,1)S(1)} %get-tuple-element.25.far_ref, bf16[512,256]{1,0:T(8,128)(2,1)S(1)} %shard_map.62.head_ref, bf16[512,256]{1,0:T(8,128)(2,1)S(1)} %get-tuple-element.27.early_ref, bf16[512,256]{1,0:T(8,128)(2,1)S(1)} %get-tuple-element.28.middle_ref, ...), custom_call_target="tpu_custom_call" | custom-call | tf_op jit(solution)/shard_map/pallas_call | solution.py:208
  20.3 1.2 %shard_map.64 = (f32[256,256]{1,0:T(8,128)S(1)}, f32[256,256]{1,0:T(8,128)S(1)}, f32[8,256]{1,0:T(8,128)S(1)}, bf16[256,1024]{1,0:T(8,128)(2,1)S(1)}) custom-call(bf16[4096,256]{1,0:T(8,128)(2,1)S(1)} %shard_map.63.feature_ref), custom_call_target="tpu_custom_call" | custom-call | tf_op jit(solution)/shard_map/pallas_call | solution.py:248
  21.4 0.0 collective-permute-done.2.ahead_early_ref
  21.4 2.9 %collective-permute-done.1.ahead_head_ref = bf16[512,256]{1,0:T(8,128)(2,1)S(1)} collective-permute-done((bf16[512,256]{1,0:T(8,128)(2,1)S(1)}, bf16[512,256]{1,0:T(8,128)(2,1)S(1)}, u32[]{:S(2)}, u32[]{:S(2)}) %collective-permute-start.1) | collective-permute-done | bytes 262176 | tf_op jit(solution)/shard_map/ppermute | solution.py:25
  24.4 0.4 shard_map.65
  24.8 0.1 collective-permute-start.3
  24.9 1.3 %collective-permute-done.3 = f32[16,1,2176]{2,1,0:T(1,128)S(1)} collective-permute-done((f32[16,1,2176]{2,1,0:T(1,128)S(1)}, f32[16,1,2176]{2,1,0:T(1,128)S(1)}, u32[]{:S(2)}, u32[]{:S(2)}) %collective-permute-start.3) | collective-permute-done | bytes 139296 | tf_op jit(solution)/shard_map/ppermute | solution.py:491
  26.3 0.1 add.3
  26.4 14.6 %all_to_all.10 = f32[16,1,2176]{2,1,0:T(1,128)S(1)} all-to-all(f32[16,1,2176]{2,1,0:T(1,128)S(1)} %add.3), channel_id=1, replica_groups=mesh['x'=2,'core'=2,'tm'=8] {'x','tm'}, dimensions={0} | all-to-all | bytes 278528 | tf_op jit(solution)/shard_map/all_to_all | solution.py:492
  41.0 0.1 reduce_sum.9
  41.1 0.1 broadcast_in_dim.12
  41.2 10.8 %all_to_all.11.mine_ref = f32[16,1,2176]{2,1,0:T(1,128)S(1)} all-to-all(f32[16,1,2176]{2,1,0:T(1,128)S(1)} %broadcast_in_dim.12), channel_id=1, replica_groups=mesh['x'=2,'core'=2,'tm'=8] {'x','tm'}, dimensions={0} | all-to-all | bytes 278528 | tf_op jit(solution)/shard_map/all_to_all | solution.py:493
  52.0 0.0 collective-permute-start.4
  52.0 1.4 %collective-permute-done.4.other_ref = f32[16,1,2176]{2,1,0:T(1,128)S(1)} collective-permute-done((f32[16,1,2176]{2,1,0:T(1,128)S(1)}, f32[16,1,2176]{2,1,0:T(1,128)S(1)}, u32[]{:S(2)}, u32[]{:S(2)}) %collective-permute-start.4) | collective-permute-done | bytes 139296 | tf_op jit(solution)/shard_map/ppermute | solution.py:494
  53.3 11.4 %shard_map.66 = (f32[4096,256]{1,0:T(8,128)}, f32[4096,256]{1,0:T(8,128)}) custom-call(f32[1]{0:T(128)} %constant.0.clone.1.scale_ref, f32[16,1,2176]{2,1,0:T(1,128)S(1)} %all_to_all.11.mine_ref, f32[16,1,2176]{2,1,0:T(1,128)S(1)} %collective-permute-done.4.other_ref, bf16[4096,256]{1,0:T(8,128)(2,1)S(1)} %shard_map.63.feature_ref, ...), custom_call_target="tpu_custom_call" | custom-call | tf_op jit(solution)/shard_map/pallas_call | solution.py:470
Async XLA Ops:
  2.8 8.3 %collective-permute-start = (bf16[320,256]{1,0:T(8,128)(2,1)S(1)}, bf16[320,256]{1,0:T(8,128)(2,1)S(1)}, u32[]{:S(2)}, u32[]{:S(2)}) collective-permute-start(bf16[320,256]{1,0:T(8,128)(2,1)S(1)} %get-tuple-element.26), channel_id=1, source_target_pairs={{0,1},{1,2},{2,3},{3,4},{4,5},{5,6},{6,7},{8,9},{9,10},{10,11},{11... | collective-permute-start | bytes 491528 | tf_op jit(solution)/shard_map/ppermute | solution.py:25
  9.1 12.3 %collective-permute-start.2 = (bf16[512,256]{1,0:T(8,128)(2,1)S(1)}, bf16[512,256]{1,0:T(8,128)(2,1)S(1)}, u32[]{:S(2)}, u32[]{:S(2)}) collective-permute-start(bf16[512,256]{1,0:T(8,128)(2,1)S(1)} %get-tuple-element.27.early_ref), channel_id=1, source_target_pairs={{1,0},{2,1},{3,2},{4,3},{5,4},{6,5},{7,6},{9,8},{10,9},{11,10},{12... | collective-permute-start | bytes 786440 | tf_op jit(solution)/shard_map/ppermute | solution.py:25
  12.2 12.1 %collective-permute-start.1 = (bf16[512,256]{1,0:T(8,128)(2,1)S(1)}, bf16[512,256]{1,0:T(8,128)(2,1)S(1)}, u32[]{:S(2)}, u32[]{:S(2)}) collective-permute-start(bf16[512,256]{1,0:T(8,128)(2,1)S(1)} %shard_map.62.head_ref), channel_id=1, source_target_pairs={{1,0},{2,1},{3,2},{4,3},{5,4},{6,5},{7,6},{9,8},{10,9},{11,10},{12... | collective-permute-start | bytes 786440 | tf_op jit(solution)/shard_map/ppermute | solution.py:25
  24.8 1.4 %collective-permute-start.3 = (f32[16,1,2176]{2,1,0:T(1,128)S(1)}, f32[16,1,2176]{2,1,0:T(1,128)S(1)}, u32[]{:S(2)}, u32[]{:S(2)}) collective-permute-start(f32[16,1,2176]{2,1,0:T(1,128)S(1)} %get-tuple-element.35), channel_id=1, source_target_pairs={{0,8},{8,0},{1,9},{9,1},{2,10},{10,2},{3,11},{11,3},{4,12},{12,4},... | collective-permute-start | bytes 417800 | tf_op jit(solution)/shard_map/ppermute | solution.py:491
  52.0 1.4 %collective-permute-start.4 = (f32[16,1,2176]{2,1,0:T(1,128)S(1)}, f32[16,1,2176]{2,1,0:T(1,128)S(1)}, u32[]{:S(2)}, u32[]{:S(2)}) collective-permute-start(f32[16,1,2176]{2,1,0:T(1,128)S(1)} %all_to_all.11.mine_ref), channel_id=1, source_target_pairs={{0,8},{8,0},{1,9},{9,1},{2,10},{10,2},{3,11},{11,3},{4,12},{12,4},... | collective-permute-start | bytes 417800 | tf_op jit(solution)/shard_map/ppermute | solution.py:494

commit v19 on v18

--- a/solution.py
+++ b/solution.py
@@ -10,6 +10,7 @@
 LAG = 1024
 RIDGE = 0.001
 CHUNK = 512
+PIECE = 256
 EARLY = 1536
 PANEL = 16
 SUPER = 32
@@ -443,13 +444,15 @@
         return jnp.dot(twice, split_ref[index], preferred_element_type=F32) - shift_ref[index][0:1]
 
     copies = []
-    for step in range(rows // CHUNK):
-        here = slice(step * CHUNK, (step + 1) * CHUNK)
-        start = step * CHUNK + LAG
+    for step in range(rows // PIECE):
+        here = slice(step * PIECE, (step + 1) * PIECE)
+        start = step * PIECE + LAG
         if start < rows:
-            later = feature_ref[start : start + CHUNK, :]
+            later = feature_ref[start : start + PIECE, :]
         else:
-            later = (ahead_head_ref if start == rows else ahead_early_ref)[...]
+            ahead_ref = ahead_head_ref if start - rows < LAG // 2 else ahead_early_ref
+            at = (start - rows) % (LAG // 2)
+            later = ahead_ref[at : at + PIECE, :]
         now = image(feature_ref[here, :], 1)
         moved[here, :] = now
         gap = image(later, 0) - now
@@ -479,7 +482,7 @@
             pltpu.VMEM((2, 8, feat), F32),
             pltpu.VMEM((rows, feat), F32),
             pltpu.VMEM((rows, feat), F32),
-            pltpu.SemaphoreType.DMA((2, rows // CHUNK)),
+            pltpu.SemaphoreType.DMA((2, rows // PIECE)),
         ],
         compiler_params=pltpu.CompilerParams(vmem_limit_bytes=32 * MIB),
     )(scale, mine, other, feature, ahead_head, ahead_early)

time: 65.1 us -> 65 us (level)
  no operation moved by 1% of the time
where the time goes in v19:
time: 65 us; the launch traced here: 64.8 us
  blocking collectives  25.4 us (39%)
  Pallas kernels  24.3 us (37%)
  starting transfers between devices  7.54 us (12%)
  waiting for transfers between devices  6.36 us (10%)
  between operations  0.9 us (1%)
    all_to_all x1, blocking collectives, summed(): lax.all_to_all(parts, chips, 0, 0, tiled=True)  14.6 us
    pallas_call x1, Pallas kernels, project(): pl.pallas_call(koopman_kernel, in_specs=[pl.BlockSpec(memory_space=pltpu....  11.3 us
    all_to_all x1, blocking collectives, summed(): lax.all_to_all(jnp.broadcast_to(mine, parts.shape), chips, 0, 0, tiled=True)  10.8 us
    ppermute x3, starting transfers between devices, passed_along(): lax.ppermute(value, axis, [(source, source + steps) for source in range(f...  7.46 us
    pallas_call x1, Pallas kernels, body(): pl.pallas_call(body_kernel, in_specs=[vmem] * 8, out_specs=vmem, out_shap...  4.53 us
    ppermute x3, waiting for transfers between devices, passed_along(): lax.ppermute(value, axis, [(source, source + steps) for source in range(f...  3.66 us
    pallas_call x1, Pallas kernels, middle_rows(): pl.pallas_call(middle_kernel, in_specs=[hbm] + [vmem] * 5, out_specs=(vme...  2.17 us
    pallas_call x1, Pallas kernels, tail_rows(): pl.pallas_call(tail_kernel, in_specs=[hbm] * 4, out_specs=(vmem,) * 5, ou...  2.16 us
  transfers between devices with their start and end apart: 5, of which 4 were waited for; matrix products, arithmetic and copies ran while one was open for 0% of the time, Pallas kernels for 16%

profile of v19, /device:TPU:0, one launch (start us, length us, event | category | flops | bytes accessed | tf_op | source)
XLA Modules:
  0.0 64.8 jit_solution(9923551711552301683)
XLA Ops:
  0.6 2.2 %shard_map.59 = (bf16[320,256]{1,0:T(8,128)(2,1)S(1)}, bf16[1024,512]{1,0:T(8,128)(2,1)S(1)}, bf16[1024,512]{1,0:T(8,128)(2,1)S(1)}, f32[1,512]{1,0:T(1,128)S(1)}, bf16[1024,256]{1,0:T(8,128)(2,1)S(1)}) custom-call(bf16[4096,512]{1,0:T(8,128)(2,1)} %bitcast.6, bf16[1024,512]{1,0:T(8,128)(2,1)} %bitcast.8, f32[1,512]{1,0:T(1,128)} %bitcast.10, ...), custom_call_target="tpu_custom_call" | custom-call | tf_op jit(solution)/shard_map/pallas_call | solution.py:89
  2.8 4.9 %collective-permute-start = (bf16[320,256]{1,0:T(8,128)(2,1)S(1)}, bf16[320,256]{1,0:T(8,128)(2,1)S(1)}, u32[]{:S(2)}, u32[]{:S(2)}) collective-permute-start(bf16[320,256]{1,0:T(8,128)(2,1)S(1)} %get-tuple-element.26), channel_id=1, source_target_pairs={{0,1},{1,2},{2,3},{3,4},{4,5},{5,6},{6,7},{8,9},{9,10},{10,11},{11... | collective-permute-start | bytes 491528 | tf_op jit(solution)/shard_map/ppermute | solution.py:26
  7.7 1.4 %shard_map.60 = (bf16[512,256]{1,0:T(8,128)(2,1)S(1)}, bf16[256,512]{1,0:T(8,128)(2,1)S(1)}) custom-call(bf16[1024,512]{1,0:T(8,128)(2,1)S(1)} %get-tuple-element.20.near_ref, bf16[1024,512]{1,0:T(8,128)(2,1)S(1)} %get-tuple-element.21.w1_ref, f32[1,512]{1,0:T(1,128)S(1)} %get-tuple-element.22.b1_ref, bf16[1024,256]{1,0:T(8,128)(2,1)S(1)} %get-tuple-element.23.w2_ref), custom_call_target="tpu_custom_call" | custom-call | tf_op jit(solution)/shard_map/pallas_call | solution.py:110
  9.1 1.3 %collective-permute-start.2 = (bf16[512,256]{1,0:T(8,128)(2,1)S(1)}, bf16[512,256]{1,0:T(8,128)(2,1)S(1)}, u32[]{:S(2)}, u32[]{:S(2)}) collective-permute-start(bf16[512,256]{1,0:T(8,128)(2,1)S(1)} %get-tuple-element.27.early_ref), channel_id=1, source_target_pairs={{1,0},{2,1},{3,2},{4,3},{5,4},{6,5},{7,6},{9,8},{10,9},{11,10},{12... | collective-permute-start | bytes 786440 | tf_op jit(solution)/shard_map/ppermute | solution.py:26
  10.4 0.7 %collective-permute-done.halo_ref = bf16[320,256]{1,0:T(8,128)(2,1)S(1)} collective-permute-done((bf16[320,256]{1,0:T(8,128)(2,1)S(1)}, bf16[320,256]{1,0:T(8,128)(2,1)S(1)}, u32[]{:S(2)}, u32[]{:S(2)}) %collective-permute-start) | collective-permute-done | bytes 163872 | tf_op jit(solution)/shard_map/ppermute | solution.py:26
  11.1 1.1 %shard_map.62.head_ref = bf16[512,256]{1,0:T(8,128)(2,1)S(1)} custom-call(bf16[1024,512]{1,0:T(8,128)(2,1)S(1)} %get-tuple-element.20.near_ref, bf16[320,256]{1,0:T(8,128)(2,1)S(1)} %collective-permute-done.halo_ref, bf16[1024,512]{1,0:T(8,128)(2,1)S(1)} %get-tuple-element.21.w1_ref, f32[1,512]{1,0:T(1,128)S(1)} %get-tuple-element.22.b1_ref, ...), custom_call_target="tpu_custom_call" | custom-call | tf_op jit(solution)/shard_map/pallas_call | solution.py:180
  12.2 1.3 %collective-permute-start.1 = (bf16[512,256]{1,0:T(8,128)(2,1)S(1)}, bf16[512,256]{1,0:T(8,128)(2,1)S(1)}, u32[]{:S(2)}, u32[]{:S(2)}) collective-permute-start(bf16[512,256]{1,0:T(8,128)(2,1)S(1)} %shard_map.62.head_ref), channel_id=1, source_target_pairs={{1,0},{2,1},{3,2},{4,3},{5,4},{6,5},{7,6},{9,8},{10,9},{11,10},{12... | collective-permute-start | bytes 786440 | tf_op jit(solution)/shard_map/ppermute | solution.py:26
  13.5 2.2 %shard_map.61 = (bf16[512,256]{1,0:T(8,128)(2,1)S(1)}, bf16[256,512]{1,0:T(8,128)(2,1)S(1)}, bf16[2592,512]{1,0:T(8,128)(2,1)S(1)}) custom-call(bf16[4096,512]{1,0:T(8,128)(2,1)} %bitcast.7, bf16[1024,512]{1,0:T(8,128)(2,1)S(1)} %get-tuple-element.20.near_ref, bf16[256,512]{1,0:T(8,128)(2,1)S(1)} %get-tuple-element.24.before_ref, ...), custom_call_target="tpu_custom_call" | custom-call | tf_op jit(solution)/shard_map/pallas_call | solution.py:149
  15.7 4.5 %shard_map.63.feature_ref = bf16[4096,256]{1,0:T(8,128)(2,1)S(1)} custom-call(bf16[2592,512]{1,0:T(8,128)(2,1)S(1)} %get-tuple-element.25.far_ref, bf16[512,256]{1,0:T(8,128)(2,1)S(1)} %shard_map.62.head_ref, bf16[512,256]{1,0:T(8,128)(2,1)S(1)} %get-tuple-element.27.early_ref, bf16[512,256]{1,0:T(8,128)(2,1)S(1)} %get-tuple-element.28.middle_ref, ...), custom_call_target="tpu_custom_call" | custom-call | tf_op jit(solution)/shard_map/pallas_call | solution.py:209
  20.3 1.2 %shard_map.64 = (f32[256,256]{1,0:T(8,128)S(1)}, f32[256,256]{1,0:T(8,128)S(1)}, f32[8,256]{1,0:T(8,128)S(1)}, bf16[256,1024]{1,0:T(8,128)(2,1)S(1)}) custom-call(bf16[4096,256]{1,0:T(8,128)(2,1)S(1)} %shard_map.63.feature_ref), custom_call_target="tpu_custom_call" | custom-call | tf_op jit(solution)/shard_map/pallas_call | solution.py:249
  21.4 0.0 collective-permute-done.2.ahead_early_ref
  21.4 2.9 %collective-permute-done.1.ahead_head_ref = bf16[512,256]{1,0:T(8,128)(2,1)S(1)} collective-permute-done((bf16[512,256]{1,0:T(8,128)(2,1)S(1)}, bf16[512,256]{1,0:T(8,128)(2,1)S(1)}, u32[]{:S(2)}, u32[]{:S(2)}) %collective-permute-start.1) | collective-permute-done | bytes 262176 | tf_op jit(solution)/shard_map/ppermute | solution.py:26
  24.4 0.4 shard_map.65
  24.8 0.1 collective-permute-start.3
  24.9 1.3 %collective-permute-done.3 = f32[16,1,2176]{2,1,0:T(1,128)S(1)} collective-permute-done((f32[16,1,2176]{2,1,0:T(1,128)S(1)}, f32[16,1,2176]{2,1,0:T(1,128)S(1)}, u32[]{:S(2)}, u32[]{:S(2)}) %collective-permute-start.3) | collective-permute-done | bytes 139296 | tf_op jit(solution)/shard_map/ppermute | solution.py:494
  26.3 0.1 add.3
  26.4 14.6 %all_to_all.10 = f32[16,1,2176]{2,1,0:T(1,128)S(1)} all-to-all(f32[16,1,2176]{2,1,0:T(1,128)S(1)} %add.3), channel_id=1, replica_groups=mesh['x'=2,'core'=2,'tm'=8] {'x','tm'}, dimensions={0} | all-to-all | bytes 278528 | tf_op jit(solution)/shard_map/all_to_all | solution.py:495
  41.0 0.1 reduce_sum.9
  41.1 0.1 broadcast_in_dim.12
  41.2 10.8 %all_to_all.11.mine_ref = f32[16,1,2176]{2,1,0:T(1,128)S(1)} all-to-all(f32[16,1,2176]{2,1,0:T(1,128)S(1)} %broadcast_in_dim.12), channel_id=1, replica_groups=mesh['x'=2,'core'=2,'tm'=8] {'x','tm'}, dimensions={0} | all-to-all | bytes 278528 | tf_op jit(solution)/shard_map/all_to_all | solution.py:496
  52.0 0.0 collective-permute-start.4
  52.0 1.4 %collective-permute-done.4.other_ref = f32[16,1,2176]{2,1,0:T(1,128)S(1)} collective-permute-done((f32[16,1,2176]{2,1,0:T(1,128)S(1)}, f32[16,1,2176]{2,1,0:T(1,128)S(1)}, u32[]{:S(2)}, u32[]{:S(2)}) %collective-permute-start.4) | collective-permute-done | bytes 139296 | tf_op jit(solution)/shard_map/ppermute | solution.py:497
  53.3 11.3 %shard_map.66 = (f32[4096,256]{1,0:T(8,128)}, f32[4096,256]{1,0:T(8,128)}) custom-call(f32[1]{0:T(128)} %constant.0.clone.1.scale_ref, f32[16,1,2176]{2,1,0:T(1,128)S(1)} %all_to_all.11.mine_ref, f32[16,1,2176]{2,1,0:T(1,128)S(1)} %collective-permute-done.4.other_ref, bf16[4096,256]{1,0:T(8,128)(2,1)S(1)} %shard_map.63.feature_ref, ...), custom_call_target="tpu_custom_call" | custom-call | tf_op jit(solution)/shard_map/pallas_call | solution.py:473
Async XLA Ops:
  2.8 8.3 %collective-permute-start = (bf16[320,256]{1,0:T(8,128)(2,1)S(1)}, bf16[320,256]{1,0:T(8,128)(2,1)S(1)}, u32[]{:S(2)}, u32[]{:S(2)}) collective-permute-start(bf16[320,256]{1,0:T(8,128)(2,1)S(1)} %get-tuple-element.26), channel_id=1, source_target_pairs={{0,1},{1,2},{2,3},{3,4},{4,5},{5,6},{6,7},{8,9},{9,10},{10,11},{11... | collective-permute-start | bytes 491528 | tf_op jit(solution)/shard_map/ppermute | solution.py:26
  9.1 12.3 %collective-permute-start.2 = (bf16[512,256]{1,0:T(8,128)(2,1)S(1)}, bf16[512,256]{1,0:T(8,128)(2,1)S(1)}, u32[]{:S(2)}, u32[]{:S(2)}) collective-permute-start(bf16[512,256]{1,0:T(8,128)(2,1)S(1)} %get-tuple-element.27.early_ref), channel_id=1, source_target_pairs={{1,0},{2,1},{3,2},{4,3},{5,4},{6,5},{7,6},{9,8},{10,9},{11,10},{12... | collective-permute-start | bytes 786440 | tf_op jit(solution)/shard_map/ppermute | solution.py:26
  12.2 12.1 %collective-permute-start.1 = (bf16[512,256]{1,0:T(8,128)(2,1)S(1)}, bf16[512,256]{1,0:T(8,128)(2,1)S(1)}, u32[]{:S(2)}, u32[]{:S(2)}) collective-permute-start(bf16[512,256]{1,0:T(8,128)(2,1)S(1)} %shard_map.62.head_ref), channel_id=1, source_target_pairs={{1,0},{2,1},{3,2},{4,3},{5,4},{6,5},{7,6},{9,8},{10,9},{11,10},{12... | collective-permute-start | bytes 786440 | tf_op jit(solution)/shard_map/ppermute | solution.py:26
  24.8 1.4 %collective-permute-start.3 = (f32[16,1,2176]{2,1,0:T(1,128)S(1)}, f32[16,1,2176]{2,1,0:T(1,128)S(1)}, u32[]{:S(2)}, u32[]{:S(2)}) collective-permute-start(f32[16,1,2176]{2,1,0:T(1,128)S(1)} %get-tuple-element.35), channel_id=1, source_target_pairs={{0,8},{8,0},{1,9},{9,1},{2,10},{10,2},{3,11},{11,3},{4,12},{12,4},... | collective-permute-start | bytes 417800 | tf_op jit(solution)/shard_map/ppermute | solution.py:494
  52.0 1.4 %collective-permute-start.4 = (f32[16,1,2176]{2,1,0:T(1,128)S(1)}, f32[16,1,2176]{2,1,0:T(1,128)S(1)}, u32[]{:S(2)}, u32[]{:S(2)}) collective-permute-start(f32[16,1,2176]{2,1,0:T(1,128)S(1)} %all_to_all.11.mine_ref), channel_id=1, source_target_pairs={{0,8},{8,0},{1,9},{9,1},{2,10},{10,2},{3,11},{11,3},{4,12},{12,4},... | collective-permute-start | bytes 417800 | tf_op jit(solution)/shard_map/ppermute | solution.py:497

commit v20 on v19

--- a/solution.py
+++ b/solution.py
@@ -511,6 +511,7 @@
     early, before = early_rows(near, *weights)
     ahead_early = passed_along(early, "tm", -1)
     middle, hidden, far = middle_rows(frame_block, near, before, *weights)
+    halo, hidden = lax.optimization_barrier((halo, hidden))
     head = head_rows(near, halo, *weights)
     ahead_head = passed_along(head, "tm", -1)
     feature = body(far, head, early, middle, hidden, *weights)

time: 65 us -> 64.8 us (level)
  transfers between devices with their start and end apart: 5 -> 5, of which waited for: 4 -> 3; matrix products, arithmetic and copies ran while one was open for 0% -> 0% of each run, Pallas kernels for 16% -> 16%
where the time goes in v20:
time: 64.8 us; the launch traced here: 64.6 us
  blocking collectives  25.2 us (39%)
  Pallas kernels  24.3 us (38%)
  starting transfers between devices  7.54 us (12%)
  waiting for transfers between devices  6.35 us (10%)
  between operations  0.9 us (1%)
    all_to_all x1, blocking collectives, summed(): lax.all_to_all(parts, chips, 0, 0, tiled=True)  14.4 us
    pallas_call x1, Pallas kernels, project(): pl.pallas_call(koopman_kernel, in_specs=[pl.BlockSpec(memory_space=pltpu....  11.3 us
    all_to_all x1, blocking collectives, summed(): lax.all_to_all(jnp.broadcast_to(mine, parts.shape), chips, 0, 0, tiled=True)  10.8 us
    ppermute x3, starting transfers between devices, passed_along(): lax.ppermute(value, axis, [(source, source + steps) for source in range(f...  7.46 us
    pallas_call x1, Pallas kernels, body(): pl.pallas_call(body_kernel, in_specs=[vmem] * 8, out_specs=vmem, out_shap...  4.53 us
    ppermute x3, waiting for transfers between devices, passed_along(): lax.ppermute(value, axis, [(source, source + steps) for source in range(f...  3.65 us
    pallas_call x1, Pallas kernels, middle_rows(): pl.pallas_call(middle_kernel, in_specs=[hbm] + [vmem] * 5, out_specs=(vme...  2.17 us
    pallas_call x1, Pallas kernels, tail_rows(): pl.pallas_call(tail_kernel, in_specs=[hbm] * 4, out_specs=(vmem,) * 5, ou...  2.16 us
  transfers between devices with their start and end apart: 5, of which 3 were waited for; matrix products, arithmetic and copies ran while one was open for 0% of the time, Pallas kernels for 16%

profile of v20, /device:TPU:0, one launch (start us, length us, event | category | flops | bytes accessed | tf_op | source)
XLA Modules:
  0.0 64.6 jit_solution(15015445204930436221)
XLA Ops:
  0.6 2.2 %shard_map.59 = (bf16[320,256]{1,0:T(8,128)(2,1)S(1)}, bf16[1024,512]{1,0:T(8,128)(2,1)S(1)}, bf16[1024,512]{1,0:T(8,128)(2,1)S(1)}, f32[1,512]{1,0:T(1,128)S(1)}, bf16[1024,256]{1,0:T(8,128)(2,1)S(1)}) custom-call(bf16[4096,512]{1,0:T(8,128)(2,1)} %bitcast.6, bf16[1024,512]{1,0:T(8,128)(2,1)} %bitcast.8, f32[1,512]{1,0:T(1,128)} %bitcast.10, ...), custom_call_target="tpu_custom_call" | custom-call | tf_op jit(solution)/shard_map/pallas_call | solution.py:89
  2.8 4.9 %collective-permute-start = (bf16[320,256]{1,0:T(8,128)(2,1)S(1)}, bf16[320,256]{1,0:T(8,128)(2,1)S(1)}, u32[]{:S(2)}, u32[]{:S(2)}) collective-permute-start(bf16[320,256]{1,0:T(8,128)(2,1)S(1)} %get-tuple-element.28), channel_id=1, source_target_pairs={{0,1},{1,2},{2,3},{3,4},{4,5},{5,6},{6,7},{8,9},{9,10},{10,11},{11... | collective-permute-start | bytes 491528 | tf_op jit(solution)/shard_map/ppermute | solution.py:26
  7.7 1.4 %shard_map.60 = (bf16[512,256]{1,0:T(8,128)(2,1)S(1)}, bf16[256,512]{1,0:T(8,128)(2,1)S(1)}) custom-call(bf16[1024,512]{1,0:T(8,128)(2,1)S(1)} %get-tuple-element.22.near_ref, bf16[1024,512]{1,0:T(8,128)(2,1)S(1)} %get-tuple-element.23.w1_ref, f32[1,512]{1,0:T(1,128)S(1)} %get-tuple-element.24.b1_ref, bf16[1024,256]{1,0:T(8,128)(2,1)S(1)} %get-tuple-element.25.w2_ref), custom_call_target="tpu_custom_call" | custom-call | tf_op jit(solution)/shard_map/pallas_call | solution.py:110
  9.1 1.3 %collective-permute-start.2 = (bf16[512,256]{1,0:T(8,128)(2,1)S(1)}, bf16[512,256]{1,0:T(8,128)(2,1)S(1)}, u32[]{:S(2)}, u32[]{:S(2)}) collective-permute-start(bf16[512,256]{1,0:T(8,128)(2,1)S(1)} %get-tuple-element.31.early_ref), channel_id=1, source_target_pairs={{1,0},{2,1},{3,2},{4,3},{5,4},{6,5},{7,6},{9,8},{10,9},{11,10},{12... | collective-permute-start | bytes 786440 | tf_op jit(solution)/shard_map/ppermute | solution.py:26
  10.4 2.2 %shard_map.61 = (bf16[512,256]{1,0:T(8,128)(2,1)S(1)}, bf16[256,512]{1,0:T(8,128)(2,1)S(1)}, bf16[2592,512]{1,0:T(8,128)(2,1)S(1)}) custom-call(bf16[4096,512]{1,0:T(8,128)(2,1)} %bitcast.7, bf16[1024,512]{1,0:T(8,128)(2,1)S(1)} %get-tuple-element.22.near_ref, bf16[256,512]{1,0:T(8,128)(2,1)S(1)} %get-tuple-element.26.before_ref, ...), custom_call_target="tpu_custom_call" | custom-call | tf_op jit(solution)/shard_map/pallas_call | solution.py:149
  12.6 0.0 collective-permute-done.halo_ref
  12.6 1.1 %shard_map.62.head_ref = bf16[512,256]{1,0:T(8,128)(2,1)S(1)} custom-call(bf16[1024,512]{1,0:T(8,128)(2,1)S(1)} %get-tuple-element.22.near_ref, bf16[320,256]{1,0:T(8,128)(2,1)S(1)} %collective-permute-done.halo_ref, bf16[1024,512]{1,0:T(8,128)(2,1)S(1)} %get-tuple-element.23.w1_ref, f32[1,512]{1,0:T(1,128)S(1)} %get-tuple-element.24.b1_ref, ...), custom_call_target="tpu_custom_call" | custom-call | tf_op jit(solution)/shard_map/pallas_call | solution.py:180
  13.7 1.3 %collective-permute-start.1 = (bf16[512,256]{1,0:T(8,128)(2,1)S(1)}, bf16[512,256]{1,0:T(8,128)(2,1)S(1)}, u32[]{:S(2)}, u32[]{:S(2)}) collective-permute-start(bf16[512,256]{1,0:T(8,128)(2,1)S(1)} %shard_map.62.head_ref), channel_id=1, source_target_pairs={{1,0},{2,1},{3,2},{4,3},{5,4},{6,5},{7,6},{9,8},{10,9},{11,10},{12... | collective-permute-start | bytes 786440 | tf_op jit(solution)/shard_map/ppermute | solution.py:26
  15.0 4.5 %shard_map.63.feature_ref = bf16[4096,256]{1,0:T(8,128)(2,1)S(1)} custom-call(bf16[2592,512]{1,0:T(8,128)(2,1)S(1)} %get-tuple-element.27.far_ref, bf16[512,256]{1,0:T(8,128)(2,1)S(1)} %shard_map.62.head_ref, bf16[512,256]{1,0:T(8,128)(2,1)S(1)} %get-tuple-element.31.early_ref, bf16[512,256]{1,0:T(8,128)(2,1)S(1)} %get-tuple-element.32.middle_ref, ...), custom_call_target="tpu_custom_call" | custom-call | tf_op jit(solution)/shard_map/pallas_call | solution.py:209
  19.6 1.2 %shard_map.64 = (f32[256,256]{1,0:T(8,128)S(1)}, f32[256,256]{1,0:T(8,128)S(1)}, f32[8,256]{1,0:T(8,128)S(1)}, bf16[256,1024]{1,0:T(8,128)(2,1)S(1)}) custom-call(bf16[4096,256]{1,0:T(8,128)(2,1)S(1)} %shard_map.63.feature_ref), custom_call_target="tpu_custom_call" | custom-call | tf_op jit(solution)/shard_map/pallas_call | solution.py:249
  20.7 0.0 collective-permute-done.2.ahead_early_ref
  20.7 3.6 %collective-permute-done.1.ahead_head_ref = bf16[512,256]{1,0:T(8,128)(2,1)S(1)} collective-permute-done((bf16[512,256]{1,0:T(8,128)(2,1)S(1)}, bf16[512,256]{1,0:T(8,128)(2,1)S(1)}, u32[]{:S(2)}, u32[]{:S(2)}) %collective-permute-start.1) | collective-permute-done | bytes 262176 | tf_op jit(solution)/shard_map/ppermute | solution.py:26
  24.4 0.4 shard_map.65
  24.8 0.1 collective-permute-start.3
  24.9 1.3 %collective-permute-done.3 = f32[16,1,2176]{2,1,0:T(1,128)S(1)} collective-permute-done((f32[16,1,2176]{2,1,0:T(1,128)S(1)}, f32[16,1,2176]{2,1,0:T(1,128)S(1)}, u32[]{:S(2)}, u32[]{:S(2)}) %collective-permute-start.3) | collective-permute-done | bytes 139296 | tf_op jit(solution)/shard_map/ppermute | solution.py:494
  26.3 0.1 add.3
  26.4 14.4 %all_to_all.10 = f32[16,1,2176]{2,1,0:T(1,128)S(1)} all-to-all(f32[16,1,2176]{2,1,0:T(1,128)S(1)} %add.3), channel_id=1, replica_groups=mesh['x'=2,'core'=2,'tm'=8] {'x','tm'}, dimensions={0} | all-to-all | bytes 278528 | tf_op jit(solution)/shard_map/all_to_all | solution.py:495
  40.8 0.1 reduce_sum.9
  40.9 0.1 broadcast_in_dim.12
  41.0 10.8 %all_to_all.11.mine_ref = f32[16,1,2176]{2,1,0:T(1,128)S(1)} all-to-all(f32[16,1,2176]{2,1,0:T(1,128)S(1)} %broadcast_in_dim.12), channel_id=1, replica_groups=mesh['x'=2,'core'=2,'tm'=8] {'x','tm'}, dimensions={0} | all-to-all | bytes 278528 | tf_op jit(solution)/shard_map/all_to_all | solution.py:496
  51.8 0.0 collective-permute-start.4
  51.8 1.4 %collective-permute-done.4.other_ref = f32[16,1,2176]{2,1,0:T(1,128)S(1)} collective-permute-done((f32[16,1,2176]{2,1,0:T(1,128)S(1)}, f32[16,1,2176]{2,1,0:T(1,128)S(1)}, u32[]{:S(2)}, u32[]{:S(2)}) %collective-permute-start.4) | collective-permute-done | bytes 139296 | tf_op jit(solution)/shard_map/ppermute | solution.py:497
  53.1 11.3 %shard_map.66 = (f32[4096,256]{1,0:T(8,128)}, f32[4096,256]{1,0:T(8,128)}) custom-call(f32[1]{0:T(128)} %constant.0.clone.1.scale_ref, f32[16,1,2176]{2,1,0:T(1,128)S(1)} %all_to_all.11.mine_ref, f32[16,1,2176]{2,1,0:T(1,128)S(1)} %collective-permute-done.4.other_ref, bf16[4096,256]{1,0:T(8,128)(2,1)S(1)} %shard_map.63.feature_ref, ...), custom_call_target="tpu_custom_call" | custom-call | tf_op jit(solution)/shard_map/pallas_call | solution.py:473
Async XLA Ops:
  2.8 9.8 %collective-permute-start = (bf16[320,256]{1,0:T(8,128)(2,1)S(1)}, bf16[320,256]{1,0:T(8,128)(2,1)S(1)}, u32[]{:S(2)}, u32[]{:S(2)}) collective-permute-start(bf16[320,256]{1,0:T(8,128)(2,1)S(1)} %get-tuple-element.28), channel_id=1, source_target_pairs={{0,1},{1,2},{2,3},{3,4},{4,5},{5,6},{6,7},{8,9},{9,10},{10,11},{11... | collective-permute-start | bytes 491528 | tf_op jit(solution)/shard_map/ppermute | solution.py:26
  9.1 11.6 %collective-permute-start.2 = (bf16[512,256]{1,0:T(8,128)(2,1)S(1)}, bf16[512,256]{1,0:T(8,128)(2,1)S(1)}, u32[]{:S(2)}, u32[]{:S(2)}) collective-permute-start(bf16[512,256]{1,0:T(8,128)(2,1)S(1)} %get-tuple-element.31.early_ref), channel_id=1, source_target_pairs={{1,0},{2,1},{3,2},{4,3},{5,4},{6,5},{7,6},{9,8},{10,9},{11,10},{12... | collective-permute-start | bytes 786440 | tf_op jit(solution)/shard_map/ppermute | solution.py:26
  13.7 10.7 %collective-permute-start.1 = (bf16[512,256]{1,0:T(8,128)(2,1)S(1)}, bf16[512,256]{1,0:T(8,128)(2,1)S(1)}, u32[]{:S(2)}, u32[]{:S(2)}) collective-permute-start(bf16[512,256]{1,0:T(8,128)(2,1)S(1)} %shard_map.62.head_ref), channel_id=1, source_target_pairs={{1,0},{2,1},{3,2},{4,3},{5,4},{6,5},{7,6},{9,8},{10,9},{11,10},{12... | collective-permute-start | bytes 786440 | tf_op jit(solution)/shard_map/ppermute | solution.py:26
  24.8 1.4 %collective-permute-start.3 = (f32[16,1,2176]{2,1,0:T(1,128)S(1)}, f32[16,1,2176]{2,1,0:T(1,128)S(1)}, u32[]{:S(2)}, u32[]{:S(2)}) collective-permute-start(f32[16,1,2176]{2,1,0:T(1,128)S(1)} %get-tuple-element.39), channel_id=1, source_target_pairs={{0,8},{8,0},{1,9},{9,1},{2,10},{10,2},{3,11},{11,3},{4,12},{12,4},... | collective-permute-start | bytes 417800 | tf_op jit(solution)/shard_map/ppermute | solution.py:494
  51.8 1.4 %collective-permute-start.4 = (f32[16,1,2176]{2,1,0:T(1,128)S(1)}, f32[16,1,2176]{2,1,0:T(1,128)S(1)}, u32[]{:S(2)}, u32[]{:S(2)}) collective-permute-start(f32[16,1,2176]{2,1,0:T(1,128)S(1)} %all_to_all.11.mine_ref), channel_id=1, source_target_pairs={{0,8},{8,0},{1,9},{9,1},{2,10},{10,2},{3,11},{11,3},{4,12},{12,4},... | collective-permute-start | bytes 417800 | tf_op jit(solution)/shard_map/ppermute | solution.py:497
